TPU v7x, 32 devices: a whole 2x2x4 slice. The times are simulated.
32 devices in a mesh: elem: 8 (over z, y), pts: 4 (over x, core).
Axes of the slice: x: 2, y: 2, z: 4, core: 2. Of those that a mesh axis runs over, the one named last changes fastest.
Arguments:
- basis: float32 [32, 2048, 256], P('elem', 'pts'), may hold values from -6 to 6
- applied: float32 [32, 2048, 256], P('elem', 'pts'), may hold values from -6 to 6
- quad: float32 [32, 2048], P('elem', 'pts'), may hold values from 0.00034526698 to 0.0013810679
- face_index: int32 [32, 4, 256], P('elem', None, 'pts'), may hold values from 0 to 511
- face_pairing: int32 [32, 256], P('elem', 'pts'), may hold values from 0 to 63, as said below
- orbitals: float32 [8192, 2048], P('elem', 'pts'), may hold values from -6 to 6
Outputs:
- filtered: float32 [8192, 2048], P('elem', 'pts')
Inputs may be any that keep to these rules, and one draw needn't show every extreme that they name: `face_pairing`: each aligned block of 64 entries of a row is a permutation of 0 to 63.
All inputs are finite; a program needn't handle non-finite values.
Results may differ from a plain program's by a relative error of at most 0.0003.
Values sent between devices are 32-bit elements; how exact they have to be, the bound alone decides.
No kernel may reach another device: no remote copies, remote signals or barrier semaphores. Data moves between devices by JAX's collectives and lax.ppermute only.
A program may use at most 64 MiB of HBM per device.

v0:
```python
import functools

import jax
import jax.numpy as jnp
from jax import lax
from jax.experimental import pallas as pl
from jax.experimental.pallas import tpu as pltpu
from jax.sharding import PartitionSpec as P

NB = 256
DEG = 4

penalty = 3.0
center = 4.0
half_width = 12.0

PARAMS = pltpu.CompilerParams(vmem_limit_bytes=40 * 1024 * 1024)
NN = (((1,), (0,)), ((), ()))
NT = (((1,), (1,)), ((), ()))


def split(value):
    high = value.astype(jnp.bfloat16)
    low = (value - high.astype(jnp.float32)).astype(jnp.bfloat16)
    return high, low


def dot(first, second, dims=NN):
    return lax.dot_general(first, second, dims, preferred_element_type=jnp.float32)


def dot3(first, second, dims=NN):
    first_high, first_low = first
    second_high, second_low = second
    return dot(first_high, second_high, dims) + (dot(first_high, second_low, dims) + dot(first_low, second_high, dims))


def picked(parts, chosen):
    return dot(parts[0], chosen) + dot(parts[1], chosen)


def one_hot(index_row, rows, offset=0):
    at = lax.broadcasted_iota(jnp.int32, (rows, index_row.shape[1]), 0) - offset
    return (at == index_row).astype(jnp.float32).astype(jnp.bfloat16)


def edge_kernel(index_ref, basis_ref, traces_ref):
    parts = split(basis_ref[0].T)
    traces_ref[...] = picked(parts, one_hot(index_ref[0], basis_ref.shape[1]))


def volume_kernel(faces_total, index_ref, quad_ref, basis_ref, applied_ref, traces_ref, volume_ref):
    flipped = basis_ref[0].T
    traces = picked(split(flipped), one_hot(index_ref[0], basis_ref.shape[1]))
    traces_ref[0] = traces
    width = traces.shape[1] // 2
    outer, layer = traces[:, :width], traces[:, width:]
    total = dot3(split(flipped * quad_ref[0]), split(applied_ref[0]))
    total = total + dot3(split((2.0 * outer + layer) * (1.0 / faces_total)), split(outer), NT)
    volume_ref[0] = 0.5 * (total + total.T)


def coupling_kernel(faces_total, count, pair_ref, own_ref, next_ref, lead_ref, coupling_ref):
    step = pl.program_id(0)
    own = own_ref[0]
    width = own.shape[1] // 2
    outer, layer = own[:, :width], own[:, width:]
    near = split((penalty * outer + 0.5 * layer) * (-1.0 / faces_total))
    far = split(outer * (0.5 / faces_total))

    def finish(face, inside):
        coupling_ref[0] = dot3(near, split(face), NT) + dot3(far, split(inside), NT)

    @pl.when(step < count - 1)
    def _():
        order = one_hot(pair_ref[0], width)
        following = next_ref[0]
        finish(picked(split(following[:, :width]), order), picked(split(following[:, width:]), order))

    @pl.when(step == count - 1)
    def _():
        lead = split(lead_ref[...])
        finish(picked(lead, one_hot(pair_ref[0], width)), picked(lead, one_hot(pair_ref[0], width, width // 2)))


def weights_kernel(volume_ref, coupling_ref, earlier_ref, before_ref, high_ref, low_ref):
    step = pl.program_id(0)
    size = volume_ref.shape[1]
    diagonal = lax.broadcasted_iota(jnp.int32, (size, size), 0) == lax.broadcasted_iota(jnp.int32, (size, size), 1)
    own = (volume_ref[0] - jnp.where(diagonal, center, 0.0)) * (1.0 / half_width)
    earlier = jnp.where(step == 0, before_ref[0], earlier_ref[0])
    for at, value in enumerate((earlier.T, own, coupling_ref[0])):
        high, low = split(value * (1.0 / half_width) if at != 1 else value)
        high_ref[0, :, at * size : (at + 1) * size] = high
        low_ref[0, :, at * size : (at + 1) * size] = low


def apply_row(high, low, below, middle, above):
    total = None
    size = middle.shape[0]
    for at, value in enumerate((below, middle, above)):
        value_high, value_low = split(value)
        part_high, part_low = high[:, at * size : (at + 1) * size], low[:, at * size : (at + 1) * size]
        term = dot3((part_high, part_low), (value_high, value_low))
        total = term if total is None else total + term
    return total


def advance(first, result, before):
    return result if first else 2.0 * result - before


def ends_kernel(first, count, high0, low0, high1, low1, ends, inner, below, above, before, out):
    row = apply_row(high0[0], low0[0], below[0], ends[0], inner[0])
    out[0] = advance(first, row, None if first else before[0])
    row = apply_row(high1[0], low1[0], inner[count - 3], ends[1], above[0])
    out[1] = advance(first, row, None if first else before[1])


def inner_kernel(first, count, high, low, ends, inner, before, out):
    for at in range(1, count - 1):
        lower = ends[0] if at == 1 else inner[at - 2]
        upper = ends[1] if at == count - 2 else inner[at]
        row = apply_row(high[at], low[at], lower, inner[at - 1], upper)
        out[at - 1] = advance(first, row, None if first else before[at - 1])


def whole(shape):
    return pl.BlockSpec(shape, lambda *steps: (0,) * len(shape))


def edge_traces(index, basis):
    points, size = basis.shape[1:]
    return pl.pallas_call(
        edge_kernel,
        grid=(1,),
        in_specs=[pl.BlockSpec((1, 1, index.shape[2]), lambda s: (0, 0, 0)), pl.BlockSpec((1, points, size), lambda s: (0, 0, 0))],
        out_specs=whole((size, index.shape[2])),
        out_shape=jax.ShapeDtypeStruct((size, index.shape[2]), jnp.float32),
        compiler_params=PARAMS,
    )(index, basis)


def volumes(index, quad, basis, applied, faces_total):
    count, points, size = basis.shape
    spots = index.shape[2]
    per = lambda *shape: pl.BlockSpec((1, *shape), lambda s: (s, 0, 0))
    return pl.pallas_call(
        functools.partial(volume_kernel, faces_total),
        grid=(count,),
        in_specs=[per(1, spots), per(1, points), per(points, size), per(points, size)],
        out_specs=[per(size, spots), per(size, size)],
        out_shape=[
            jax.ShapeDtypeStruct((count, size, spots), jnp.float32),
            jax.ShapeDtypeStruct((count, size, size), jnp.float32),
        ],
        compiler_params=PARAMS,
    )(index, quad, basis, applied)


def couplings(pairs, traces, lead, faces_total):
    count, size, spots = traces.shape
    per = lambda *shape: pl.BlockSpec((1, *shape), lambda s: (s, 0, 0))
    return pl.pallas_call(
        functools.partial(coupling_kernel, faces_total, count),
        grid=(count,),
        in_specs=[
            per(1, pairs.shape[2]),
            per(size, spots),
            pl.BlockSpec((1, size, spots), lambda s: (jnp.minimum(s + 1, count - 1), 0, 0)),
            whole(lead.shape),
        ],
        out_specs=per(size, size),
        out_shape=jax.ShapeDtypeStruct((count, size, size), jnp.float32),
        compiler_params=PARAMS,
    )(pairs, traces, traces, lead)


def weights(volume, coupling, before):
    count, size, _ = volume.shape
    per = lambda *shape: pl.BlockSpec((1, *shape), lambda s: (s, 0, 0))
    return pl.pallas_call(
        weights_kernel,
        grid=(count,),
        in_specs=[
            per(size, size),
            per(size, size),
            pl.BlockSpec((1, size, size), lambda s: (jnp.maximum(s - 1, 0), 0, 0)),
            whole(before.shape),
        ],
        out_specs=[per(size, 3 * size), per(size, 3 * size)],
        out_shape=[jax.ShapeDtypeStruct((count, size, 3 * size), jnp.bfloat16)] * 2,
        compiler_params=PARAMS,
    )(volume, coupling, coupling, before)


def chunk_of(columns):
    return 256 if columns % 256 == 0 else columns


def apply_ends(first, high, low, ends, inner, below, above, before):
    count, size, depth = high.shape
    columns = ends.shape[2]
    chunk = chunk_of(columns)
    part = lambda n: pl.BlockSpec((n, size, chunk), lambda s: (0, 0, s))
    head = pl.BlockSpec((1, size, depth), lambda s: (0, 0, 0))
    tail = pl.BlockSpec((1, size, depth), lambda s: (count - 1, 0, 0))
    return pl.pallas_call(
        functools.partial(ends_kernel, first, count),
        grid=(columns // chunk,),
        in_specs=[head, head, tail, tail, part(2), part(count - 2), part(1), part(1), part(2)],
        out_specs=part(2),
        out_shape=jax.ShapeDtypeStruct((2, size, columns), jnp.float32),
        compiler_params=PARAMS,
    )(high, low, high, low, ends, inner, below, above, before)


def apply_inner(first, high, low, ends, inner, before):
    count, size, depth = high.shape
    columns = ends.shape[2]
    chunk = chunk_of(columns)
    part = lambda n: pl.BlockSpec((n, size, chunk), lambda s: (0, 0, s))
    return pl.pallas_call(
        functools.partial(inner_kernel, first, count),
        grid=(columns // chunk,),
        in_specs=[whole(high.shape), whole(low.shape), part(2), part(count - 2), part(count - 2)],
        out_specs=part(count - 2),
        out_shape=jax.ShapeDtypeStruct((count - 2, size, columns), jnp.float32),
        compiler_params=PARAMS,
    )(high, low, ends, inner, before)


def flipped(value, axis, bit):
    count = lax.axis_size(axis)
    return lax.ppermute(value, axis, [(i, i ^ bit) for i in range(count)])


def shifted(value, axis, steps):
    count = lax.axis_size(axis)
    return lax.ppermute(value, axis, [(i, (i + steps) % count) for i in range(count)])


def summed_half(value, core):
    half = value.shape[0] // 2
    send = lax.dynamic_slice_in_dim(value, (1 - core) * half, half)
    keep = lax.dynamic_slice_in_dim(value, core * half, half)
    keep = keep + flipped(send, "pts", 1)
    bit = 2
    while bit < lax.axis_size("pts"):
        keep = keep + flipped(keep, "pts", bit)
        bit *= 2
    return keep


def both_halves(value, core):
    other = flipped(value, "pts", 1)
    return jnp.where(core == 0, jnp.concatenate([value, other]), jnp.concatenate([other, value]))


def body(basis, applied, quad, face_index, face_pairing, orbitals):
    count, points, size = basis.shape
    spots = face_index.shape[2]
    columns = orbitals.shape[1]
    faces_total = float(spots * lax.axis_size("pts"))
    core = lax.axis_index("pts") % 2

    vector = orbitals.reshape(count, size, columns)
    ends = jnp.concatenate([vector[:1], vector[-1:]])
    inner = vector[1:-1]
    below = shifted(vector[-1:], "elem", 1)
    above = shifted(vector[:1], "elem", -1)

    lead_index = face_index[:1, 0:2].reshape(1, 1, 2 * spots)
    lead = shifted(edge_traces(lead_index, basis), "elem", -1)
    index = jnp.stack([face_index[:, 0], face_index[:, 2], face_index[:, 1], face_index[:, 3]], axis=1)
    index = index.reshape(count, 1, 4 * spots)
    pairs = jnp.concatenate([jnp.full_like(face_pairing, -points), face_pairing], axis=1).reshape(count, 1, 2 * spots)
    traces, volume = volumes(index, quad.reshape(count, 1, points), basis, applied, faces_total)
    coupling = couplings(pairs, traces, lead, faces_total)
    volume = both_halves(summed_half(volume, core), core)
    coupling = both_halves(summed_half(coupling, core), core)
    before = shifted(coupling[-1:], "elem", 1)
    high, low = weights(volume, coupling, before)

    old_ends, old_inner = ends, inner
    for degree in range(DEG):
        first = degree == 0
        new_inner = apply_inner(first, high, low, ends, inner, old_inner)
        new_ends = apply_ends(first, high, low, ends, inner, below, above, old_ends)
        old_ends, old_inner, ends, inner = ends, inner, new_ends, new_inner
        if degree < DEG - 1:
            below = shifted(ends[1:], "elem", 1)
            above = shifted(ends[:1], "elem", -1)
    result = jnp.concatenate([ends[:1], inner, ends[1:]])
    return result.reshape(count * size, columns)


def solution(mesh):
    return jax.shard_map(
        body,
        mesh=mesh,
        in_specs=(
            P("elem", "pts", None),
            P("elem", "pts", None),
            P("elem", "pts"),
            P("elem", None, "pts"),
            P("elem", "pts"),
            P("elem", "pts"),
        ),
        out_specs=P("elem", "pts"),
        check_vma=False,
    )
```

profile of v0, /device:TPU:0, one launch (start us, length us, event | category | flops | bytes accessed | tf_op | source)
XLA Modules:
  0.0 161.9 jit_solution(17706752873775581430)
XLA Ops:
  0.8 1.6 copy-done
  2.8 6.1 %collective-permute-start.3 = (f32[256,128]{1,0:T(8,128)S(1)}, f32[256,128]{1,0:T(8,128)S(1)}, u32[]{:S(2)}, u32[]{:S(2)}) collective-permute-start(f32[256,128]{1,0:T(8,128)S(1)} %shard_map.65), channel_id=1, source_target_pairs={{0,28},{4,0},{8,4},{12,8},{16,12},{20,16},{24,20},{28,24},{1,29},{... | collective-permute-start | bytes 393224 | tf_op jit(solution)/shard_map/ppermute | solution.py:240
  9.1 1.6 copy-done.2
  10.7 3.6 %shard_map.64 = (f32[4,256,256]{2,1,0:T(8,128)S(1)}, f32[4,256,256]{2,1,0:T(8,128)S(1)}) custom-call(s32[4,1,256]{2,1,0:T(1,128)S(1)} %reshape.19.index_ref, f32[4,1,512]{2,1,0:T(1,128)S(1)} %reshape.20.quad_ref, f32[4,512,256]{2,1,0:T(8,128)S(1)} %copy-done.1, f32[4,512,256]{2,1,0:T(8,128)S(1)} %copy-done.2), custom_call_target="tpu_custom_call" | custom-call | tf_op jit(solution)/shard_map/pallas_call | solution.py:148
  14.3 2.6 %shard_map.66 = f32[4,256,256]{2,1,0:T(8,128)S(1)} custom-call(s32[4,1,128]{2,1,0:T(1,128)S(1)} %bitcast.11, f32[4,256,256]{2,1,0:T(8,128)S(1)} %get-tuple-element.10.own_ref.next_ref, f32[4,256,256]{2,1,0:T(8,128)S(1)} %get-tuple-element.10.own_ref.next_ref, f32[256,128]{1,0:T(8,128)S(1)} %collective-permute-done.3.lead_ref), custom_call_target="tpu_custom_call" | custom-call | tf_op jit(solution)/shard_map/pallas_call | solution.py:164
  16.9 0.9 constant_dynamic-slice_fusion
  20.0 1.6 collective-permute-start.5
  21.6 0.9 collective-permute-start.1
  22.5 12.3 %collective-permute-done.5 = f32[2,256,256]{2,1,0:T(8,128)S(1)} collective-permute-done((f32[2,256,256]{2,1,0:T(8,128)S(1)}, f32[2,256,256]{2,1,0:T(8,128)S(1)}, u32[]{:S(2)}, u32[]{:S(2)}) %collective-permute-start.5) | collective-permute-done | bytes 524320 | tf_op jit(solution)/shard_map/ppermute | solution.py:235
  35.0 10.3 %collective-permute-done.1 = f32[2,256,256]{2,1,0:T(8,128)S(1)} collective-permute-done((f32[2,256,256]{2,1,0:T(8,128)S(1)}, f32[2,256,256]{2,1,0:T(8,128)S(1)}, u32[]{:S(2)}, u32[]{:S(2)}) %collective-permute-start.1) | collective-permute-done | bytes 524320 | tf_op jit(solution)/shard_map/ppermute | solution.py:235
  45.5 2.5 %collective-permute-start.9 = (f32[1,256,512]{2,1,0:T(8,128)S(1)}, f32[1,256,512]{2,1,0:T(8,128)S(1)}, u32[]{:S(2)}, u32[]{:S(2)}) collective-permute-start(f32[1,256,512]{2,1,0:T(8,128)S(1)} %get-tuple-element.13), channel_id=1, source_target_pairs={{0,28},{4,0},{8,4},{12,8},{16,12},{20,16},{24,20},{28,24},{1,29},{... | collective-permute-start | bytes 1572872 | tf_op jit(solution)/shard_map/ppermute | solution.py:240
  48.0 1.3 slice.72
  49.3 1.3 maximum_select_fusion.1.coupling_ref.earlier_ref
  50.8 1.3 maximum_select_fusion.volume_ref
  52.1 20.9 %collective-permute-done.7.before_ref = f32[1,256,256]{2,1,0:T(8,128)S(1)} collective-permute-done((f32[1,256,256]{2,1,0:T(8,128)S(1)}, f32[1,256,256]{2,1,0:T(8,128)S(1)}, u32[]{:S(2)}, u32[]{:S(2)}) %collective-permute-start.7) | collective-permute-done | bytes 262176 | tf_op jit(solution)/shard_map/ppermute | solution.py:240
  73.0 1.1 shard_map.67
  74.1 2.6 %collective-permute-done.9.above = f32[1,256,512]{2,1,0:T(8,128)S(1)} collective-permute-done((f32[1,256,512]{2,1,0:T(8,128)S(1)}, f32[1,256,512]{2,1,0:T(8,128)S(1)}, u32[]{:S(2)}, u32[]{:S(2)}) %collective-permute-start.9) | collective-permute-done | bytes 524320 | tf_op jit(solution)/shard_map/ppermute | solution.py:240
  76.7 1.9 %shard_map.68.ends.before = f32[2,256,512]{2,1,0:T(8,128)S(1)} custom-call(bf16[4,256,768]{2,1,0:T(8,128)(2,1)S(1)} %get-tuple-element.11.high0.high1.high, bf16[4,256,768]{2,1,0:T(8,128)(2,1)S(1)} %get-tuple-element.12.low0.low1.low, bf16[4,256,768]{2,1,0:T(8,128)(2,1)S(1)} %get-tuple-element.11.high0.high1.high, ...), custom_call_target="tpu_custom_call" | custom-call | tf_op jit(solution)/shard_map/pallas_call | solution.py:208
  78.7 3.7 %collective-permute-start.11 = (f32[1,256,512]{2,1,0:T(8,128)S(1)}, f32[1,256,512]{2,1,0:T(8,128)S(1)}, u32[]{:S(2)}, u32[]{:S(2)}) collective-permute-start(f32[1,256,512]{2,1,0:T(8,128)S(1)} %get-tuple-element.21), channel_id=1, source_target_pairs={{0,28},{4,0},{8,4},{12,8},{16,12},{20,16},{24,20},{28,24},{1,29},{... | collective-permute-start | bytes 1572872 | tf_op jit(solution)/shard_map/ppermute | solution.py:240
  82.4 1.8 %shard_map.69.inner.before = f32[2,256,512]{2,1,0:T(8,128)S(1)} custom-call(bf16[4,256,768]{2,1,0:T(8,128)(2,1)S(1)} %get-tuple-element.11.high0.high1.high, bf16[4,256,768]{2,1,0:T(8,128)(2,1)S(1)} %get-tuple-element.12.low0.low1.low, f32[2,256,512]{2,1,0:T(8,128)S(1)} %pad_maximum_fusion.1.ends.before, f32[2,256,512]{2,1,0:T(8,128)S(1)} %bitcast.8, ...), custom_call_target="tpu_custom_call" | custom-call | tf_op jit(solution)/shard_map/pallas_call | solution.py:223
  84.3 19.3 %collective-permute-done.11.above = f32[1,256,512]{2,1,0:T(8,128)S(1)} collective-permute-done((f32[1,256,512]{2,1,0:T(8,128)S(1)}, f32[1,256,512]{2,1,0:T(8,128)S(1)}, u32[]{:S(2)}, u32[]{:S(2)}) %collective-permute-start.11) | collective-permute-done | bytes 524320 | tf_op jit(solution)/shard_map/ppermute | solution.py:240
  103.5 2.0 %shard_map.70.ends.before = f32[2,256,512]{2,1,0:T(8,128)S(1)} custom-call(bf16[4,256,768]{2,1,0:T(8,128)(2,1)S(1)} %get-tuple-element.11.high0.high1.high, bf16[4,256,768]{2,1,0:T(8,128)(2,1)S(1)} %get-tuple-element.12.low0.low1.low, bf16[4,256,768]{2,1,0:T(8,128)(2,1)S(1)} %get-tuple-element.11.high0.high1.high, ...), custom_call_target="tpu_custom_call" | custom-call | tf_op jit(solution)/shard_map/pallas_call | solution.py:208
  105.6 3.8 %collective-permute-start.13 = (f32[1,256,512]{2,1,0:T(8,128)S(1)}, f32[1,256,512]{2,1,0:T(8,128)S(1)}, u32[]{:S(2)}, u32[]{:S(2)}) collective-permute-start(f32[1,256,512]{2,1,0:T(8,128)S(1)} %get-tuple-element.19), channel_id=1, source_target_pairs={{0,28},{4,0},{8,4},{12,8},{16,12},{20,16},{24,20},{28,24},{1,29},{... | collective-permute-start | bytes 1572872 | tf_op jit(solution)/shard_map/ppermute | solution.py:240
  109.4 1.9 %shard_map.71.inner.before = f32[2,256,512]{2,1,0:T(8,128)S(1)} custom-call(bf16[4,256,768]{2,1,0:T(8,128)(2,1)S(1)} %get-tuple-element.11.high0.high1.high, bf16[4,256,768]{2,1,0:T(8,128)(2,1)S(1)} %get-tuple-element.12.low0.low1.low, f32[2,256,512]{2,1,0:T(8,128)S(1)} %shard_map.68.ends.before, f32[2,256,512]{2,1,0:T(8,128)S(1)} %shard_map.69.inner.before, ...), custom_call_target="tpu_custom_call" | custom-call | tf_op jit(solution)/shard_map/pallas_call | solution.py:223
  111.3 18.9 %collective-permute-done.13.above = f32[1,256,512]{2,1,0:T(8,128)S(1)} collective-permute-done((f32[1,256,512]{2,1,0:T(8,128)S(1)}, f32[1,256,512]{2,1,0:T(8,128)S(1)}, u32[]{:S(2)}, u32[]{:S(2)}) %collective-permute-start.13) | collective-permute-done | bytes 524320 | tf_op jit(solution)/shard_map/ppermute | solution.py:240
  130.3 2.0 %shard_map.72.ends = f32[2,256,512]{2,1,0:T(8,128)S(1)} custom-call(bf16[4,256,768]{2,1,0:T(8,128)(2,1)S(1)} %get-tuple-element.11.high0.high1.high, bf16[4,256,768]{2,1,0:T(8,128)(2,1)S(1)} %get-tuple-element.12.low0.low1.low, bf16[4,256,768]{2,1,0:T(8,128)(2,1)S(1)} %get-tuple-element.11.high0.high1.high, ...), custom_call_target="tpu_custom_call" | custom-call | tf_op jit(solution)/shard_map/pallas_call | solution.py:208
  132.4 3.2 %collective-permute-start.15 = (f32[1,256,512]{2,1,0:T(8,128)S(1)}, f32[1,256,512]{2,1,0:T(8,128)S(1)}, u32[]{:S(2)}, u32[]{:S(2)}) collective-permute-start(f32[1,256,512]{2,1,0:T(8,128)S(1)} %get-tuple-element.17), channel_id=1, source_target_pairs={{0,28},{4,0},{8,4},{12,8},{16,12},{20,16},{24,20},{28,24},{1,29},{... | collective-permute-start | bytes 1572872 | tf_op jit(solution)/shard_map/ppermute | solution.py:240
  135.7 1.9 %shard_map.73.inner = f32[2,256,512]{2,1,0:T(8,128)S(1)} custom-call(bf16[4,256,768]{2,1,0:T(8,128)(2,1)S(1)} %get-tuple-element.11.high0.high1.high, bf16[4,256,768]{2,1,0:T(8,128)(2,1)S(1)} %get-tuple-element.12.low0.low1.low, f32[2,256,512]{2,1,0:T(8,128)S(1)} %shard_map.70.ends.before, f32[2,256,512]{2,1,0:T(8,128)S(1)} %shard_map.71.inner.before, ...), custom_call_target="tpu_custom_call" | custom-call | tf_op jit(solution)/shard_map/pallas_call | solution.py:223
  137.6 1.9 %shard_map.75 = f32[2,256,512]{2,1,0:T(8,128)S(1)} custom-call(bf16[4,256,768]{2,1,0:T(8,128)(2,1)S(1)} %get-tuple-element.11.high0.high1.high, bf16[4,256,768]{2,1,0:T(8,128)(2,1)S(1)} %get-tuple-element.12.low0.low1.low, f32[2,256,512]{2,1,0:T(8,128)S(1)} %shard_map.72.ends, f32[2,256,512]{2,1,0:T(8,128)S(1)} %shard_map.73.inner, ...), custom_call_target="tpu_custom_call" | custom-call | tf_op jit(solution)/shard_map/pallas_call | solution.py:223
  139.5 18.8 %collective-permute-done.15.above = f32[1,256,512]{2,1,0:T(8,128)S(1)} collective-permute-done((f32[1,256,512]{2,1,0:T(8,128)S(1)}, f32[1,256,512]{2,1,0:T(8,128)S(1)}, u32[]{:S(2)}, u32[]{:S(2)}) %collective-permute-start.15) | collective-permute-done | bytes 524320 | tf_op jit(solution)/shard_map/ppermute | solution.py:240
  158.3 2.0 %shard_map.74 = f32[2,256,512]{2,1,0:T(8,128)S(1)} custom-call(bf16[4,256,768]{2,1,0:T(8,128)(2,1)S(1)} %get-tuple-element.11.high0.high1.high, bf16[4,256,768]{2,1,0:T(8,128)(2,1)S(1)} %get-tuple-element.12.low0.low1.low, bf16[4,256,768]{2,1,0:T(8,128)(2,1)S(1)} %get-tuple-element.11.high0.high1.high, ...), custom_call_target="tpu_custom_call" | custom-call | tf_op jit(solution)/shard_map/pallas_call | solution.py:208
  160.4 1.5 pad_maximum_fusion
  (50 shorter events, 4.6 us)
Async XLA Ops:
  0.0 9.0 %copy-start.6 = (s32[4,64]{1,0:T(4,128)S(1)}, s32[4,64]{1,0:T(4,128)}, u32[]{:S(2)}) copy-start(s32[4,64]{1,0:T(4,128)} %param.10) | copy-start | bytes 3076
  0.8 1.6 copy-start
  2.4 6.5 %copy-start.4 = (s32[4,4,64]{2,1,0:T(4,128)S(1)}, s32[4,4,64]{2,1,0:T(4,128)}, u32[]{:S(2)}) copy-start(s32[4,4,64]{2,1,0:T(4,128)} %param.9) | copy-start | bytes 12292
  2.4 6.5 %copy-start.5 = (f32[4,512]{1,0:T(4,128)S(1)}, f32[4,512]{1,0:T(4,128)}, u32[]{:S(2)}) copy-start(f32[4,512]{1,0:T(4,128)} %param.8) | copy-start | bytes 24580
  2.4 6.7 %copy-start.1 = (f32[4,512,256]{2,1,0:T(8,128)S(1)}, f32[4,512,256]{2,1,0:T(8,128)}, u32[]{:S(2)}) copy-start(f32[4,512,256]{2,1,0:T(8,128)} %basis_ref.3) | copy-start | bytes 6291460
  2.8 11.5 %collective-permute-start.3 = (f32[256,128]{1,0:T(8,128)S(1)}, f32[256,128]{1,0:T(8,128)S(1)}, u32[]{:S(2)}, u32[]{:S(2)}) collective-permute-start(f32[256,128]{1,0:T(8,128)S(1)} %shard_map.65), channel_id=1, source_target_pairs={{0,28},{4,0},{8,4},{12,8},{16,12},{20,16},{24,20},{28,24},{1,29},{... | collective-permute-start | bytes 393224 | tf_op jit(solution)/shard_map/ppermute | solution.py:240
  9.1 1.6 copy-start.2
  17.8 2.1 %collective-permute-start.4 = (f32[2,256,256]{2,1,0:T(8,128)}, f32[2,256,256]{2,1,0:T(8,128)S(1)}, u32[]{:S(2)}, u32[]{:S(2)}) collective-permute-start(f32[2,256,256]{2,1,0:T(8,128)} %constant_dynamic-slice_fusion), channel_id=1, source_target_pairs={{0,1},{1,0},{2,3},{3,2},{4,5},{5,4},{6,7},{7,6},{8,9},{9,8},{10,11... | collective-permute-start | bytes 1572872 | tf_op jit(solution)/shard_map/ppermute | solution.py:235
  18.6 2.9 %collective-permute-start = (f32[2,256,256]{2,1,0:T(8,128)}, f32[2,256,256]{2,1,0:T(8,128)S(1)}, u32[]{:S(2)}, u32[]{:S(2)}) collective-permute-start(f32[2,256,256]{2,1,0:T(8,128)} %constant_dynamic-slice_fusion.1), channel_id=1, source_target_pairs={{0,1},{1,0},{2,3},{3,2},{4,5},{5,4},{6,7},{7,6},{8,9},{9,8},{10,11... | collective-permute-start | bytes 1572872 | tf_op jit(solution)/shard_map/ppermute | solution.py:235
  20.0 25.4 %copy-start.3 = (f32[1024,512]{1,0:T(8,128)S(1)}, f32[1024,512]{1,0:T(8,128)}, u32[]{:S(2)}) copy-start(f32[1024,512]{1,0:T(8,128)} %param.11) | copy-start | bytes 6291460
  20.0 14.8 %collective-permute-start.5 = (f32[2,256,256]{2,1,0:T(8,128)S(1)}, f32[2,256,256]{2,1,0:T(8,128)S(1)}, u32[]{:S(2)}, u32[]{:S(2)}) collective-permute-start(f32[2,256,256]{2,1,0:T(8,128)S(1)} %dynamic-slice_add_fusion), channel_id=1, source_target_pairs={{0,2},{1,3},{2,0},{3,1},{4,6},{5,7},{6,4},{7,5},{8,10},{9,11},{10,... | collective-permute-start | bytes 1572872 | tf_op jit(solution)/shard_map/ppermute | solution.py:235
  21.6 23.6 %collective-permute-start.1 = (f32[2,256,256]{2,1,0:T(8,128)S(1)}, f32[2,256,256]{2,1,0:T(8,128)S(1)}, u32[]{:S(2)}, u32[]{:S(2)}) collective-permute-start(f32[2,256,256]{2,1,0:T(8,128)S(1)} %dynamic-slice_add_fusion.1), channel_id=1, source_target_pairs={{0,2},{1,3},{2,0},{3,1},{4,6},{5,7},{6,4},{7,5},{8,10},{9,11},{10,... | collective-permute-start | bytes 1572872 | tf_op jit(solution)/shard_map/ppermute | solution.py:235
  34.9 14.4 %collective-permute-start.6 = (f32[2,256,256]{2,1,0:T(8,128)S(1)}, f32[2,256,256]{2,1,0:T(8,128)}, u32[]{:S(2)}, u32[]{:S(2)}) collective-permute-start(f32[2,256,256]{2,1,0:T(8,128)S(1)} %add.32), channel_id=1, source_target_pairs={{0,1},{1,0},{2,3},{3,2},{4,5},{5,4},{6,7},{7,6},{8,9},{9,8},{10,11... | collective-permute-start | bytes 1572872 | tf_op jit(solution)/shard_map/ppermute | solution.py:235
  45.3 5.5 %collective-permute-start.2 = (f32[2,256,256]{2,1,0:T(8,128)S(1)}, f32[2,256,256]{2,1,0:T(8,128)}, u32[]{:S(2)}, u32[]{:S(2)}) collective-permute-start(f32[2,256,256]{2,1,0:T(8,128)S(1)} %add.30), channel_id=1, source_target_pairs={{0,1},{1,0},{2,3},{3,2},{4,5},{5,4},{6,7},{7,6},{8,9},{9,8},{10,11... | collective-permute-start | bytes 1572872 | tf_op jit(solution)/shard_map/ppermute | solution.py:235
  45.5 31.2 %collective-permute-start.9 = (f32[1,256,512]{2,1,0:T(8,128)S(1)}, f32[1,256,512]{2,1,0:T(8,128)S(1)}, u32[]{:S(2)}, u32[]{:S(2)}) collective-permute-start(f32[1,256,512]{2,1,0:T(8,128)S(1)} %get-tuple-element.13), channel_id=1, source_target_pairs={{0,28},{4,0},{8,4},{12,8},{16,12},{20,16},{24,20},{28,24},{1,29},{... | collective-permute-start | bytes 1572872 | tf_op jit(solution)/shard_map/ppermute | solution.py:240
  48.0 28.7 %collective-permute-start.8 = (f32[1,256,512]{2,1,0:T(8,128)S(1)}, f32[1,256,512]{2,1,0:T(8,128)S(1)}, u32[]{:S(2)}, u32[]{:S(2)}) collective-permute-start(f32[1,256,512]{2,1,0:T(8,128)S(1)} %get-tuple-element.14), channel_id=1, source_target_pairs={{0,4},{4,8},{8,12},{12,16},{16,20},{20,24},{24,28},{28,0},{1,5},{5... | collective-permute-start | bytes 1572872 | tf_op jit(solution)/shard_map/ppermute | solution.py:240
  50.6 22.4 %collective-permute-start.7 = (f32[1,256,256]{2,1,0:T(8,128)S(1)}, f32[1,256,256]{2,1,0:T(8,128)S(1)}, u32[]{:S(2)}, u32[]{:S(2)}) collective-permute-start(f32[1,256,256]{2,1,0:T(8,128)S(1)} %slice.82), channel_id=1, source_target_pairs={{0,4},{4,8},{8,12},{12,16},{16,20},{20,24},{24,28},{28,0},{1,5},{5... | collective-permute-start | bytes 786440 | tf_op jit(solution)/shard_map/ppermute | solution.py:240
  78.7 24.8 %collective-permute-start.11 = (f32[1,256,512]{2,1,0:T(8,128)S(1)}, f32[1,256,512]{2,1,0:T(8,128)S(1)}, u32[]{:S(2)}, u32[]{:S(2)}) collective-permute-start(f32[1,256,512]{2,1,0:T(8,128)S(1)} %get-tuple-element.21), channel_id=1, source_target_pairs={{0,28},{4,0},{8,4},{12,8},{16,12},{20,16},{24,20},{28,24},{1,29},{... | collective-permute-start | bytes 1572872 | tf_op jit(solution)/shard_map/ppermute | solution.py:240
  82.4 21.1 %collective-permute-start.10 = (f32[1,256,512]{2,1,0:T(8,128)S(1)}, f32[1,256,512]{2,1,0:T(8,128)S(1)}, u32[]{:S(2)}, u32[]{:S(2)}) collective-permute-start(f32[1,256,512]{2,1,0:T(8,128)S(1)} %get-tuple-element.22), channel_id=1, source_target_pairs={{0,4},{4,8},{8,12},{12,16},{16,20},{20,24},{24,28},{28,0},{1,5},{5... | collective-permute-start | bytes 1572872 | tf_op jit(solution)/shard_map/ppermute | solution.py:240
  105.6 24.6 %collective-permute-start.13 = (f32[1,256,512]{2,1,0:T(8,128)S(1)}, f32[1,256,512]{2,1,0:T(8,128)S(1)}, u32[]{:S(2)}, u32[]{:S(2)}) collective-permute-start(f32[1,256,512]{2,1,0:T(8,128)S(1)} %get-tuple-element.19), channel_id=1, source_target_pairs={{0,28},{4,0},{8,4},{12,8},{16,12},{20,16},{24,20},{28,24},{1,29},{... | collective-permute-start | bytes 1572872 | tf_op jit(solution)/shard_map/ppermute | solution.py:240
  109.4 20.9 %collective-permute-start.12 = (f32[1,256,512]{2,1,0:T(8,128)S(1)}, f32[1,256,512]{2,1,0:T(8,128)S(1)}, u32[]{:S(2)}, u32[]{:S(2)}) collective-permute-start(f32[1,256,512]{2,1,0:T(8,128)S(1)} %get-tuple-element.20), channel_id=1, source_target_pairs={{0,4},{4,8},{8,12},{12,16},{16,20},{20,24},{24,28},{28,0},{1,5},{5... | collective-permute-start | bytes 1572872 | tf_op jit(solution)/shard_map/ppermute | solution.py:240
  132.4 25.9 %collective-permute-start.15 = (f32[1,256,512]{2,1,0:T(8,128)S(1)}, f32[1,256,512]{2,1,0:T(8,128)S(1)}, u32[]{:S(2)}, u32[]{:S(2)}) collective-permute-start(f32[1,256,512]{2,1,0:T(8,128)S(1)} %get-tuple-element.17), channel_id=1, source_target_pairs={{0,28},{4,0},{8,4},{12,8},{16,12},{20,16},{24,20},{28,24},{1,29},{... | collective-permute-start | bytes 1572872 | tf_op jit(solution)/shard_map/ppermute | solution.py:240
  135.7 22.6 %collective-permute-start.14 = (f32[1,256,512]{2,1,0:T(8,128)S(1)}, f32[1,256,512]{2,1,0:T(8,128)S(1)}, u32[]{:S(2)}, u32[]{:S(2)}) collective-permute-start(f32[1,256,512]{2,1,0:T(8,128)S(1)} %get-tuple-element.18), channel_id=1, source_target_pairs={{0,4},{4,8},{8,12},{12,16},{16,20},{20,24},{24,28},{28,0},{1,5},{5... | collective-permute-start | bytes 1572872 | tf_op jit(solution)/shard_map/ppermute | solution.py:240
where the time goes:
time: 162 us
  waiting for transfers between devices  104 us (64%)
  Pallas kernels  23.2 us (14%)
  starting transfers between devices  22.5 us (14%)
  local copies, waits for them, and re-layouts  7.51 us (5%)
  other arithmetic  4.5 us (3%)
    ppermute x10, waiting for transfers between devices, shifted(): lax.ppermute(value, axis, [(i, (i + steps) % count) for i in range(count)])  80.5 us
    ppermute x6, waiting for transfers between devices, flipped(): return lax.ppermute(value, axis, [(i, i ^ bit) for i in range(count)])  23.4 us
    ppermute x10, starting transfers between devices, shifted(): lax.ppermute(value, axis, [(i, (i + steps) % count) for i in range(count)])  19.4 us
    pallas_call x4, Pallas kernels, apply_ends(): pl.pallas_call(functools.partial(ends_kernel, first, count), grid=(column...  7.9 us
    pallas_call x4, Pallas kernels, apply_inner(): pl.pallas_call(functools.partial(inner_kernel, first, count), grid=(colum...  7.6 us
    pallas_call x1, Pallas kernels, volumes(): pl.pallas_call(functools.partial(volume_kernel, faces_total), grid=(count...  3.61 us
  transfers between devices with their start and end apart: 16, of which 9 were waited for; matrix products, arithmetic and copies ran while one was open for 3% of the time, Pallas kernels for 8%

commit v1 on v0

v1 whole, which is shorter than its diff:
```python
import functools

import jax
import jax.numpy as jnp
from jax import lax
from jax.experimental import pallas as pl
from jax.experimental.pallas import tpu as pltpu
from jax.sharding import PartitionSpec as P

NB = 256
DEG = 4

penalty = 3.0
center = 4.0
half_width = 12.0

PARAMS = pltpu.CompilerParams(vmem_limit_bytes=40 * 1024 * 1024)
NN = (((1,), (0,)), ((), ()))
NT = (((1,), (1,)), ((), ()))


def split(value):
    high = value.astype(jnp.bfloat16)
    low = (value - high.astype(jnp.float32)).astype(jnp.bfloat16)
    return high, low


def dot(first, second, dims=NN):
    return lax.dot_general(first, second, dims, preferred_element_type=jnp.float32)


def dot3(first, second, dims=NN):
    first_high, first_low = first
    second_high, second_low = second
    return dot(first_high, second_high, dims) + (dot(first_high, second_low, dims) + dot(first_low, second_high, dims))


def picked(parts, chosen):
    return dot(parts[0], chosen) + dot(parts[1], chosen)


def one_hot(index_row, rows, offset=0):
    at = lax.broadcasted_iota(jnp.int32, (rows, index_row.shape[1]), 0) - offset
    return (at == index_row).astype(jnp.float32).astype(jnp.bfloat16)


def edge_kernel(index_ref, basis_ref, traces_ref):
    parts = split(basis_ref[0].T)
    traces_ref[...] = picked(parts, one_hot(index_ref[0], basis_ref.shape[1]))


def volume_kernel(faces_total, index_ref, quad_ref, basis_ref, applied_ref, traces_ref, volume_ref):
    flipped = basis_ref[0].T
    traces = picked(split(flipped), one_hot(index_ref[0], basis_ref.shape[1]))
    traces_ref[0] = traces
    width = traces.shape[1] // 2
    outer, layer = traces[:, :width], traces[:, width:]
    total = dot3(split(flipped * quad_ref[0]), split(applied_ref[0]))
    total = total + dot3(split((2.0 * outer + layer) * (1.0 / faces_total)), split(outer), NT)
    volume_ref[0] = 0.5 * (total + total.T)


def packed(volume):
    half = volume.shape[0] // 2
    row = lax.broadcasted_iota(jnp.int32, (half, half), 0)
    column = lax.broadcasted_iota(jnp.int32, (half, half), 1)
    corner = volume[half:, half:]
    mixed = jnp.where(column >= row, volume[:half, :half], corner)
    diagonal = jnp.sum(jnp.where(column == row, corner, 0.0), axis=0, keepdims=True)
    return mixed, volume[:half, half:], diagonal


def unpacked(mixed, side, diagonal):
    half = mixed.shape[0]
    row = lax.broadcasted_iota(jnp.int32, (half, half), 0)
    column = lax.broadcasted_iota(jnp.int32, (half, half), 1)
    turned = mixed.T
    first = jnp.where(column >= row, mixed, turned)
    corner = jnp.where(column < row, mixed, jnp.where(column == row, diagonal, turned))
    top = jnp.concatenate([first, side], axis=1)
    return jnp.concatenate([top, jnp.concatenate([side.T, corner], axis=1)], axis=0)


def coupling_kernel(faces_total, count, order_ref, pair_ref, own_ref, next_ref, lead_ref, volume_ref, send_ref, keep_ref):
    step = pl.program_id(0)
    element = order_ref[step]
    own = own_ref[0]
    size = own.shape[0]
    width = own.shape[1] // 2
    outer, layer = own[:, :width], own[:, width:]
    near = split((penalty * outer + 0.5 * layer) * (-1.0 / faces_total))
    far = split(outer * (0.5 / faces_total))
    mixed, side, diagonal = packed(volume_ref[0])
    half = size // 2

    def store(out_ref, coupling):
        out_ref[0, :size] = coupling
        out_ref[0, size : size + half, :half] = mixed
        out_ref[0, size : size + half, half:] = side
        out_ref[0, size + half :, :] = jnp.broadcast_to(jnp.concatenate([diagonal, diagonal], axis=1), (8, size))

    def finish(face, inside):
        coupling = dot3(near, split(face), NT) + dot3(far, split(inside), NT)

        @pl.when(step < count // 2)
        def _():
            store(send_ref, coupling)

        @pl.when(step >= count // 2)
        def _():
            store(keep_ref, coupling)

    @pl.when(element < count - 1)
    def _():
        order = one_hot(pair_ref[0], width)
        following = next_ref[0]
        finish(picked(split(following[:, :width]), order), picked(split(following[:, width:]), order))

    @pl.when(element == count - 1)
    def _():
        lead = split(lead_ref[...])
        finish(picked(lead, one_hot(pair_ref[0], width)), picked(lead, one_hot(pair_ref[0], width, width // 2)))


def weights_kernel(me_ref, own_ref, other_ref, before_own_ref, before_other_ref, high_ref, low_ref):
    step = pl.program_id(0)
    me = me_ref[0]
    size = own_ref.shape[2]
    half = size // 2
    away = ((step ^ me) >> 1) & 1
    block = jnp.where(away == 1, other_ref[0], own_ref[0])
    volume = unpacked(block[size : size + half, :half], block[size : size + half, half:], block[size + half : size + half + 1, :half])
    diagonal = lax.broadcasted_iota(jnp.int32, (size, size), 0) == lax.broadcasted_iota(jnp.int32, (size, size), 1)
    volume = (volume - jnp.where(diagonal, center, 0.0)) * (1.0 / half_width)
    away = (((step - 1) ^ me) >> 1) & 1
    earlier = jnp.where(away == 1, before_other_ref[0], before_own_ref[0]) * (1.0 / half_width)
    for at, value in enumerate((earlier.T, volume, block[:size] * (1.0 / half_width))):
        high, low = split(value)
        high_ref[0, :, at * size : (at + 1) * size] = high
        low_ref[0, :, at * size : (at + 1) * size] = low


def apply_row(weights, values):
    total = None
    for weight, value in zip(weights, values):
        term = dot3(weight, split(value))
        total = term if total is None else total + term
    return total


def row_weights(high, low):
    size = high.shape[0]
    return [(high[:, at * size : (at + 1) * size], low[:, at * size : (at + 1) * size]) for at in range(3)]


def advance(first, result, before):
    return result if first else 2.0 * result - before


def ends_kernel(first, count, before, high0, low0, high1, low1, head, tail, inner, below, above, old_head, old_tail, new_head, new_tail):
    rows = row_weights(high0[0], low0[0])
    rows[0] = split((before[...] * (1.0 / half_width)).T)
    row = apply_row(rows, (below[...], head[...], inner[0]))
    new_head[...] = advance(first, row, None if first else old_head[...])
    row = apply_row(row_weights(high1[0], low1[0]), (inner[count - 3], tail[...], above[...]))
    new_tail[...] = advance(first, row, None if first else old_tail[...])


def inner_kernel(first, count, high, low, head, tail, inner, old, out):
    for at in range(1, count - 1):
        lower = head[...] if at == 1 else inner[at - 2]
        upper = tail[...] if at == count - 2 else inner[at]
        row = apply_row(row_weights(high[at], low[at]), (lower, inner[at - 1], upper))
        out[at - 1] = advance(first, row, None if first else old[at - 1])


def arrange_kernel(count, side_ref, own_ref, got_ref, head_ref, tail_ref, inner_ref):
    step = pl.program_id(0)
    value = jnp.where(step // (count // 2) == side_ref[0], own_ref[0], got_ref[0])

    @pl.when(step == 0)
    def _():
        head_ref[...] = value

    @pl.when(step == count - 1)
    def _():
        tail_ref[...] = value

    @pl.when((step > 0) & (step < count - 1))
    def _():
        inner_ref[0] = value


def collect_kernel(count, side_ref, head_ref, tail_ref, inner_ref, got_end_ref, got_inner_ref, out_ref):
    step = pl.program_id(0)
    side = side_ref[0]
    end = jnp.where(side == 0, head_ref[...], tail_ref[...])
    at_end = step == side * (count - 1)
    mine = jnp.where(at_end, end, inner_ref[0])
    theirs = jnp.where(at_end, got_end_ref[...], got_inner_ref[0])
    columns = mine.shape[1]
    out_ref[0, :, :columns] = jnp.where(side == 0, mine, theirs)
    out_ref[0, :, columns:] = jnp.where(side == 0, theirs, mine)


def whole(shape):
    return pl.BlockSpec(shape, lambda *steps: (0,) * len(shape))


def edge_traces(index, basis):
    points, size = basis.shape[1:]
    return pl.pallas_call(
        edge_kernel,
        grid=(1,),
        in_specs=[pl.BlockSpec((1, 1, index.shape[2]), lambda s: (0, 0, 0)), pl.BlockSpec((1, points, size), lambda s: (0, 0, 0))],
        out_specs=whole((size, index.shape[2])),
        out_shape=jax.ShapeDtypeStruct((size, index.shape[2]), jnp.float32),
        compiler_params=PARAMS,
    )(index, basis)


def volumes(index, quad, basis, applied, faces_total):
    count, points, size = basis.shape
    spots = index.shape[2]
    per = lambda *shape: pl.BlockSpec((1, *shape), lambda s: (s, 0, 0))
    return pl.pallas_call(
        functools.partial(volume_kernel, faces_total),
        grid=(count,),
        in_specs=[per(1, spots), per(1, points), per(points, size), per(points, size)],
        out_specs=[per(size, spots), per(size, size)],
        out_shape=[
            jax.ShapeDtypeStruct((count, size, spots), jnp.float32),
            jax.ShapeDtypeStruct((count, size, size), jnp.float32),
        ],
        compiler_params=PARAMS,
    )(index, quad, basis, applied)


def couplings(order, pairs, traces, lead, volume, faces_total):
    count, size, spots = traces.shape
    rows = size + size // 2 + 8
    per = lambda *shape: pl.BlockSpec((1, *shape), lambda s, o: (o[s], 0, 0))
    half = count // 2
    return pl.pallas_call(
        functools.partial(coupling_kernel, faces_total, count),
        grid_spec=pltpu.PrefetchScalarGridSpec(
            num_scalar_prefetch=1,
            grid=(count,),
            in_specs=[
                per(1, pairs.shape[2]),
                per(size, spots),
                pl.BlockSpec((1, size, spots), lambda s, o: (jnp.minimum(o[s] + 1, count - 1), 0, 0)),
                whole(lead.shape),
                per(size, size),
            ],
            out_specs=[
                pl.BlockSpec((1, rows, size), lambda s, o: (jnp.minimum(s, half - 1), 0, 0)),
                pl.BlockSpec((1, rows, size), lambda s, o: (jnp.maximum(s - half, 0), 0, 0)),
            ],
        ),
        out_shape=[jax.ShapeDtypeStruct((half, rows, size), jnp.float32)] * 2,
        compiler_params=PARAMS,
    )(order, pairs, traces, traces, lead, volume)


def weights(me, own, other, size):
    count = 2 * own.shape[0]
    rows = own.shape[1]

    def spot(element, mine):
        away = element ^ mine
        return (away >> 2) * 2 + (away & 1)

    block = pl.BlockSpec((1, rows, size), lambda s, m: (spot(s, m[0]), 0, 0))
    prior = pl.BlockSpec((1, size, size), lambda s, m: (spot(jnp.maximum(s - 1, 0), m[0]), 0, 0))
    return pl.pallas_call(
        weights_kernel,
        grid_spec=pltpu.PrefetchScalarGridSpec(
            num_scalar_prefetch=1,
            grid=(count,),
            in_specs=[block, block, prior, prior],
            out_specs=[pl.BlockSpec((1, size, 3 * size), lambda s, m: (s, 0, 0))] * 2,
        ),
        out_shape=[jax.ShapeDtypeStruct((count, size, 3 * size), jnp.bfloat16)] * 2,
        compiler_params=PARAMS,
    )(me, own, other, own, other)


def apply_ends(first, before, high, low, head, tail, inner, below, above, old_head, old_tail):
    count, size, depth = high.shape
    columns = head.shape[1]
    flat = pl.BlockSpec((size, columns), lambda s: (0, 0))
    row = lambda at: pl.BlockSpec((1, size, depth), lambda s: (at, 0, 0))
    return pl.pallas_call(
        functools.partial(ends_kernel, first, count),
        grid=(1,),
        in_specs=[whole(before.shape), row(0), row(0), row(count - 1), row(count - 1), flat, flat, whole(inner.shape)] + [flat] * 4,
        out_specs=[flat, flat],
        out_shape=[jax.ShapeDtypeStruct((size, columns), jnp.float32)] * 2,
        compiler_params=PARAMS,
    )(before, high, low, high, low, head, tail, inner, below, above, old_head, old_tail)


def apply_inner(first, high, low, head, tail, inner, old):
    count, size, depth = high.shape
    return pl.pallas_call(
        functools.partial(inner_kernel, first, count),
        grid=(1,),
        in_specs=[whole(high.shape), whole(low.shape), whole(head.shape), whole(tail.shape), whole(inner.shape), whole(inner.shape)],
        out_specs=whole(inner.shape),
        out_shape=jax.ShapeDtypeStruct(inner.shape, jnp.float32),
        compiler_params=PARAMS,
    )(high, low, head, tail, inner, old)


def arranged(side, own, got):
    half, size, columns = own.shape
    count = 2 * half
    block = pl.BlockSpec((1, size, columns), lambda s, o: (s % half, 0, 0))
    flat = pl.BlockSpec((size, columns), lambda s, o: (0, 0))
    return pl.pallas_call(
        functools.partial(arrange_kernel, count),
        grid_spec=pltpu.PrefetchScalarGridSpec(
            num_scalar_prefetch=1,
            grid=(count,),
            in_specs=[block, block],
            out_specs=[flat, flat, pl.BlockSpec((1, size, columns), lambda s, o: (jnp.clip(s - 1, 0, count - 3), 0, 0))],
        ),
        out_shape=[jax.ShapeDtypeStruct((size, columns), jnp.float32)] * 2
        + [jax.ShapeDtypeStruct((count - 2, size, columns), jnp.float32)],
        compiler_params=PARAMS,
    )(side, own, got)


def collected(side, head, tail, inner, got_end, got_inner):
    size, columns = head.shape
    half = got_inner.shape[0] + 1
    spot = lambda s, o: jnp.where(o[0] == 0, jnp.maximum(s - 1, 0), jnp.minimum(s, half - 2))
    return pl.pallas_call(
        functools.partial(collect_kernel, half),
        grid_spec=pltpu.PrefetchScalarGridSpec(
            num_scalar_prefetch=1,
            grid=(half,),
            in_specs=[
                pl.BlockSpec((size, columns), lambda s, o: (0, 0)),
                pl.BlockSpec((size, columns), lambda s, o: (0, 0)),
                pl.BlockSpec((1, size, columns), lambda s, o: (o[0] * (half - 1) + spot(s, o), 0, 0)),
                pl.BlockSpec((size, columns), lambda s, o: (0, 0)),
                pl.BlockSpec((1, size, columns), lambda s, o: (spot(s, o), 0, 0)),
            ],
            out_specs=pl.BlockSpec((1, size, 2 * columns), lambda s, o: (s, 0, 0)),
        ),
        out_shape=jax.ShapeDtypeStruct((half, size, 2 * columns), jnp.float32),
        compiler_params=PARAMS,
    )(side, head, tail, inner, got_end, got_inner)


def flipped(value, axis, bit):
    count = lax.axis_size(axis)
    return lax.ppermute(value, axis, [(i, i ^ bit) for i in range(count)])


def shifted(value, axis, steps):
    count = lax.axis_size(axis)
    return lax.ppermute(value, axis, [(i, (i + steps) % count) for i in range(count)])


def body(basis, applied, quad, face_index, face_pairing, orbitals):
    count, points, size = basis.shape
    spots = face_index.shape[2]
    columns = orbitals.shape[1] // 2
    elems, width = lax.axis_size("elem"), lax.axis_size("pts")
    faces_total = float(spots * width)
    side = lax.axis_index("elem") % 2
    core = lax.axis_index("pts") % 2
    lane = lax.axis_index("pts") // 2 % 2
    side_at = side.reshape(1).astype(jnp.int32)

    vector = orbitals.reshape(count, size, 2 * columns)
    got = flipped(lax.dynamic_slice_in_dim(vector, (1 - side) * columns, columns, axis=2), "elem", 1)

    lead_index = face_index[:1, 0:2].reshape(1, 1, 2 * spots)
    lead = shifted(edge_traces(lead_index, basis), "elem", -1)
    index = jnp.stack([face_index[:, 0], face_index[:, 2], face_index[:, 1], face_index[:, 3]], axis=1)
    index = index.reshape(count, 1, 4 * spots)
    pairs = jnp.concatenate([jnp.full_like(face_pairing, -points), face_pairing], axis=1).reshape(count, 1, 2 * spots)
    traces, volume = volumes(index, quad.reshape(count, 1, points), basis, applied, faces_total)
    half = count // 2
    order = jnp.arange(count, dtype=jnp.int32) ^ ((1 - core).astype(jnp.int32) * half)
    send, keep = couplings(order, pairs, traces, lead, volume, faces_total)

    other = flipped(send, "pts", 1)
    quarter = half // 2
    pick = lambda value, at: lax.dynamic_slice_in_dim(value, at * quarter, quarter)
    send = pick(keep, 1 - lane) + pick(other, 1 - lane)
    mine = pick(keep, lane) + pick(other, lane) + flipped(send, "pts", 2)
    bit = 4
    while bit < width:
        mine = mine + flipped(mine, "pts", bit)
        bit *= 2
    beside = flipped(mine, "pts", 2)
    across = flipped(mine, "elem", 1)
    both = flipped(across, "pts", 2)
    own = jnp.concatenate([mine, beside, across, both])
    other = flipped(own, "pts", 1)

    last = lax.dynamic_slice(own, ((1 - side) * 2 + 1 - lane, 0, 0), (1, size, size))[0]
    flat = lambda e, p: e % elems * width + p
    odd = [(e, p) for e in range(elems) for p in range(1, width, 2)]
    before = lax.ppermute(last, ("elem", "pts"), [(flat(e, p), flat(e + 2, p)) for e, p in odd])
    before = before + lax.ppermute(before, ("elem", "pts"), [(flat(e, p), flat(e, p - 1)) for e, p in odd])

    own_half = lax.dynamic_slice_in_dim(vector, side * columns, columns, axis=2)
    head, tail, inner = arranged(side_at, own_half, got)
    below = shifted(tail, "elem", 2)
    above = shifted(head, "elem", -2)

    me = (side * 4 + core * 2 + lane).reshape(1).astype(jnp.int32)
    high, low = weights(me, own, other, size)

    old = head, tail, inner
    for degree in range(DEG):
        first = degree == 0
        new_head, new_tail = apply_ends(first, before, high, low, head, tail, inner, below, above, old[0], old[1])
        new_inner = apply_inner(first, high, low, head, tail, inner, old[2])
        old = head, tail, inner
        head, tail, inner = new_head, new_tail, new_inner
        if degree < DEG - 1:
            below = shifted(tail, "elem", 2)
            above = shifted(head, "elem", -2)

    got_inner = flipped(lax.dynamic_slice_in_dim(inner, (1 - side) * (count - 1), count - 1), "elem", 1)
    got_end = flipped(jnp.where(side == 0, tail, head), "elem", 1)
    result = collected(side_at, head, tail, inner, got_end, got_inner)
    return result.reshape(count * size, 2 * columns)


def solution(mesh):
    return jax.shard_map(
        body,
        mesh=mesh,
        in_specs=(
            P("elem", "pts", None),
            P("elem", "pts", None),
            P("elem", "pts"),
            P("elem", None, "pts"),
            P("elem", "pts"),
            P("elem", "pts"),
        ),
        out_specs=P("elem", "pts"),
        check_vma=False,
    )
```

time: 162 us -> 173 us (1.068)
  waiting for transfers between devices: 104 us -> 73.3 us
  Pallas kernels: 23.2 us -> 43.9 us
  local copies, waits for them, and re-layouts: 7.51 us -> 22 us
  starting transfers between devices: 22.5 us -> 31.2 us
  other arithmetic: 4.5 us -> 1.3 us
    ppermute x10 -> x9, waiting for transfers between devices: 80.5 us -> 15.8 us  [shifted(): lax.ppermute(value, axis, [(i, (i + steps) % count) for i in range(count)])]
    ppermute x6 -> x9, waiting for transfers between devices: 23.4 us -> 57.5 us  [flipped(): return lax.ppermute(value, axis, [(i, i ^ bit) for i in range(count)])]
    pallas_call x9 -> x11, Pallas kernels: 16.6 us -> 36.5 us  [the longest x4 11.4 us: apply_inner(): pl.pallas_call(functools.partial(inner_kernel, first, count), grid=(1,),...]
    unnamed x14 -> x52, local copies, waits for them, and re-layouts: 3.2 us -> 16.9 us
    ppermute x6 -> x9, starting transfers between devices: 3.1 us -> 7.83 us  [flipped(): return lax.ppermute(value, axis, [(i, i ^ bit) for i in range(count)])]
    select_n x2 -> x1, other arithmetic: 2.61 us -> 0.04 us  [body(): got_end = flipped(jnp.where(side == 0, tail, head), 'elem', 1)]
    dynamic_slice x2, local copies, waits for them, and re-layouts: 1.69 us -> 4.13 us  [the longest x1 3.18 us: body(): lax.dynamic_slice_in_dim(vector, (1 - side) * columns, columns, axis=2)]
    ppermute x10 -> x9, starting transfers between devices: 19.4 us -> 21.4 us  [shifted(): lax.ppermute(value, axis, [(i, (i + steps) % count) for i in range(count)])]
  transfers between devices with their start and end apart: 16 -> 20, of which waited for: 9 -> 11; matrix products, arithmetic and copies ran while one was open for 3% -> 3% of each run, Pallas kernels for 8% -> 15%
where the time goes in v1:
time: 173 us; the launch traced here: 172 us
  waiting for transfers between devices  73.3 us (42%)
  Pallas kernels  43.9 us (25%)
  starting transfers between devices  31.2 us (18%)
  local copies, waits for them, and re-layouts  22 us (13%)
    ppermute x9, waiting for transfers between devices, flipped(): return lax.ppermute(value, axis, [(i, i ^ bit) for i in range(count)])  57.5 us
    ppermute x9, starting transfers between devices, shifted(): lax.ppermute(value, axis, [(i, (i + steps) % count) for i in range(count)])  21.4 us
    unnamed x52, local copies, waits for them, and re-layouts  16.9 us
    ppermute x9, waiting for transfers between devices, shifted(): lax.ppermute(value, axis, [(i, (i + steps) % count) for i in range(count)])  15.8 us
    pallas_call x4, Pallas kernels, apply_inner(): pl.pallas_call(functools.partial(inner_kernel, first, count), grid=(1,),...  11.4 us
    pallas_call x4, Pallas kernels, apply_ends(): pl.pallas_call(functools.partial(ends_kernel, first, count), grid=(1,), i...  10.4 us
    ppermute x9, starting transfers between devices, flipped(): return lax.ppermute(value, axis, [(i, i ^ bit) for i in range(count)])  7.83 us
    pallas_call x1, Pallas kernels, weights(): pl.pallas_call(weights_kernel, grid_spec=pltpu.PrefetchScalarGridSpec(num...  6.07 us
  transfers between devices with their start and end apart: 20, of which 11 were waited for; matrix products, arithmetic and copies ran while one was open for 3% of the time, Pallas kernels for 15%

profile of v1, /device:TPU:0, one launch (start us, length us, event | category | flops | bytes accessed | tf_op | source)
XLA Modules:
  0.0 172.1 jit_solution(8001626435288422517)
XLA Ops:
  2.8 6.1 %collective-permute-start = (f32[256,128]{1,0:T(8,128)S(1)}, f32[256,128]{1,0:T(8,128)S(1)}, u32[]{:S(2)}, u32[]{:S(2)}) collective-permute-start(f32[256,128]{1,0:T(8,128)S(1)} %shard_map.65), channel_id=1, source_target_pairs={{0,28},{4,0},{8,4},{12,8},{16,12},{20,16},{24,20},{28,24},{1,29},{... | collective-permute-start | bytes 393224 | tf_op jit(solution)/shard_map/ppermute | solution.py:365
  9.1 1.6 copy-done.22
  10.7 3.6 %shard_map.64 = (f32[4,256,256]{2,1,0:T(8,128)S(1)}, f32[4,256,256]{2,1,0:T(8,128)S(1)}) custom-call(s32[4,1,256]{2,1,0:T(1,128)S(1)} %reshape.26.index_ref, f32[4,1,512]{2,1,0:T(1,128)S(1)} %reshape.27.quad_ref, f32[4,512,256]{2,1,0:T(8,128)S(1)} %copy-done.16, f32[4,512,256]{2,1,0:T(8,128)S(1)} %copy-done.22), custom_call_target="tpu_custom_call" | custom-call | tf_op jit(solution)/shard_map/pallas_call | solution.py:226
  14.3 3.4 %shard_map.66 = (f32[2,392,256]{2,1,0:T(8,128)S(1)}, f32[2,392,256]{2,1,0:T(8,128)S(1)}) custom-call(s32[4]{0:T(128)S(1)} %iota_xor_fusion.order_ref, s32[4,1,128]{2,1,0:T(1,128)S(1)} %bitcast.7, f32[4,256,256]{2,1,0:T(8,128)S(1)} %get-tuple-element.22.own_ref.next_ref, f32[4,256,256]{2,1,0:T(8,128)S(1)} %get-tuple-element.22.own_ref.next_ref, ...), custom_call_target="tpu_custom_call" | custom-call | tf_op jit(solution)/shard_map/pallas_call | solution.py:244
  17.8 2.3 %collective-permute-done.1 = f32[2,392,256]{2,1,0:T(8,128)S(1)} collective-permute-done((f32[2,392,256]{2,1,0:T(8,128)S(1)}, f32[2,392,256]{2,1,0:T(8,128)S(1)}, u32[]{:S(2)}, u32[]{:S(2)}) %collective-permute-start.1) | collective-permute-done | bytes 802848 | tf_op jit(solution)/shard_map/ppermute | solution.py:360
  21.7 9.8 %collective-permute-done.2 = f32[1,392,256]{2,1,0:T(8,128)S(1)} collective-permute-done((f32[1,392,256]{2,1,0:T(8,128)S(1)}, f32[1,392,256]{2,1,0:T(8,128)S(1)}, u32[]{:S(2)}, u32[]{:S(2)}) %collective-permute-start.2) | collective-permute-done | bytes 401440 | tf_op jit(solution)/shard_map/ppermute | solution.py:360
  33.2 8.9 %collective-permute-done.4 = f32[1,392,256]{2,1,0:T(8,128)S(1)} collective-permute-done((f32[1,392,256]{2,1,0:T(8,128)S(1)}, f32[1,392,256]{2,1,0:T(8,128)S(1)}, u32[]{:S(2)}, u32[]{:S(2)}) %collective-permute-start.4) | collective-permute-done | bytes 401440 | tf_op jit(solution)/shard_map/ppermute | solution.py:360
  43.7 8.1 %collective-permute-done.5 = f32[1,392,256]{2,1,0:T(8,128)S(1)} collective-permute-done((f32[1,392,256]{2,1,0:T(8,128)S(1)}, f32[1,392,256]{2,1,0:T(8,128)S(1)}, u32[]{:S(2)}, u32[]{:S(2)}) %collective-permute-start.5) | collective-permute-done | bytes 401440 | tf_op jit(solution)/shard_map/ppermute | solution.py:360
  52.0 3.2 %constant_dynamic-slice_fusion = (f32[4,256,256]{2,1,0:T(8,128)}, f32[4,256,256]{2,1,0:T(8,128)S(1)}) fusion(f32[4,256,512]{2,1,0:T(8,128)} %bitcast.8, s32[]{:T(128)S(6)} %select_n.55, s32[]{:T(128)S(6)} %select_n.54), kind=kLoop, calls=%fused_computation.6 | loop fusion | bytes 4194312 | tf_op jit(solution)/shard_map/dynamic_slice | solution.py:380
  58.0 22.6 %collective-permute-done.9.got_ref = f32[4,256,256]{2,1,0:T(8,128)} collective-permute-done((f32[4,256,256]{2,1,0:T(8,128)}, f32[4,256,256]{2,1,0:T(8,128)}, u32[]{:S(2)}, u32[]{:S(2)}) %collective-permute-start.9) | collective-permute-done | bytes 1048608 | tf_op jit(solution)/shard_map/ppermute | solution.py:360
  80.6 5.0 %shard_map.68 = (f32[256,256]{1,0:T(8,128)}, f32[256,256]{1,0:T(8,128)}, f32[6,256,256]{2,1,0:T(8,128)S(1)}) custom-call(s32[1]{0:T(128)} %bitcast.side_ref, f32[4,256,256]{2,1,0:T(8,128)S(1)} %get-tuple-element.40.own_ref, f32[4,256,256]{2,1,0:T(8,128)} %collective-permute-done.9.got_ref), custom_call_target="tpu_custom_call" | custom-call | tf_op jit(solution)/shard_map/pallas_call | solution.py:321
  86.7 3.8 %collective-permute-start.11 = (f32[256,256]{1,0:T(8,128)}, f32[256,256]{1,0:T(8,128)}, u32[]{:S(2)}, u32[]{:S(2)}) collective-permute-start(f32[256,256]{1,0:T(8,128)} %get-tuple-element.28.head.old_head), channel_id=1, source_target_pairs={{0,24},{4,28},{8,0},{12,4},{16,8},{20,12},{24,16},{28,20},{1,25},{... | collective-permute-start | bytes 786440 | tf_op jit(solution)/shard_map/ppermute | solution.py:365
  92.9 6.1 %shard_map.67 = (bf16[8,256,768]{2,1,0:T(8,128)(2,1)S(1)}, bf16[8,256,768]{2,1,0:T(8,128)(2,1)S(1)}) custom-call(s32[1]{0:T(128)} %bitcast.3.me_ref, f32[4,392,256]{2,1,0:T(8,128)S(1)} %copy-done.10, f32[4,392,256]{2,1,0:T(8,128)} %collective-permute-done.8.other_ref.before_other_ref, f32[4,392,256]{2,1,0:T(8,128)S(1)} %copy-done.10, ...), custom_call_target="tpu_custom_call" | custom-call | tf_op jit(solution)/shard_map/pallas_call | solution.py:276
  100.0 2.3 %shard_map.69 = (f32[256,256]{1,0:T(8,128)S(1)}, f32[256,256]{1,0:T(8,128)S(1)}) custom-call(f32[256,256]{1,0:T(8,128)S(1)} %add.65.before, bf16[8,256,768]{2,1,0:T(8,128)(2,1)S(1)} %get-tuple-element.26.high0.high1.high, bf16[8,256,768]{2,1,0:T(8,128)(2,1)S(1)} %get-tuple-element.27.low0.low1.low, ...), custom_call_target="tpu_custom_call" | custom-call | tf_op jit(solution)/shard_map/pallas_call | solution.py:294
  103.1 3.1 %collective-permute-start.13 = (f32[256,256]{1,0:T(8,128)S(1)}, f32[256,256]{1,0:T(8,128)S(1)}, u32[]{:S(2)}, u32[]{:S(2)}) collective-permute-start(f32[256,256]{1,0:T(8,128)S(1)} %get-tuple-element.31.head.old_head), channel_id=1, source_target_pairs={{0,24},{4,28},{8,0},{12,4},{16,8},{20,12},{24,16},{28,20},{1,25},{... | collective-permute-start | bytes 786440 | tf_op jit(solution)/shard_map/ppermute | solution.py:365
  106.1 3.1 %shard_map.70.inner.old = f32[6,256,256]{2,1,0:T(8,128)S(1)} custom-call(bf16[8,256,768]{2,1,0:T(8,128)(2,1)S(1)} %get-tuple-element.26.high0.high1.high, bf16[8,256,768]{2,1,0:T(8,128)(2,1)S(1)} %get-tuple-element.27.low0.low1.low, f32[256,256]{1,0:T(8,128)} %get-tuple-element.28.head.old_head, f32[256,256]{1,0:T(8,128)} %get-tuple-element.29.tail.old_tail, ...), custom_call_target="tpu_custom_call" | custom-call | tf_op jit(solution)/shard_map/pallas_call | solution.py:306
  109.2 4.1 %collective-permute-done.12.below = f32[256,256]{1,0:T(8,128)S(1)} collective-permute-done((f32[256,256]{1,0:T(8,128)S(1)}, f32[256,256]{1,0:T(8,128)S(1)}, u32[]{:S(2)}, u32[]{:S(2)}) %collective-permute-start.12) | collective-permute-done | bytes 262176 | tf_op jit(solution)/shard_map/ppermute | solution.py:365
  113.3 1.9 %collective-permute-done.13.above = f32[256,256]{1,0:T(8,128)S(1)} collective-permute-done((f32[256,256]{1,0:T(8,128)S(1)}, f32[256,256]{1,0:T(8,128)S(1)}, u32[]{:S(2)}, u32[]{:S(2)}) %collective-permute-start.13) | collective-permute-done | bytes 262176 | tf_op jit(solution)/shard_map/ppermute | solution.py:365
  115.3 2.6 %shard_map.71 = (f32[256,256]{1,0:T(8,128)}, f32[256,256]{1,0:T(8,128)}) custom-call(f32[256,256]{1,0:T(8,128)S(1)} %add.65.before, bf16[8,256,768]{2,1,0:T(8,128)(2,1)S(1)} %get-tuple-element.26.high0.high1.high, bf16[8,256,768]{2,1,0:T(8,128)(2,1)S(1)} %get-tuple-element.27.low0.low1.low, bf16[8,256,768]{2,1,0:T(8,128)(2,1)S(1)} %get-tuple-element.26.high0.high1.high, ...), custom_call_target="tpu_custom_call" | custom-call | tf_op jit(solution)/shard_map/pallas_call | solution.py:294
  117.8 1.7 %collective-permute-start.14 = (f32[256,256]{1,0:T(8,128)}, f32[256,256]{1,0:T(8,128)}, u32[]{:S(2)}, u32[]{:S(2)}) collective-permute-start(f32[256,256]{1,0:T(8,128)} %get-tuple-element.34.tail.old_tail), channel_id=1, source_target_pairs={{0,8},{4,12},{8,16},{12,20},{16,24},{20,28},{24,0},{28,4},{1,9},{5... | collective-permute-start | bytes 786440 | tf_op jit(solution)/shard_map/ppermute | solution.py:365
  119.6 2.1 %collective-permute-start.15 = (f32[256,256]{1,0:T(8,128)}, f32[256,256]{1,0:T(8,128)}, u32[]{:S(2)}, u32[]{:S(2)}) collective-permute-start(f32[256,256]{1,0:T(8,128)} %get-tuple-element.33.head.old_head), channel_id=1, source_target_pairs={{0,24},{4,28},{8,0},{12,4},{16,8},{20,12},{24,16},{28,20},{1,25},{... | collective-permute-start | bytes 786440 | tf_op jit(solution)/shard_map/ppermute | solution.py:365
  121.7 1.9 %copy-done.1 = bf16[8,256,768]{2,1,0:T(8,128)(2,1)S(1)} copy-done((bf16[8,256,768]{2,1,0:T(8,128)(2,1)S(1)}, bf16[8,256,768]{2,1,0:T(8,128)(2,1)}, u32[]{:S(2)}) %copy-start.1) | copy-done | bytes 3145752
  128.3 2.0 %shard_map.72.inner.old = f32[6,256,256]{2,1,0:T(8,128)S(1)} custom-call(bf16[8,256,768]{2,1,0:T(8,128)(2,1)S(1)} %get-tuple-element.26.high0.high1.high, bf16[8,256,768]{2,1,0:T(8,128)(2,1)S(1)} %copy-done.1, f32[256,256]{1,0:T(8,128)S(1)} %copy-done.18, f32[256,256]{1,0:T(8,128)S(1)} %copy-done.21, f32[6,256,256]{2,1,0:T(8,128)S(1)} %copy-done.7, ...), custom_call_target="tpu_custom_call" | custom-call | tf_op jit(solution)/shard_map/pallas_call | solution.py:306
  130.4 3.1 %shard_map.74.inner = f32[6,256,256]{2,1,0:T(8,128)S(1)} custom-call(bf16[8,256,768]{2,1,0:T(8,128)(2,1)S(1)} %get-tuple-element.26.high0.high1.high, bf16[8,256,768]{2,1,0:T(8,128)(2,1)S(1)} %copy-done.1, f32[256,256]{1,0:T(8,128)} %get-tuple-element.33.head.old_head, f32[256,256]{1,0:T(8,128)} %get-tuple-element.34.tail.old_tail, ...), custom_call_target="tpu_custom_call" | custom-call | tf_op jit(solution)/shard_map/pallas_call | solution.py:306
  133.5 3.3 %shard_map.73 = (f32[256,256]{1,0:T(8,128)}, f32[256,256]{1,0:T(8,128)}) custom-call(f32[256,256]{1,0:T(8,128)S(1)} %add.65.before, bf16[8,256,768]{2,1,0:T(8,128)(2,1)S(1)} %get-tuple-element.26.high0.high1.high, bf16[8,256,768]{2,1,0:T(8,128)(2,1)S(1)} %copy-done.1, bf16[8,256,768]{2,1,0:T(8,128)(2,1)S(1)} %get-tuple-element.26.high0.high1.high, ...), custom_call_target="tpu_custom_call" | custom-call | tf_op jit(solution)/shard_map/pallas_call | solution.py:294
  136.8 3.1 %shard_map.76.inner_ref = f32[6,256,256]{2,1,0:T(8,128)S(1)} custom-call(bf16[8,256,768]{2,1,0:T(8,128)(2,1)S(1)} %get-tuple-element.26.high0.high1.high, bf16[8,256,768]{2,1,0:T(8,128)(2,1)S(1)} %copy-done.1, f32[256,256]{1,0:T(8,128)} %get-tuple-element.35.head, f32[256,256]{1,0:T(8,128)} %get-tuple-element.36.tail, f32[6,256,256]{2,1,0:T(8,128)S(1)} %shard_map.74.inner, ...), custom_call_target="tpu_custom_call" | custom-call | tf_op jit(solution)/shard_map/pallas_call | solution.py:306
  143.6 3.8 %collective-permute-start.17 = (f32[256,256]{1,0:T(8,128)}, f32[256,256]{1,0:T(8,128)}, u32[]{:S(2)}, u32[]{:S(2)}) collective-permute-start(f32[256,256]{1,0:T(8,128)} %get-tuple-element.35.head), channel_id=1, source_target_pairs={{0,24},{4,28},{8,0},{12,4},{16,8},{20,12},{24,16},{28,20},{1,25},{... | collective-permute-start | bytes 786440 | tf_op jit(solution)/shard_map/ppermute | solution.py:365
  147.4 7.5 %collective-permute-done.16.below = f32[256,256]{1,0:T(8,128)} collective-permute-done((f32[256,256]{1,0:T(8,128)}, f32[256,256]{1,0:T(8,128)}, u32[]{:S(2)}, u32[]{:S(2)}) %collective-permute-start.16) | collective-permute-done | bytes 262176 | tf_op jit(solution)/shard_map/ppermute | solution.py:365
  156.3 1.9 %copy-done.2 = bf16[8,256,768]{2,1,0:T(8,128)(2,1)S(1)} copy-done((bf16[8,256,768]{2,1,0:T(8,128)(2,1)S(1)}, bf16[8,256,768]{2,1,0:T(8,128)(2,1)}, u32[]{:S(2)}) %copy-start.2) | copy-done | bytes 3145752
  159.6 2.3 %shard_map.75 = (f32[256,256]{1,0:T(8,128)S(1)}, f32[256,256]{1,0:T(8,128)S(1)}) custom-call(f32[256,256]{1,0:T(8,128)S(1)} %add.65.before, bf16[8,256,768]{2,1,0:T(8,128)(2,1)S(1)} %get-tuple-element.26.high0.high1.high, bf16[8,256,768]{2,1,0:T(8,128)(2,1)S(1)} %copy-done.2, bf16[8,256,768]{2,1,0:T(8,128)(2,1)S(1)} %get-tuple-element.26.high0.high1.high, ...), custom_call_target="tpu_custom_call" | custom-call | tf_op jit(solution)/shard_map/pallas_call | solution.py:294
  162.6 5.8 %collective-permute-done.18.got_end_ref = f32[256,256]{1,0:T(8,128)S(1)} collective-permute-done((f32[256,256]{1,0:T(8,128)S(1)}, f32[256,256]{1,0:T(8,128)S(1)}, u32[]{:S(2)}, u32[]{:S(2)}) %collective-permute-start.18) | collective-permute-done | bytes 262176 | tf_op jit(solution)/shard_map/ppermute | solution.py:360
  168.4 3.7 %shard_map.77 = f32[4,256,512]{2,1,0:T(8,128)} custom-call(s32[1]{0:T(128)} %bitcast.side_ref, f32[256,256]{1,0:T(8,128)S(1)} %get-tuple-element.37.head_ref, f32[256,256]{1,0:T(8,128)S(1)} %get-tuple-element.38.tail_ref, f32[6,256,256]{2,1,0:T(8,128)S(1)} %copy-done.14, f32[256,256]{1,0:T(8,128)S(1)} %collective-permute-done.18.got_end_ref, ...), custom_call_target="tpu_custom_call" | custom-call | tf_op jit(solution)/shard_map/pallas_call | solution.py:339
  (90 shorter events, 28.0 us)
Async XLA Ops:
  0.0 9.0 %copy-start.25 = (s32[4,64]{1,0:T(4,128)S(1)}, s32[4,64]{1,0:T(4,128)}, u32[]{:S(2)}) copy-start(s32[4,64]{1,0:T(4,128)} %param.10) | copy-start | bytes 3076
  2.4 6.5 %copy-start.23 = (s32[4,4,64]{2,1,0:T(4,128)S(1)}, s32[4,4,64]{2,1,0:T(4,128)}, u32[]{:S(2)}) copy-start(s32[4,4,64]{2,1,0:T(4,128)} %param.9) | copy-start | bytes 12292
  2.4 6.6 %copy-start.24 = (f32[4,512]{1,0:T(4,128)S(1)}, f32[4,512]{1,0:T(4,128)}, u32[]{:S(2)}) copy-start(f32[4,512]{1,0:T(4,128)} %param.8) | copy-start | bytes 24580
  2.4 6.7 %copy-start.16 = (f32[4,512,256]{2,1,0:T(8,128)S(1)}, f32[4,512,256]{2,1,0:T(8,128)}, u32[]{:S(2)}) copy-start(f32[4,512,256]{2,1,0:T(8,128)} %basis_ref.3) | copy-start | bytes 6291460
  2.8 11.5 %collective-permute-start = (f32[256,128]{1,0:T(8,128)S(1)}, f32[256,128]{1,0:T(8,128)S(1)}, u32[]{:S(2)}, u32[]{:S(2)}) collective-permute-start(f32[256,128]{1,0:T(8,128)S(1)} %shard_map.65), channel_id=1, source_target_pairs={{0,28},{4,0},{8,4},{12,8},{16,12},{20,16},{24,20},{28,24},{1,29},{... | collective-permute-start | bytes 393224 | tf_op jit(solution)/shard_map/ppermute | solution.py:365
  17.7 2.4 %collective-permute-start.1 = (f32[2,392,256]{2,1,0:T(8,128)S(1)}, f32[2,392,256]{2,1,0:T(8,128)S(1)}, u32[]{:S(2)}, u32[]{:S(2)}) collective-permute-start(f32[2,392,256]{2,1,0:T(8,128)S(1)} %get-tuple-element.25), channel_id=1, source_target_pairs={{0,1},{1,0},{2,3},{3,2},{4,5},{5,4},{6,7},{7,6},{8,9},{9,8},{10,11... | collective-permute-start | bytes 2408456 | tf_op jit(solution)/shard_map/ppermute | solution.py:360
  20.1 11.4 %collective-permute-start.2 = (f32[1,392,256]{2,1,0:T(8,128)S(1)}, f32[1,392,256]{2,1,0:T(8,128)S(1)}, u32[]{:S(2)}, u32[]{:S(2)}) collective-permute-start(f32[1,392,256]{2,1,0:T(8,128)S(1)} %dynamic-slice_add_fusion), channel_id=1, source_target_pairs={{0,2},{1,3},{2,0},{3,1},{4,6},{5,7},{6,4},{7,5},{8,10},{9,11},{10,... | collective-permute-start | bytes 1204232 | tf_op jit(solution)/shard_map/ppermute | solution.py:360
  31.6 10.6 %collective-permute-start.4 = (f32[1,392,256]{2,1,0:T(8,128)S(1)}, f32[1,392,256]{2,1,0:T(8,128)S(1)}, u32[]{:S(2)}, u32[]{:S(2)}) collective-permute-start(f32[1,392,256]{2,1,0:T(8,128)S(1)} %add_add_fusion), channel_id=1, source_target_pairs={{0,4},{4,0},{8,12},{12,8},{16,20},{20,16},{24,28},{28,24},{1,5},{5... | collective-permute-start | bytes 1204232 | tf_op jit(solution)/shard_map/ppermute | solution.py:360
  31.7 12.0 %collective-permute-start.3 = (f32[1,392,256]{2,1,0:T(8,128)S(1)}, f32[1,392,256]{2,1,0:T(8,128)S(1)}, u32[]{:S(2)}, u32[]{:S(2)}) collective-permute-start(f32[1,392,256]{2,1,0:T(8,128)S(1)} %add_add_fusion), channel_id=1, source_target_pairs={{0,2},{1,3},{2,0},{3,1},{4,6},{5,7},{6,4},{7,5},{8,10},{9,11},{10,... | collective-permute-start | bytes 1204232 | tf_op jit(solution)/shard_map/ppermute | solution.py:360
  42.2 9.6 %collective-permute-start.5 = (f32[1,392,256]{2,1,0:T(8,128)S(1)}, f32[1,392,256]{2,1,0:T(8,128)S(1)}, u32[]{:S(2)}, u32[]{:S(2)}) collective-permute-start(f32[1,392,256]{2,1,0:T(8,128)S(1)} %collective-permute-done.4), channel_id=1, source_target_pairs={{0,2},{1,3},{2,0},{3,1},{4,6},{5,7},{6,4},{7,5},{8,10},{9,11},{10,... | collective-permute-start | bytes 1204232 | tf_op jit(solution)/shard_map/ppermute | solution.py:360
  51.9 4.1 %copy-start.9 = (f32[4,392,256]{2,1,0:T(8,128)}, f32[4,392,256]{2,1,0:T(8,128)S(1)}, u32[]{:S(2)}) copy-start(f32[4,392,256]{2,1,0:T(8,128)S(1)} %pad_maximum_fusion.own_ref.before_own_ref) | copy-start | bytes 4816900
  51.9 39.6 %collective-permute-start.8 = (f32[4,392,256]{2,1,0:T(8,128)S(1)}, f32[4,392,256]{2,1,0:T(8,128)}, u32[]{:S(2)}, u32[]{:S(2)}) collective-permute-start(f32[4,392,256]{2,1,0:T(8,128)S(1)} %pad_maximum_fusion.own_ref.before_own_ref), channel_id=1, source_target_pairs={{0,1},{1,0},{2,3},{3,2},{4,5},{5,4},{6,7},{7,6},{8,9},{9,8},{10,11... | collective-permute-start | bytes 4816904 | tf_op jit(solution)/shard_map/ppermute | solution.py:360
  55.2 25.4 %collective-permute-start.9 = (f32[4,256,256]{2,1,0:T(8,128)}, f32[4,256,256]{2,1,0:T(8,128)}, u32[]{:S(2)}, u32[]{:S(2)}) collective-permute-start(f32[4,256,256]{2,1,0:T(8,128)} %get-tuple-element.39), channel_id=1, source_target_pairs={{0,4},{4,0},{8,12},{12,8},{16,20},{20,16},{24,28},{28,24},{1,5},{5... | collective-permute-start | bytes 3145736 | tf_op jit(solution)/shard_map/ppermute | solution.py:360
  56.0 0.7 collective-permute-start.6
  56.7 33.8 %collective-permute-start.7 = (f32[256,256]{1,0:T(8,128)S(1)}, f32[256,256]{1,0:T(8,128)}, u32[]{:S(2)}, u32[]{:S(2)}) collective-permute-start(f32[256,256]{1,0:T(8,128)S(1)} %collective-permute-done.6), channel_id=1, source_target_pairs={{1,0},{3,2},{5,4},{7,6},{9,8},{11,10},{13,12},{15,14},{17,16},{19,... | collective-permute-start | bytes 786440 | tf_op jit(solution)/shard_map/ppermute | solution.py:411
  86.7 12.3 %collective-permute-start.10 = (f32[256,256]{1,0:T(8,128)}, f32[256,256]{1,0:T(8,128)}, u32[]{:S(2)}, u32[]{:S(2)}) collective-permute-start(f32[256,256]{1,0:T(8,128)} %get-tuple-element.29.tail.old_tail), channel_id=1, source_target_pairs={{0,8},{4,12},{8,16},{12,20},{16,24},{20,28},{24,0},{28,4},{1,9},{5... | collective-permute-start | bytes 786440 | tf_op jit(solution)/shard_map/ppermute | solution.py:365
  86.7 13.3 %collective-permute-start.11 = (f32[256,256]{1,0:T(8,128)}, f32[256,256]{1,0:T(8,128)}, u32[]{:S(2)}, u32[]{:S(2)}) collective-permute-start(f32[256,256]{1,0:T(8,128)} %get-tuple-element.28.head.old_head), channel_id=1, source_target_pairs={{0,24},{4,28},{8,0},{12,4},{16,8},{20,12},{24,16},{28,20},{1,25},{... | collective-permute-start | bytes 786440 | tf_op jit(solution)/shard_map/ppermute | solution.py:365
  92.9 7.0 %copy-start.4 = (f32[6,256,256]{2,1,0:T(8,128)S(1)}, f32[6,256,256]{2,1,0:T(8,128)}, u32[]{:S(2)}) copy-start(f32[6,256,256]{2,1,0:T(8,128)} %copy-done.3) | copy-start | bytes 4718596
  99.0 16.2 %copy-start = (bf16[8,256,768]{2,1,0:T(8,128)(2,1)}, bf16[8,256,768]{2,1,0:T(8,128)(2,1)S(1)}, u32[]{:S(2)}) copy-start(bf16[8,256,768]{2,1,0:T(8,128)(2,1)S(1)} %get-tuple-element.27.low0.low1.low) | copy-start | bytes 9437188
  102.2 13.0 %copy-start.17 = (f32[256,256]{1,0:T(8,128)}, f32[256,256]{1,0:T(8,128)S(1)}, u32[]{:S(2)}) copy-start(f32[256,256]{1,0:T(8,128)S(1)} %get-tuple-element.31.head.old_head) | copy-start | bytes 786436
  102.2 13.0 %copy-start.20 = (f32[256,256]{1,0:T(8,128)}, f32[256,256]{1,0:T(8,128)S(1)}, u32[]{:S(2)}) copy-start(f32[256,256]{1,0:T(8,128)S(1)} %get-tuple-element.32.tail.old_tail) | copy-start | bytes 786436
  102.3 11.1 %collective-permute-start.12 = (f32[256,256]{1,0:T(8,128)S(1)}, f32[256,256]{1,0:T(8,128)S(1)}, u32[]{:S(2)}, u32[]{:S(2)}) collective-permute-start(f32[256,256]{1,0:T(8,128)S(1)} %get-tuple-element.32.tail.old_tail), channel_id=1, source_target_pairs={{0,8},{4,12},{8,16},{12,20},{16,24},{20,28},{24,0},{28,4},{1,9},{5... | collective-permute-start | bytes 786440 | tf_op jit(solution)/shard_map/ppermute | solution.py:365
  103.1 12.2 %collective-permute-start.13 = (f32[256,256]{1,0:T(8,128)S(1)}, f32[256,256]{1,0:T(8,128)S(1)}, u32[]{:S(2)}, u32[]{:S(2)}) collective-permute-start(f32[256,256]{1,0:T(8,128)S(1)} %get-tuple-element.31.head.old_head), channel_id=1, source_target_pairs={{0,24},{4,28},{8,0},{12,4},{16,8},{20,12},{24,16},{28,20},{1,25},{... | collective-permute-start | bytes 786440 | tf_op jit(solution)/shard_map/ppermute | solution.py:365
  109.2 8.6 %copy-start.6 = (f32[6,256,256]{2,1,0:T(8,128)}, f32[6,256,256]{2,1,0:T(8,128)S(1)}, u32[]{:S(2)}) copy-start(f32[6,256,256]{2,1,0:T(8,128)S(1)} %shard_map.70.inner.old) | copy-start | bytes 4718596
  117.8 15.7 %collective-permute-start.14 = (f32[256,256]{1,0:T(8,128)}, f32[256,256]{1,0:T(8,128)}, u32[]{:S(2)}, u32[]{:S(2)}) collective-permute-start(f32[256,256]{1,0:T(8,128)} %get-tuple-element.34.tail.old_tail), channel_id=1, source_target_pairs={{0,8},{4,12},{8,16},{12,20},{16,24},{20,28},{24,0},{28,4},{1,9},{5... | collective-permute-start | bytes 786440 | tf_op jit(solution)/shard_map/ppermute | solution.py:365
  119.6 13.9 %collective-permute-start.15 = (f32[256,256]{1,0:T(8,128)}, f32[256,256]{1,0:T(8,128)}, u32[]{:S(2)}, u32[]{:S(2)}) collective-permute-start(f32[256,256]{1,0:T(8,128)} %get-tuple-element.33.head.old_head), channel_id=1, source_target_pairs={{0,24},{4,28},{8,0},{12,4},{16,8},{20,12},{24,16},{28,20},{1,25},{... | collective-permute-start | bytes 786440 | tf_op jit(solution)/shard_map/ppermute | solution.py:365
  133.5 3.3 %copy-start.11 = (f32[6,256,256]{2,1,0:T(8,128)}, f32[6,256,256]{2,1,0:T(8,128)S(1)}, u32[]{:S(2)}) copy-start(f32[6,256,256]{2,1,0:T(8,128)S(1)} %shard_map.74.inner) | copy-start | bytes 4718596
  142.0 26.3 %collective-permute-start.19 = (f32[3,256,256]{2,1,0:T(8,128)}, f32[3,256,256]{2,1,0:T(8,128)}, u32[]{:S(2)}, u32[]{:S(2)}) collective-permute-start(f32[3,256,256]{2,1,0:T(8,128)} %constant_dynamic-slice_fusion.2), channel_id=1, source_target_pairs={{0,4},{4,0},{8,12},{12,8},{16,20},{20,16},{24,28},{28,24},{1,5},{5... | collective-permute-start | bytes 2359304 | tf_op jit(solution)/shard_map/ppermute | solution.py:360
  143.6 11.4 %collective-permute-start.16 = (f32[256,256]{1,0:T(8,128)}, f32[256,256]{1,0:T(8,128)}, u32[]{:S(2)}, u32[]{:S(2)}) collective-permute-start(f32[256,256]{1,0:T(8,128)} %get-tuple-element.36.tail), channel_id=1, source_target_pairs={{0,8},{4,12},{8,16},{12,20},{16,24},{20,28},{24,0},{28,4},{1,9},{5... | collective-permute-start | bytes 786440 | tf_op jit(solution)/shard_map/ppermute | solution.py:365
  143.6 12.7 %collective-permute-start.17 = (f32[256,256]{1,0:T(8,128)}, f32[256,256]{1,0:T(8,128)}, u32[]{:S(2)}, u32[]{:S(2)}) collective-permute-start(f32[256,256]{1,0:T(8,128)} %get-tuple-element.35.head), channel_id=1, source_target_pairs={{0,24},{4,28},{8,0},{12,4},{16,8},{20,12},{24,16},{28,20},{1,25},{... | collective-permute-start | bytes 786440 | tf_op jit(solution)/shard_map/ppermute | solution.py:365
  159.6 8.8 %copy-start.14 = (f32[6,256,256]{2,1,0:T(8,128)S(1)}, f32[6,256,256]{2,1,0:T(8,128)}, u32[]{:S(2)}) copy-start(f32[6,256,256]{2,1,0:T(8,128)} %copy-done.13) | copy-start | bytes 4718596
  161.9 6.4 %collective-permute-start.18 = (f32[256,256]{1,0:T(8,128)S(1)}, f32[256,256]{1,0:T(8,128)S(1)}, u32[]{:S(2)}, u32[]{:S(2)}) collective-permute-start(f32[256,256]{1,0:T(8,128)S(1)} %broadcast_select_fusion), channel_id=1, source_target_pairs={{0,4},{4,0},{8,12},{12,8},{16,20},{20,16},{24,28},{28,24},{1,5},{5... | collective-permute-start | bytes 786440 | tf_op jit(solution)/shard_map/ppermute | solution.py:360
  (14 other events, 22.1 us)

commit v2 on v1

v2 whole, which is shorter than its diff:
```python
import functools

import jax
import jax.numpy as jnp
from jax import lax
from jax.experimental import pallas as pl
from jax.experimental.pallas import tpu as pltpu
from jax.sharding import PartitionSpec as P

NB = 256
DEG = 4

penalty = 3.0
center = 4.0
half_width = 12.0

LARGE = pltpu.CompilerParams(vmem_limit_bytes=48 * 1024 * 1024)
SMALL = pltpu.CompilerParams(vmem_limit_bytes=24 * 1024 * 1024)
VMEM = pl.BlockSpec(memory_space=pltpu.VMEM)
NN = (((1,), (0,)), ((), ()))
NT = (((1,), (1,)), ((), ()))


def split(value):
    high = value.astype(jnp.bfloat16)
    low = (value - high.astype(jnp.float32)).astype(jnp.bfloat16)
    return high, low


def dot(first, second, dims=NN):
    return lax.dot_general(first, second, dims, preferred_element_type=jnp.float32)


def dot3(first, second, dims=NN):
    first_high, first_low = first
    second_high, second_low = second
    return dot(first_high, second_high, dims) + (dot(first_high, second_low, dims) + dot(first_low, second_high, dims))


def picked(parts, chosen):
    return dot(parts[0], chosen) + dot(parts[1], chosen)


def one_hot(index_row, rows, offset=0):
    at = lax.broadcasted_iota(jnp.int32, (rows, index_row.shape[1]), 0) - offset
    return (at == index_row).astype(jnp.float32).astype(jnp.bfloat16)


def edge_kernel(index_ref, basis_ref, traces_ref):
    parts = split(basis_ref[0].T)
    traces_ref[...] = picked(parts, one_hot(index_ref[0], basis_ref.shape[1]))


def volume_kernel(faces_total, index_ref, quad_ref, basis_ref, applied_ref, traces_ref, volume_ref):
    flipped = basis_ref[0].T
    traces = picked(split(flipped), one_hot(index_ref[0], basis_ref.shape[1]))
    traces_ref[0] = traces
    width = traces.shape[1] // 2
    outer, layer = traces[:, :width], traces[:, width:]
    total = dot3(split(flipped * quad_ref[0]), split(applied_ref[0]))
    total = total + dot3(split((2.0 * outer + layer) * (1.0 / faces_total)), split(outer), NT)
    volume_ref[0] = 0.5 * (total + total.T)


def packed(volume):
    half = volume.shape[0] // 2
    row = lax.broadcasted_iota(jnp.int32, (half, half), 0)
    column = lax.broadcasted_iota(jnp.int32, (half, half), 1)
    corner = volume[half:, half:]
    mixed = jnp.where(column >= row, volume[:half, :half], corner)
    diagonal = jnp.sum(jnp.where(column == row, corner, 0.0), axis=0, keepdims=True)
    return mixed, volume[:half, half:], diagonal


def unpacked(mixed, side, diagonal):
    half = mixed.shape[0]
    row = lax.broadcasted_iota(jnp.int32, (half, half), 0)
    column = lax.broadcasted_iota(jnp.int32, (half, half), 1)
    turned = mixed.T
    first = jnp.where(column >= row, mixed, turned)
    corner = jnp.where(column < row, mixed, jnp.where(column == row, diagonal, turned))
    top = jnp.concatenate([first, side], axis=1)
    return jnp.concatenate([top, jnp.concatenate([side.T, corner], axis=1)], axis=0)


def coupling_kernel(faces_total, count, order_ref, pair_ref, own_ref, next_ref, lead_ref, volume_ref, send_ref, keep_ref):
    step = pl.program_id(0)
    element = order_ref[step]
    own = own_ref[0]
    size = own.shape[0]
    width = own.shape[1] // 2
    outer, layer = own[:, :width], own[:, width:]
    near = split((penalty * outer + 0.5 * layer) * (-1.0 / faces_total))
    far = split(outer * (0.5 / faces_total))
    mixed, side, diagonal = packed(volume_ref[0])
    half = size // 2

    def store(out_ref, coupling):
        out_ref[0, :size] = coupling
        out_ref[0, size : size + half, :half] = mixed
        out_ref[0, size : size + half, half:] = side
        out_ref[0, size + half :, :] = jnp.broadcast_to(jnp.concatenate([diagonal, diagonal], axis=1), (8, size))

    def finish(face, inside):
        coupling = dot3(near, split(face), NT) + dot3(far, split(inside), NT)

        @pl.when(step < count // 2)
        def _():
            store(send_ref, coupling)

        @pl.when(step >= count // 2)
        def _():
            store(keep_ref, coupling)

    @pl.when(element < count - 1)
    def _():
        order = one_hot(pair_ref[0], width)
        following = next_ref[0]
        finish(picked(split(following[:, :width]), order), picked(split(following[:, width:]), order))

    @pl.when(element == count - 1)
    def _():
        lead = split(lead_ref[...])
        finish(picked(lead, one_hot(pair_ref[0], width)), picked(lead, one_hot(pair_ref[0], width, width // 2)))


def weights_kernel(me_ref, mine, beside, across, both, near_ref, far_ref, high_ref, low_ref):
    me = me_ref[0]
    size = mine.shape[2]
    half = size // 2
    pieces = {0: (mine, 0), 1: (beside, 0), 4: (across, 0), 5: (both, 0), 2: (near_ref, 0), 3: (near_ref, 1), 6: (near_ref, 2), 7: (far_ref, 0)}
    row = lax.broadcasted_iota(jnp.int32, (size, size), 0)
    diagonal = row == lax.broadcasted_iota(jnp.int32, (size, size), 1)

    for away, (piece, at) in pieces.items():
        element = away ^ me
        volume = unpacked(
            piece[at, size : size + half, :half], piece[at, size : size + half, half:], piece[at, size + half : size + half + 1, :half]
        )
        volume = (volume - jnp.where(diagonal, center, 0.0)) * (1.0 / half_width)
        coupling = piece[at, :size] * (1.0 / half_width)
        following = lax.rem(element + 1, len(pieces))
        for place, at_column, value in ((following, 0, coupling.T), (element, 1, volume), (element, 2, coupling)):
            high, low = split(value)
            high_ref[place, :, at_column * size : (at_column + 1) * size] = high
            low_ref[place, :, at_column * size : (at_column + 1) * size] = low


def apply_row(weights, values):
    total = None
    for weight, value in zip(weights, values):
        term = dot3(weight, split(value))
        total = term if total is None else total + term
    return total


def row_weights(high, low):
    size = high.shape[0]
    return [(high[:, at * size : (at + 1) * size], low[:, at * size : (at + 1) * size]) for at in range(3)]


def advance(first, result, before):
    return result if first else 2.0 * result - before


def head_kernel(first, before, high, low, head, inner, below, old, out):
    rows = row_weights(high[0], low[0])
    rows[0] = split((before[...] * (1.0 / half_width)).T)
    out[...] = advance(first, apply_row(rows, (below[...], head[...], inner[0])), None if first else old[...])


def tail_kernel(first, high, low, tail, inner, above, old, out):
    rows = row_weights(high[high.shape[0] - 1], low[high.shape[0] - 1])
    values = (inner[inner.shape[0] - 1], tail[...], above[...])
    out[...] = advance(first, apply_row(rows, values), None if first else old[...])


def inner_kernel(first, high, low, head, tail, inner, old, out):
    count = inner.shape[0]

    @pl.loop(0, count)
    def _(at):
        lower = jnp.where(at == 0, head[...], inner[jnp.maximum(at - 1, 0)])
        upper = jnp.where(at == count - 1, tail[...], inner[jnp.minimum(at + 1, count - 1)])
        row = apply_row(row_weights(high[at + 1], low[at + 1]), (lower, inner[at], upper))
        out[at] = advance(first, row, None if first else old[at])


def cut_kernel(vector_ref, *out_refs):
    width = out_refs[0].shape[2]
    for at, out_ref in enumerate(out_refs):
        out_ref[...] = vector_ref[:, :, at * width : (at + 1) * width]


def arrange_kernel(count, side_ref, own_ref, got_ref, head_ref, tail_ref, inner_ref):
    step = pl.program_id(0)
    value = jnp.where(step // (count // 2) == side_ref[0], own_ref[0], got_ref[0])

    @pl.when(step == 0)
    def _():
        head_ref[...] = value

    @pl.when(step == count - 1)
    def _():
        tail_ref[...] = value

    @pl.when((step > 0) & (step < count - 1))
    def _():
        inner_ref[0] = value


def collect_kernel(count, chunks, side_ref, *refs):
    out_ref = refs[-1]
    step = pl.program_id(0)
    side = side_ref[0]
    at_end = step == side * (count - 1)
    for chunk in range(chunks):
        head_ref, tail_ref, inner_ref, got_end_ref, got_inner_ref = refs[5 * chunk : 5 * chunk + 5]
        end = jnp.where(side == 0, head_ref[...], tail_ref[...])
        mine = jnp.where(at_end, end, inner_ref[0])
        theirs = jnp.where(at_end, got_end_ref[...], got_inner_ref[0])
        width = mine.shape[1]
        first = chunk * width
        second = (chunks + chunk) * width
        out_ref[0, :, first : first + width] = jnp.where(side == 0, mine, theirs)
        out_ref[0, :, second : second + width] = jnp.where(side == 0, theirs, mine)


def whole(shape):
    return pl.BlockSpec(shape, lambda *steps: (0,) * len(shape))


def edge_traces(index, basis):
    points, size = basis.shape[1:]
    return pl.pallas_call(
        edge_kernel,
        grid=(1,),
        in_specs=[pl.BlockSpec((1, 1, index.shape[2]), lambda s: (0, 0, 0)), pl.BlockSpec((1, points, size), lambda s: (0, 0, 0))],
        out_specs=whole((size, index.shape[2])),
        out_shape=jax.ShapeDtypeStruct((size, index.shape[2]), jnp.float32),
        compiler_params=LARGE,
    )(index, basis)


def volumes(index, quad, basis, applied, faces_total):
    count, points, size = basis.shape
    spots = index.shape[2]
    per = lambda *shape: pl.BlockSpec((1, *shape), lambda s: (s, 0, 0))
    return pl.pallas_call(
        functools.partial(volume_kernel, faces_total),
        grid=(count,),
        in_specs=[per(1, spots), per(1, points), per(points, size), per(points, size)],
        out_specs=[per(size, spots), per(size, size)],
        out_shape=[
            jax.ShapeDtypeStruct((count, size, spots), jnp.float32),
            jax.ShapeDtypeStruct((count, size, size), jnp.float32),
        ],
        compiler_params=LARGE,
    )(index, quad, basis, applied)


def couplings(order, pairs, traces, lead, volume, faces_total):
    count, size, spots = traces.shape
    rows = size + size // 2 + 8
    per = lambda *shape: pl.BlockSpec((1, *shape), lambda s, o: (o[s], 0, 0))
    half = count // 2
    return pl.pallas_call(
        functools.partial(coupling_kernel, faces_total, count),
        grid_spec=pltpu.PrefetchScalarGridSpec(
            num_scalar_prefetch=1,
            grid=(count,),
            in_specs=[
                per(1, pairs.shape[2]),
                per(size, spots),
                pl.BlockSpec((1, size, spots), lambda s, o: (jnp.minimum(o[s] + 1, count - 1), 0, 0)),
                whole(lead.shape),
                per(size, size),
            ],
            out_specs=[
                pl.BlockSpec((1, rows, size), lambda s, o: (jnp.minimum(s, half - 1), 0, 0)),
                pl.BlockSpec((1, rows, size), lambda s, o: (jnp.maximum(s - half, 0), 0, 0)),
            ],
        ),
        out_shape=[jax.ShapeDtypeStruct((half, rows, size), jnp.float32)] * 2,
        compiler_params=LARGE,
    )(order, pairs, traces, traces, lead, volume)


def weights(me, mine, beside, across, both, near, far):
    size = mine.shape[2]
    return pl.pallas_call(
        weights_kernel,
        in_specs=[pl.BlockSpec(memory_space=pltpu.SMEM)] + [VMEM] * 6,
        out_specs=[VMEM] * 2,
        out_shape=[jax.ShapeDtypeStruct((8, size, 3 * size), jnp.bfloat16)] * 2,
        compiler_params=SMALL,
    )(me, mine, beside, across, both, near, far)


def apply_head(first, before, high, low, head, inner, below, old):
    return pl.pallas_call(
        functools.partial(head_kernel, first),
        in_specs=[VMEM] * 7,
        out_specs=VMEM,
        out_shape=jax.ShapeDtypeStruct(head.shape, jnp.float32),
        compiler_params=SMALL,
    )(before, high, low, head, inner, below, old)


def apply_tail(first, high, low, tail, inner, above, old):
    return pl.pallas_call(
        functools.partial(tail_kernel, first),
        in_specs=[VMEM] * 6,
        out_specs=VMEM,
        out_shape=jax.ShapeDtypeStruct(tail.shape, jnp.float32),
        compiler_params=SMALL,
    )(high, low, tail, inner, above, old)


def apply_inner(first, high, low, head, tail, inner, old):
    return pl.pallas_call(
        functools.partial(inner_kernel, first),
        in_specs=[VMEM] * 6,
        out_specs=VMEM,
        out_shape=jax.ShapeDtypeStruct(inner.shape, jnp.float32),
        compiler_params=SMALL,
    )(high, low, head, tail, inner, old)


def cut_columns(side, vector, chunks):
    count, size, columns = vector.shape
    half = columns // 2
    return pl.pallas_call(
        lambda side_ref, *refs: cut_kernel(*refs),
        grid_spec=pltpu.PrefetchScalarGridSpec(
            num_scalar_prefetch=1,
            grid=(count,),
            in_specs=[pl.BlockSpec((1, size, half), lambda s, o: (s, 0, o[0]))],
            out_specs=[pl.BlockSpec((1, size, half // chunks), lambda s, o: (s, 0, 0))] * chunks,
        ),
        out_shape=[jax.ShapeDtypeStruct((count, size, half // chunks), jnp.float32)] * chunks,
        compiler_params=LARGE,
    )(side, vector)


def arranged(side, vector, got, chunk):
    half, size, columns = got.shape
    count = 2 * half
    chunks = max(vector.shape[2] // 2 // columns, 1)
    block = pl.BlockSpec((1, size, columns), lambda s, o: (s % half, 0, 0))
    own = pl.BlockSpec((1, size, columns), lambda s, o: (s % half, 0, o[1] * chunks + chunk))
    flat = pl.BlockSpec((size, columns), lambda s, o: (0, 0))
    return pl.pallas_call(
        functools.partial(arrange_kernel, count),
        grid_spec=pltpu.PrefetchScalarGridSpec(
            num_scalar_prefetch=1,
            grid=(count,),
            in_specs=[own, block],
            out_specs=[flat, flat, pl.BlockSpec((1, size, columns), lambda s, o: (jnp.clip(s - 1, 0, count - 3), 0, 0))],
        ),
        out_shape=[jax.ShapeDtypeStruct((size, columns), jnp.float32)] * 2
        + [jax.ShapeDtypeStruct((count - 2, size, columns), jnp.float32)],
        compiler_params=LARGE,
    )(side, vector, got)


def collected(side, parts):
    size, width = parts[0][0].shape
    chunks = len(parts)
    half = parts[0][4].shape[0] + 1
    spot = lambda s, o: jnp.where(o[0] == 0, jnp.maximum(s - 1, 0), jnp.minimum(s, half - 2))
    flat = pl.BlockSpec((size, width), lambda s, o: (0, 0))
    return pl.pallas_call(
        functools.partial(collect_kernel, half, chunks),
        grid_spec=pltpu.PrefetchScalarGridSpec(
            num_scalar_prefetch=1,
            grid=(half,),
            in_specs=[
                flat,
                flat,
                pl.BlockSpec((1, size, width), lambda s, o: (o[0] * (half - 1) + spot(s, o), 0, 0)),
                flat,
                pl.BlockSpec((1, size, width), lambda s, o: (spot(s, o), 0, 0)),
            ]
            * chunks,
            out_specs=pl.BlockSpec((1, size, 2 * chunks * width), lambda s, o: (s, 0, 0)),
        ),
        out_shape=jax.ShapeDtypeStruct((half, size, 2 * chunks * width), jnp.float32),
        compiler_params=LARGE,
    )(side, *[value for part in parts for value in part])


def flipped(value, axis, bit):
    count = lax.axis_size(axis)
    return lax.ppermute(value, axis, [(i, i ^ bit) for i in range(count)])


def shifted(value, axis, steps):
    count = lax.axis_size(axis)
    return lax.ppermute(value, axis, [(i, (i + steps) % count) for i in range(count)])


def body(basis, applied, quad, face_index, face_pairing, orbitals):
    count, points, size = basis.shape
    spots = face_index.shape[2]
    columns = orbitals.shape[1]
    chunks = 2 if columns % 512 == 0 else 1
    elems, width = lax.axis_size("elem"), lax.axis_size("pts")
    faces_total = float(spots * width)
    side = lax.axis_index("elem") % 2
    core = lax.axis_index("pts") % 2
    lane = lax.axis_index("pts") // 2 % 2
    side_at = side.reshape(1).astype(jnp.int32)
    vector = orbitals.reshape(count, size, columns)

    if columns // 2 % 128 == 0:
        own, own_at = vector, side_at
        foreign = cut_columns(1 - side_at, vector, chunks)
    else:
        own, own_at = lax.dynamic_slice_in_dim(vector, side * (columns // 2), columns // 2, axis=2), jnp.zeros_like(side_at)
        foreign = [lax.dynamic_slice_in_dim(vector, (1 - side) * (columns // 2), columns // 2, axis=2)]
    got = [flipped(value, "elem", 1) for value in foreign]

    lead_index = face_index[:1, 0:2].reshape(1, 1, 2 * spots)
    lead = shifted(edge_traces(lead_index, basis), "elem", -1)
    index = jnp.stack([face_index[:, 0], face_index[:, 2], face_index[:, 1], face_index[:, 3]], axis=1)
    index = index.reshape(count, 1, 4 * spots)
    pairs = jnp.concatenate([jnp.full_like(face_pairing, -points), face_pairing], axis=1).reshape(count, 1, 2 * spots)
    traces, volume = volumes(index, quad.reshape(count, 1, points), basis, applied, faces_total)
    got[0], lead, traces, volume = lax.optimization_barrier((got[0], lead, traces, volume))
    half = count // 2
    order = jnp.arange(count, dtype=jnp.int32) ^ ((1 - core).astype(jnp.int32) * half)
    send, keep = couplings(order, pairs, traces, lead, volume, faces_total)

    state, belows, aboves = [], [], []

    def arrange(chunk, received):
        state.append(arranged(jnp.concatenate([side_at, own_at]), own, received, chunk))
        belows.append(shifted(state[chunk][1], "elem", 2))
        aboves.append(shifted(state[chunk][0], "elem", -2))

    arrange(0, got[0])

    other = flipped(send, "pts", 1)
    quarter = half // 2
    pick = lambda value, at: lax.dynamic_slice_in_dim(value, at * quarter, quarter)
    send = pick(keep, 1 - lane) + pick(other, 1 - lane)
    mine = pick(keep, lane) + pick(other, lane) + flipped(send, "pts", 2)
    bit = 4
    while bit < width:
        mine = mine + flipped(mine, "pts", bit)
        bit *= 2
    belows[0], aboves[0], got_last, mine = lax.optimization_barrier((belows[0], aboves[0], got[-1], mine))
    if chunks > 1:
        arrange(1, got_last)
    beside = flipped(mine, "pts", 2)
    across = flipped(mine, "elem", 1)
    both = flipped(across, "pts", 2)
    near = flipped(jnp.concatenate([mine, beside, across]), "pts", 1)
    belows[-1], aboves[-1], both = lax.optimization_barrier((belows[-1], aboves[-1], both))
    far = flipped(both, "pts", 1)

    last = jnp.where(
        side == 1, jnp.where(lane == 1, mine[0, :size], beside[0, :size]), jnp.where(lane == 1, across[0, :size], both[0, :size])
    )
    flat = lambda e, p: e % elems * width + p
    odd = [(e, p) for e in range(elems) for p in range(1, width, 2)]
    before = lax.ppermute(last, ("elem", "pts"), [(flat(e, p), flat(e + 2, p)) for e, p in odd])
    before = before + lax.ppermute(before, ("elem", "pts"), [(flat(e, p), flat(e, p - 1)) for e, p in odd])

    me = (side * 4 + core * 2 + lane).reshape(1).astype(jnp.int32)
    high, low = weights(me, mine, beside, across, both, near, far)

    old = list(state)
    parts = []
    for degree in range(DEG):
        first = degree == 0
        for c in range(chunks):
            head, tail, inner = state[c]
            new_tail = apply_tail(first, high, low, tail, inner, aboves[c], old[c][1])
            new_head = apply_head(first, before, high, low, head, inner, belows[c], old[c][0])
            new_inner = apply_inner(first, high, low, head, tail, inner, old[c][2])
            old[c] = state[c]
            state[c] = new_head, new_tail, new_inner
            if degree < DEG - 1:
                belows[c] = shifted(new_tail, "elem", 2)
                aboves[c] = shifted(new_head, "elem", -2)
            else:
                foreign = lax.dynamic_slice_in_dim(new_inner, (1 - side) * (count - 1), count - 1)
                got_inner = flipped(foreign, "elem", 1)
                got_end = flipped(jnp.where(side == 0, new_tail, new_head), "elem", 1)
                parts.append((new_head, new_tail, new_inner, got_end, got_inner))
    return collected(side_at, parts).reshape(count * size, columns)


def solution(mesh):
    return jax.shard_map(
        body,
        mesh=mesh,
        in_specs=(
            P("elem", "pts", None),
            P("elem", "pts", None),
            P("elem", "pts"),
            P("elem", None, "pts"),
            P("elem", "pts"),
            P("elem", "pts"),
        ),
        out_specs=P("elem", "pts"),
        check_vma=False,
    )
```

time: 173 us -> 177 us (1.023)
  waiting for transfers between devices: 73.3 us -> 40.2 us
  Pallas kernels: 43.9 us -> 69 us
  starting transfers between devices: 31.2 us -> 46 us
  local copies, waits for them, and re-layouts: 22 us -> 15.5 us
  other arithmetic: 1.3 us -> 4.67 us
    ppermute x9 -> x13, waiting for transfers between devices: 57.5 us -> 21.6 us  [flipped(): return lax.ppermute(value, axis, [(i, i ^ bit) for i in range(count)])]
    pallas_call x10 -> x27, Pallas kernels: 31.6 us -> 53.2 us  [the longest x8 25.3 us: apply_inner(): pl.pallas_call(functools.partial(inner_kernel, first), in_specs=[VMEM] *...]
    ppermute x9 -> x13, starting transfers between devices: 7.83 us -> 16.1 us  [flipped(): return lax.ppermute(value, axis, [(i, i ^ bit) for i in range(count)])]
    ppermute x9 -> x17, starting transfers between devices: 21.4 us -> 28 us  [shifted(): lax.ppermute(value, axis, [(i, (i + steps) % count) for i in range(count)])]
    ppermute x1, waiting for transfers between devices: 0.01 us -> 6.55 us  [body(): lax.ppermute(before, ('elem', 'pts'), [(flat(e, p), flat(e, p - 1)) for e...]
    dynamic_slice x2, local copies, waits for them, and re-layouts: 4.13 us -> 0.07 us  [body(): lax.dynamic_slice_in_dim(new_inner, (1 - side) * (count - 1), count - 1)]
    ppermute x9 -> x17, waiting for transfers between devices: 15.8 us -> 12.1 us  [shifted(): lax.ppermute(value, axis, [(i, (i + steps) % count) for i in range(count)])]
    unnamed x52 -> x98, local copies, waits for them, and re-layouts: 16.9 us -> 15.2 us
  transfers between devices with their start and end apart: 20 -> 32, of which waited for: 11 -> 11; matrix products, arithmetic and copies ran while one was open for 3% -> 2% of each run, Pallas kernels for 15% -> 33%
where the time goes in v2:
time: 177 us; the launch traced here: 176 us
  Pallas kernels  69 us (39%)
  starting transfers between devices  46 us (26%)
  waiting for transfers between devices  40.2 us (23%)
  local copies, waits for them, and re-layouts  15.5 us (9%)
  other arithmetic  4.67 us (3%)
    ppermute x17, starting transfers between devices, shifted(): lax.ppermute(value, axis, [(i, (i + steps) % count) for i in range(count)])  28 us
    pallas_call x8, Pallas kernels, apply_inner(): pl.pallas_call(functools.partial(inner_kernel, first), in_specs=[VMEM] *...  25.3 us
    ppermute x13, waiting for transfers between devices, flipped(): return lax.ppermute(value, axis, [(i, i ^ bit) for i in range(count)])  21.6 us
    ppermute x13, starting transfers between devices, flipped(): return lax.ppermute(value, axis, [(i, i ^ bit) for i in range(count)])  16.1 us
    unnamed x98, local copies, waits for them, and re-layouts  15.2 us
    ppermute x17, waiting for transfers between devices, shifted(): lax.ppermute(value, axis, [(i, (i + steps) % count) for i in range(count)])  12.1 us
    pallas_call x8, Pallas kernels, apply_head(): pl.pallas_call(functools.partial(head_kernel, first), in_specs=[VMEM] * 7...  11.8 us
    pallas_call x8, Pallas kernels, apply_tail(): pl.pallas_call(functools.partial(tail_kernel, first), in_specs=[VMEM] * 6...  10.8 us
  transfers between devices with their start and end apart: 32, of which 11 were waited for; matrix products, arithmetic and copies ran while one was open for 2% of the time, Pallas kernels for 33%

profile of v2, /device:TPU:0, one launch (start us, length us, event | category | flops | bytes accessed | tf_op | source)
XLA Modules:
  0.0 176.1 jit_solution(12585712178235801144)
XLA Ops:
  1.9 3.0 %collective-permute-start = (f32[4,256,128]{2,1,0:T(8,128)S(1)}, f32[4,256,128]{2,1,0:T(8,128)S(1)}, u32[]{:S(2)}, u32[]{:S(2)}) collective-permute-start(f32[4,256,128]{2,1,0:T(8,128)S(1)} %get-tuple-element.30), channel_id=1, source_target_pairs={{0,4},{4,0},{8,12},{12,8},{16,20},{20,16},{24,28},{28,24},{1,5},{5... | collective-permute-start | bytes 1572872 | tf_op jit(solution)/shard_map/ppermute | solution.py:395
  5.4 4.4 %collective-permute-start.1 = (f32[256,128]{1,0:T(8,128)S(1)}, f32[256,128]{1,0:T(8,128)S(1)}, u32[]{:S(2)}, u32[]{:S(2)}) collective-permute-start(f32[256,128]{1,0:T(8,128)S(1)} %shard_map.65), channel_id=1, source_target_pairs={{0,28},{4,0},{8,4},{12,8},{16,12},{20,16},{24,20},{28,24},{1,29},{... | collective-permute-start | bytes 393224 | tf_op jit(solution)/shard_map/ppermute | solution.py:400
  10.1 4.8 %shard_map.66 = (f32[4,256,256]{2,1,0:T(8,128)S(1)}, f32[4,256,256]{2,1,0:T(8,128)S(1)}) custom-call(s32[4,1,256]{2,1,0:T(1,128)S(1)} %reshape.33.index_ref, f32[4,1,512]{2,1,0:T(1,128)S(1)} %reshape.34.quad_ref, f32[4,512,256]{2,1,0:T(8,128)S(1)} %copy-done.15, f32[4,512,256]{2,1,0:T(8,128)} %applied_ref.1), custom_call_target="tpu_custom_call" | custom-call | tf_op jit(solution)/shard_map/pallas_call | solution.py:249
  14.9 4.7 %collective-permute-done.1.lead_ref = f32[256,128]{1,0:T(8,128)S(1)} collective-permute-done((f32[256,128]{1,0:T(8,128)S(1)}, f32[256,128]{1,0:T(8,128)S(1)}, u32[]{:S(2)}, u32[]{:S(2)}) %collective-permute-start.1) | collective-permute-done | bytes 131104 | tf_op jit(solution)/shard_map/ppermute | solution.py:400
  20.5 4.2 %shard_map.68 = (f32[2,392,256]{2,1,0:T(8,128)}, f32[2,392,256]{2,1,0:T(8,128)S(1)}) custom-call(s32[4]{0:T(128)S(1)} %iota_xor_fusion.order_ref, s32[4,1,128]{2,1,0:T(1,128)S(1)} %bitcast.10, f32[4,256,256]{2,1,0:T(8,128)S(1)} %get-tuple-element.37.own_ref.next_ref, f32[4,256,256]{2,1,0:T(8,128)S(1)} %get-tuple-element.37.own_ref.next_ref, ...), custom_call_target="tpu_custom_call" | custom-call | tf_op jit(solution)/shard_map/pallas_call | solution.py:267
  24.6 2.6 %collective-permute-done.5 = f32[2,392,256]{2,1,0:T(8,128)} collective-permute-done((f32[2,392,256]{2,1,0:T(8,128)}, f32[2,392,256]{2,1,0:T(8,128)}, u32[]{:S(2)}, u32[]{:S(2)}) %collective-permute-start.5) | collective-permute-done | bytes 802848 | tf_op jit(solution)/shard_map/ppermute | solution.py:395
  35.6 2.2 %collective-permute-start.3 = (f32[256,128]{1,0:T(8,128)S(1)}, f32[256,128]{1,0:T(8,128)S(1)}, u32[]{:S(2)}, u32[]{:S(2)}) collective-permute-start(f32[256,128]{1,0:T(8,128)S(1)} %get-tuple-element.35.head.old), channel_id=1, source_target_pairs={{0,24},{4,28},{8,0},{12,4},{16,8},{20,12},{24,16},{28,20},{1,25},{... | collective-permute-start | bytes 393224 | tf_op jit(solution)/shard_map/ppermute | solution.py:400
  37.8 2.0 %collective-permute-done.6 = f32[1,392,256]{2,1,0:T(8,128)} collective-permute-done((f32[1,392,256]{2,1,0:T(8,128)S(1)}, f32[1,392,256]{2,1,0:T(8,128)}, u32[]{:S(2)}, u32[]{:S(2)}) %collective-permute-start.6) | collective-permute-done | bytes 401440 | tf_op jit(solution)/shard_map/ppermute | solution.py:395
  41.1 3.0 %collective-permute-done.4.got_ref = f32[4,256,128]{2,1,0:T(8,128)} collective-permute-done((f32[4,256,128]{2,1,0:T(8,128)}, f32[4,256,128]{2,1,0:T(8,128)}, u32[]{:S(2)}, u32[]{:S(2)}) %collective-permute-start.4) | collective-permute-done | bytes 524320 | tf_op jit(solution)/shard_map/ppermute | solution.py:395
  46.2 8.1 %collective-permute-done.7.beside = f32[1,392,256]{2,1,0:T(8,128)S(1)} collective-permute-done((f32[1,392,256]{2,1,0:T(8,128)S(1)}, f32[1,392,256]{2,1,0:T(8,128)S(1)}, u32[]{:S(2)}, u32[]{:S(2)}) %collective-permute-start.7) | collective-permute-done | bytes 401440 | tf_op jit(solution)/shard_map/ppermute | solution.py:395
  57.4 5.3 %shard_map.69 = (f32[256,128]{1,0:T(8,128)}, f32[256,128]{1,0:T(8,128)}, f32[6,256,128]{2,1,0:T(8,128)S(1)}) custom-call(s32[2]{0:T(128)S(1)} %pad_add_fusion.1.side_ref, f32[4,256,512]{2,1,0:T(8,128)S(1)} %bitcast.9, f32[4,256,128]{2,1,0:T(8,128)} %collective-permute-done.4.got_ref), custom_call_target="tpu_custom_call" | custom-call | tf_op jit(solution)/shard_map/pallas_call | solution.py:353
  63.6 3.6 %collective-permute-start.10 = (f32[256,128]{1,0:T(8,128)}, f32[256,128]{1,0:T(8,128)S(1)}, u32[]{:S(2)}, u32[]{:S(2)}) collective-permute-start(f32[256,128]{1,0:T(8,128)} %get-tuple-element.45.head.old), channel_id=1, source_target_pairs={{0,24},{4,28},{8,0},{12,4},{16,8},{20,12},{24,16},{28,20},{1,25},{... | collective-permute-start | bytes 393224 | tf_op jit(solution)/shard_map/ppermute | solution.py:400
  67.2 4.2 %collective-permute-done.10.above = f32[256,128]{1,0:T(8,128)S(1)} collective-permute-done((f32[256,128]{1,0:T(8,128)}, f32[256,128]{1,0:T(8,128)S(1)}, u32[]{:S(2)}, u32[]{:S(2)}) %collective-permute-start.10) | collective-permute-done | bytes 131104 | tf_op jit(solution)/shard_map/ppermute | solution.py:400
  71.4 3.1 %collective-permute-done.9.below = f32[256,128]{1,0:T(8,128)S(1)} collective-permute-done((f32[256,128]{1,0:T(8,128)}, f32[256,128]{1,0:T(8,128)S(1)}, u32[]{:S(2)}, u32[]{:S(2)}) %collective-permute-start.9) | collective-permute-done | bytes 131104 | tf_op jit(solution)/shard_map/ppermute | solution.py:400
  79.2 6.6 %collective-permute-done.13 = f32[256,256]{1,0:T(8,128)S(1)} collective-permute-done((f32[256,256]{1,0:T(8,128)S(1)}, f32[256,256]{1,0:T(8,128)S(1)}, u32[]{:S(2)}, u32[]{:S(2)}) %collective-permute-start.13) | collective-permute-done | bytes 262176 | tf_op jit(solution)/shard_map/ppermute | solution.py:469
  90.6 3.1 %shard_map.70 = (bf16[8,256,768]{2,1,0:T(8,128)(2,1)S(1)}, bf16[8,256,768]{2,1,0:T(8,128)(2,1)S(1)}) custom-call(s32[1]{0:T(128)} %bitcast.4.me_ref, f32[1,392,256]{2,1,0:T(8,128)S(1)} %copy-done.17, f32[1,392,256]{2,1,0:T(8,128)S(1)} %copy-done.19, f32[1,392,256]{2,1,0:T(8,128)S(1)} %copy-done.21, f32[1,392,256]{2,1,0:T(8,128)} %collective-permute-done.11.both, ...), custom_call_target="tpu_custom_call" | custom-call | tf_op jit(solution)/shard_map/pallas_call | solution.py:291
  97.3 2.0 %collective-permute-start.24 = (f32[256,128]{1,0:T(8,128)S(1)}, f32[256,128]{1,0:T(8,128)S(1)}, u32[]{:S(2)}, u32[]{:S(2)}) collective-permute-start(f32[256,128]{1,0:T(8,128)S(1)} %shard_map.85.tail.old), channel_id=1, source_target_pairs={{0,8},{4,12},{8,16},{12,20},{16,24},{20,28},{24,0},{28,4},{1,9},{5... | collective-permute-start | bytes 393224 | tf_op jit(solution)/shard_map/ppermute | solution.py:400
  102.5 3.8 %shard_map.84.inner.old = f32[6,256,128]{2,1,0:T(8,128)S(1)} custom-call(bf16[8,256,768]{2,1,0:T(8,128)(2,1)S(1)} %get-tuple-element.47.high, bf16[8,256,768]{2,1,0:T(8,128)(2,1)S(1)} %get-tuple-element.48.low, f32[256,128]{1,0:T(8,128)} %get-tuple-element.45.head.old, f32[256,128]{1,0:T(8,128)} %get-tuple-element.44.tail.old, f32[6,256,128]{2,1,0:T(8,128)S(1)} %copy-done.6, ...), custom_call_target="tpu_custom_call" | custom-call | tf_op jit(solution)/shard_map/pallas_call | solution.py:321
  106.3 2.2 %shard_map.88.tail.old = f32[256,128]{1,0:T(8,128)} custom-call(bf16[8,256,768]{2,1,0:T(8,128)(2,1)S(1)} %get-tuple-element.47.high, bf16[8,256,768]{2,1,0:T(8,128)(2,1)S(1)} %get-tuple-element.48.low, f32[256,128]{1,0:T(8,128)S(1)} %shard_map.85.tail.old, f32[6,256,128]{2,1,0:T(8,128)S(1)} %shard_map.84.inner.old, ...), custom_call_target="tpu_custom_call" | custom-call | tf_op jit(solution)/shard_map/pallas_call | solution.py:311
  108.5 2.1 %shard_map.86.head.old = f32[256,128]{1,0:T(8,128)} custom-call(f32[256,256]{1,0:T(8,128)S(1)} %add.52.before, bf16[8,256,768]{2,1,0:T(8,128)(2,1)S(1)} %get-tuple-element.47.high, bf16[8,256,768]{2,1,0:T(8,128)(2,1)S(1)} %get-tuple-element.48.low, f32[256,128]{1,0:T(8,128)S(1)} %shard_map.83.head.old, f32[6,256,128]{2,1,0:T(8,128)S(1)} %shard_map.84.inner.old, ...), custom_call_target="tpu_custom_call" | custom-call | tf_op jit(solution)/shard_map/pallas_call | solution.py:301
  110.7 3.8 %collective-permute-start.27 = (f32[256,128]{1,0:T(8,128)}, f32[256,128]{1,0:T(8,128)}, u32[]{:S(2)}, u32[]{:S(2)}) collective-permute-start(f32[256,128]{1,0:T(8,128)} %shard_map.86.head.old), channel_id=1, source_target_pairs={{0,24},{4,28},{8,0},{12,4},{16,8},{20,12},{24,16},{28,20},{1,25},{... | collective-permute-start | bytes 393224 | tf_op jit(solution)/shard_map/ppermute | solution.py:400
  114.4 2.8 %shard_map.72.inner.old = f32[6,256,128]{2,1,0:T(8,128)S(1)} custom-call(bf16[8,256,768]{2,1,0:T(8,128)(2,1)S(1)} %get-tuple-element.47.high, bf16[8,256,768]{2,1,0:T(8,128)(2,1)S(1)} %get-tuple-element.48.low, f32[256,128]{1,0:T(8,128)S(1)} %get-tuple-element.35.head.old, f32[256,128]{1,0:T(8,128)S(1)} %copy-done.27, f32[6,256,128]{2,1,0:T(8,128)S(1)} %copy-done.3, ...), custom_call_target="tpu_custom_call" | custom-call | tf_op jit(solution)/shard_map/pallas_call | solution.py:321
  119.6 3.8 %collective-permute-start.19 = (f32[256,128]{1,0:T(8,128)}, f32[256,128]{1,0:T(8,128)S(1)}, u32[]{:S(2)}, u32[]{:S(2)}) collective-permute-start(f32[256,128]{1,0:T(8,128)} %shard_map.74.head.old), channel_id=1, source_target_pairs={{0,24},{4,28},{8,0},{12,4},{16,8},{20,12},{24,16},{28,20},{1,25},{... | collective-permute-start | bytes 393224 | tf_op jit(solution)/shard_map/ppermute | solution.py:400
  129.4 2.8 %shard_map.87.inner.old = f32[6,256,128]{2,1,0:T(8,128)S(1)} custom-call(bf16[8,256,768]{2,1,0:T(8,128)(2,1)S(1)} %get-tuple-element.47.high, bf16[8,256,768]{2,1,0:T(8,128)(2,1)S(1)} %copy-done.1, f32[256,128]{1,0:T(8,128)S(1)} %copy-done.25, f32[256,128]{1,0:T(8,128)S(1)} %copy-done.31, f32[6,256,128]{2,1,0:T(8,128)S(1)} %copy-done.9, ...), custom_call_target="tpu_custom_call" | custom-call | tf_op jit(solution)/shard_map/pallas_call | solution.py:321
  132.3 2.8 %shard_map.75.inner.old = f32[6,256,128]{2,1,0:T(8,128)S(1)} custom-call(bf16[8,256,768]{2,1,0:T(8,128)(2,1)S(1)} %get-tuple-element.47.high, bf16[8,256,768]{2,1,0:T(8,128)(2,1)S(1)} %copy-done.1, f32[256,128]{1,0:T(8,128)S(1)} %copy-done.23, f32[256,128]{1,0:T(8,128)S(1)} %copy-done.29, f32[6,256,128]{2,1,0:T(8,128)S(1)} %copy-done.12, ...), custom_call_target="tpu_custom_call" | custom-call | tf_op jit(solution)/shard_map/pallas_call | solution.py:321
  135.1 3.8 %shard_map.90.inner = f32[6,256,128]{2,1,0:T(8,128)S(1)} custom-call(bf16[8,256,768]{2,1,0:T(8,128)(2,1)S(1)} %get-tuple-element.47.high, bf16[8,256,768]{2,1,0:T(8,128)(2,1)S(1)} %copy-done.1, f32[256,128]{1,0:T(8,128)} %shard_map.86.head.old, f32[256,128]{1,0:T(8,128)} %shard_map.88.tail.old, f32[6,256,128]{2,1,0:T(8,128)S(1)} %shard_map.87.inner.old, ...), custom_call_target="tpu_custom_call" | custom-call | tf_op jit(solution)/shard_map/pallas_call | solution.py:321
  138.8 3.8 %shard_map.78.inner = f32[6,256,128]{2,1,0:T(8,128)S(1)} custom-call(bf16[8,256,768]{2,1,0:T(8,128)(2,1)S(1)} %get-tuple-element.47.high, bf16[8,256,768]{2,1,0:T(8,128)(2,1)S(1)} %copy-done.1, f32[256,128]{1,0:T(8,128)} %shard_map.74.head.old, f32[256,128]{1,0:T(8,128)} %shard_map.76.tail.old, f32[6,256,128]{2,1,0:T(8,128)S(1)} %shard_map.75.inner.old, ...), custom_call_target="tpu_custom_call" | custom-call | tf_op jit(solution)/shard_map/pallas_call | solution.py:321
  145.8 2.0 %collective-permute-start.28 = (f32[256,128]{1,0:T(8,128)S(1)}, f32[256,128]{1,0:T(8,128)S(1)}, u32[]{:S(2)}, u32[]{:S(2)}) collective-permute-start(f32[256,128]{1,0:T(8,128)S(1)} %shard_map.91.tail), channel_id=1, source_target_pairs={{0,8},{4,12},{8,16},{12,20},{16,24},{20,28},{24,0},{28,4},{1,9},{5... | collective-permute-start | bytes 393224 | tf_op jit(solution)/shard_map/ppermute | solution.py:400
  147.8 2.8 %shard_map.94.refs_7_ = f32[6,256,128]{2,1,0:T(8,128)S(1)} custom-call(bf16[8,256,768]{2,1,0:T(8,128)(2,1)S(1)} %get-tuple-element.47.high, bf16[8,256,768]{2,1,0:T(8,128)(2,1)S(1)} %copy-done.1, f32[256,128]{1,0:T(8,128)S(1)} %shard_map.89.head, f32[256,128]{1,0:T(8,128)S(1)} %shard_map.91.tail, f32[6,256,128]{2,1,0:T(8,128)S(1)} %shard_map.90.inner, ...), custom_call_target="tpu_custom_call" | custom-call | tf_op jit(solution)/shard_map/pallas_call | solution.py:321
  157.2 2.8 %shard_map.82.refs_2_ = f32[6,256,128]{2,1,0:T(8,128)S(1)} custom-call(bf16[8,256,768]{2,1,0:T(8,128)(2,1)S(1)} %get-tuple-element.47.high, bf16[8,256,768]{2,1,0:T(8,128)(2,1)S(1)} %copy-done.1, f32[256,128]{1,0:T(8,128)S(1)} %shard_map.77.head, f32[256,128]{1,0:T(8,128)S(1)} %shard_map.79.tail, f32[6,256,128]{2,1,0:T(8,128)S(1)} %shard_map.78.inner, ...), custom_call_target="tpu_custom_call" | custom-call | tf_op jit(solution)/shard_map/pallas_call | solution.py:321
  168.5 4.2 %collective-permute-done.30.refs_8_ = f32[256,128]{1,0:T(8,128)S(1)} collective-permute-done((f32[256,128]{1,0:T(8,128)S(1)}, f32[256,128]{1,0:T(8,128)S(1)}, u32[]{:S(2)}, u32[]{:S(2)}) %collective-permute-start.30) | collective-permute-done | bytes 131104 | tf_op jit(solution)/shard_map/ppermute | solution.py:395
  174.1 2.0 %shard_map.95 = f32[4,256,512]{2,1,0:T(8,128)} custom-call(s32[1]{0:T(128)} %bitcast.side_ref, f32[256,128]{1,0:T(8,128)S(1)} %shard_map.80.refs_0_, f32[256,128]{1,0:T(8,128)S(1)} %shard_map.81.refs_1_, f32[6,256,128]{2,1,0:T(8,128)S(1)} %shard_map.82.refs_2_, f32[256,128]{1,0:T(8,128)S(1)} %collective-permute-done.22.refs_3_, ...), custom_call_target="tpu_custom_call" | custom-call | tf_op jit(solution)/shard_map/pallas_call | solution.py:373
  (180 shorter events, 63.1 us)
Async XLA Ops:
  1.9 17.8 %collective-permute-start = (f32[4,256,128]{2,1,0:T(8,128)S(1)}, f32[4,256,128]{2,1,0:T(8,128)S(1)}, u32[]{:S(2)}, u32[]{:S(2)}) collective-permute-start(f32[4,256,128]{2,1,0:T(8,128)S(1)} %get-tuple-element.30), channel_id=1, source_target_pairs={{0,4},{4,0},{8,12},{12,8},{16,20},{20,16},{24,28},{28,24},{1,5},{5... | collective-permute-start | bytes 1572872 | tf_op jit(solution)/shard_map/ppermute | solution.py:395
  5.4 14.2 %collective-permute-start.1 = (f32[256,128]{1,0:T(8,128)S(1)}, f32[256,128]{1,0:T(8,128)S(1)}, u32[]{:S(2)}, u32[]{:S(2)}) collective-permute-start(f32[256,128]{1,0:T(8,128)S(1)} %shard_map.65), channel_id=1, source_target_pairs={{0,28},{4,0},{8,4},{12,8},{16,12},{20,16},{24,20},{28,24},{1,29},{... | collective-permute-start | bytes 393224 | tf_op jit(solution)/shard_map/ppermute | solution.py:400
  24.6 2.7 %collective-permute-start.5 = (f32[2,392,256]{2,1,0:T(8,128)}, f32[2,392,256]{2,1,0:T(8,128)}, u32[]{:S(2)}, u32[]{:S(2)}) collective-permute-start(f32[2,392,256]{2,1,0:T(8,128)} %get-tuple-element.41), channel_id=1, source_target_pairs={{0,1},{1,0},{2,3},{3,2},{4,5},{5,4},{6,7},{7,6},{8,9},{9,8},{10,11... | collective-permute-start | bytes 2408456 | tf_op jit(solution)/shard_map/ppermute | solution.py:395
  28.3 11.5 %collective-permute-start.6 = (f32[1,392,256]{2,1,0:T(8,128)S(1)}, f32[1,392,256]{2,1,0:T(8,128)}, u32[]{:S(2)}, u32[]{:S(2)}) collective-permute-start(f32[1,392,256]{2,1,0:T(8,128)S(1)} %dynamic-slice_add_fusion), channel_id=1, source_target_pairs={{0,2},{1,3},{2,0},{3,1},{4,6},{5,7},{6,4},{7,5},{8,10},{9,11},{10,... | collective-permute-start | bytes 1204232 | tf_op jit(solution)/shard_map/ppermute | solution.py:395
  30.1 14.0 %collective-permute-start.4 = (f32[4,256,128]{2,1,0:T(8,128)}, f32[4,256,128]{2,1,0:T(8,128)}, u32[]{:S(2)}, u32[]{:S(2)}) collective-permute-start(f32[4,256,128]{2,1,0:T(8,128)} %copy-done.45), channel_id=1, source_target_pairs={{0,4},{4,0},{8,12},{12,8},{16,20},{20,16},{24,28},{28,24},{1,5},{5... | collective-permute-start | bytes 1572872 | tf_op jit(solution)/shard_map/ppermute | solution.py:395
  34.0 10.2 %collective-permute-start.2 = (f32[256,128]{1,0:T(8,128)S(1)}, f32[256,128]{1,0:T(8,128)S(1)}, u32[]{:S(2)}, u32[]{:S(2)}) collective-permute-start(f32[256,128]{1,0:T(8,128)S(1)} %get-tuple-element.34.tail.old), channel_id=1, source_target_pairs={{0,8},{4,12},{8,16},{12,20},{16,24},{20,28},{24,0},{28,4},{1,9},{5... | collective-permute-start | bytes 393224 | tf_op jit(solution)/shard_map/ppermute | solution.py:400
  35.6 8.5 %collective-permute-start.3 = (f32[256,128]{1,0:T(8,128)S(1)}, f32[256,128]{1,0:T(8,128)S(1)}, u32[]{:S(2)}, u32[]{:S(2)}) collective-permute-start(f32[256,128]{1,0:T(8,128)S(1)} %get-tuple-element.35.head.old), channel_id=1, source_target_pairs={{0,24},{4,28},{8,0},{12,4},{16,8},{20,12},{24,16},{28,20},{1,25},{... | collective-permute-start | bytes 393224 | tf_op jit(solution)/shard_map/ppermute | solution.py:400
  44.2 10.2 %collective-permute-start.7 = (f32[1,392,256]{2,1,0:T(8,128)S(1)}, f32[1,392,256]{2,1,0:T(8,128)S(1)}, u32[]{:S(2)}, u32[]{:S(2)}) collective-permute-start(f32[1,392,256]{2,1,0:T(8,128)S(1)} %add_add_fusion.mine), channel_id=1, source_target_pairs={{0,2},{1,3},{2,0},{3,1},{4,6},{5,7},{6,4},{7,5},{8,10},{9,11},{10,... | collective-permute-start | bytes 1204232 | tf_op jit(solution)/shard_map/ppermute | solution.py:395
  44.6 10.0 %collective-permute-start.8 = (f32[1,392,256]{2,1,0:T(8,128)S(1)}, f32[1,392,256]{2,1,0:T(8,128)S(1)}, u32[]{:S(2)}, u32[]{:S(2)}) collective-permute-start(f32[1,392,256]{2,1,0:T(8,128)S(1)} %add_add_fusion.mine), channel_id=1, source_target_pairs={{0,4},{4,0},{8,12},{12,8},{16,20},{20,16},{24,28},{28,24},{1,5},{5... | collective-permute-start | bytes 1204232 | tf_op jit(solution)/shard_map/ppermute | solution.py:395
  55.7 30.9 %collective-permute-start.14 = (f32[3,392,256]{2,1,0:T(8,128)}, f32[3,392,256]{2,1,0:T(8,128)}, u32[]{:S(2)}, u32[]{:S(2)}) collective-permute-start(f32[3,392,256]{2,1,0:T(8,128)} %pad_maximum_fusion), channel_id=1, source_target_pairs={{0,1},{1,0},{2,3},{3,2},{4,5},{5,4},{6,7},{7,6},{8,9},{9,8},{10,11... | collective-permute-start | bytes 3612680 | tf_op jit(solution)/shard_map/ppermute | solution.py:395
  55.7 18.7 %collective-permute-start.11 = (f32[1,392,256]{2,1,0:T(8,128)S(1)}, f32[1,392,256]{2,1,0:T(8,128)}, u32[]{:S(2)}, u32[]{:S(2)}) collective-permute-start(f32[1,392,256]{2,1,0:T(8,128)S(1)} %collective-permute-done.8.across), channel_id=1, source_target_pairs={{0,2},{1,3},{2,0},{3,1},{4,6},{5,7},{6,4},{7,5},{8,10},{9,11},{10,... | collective-permute-start | bytes 1204232 | tf_op jit(solution)/shard_map/ppermute | solution.py:395
  63.6 7.8 %collective-permute-start.10 = (f32[256,128]{1,0:T(8,128)}, f32[256,128]{1,0:T(8,128)S(1)}, u32[]{:S(2)}, u32[]{:S(2)}) collective-permute-start(f32[256,128]{1,0:T(8,128)} %get-tuple-element.45.head.old), channel_id=1, source_target_pairs={{0,24},{4,28},{8,0},{12,4},{16,8},{20,12},{24,16},{28,20},{1,25},{... | collective-permute-start | bytes 393224 | tf_op jit(solution)/shard_map/ppermute | solution.py:400
  67.1 7.3 %collective-permute-start.9 = (f32[256,128]{1,0:T(8,128)}, f32[256,128]{1,0:T(8,128)S(1)}, u32[]{:S(2)}, u32[]{:S(2)}) collective-permute-start(f32[256,128]{1,0:T(8,128)} %get-tuple-element.44.tail.old), channel_id=1, source_target_pairs={{0,8},{4,12},{8,16},{12,20},{16,24},{20,28},{24,0},{28,4},{1,9},{5... | collective-permute-start | bytes 393224 | tf_op jit(solution)/shard_map/ppermute | solution.py:400
  75.6 2.4 %collective-permute-start.12 = (f32[256,256]{1,0:T(8,128)S(1)}, f32[256,256]{1,0:T(8,128)S(1)}, u32[]{:S(2)}, u32[]{:S(2)}) collective-permute-start(f32[256,256]{1,0:T(8,128)S(1)} %fusion.1), channel_id=1, source_target_pairs={{1,9},{3,11},{5,13},{7,15},{9,17},{11,19},{13,21},{15,23},{17,25},... | collective-permute-start | bytes 786440 | tf_op jit(solution)/shard_map/ppermute | solution.py:468
  76.3 9.6 %collective-permute-start.15 = (f32[1,392,256]{2,1,0:T(8,128)}, f32[1,392,256]{2,1,0:T(8,128)S(1)}, u32[]{:S(2)}, u32[]{:S(2)}) collective-permute-start(f32[1,392,256]{2,1,0:T(8,128)} %collective-permute-done.11.both), channel_id=1, source_target_pairs={{0,1},{1,0},{2,3},{3,2},{4,5},{5,4},{6,7},{7,6},{8,9},{9,8},{10,11... | collective-permute-start | bytes 1204232 | tf_op jit(solution)/shard_map/ppermute | solution.py:395
  77.9 7.8 %collective-permute-start.13 = (f32[256,256]{1,0:T(8,128)S(1)}, f32[256,256]{1,0:T(8,128)S(1)}, u32[]{:S(2)}, u32[]{:S(2)}) collective-permute-start(f32[256,256]{1,0:T(8,128)S(1)} %collective-permute-done.12), channel_id=1, source_target_pairs={{1,0},{3,2},{5,4},{7,6},{9,8},{11,10},{13,12},{15,14},{17,16},{19,... | collective-permute-start | bytes 786440 | tf_op jit(solution)/shard_map/ppermute | solution.py:469
  95.7 10.6 %collective-permute-start.25 = (f32[256,128]{1,0:T(8,128)S(1)}, f32[256,128]{1,0:T(8,128)S(1)}, u32[]{:S(2)}, u32[]{:S(2)}) collective-permute-start(f32[256,128]{1,0:T(8,128)S(1)} %shard_map.83.head.old), channel_id=1, source_target_pairs={{0,24},{4,28},{8,0},{12,4},{16,8},{20,12},{24,16},{28,20},{1,25},{... | collective-permute-start | bytes 393224 | tf_op jit(solution)/shard_map/ppermute | solution.py:400
  97.3 11.2 %collective-permute-start.24 = (f32[256,128]{1,0:T(8,128)S(1)}, f32[256,128]{1,0:T(8,128)S(1)}, u32[]{:S(2)}, u32[]{:S(2)}) collective-permute-start(f32[256,128]{1,0:T(8,128)S(1)} %shard_map.85.tail.old), channel_id=1, source_target_pairs={{0,8},{4,12},{8,16},{12,20},{16,24},{20,28},{24,0},{28,4},{1,9},{5... | collective-permute-start | bytes 393224 | tf_op jit(solution)/shard_map/ppermute | solution.py:400
  99.9 17.4 %collective-permute-start.17 = (f32[256,128]{1,0:T(8,128)S(1)}, f32[256,128]{1,0:T(8,128)S(1)}, u32[]{:S(2)}, u32[]{:S(2)}) collective-permute-start(f32[256,128]{1,0:T(8,128)S(1)} %shard_map.71.head.old), channel_id=1, source_target_pairs={{0,24},{4,28},{8,0},{12,4},{16,8},{20,12},{24,16},{28,20},{1,25},{... | collective-permute-start | bytes 393224 | tf_op jit(solution)/shard_map/ppermute | solution.py:400
  102.3 16.1 %collective-permute-start.16 = (f32[256,128]{1,0:T(8,128)S(1)}, f32[256,128]{1,0:T(8,128)S(1)}, u32[]{:S(2)}, u32[]{:S(2)}) collective-permute-start(f32[256,128]{1,0:T(8,128)S(1)} %shard_map.73.tail.old), channel_id=1, source_target_pairs={{0,8},{4,12},{8,16},{12,20},{16,24},{20,28},{24,0},{28,4},{1,9},{5... | collective-permute-start | bytes 393224 | tf_op jit(solution)/shard_map/ppermute | solution.py:400
  108.5 34.1 %collective-permute-start.26 = (f32[256,128]{1,0:T(8,128)}, f32[256,128]{1,0:T(8,128)}, u32[]{:S(2)}, u32[]{:S(2)}) collective-permute-start(f32[256,128]{1,0:T(8,128)} %shard_map.88.tail.old), channel_id=1, source_target_pairs={{0,8},{4,12},{8,16},{12,20},{16,24},{20,28},{24,0},{28,4},{1,9},{5... | collective-permute-start | bytes 393224 | tf_op jit(solution)/shard_map/ppermute | solution.py:400
  110.7 33.7 %collective-permute-start.27 = (f32[256,128]{1,0:T(8,128)}, f32[256,128]{1,0:T(8,128)}, u32[]{:S(2)}, u32[]{:S(2)}) collective-permute-start(f32[256,128]{1,0:T(8,128)} %shard_map.86.head.old), channel_id=1, source_target_pairs={{0,24},{4,28},{8,0},{12,4},{16,8},{20,12},{24,16},{28,20},{1,25},{... | collective-permute-start | bytes 393224 | tf_op jit(solution)/shard_map/ppermute | solution.py:400
  118.4 33.8 %collective-permute-start.18 = (f32[256,128]{1,0:T(8,128)}, f32[256,128]{1,0:T(8,128)}, u32[]{:S(2)}, u32[]{:S(2)}) collective-permute-start(f32[256,128]{1,0:T(8,128)} %shard_map.76.tail.old), channel_id=1, source_target_pairs={{0,8},{4,12},{8,16},{12,20},{16,24},{20,28},{24,0},{28,4},{1,9},{5... | collective-permute-start | bytes 393224 | tf_op jit(solution)/shard_map/ppermute | solution.py:400
  119.6 36.1 %collective-permute-start.19 = (f32[256,128]{1,0:T(8,128)}, f32[256,128]{1,0:T(8,128)S(1)}, u32[]{:S(2)}, u32[]{:S(2)}) collective-permute-start(f32[256,128]{1,0:T(8,128)} %shard_map.74.head.old), channel_id=1, source_target_pairs={{0,24},{4,28},{8,0},{12,4},{16,8},{20,12},{24,16},{28,20},{1,25},{... | collective-permute-start | bytes 393224 | tf_op jit(solution)/shard_map/ppermute | solution.py:400
  144.2 15.9 %collective-permute-start.29 = (f32[256,128]{1,0:T(8,128)S(1)}, f32[256,128]{1,0:T(8,128)S(1)}, u32[]{:S(2)}, u32[]{:S(2)}) collective-permute-start(f32[256,128]{1,0:T(8,128)S(1)} %shard_map.89.head), channel_id=1, source_target_pairs={{0,24},{4,28},{8,0},{12,4},{16,8},{20,12},{24,16},{28,20},{1,25},{... | collective-permute-start | bytes 393224 | tf_op jit(solution)/shard_map/ppermute | solution.py:400
  145.8 16.2 %collective-permute-start.28 = (f32[256,128]{1,0:T(8,128)S(1)}, f32[256,128]{1,0:T(8,128)S(1)}, u32[]{:S(2)}, u32[]{:S(2)}) collective-permute-start(f32[256,128]{1,0:T(8,128)S(1)} %shard_map.91.tail), channel_id=1, source_target_pairs={{0,8},{4,12},{8,16},{12,20},{16,24},{20,28},{24,0},{28,4},{1,9},{5... | collective-permute-start | bytes 393224 | tf_op jit(solution)/shard_map/ppermute | solution.py:400
  150.6 23.5 %collective-permute-start.31 = (f32[3,256,128]{2,1,0:T(8,128)S(1)}, f32[3,256,128]{2,1,0:T(8,128)S(1)}, u32[]{:S(2)}, u32[]{:S(2)}) collective-permute-start(f32[3,256,128]{2,1,0:T(8,128)S(1)} %constant_dynamic-slice_fusion), channel_id=1, source_target_pairs={{0,4},{4,0},{8,12},{12,8},{16,20},{20,16},{24,28},{28,24},{1,5},{5... | collective-permute-start | bytes 1179656 | tf_op jit(solution)/shard_map/ppermute | solution.py:395
  153.7 11.4 %collective-permute-start.21 = (f32[256,128]{1,0:T(8,128)S(1)}, f32[256,128]{1,0:T(8,128)S(1)}, u32[]{:S(2)}, u32[]{:S(2)}) collective-permute-start(f32[256,128]{1,0:T(8,128)S(1)} %shard_map.77.head), channel_id=1, source_target_pairs={{0,24},{4,28},{8,0},{12,4},{16,8},{20,12},{24,16},{28,20},{1,25},{... | collective-permute-start | bytes 393224 | tf_op jit(solution)/shard_map/ppermute | solution.py:400
  157.1 9.4 %collective-permute-start.20 = (f32[256,128]{1,0:T(8,128)S(1)}, f32[256,128]{1,0:T(8,128)S(1)}, u32[]{:S(2)}, u32[]{:S(2)}) collective-permute-start(f32[256,128]{1,0:T(8,128)S(1)} %shard_map.79.tail), channel_id=1, source_target_pairs={{0,8},{4,12},{8,16},{12,20},{16,24},{20,28},{24,0},{28,4},{1,9},{5... | collective-permute-start | bytes 393224 | tf_op jit(solution)/shard_map/ppermute | solution.py:400
  160.1 14.0 %collective-permute-start.23 = (f32[3,256,128]{2,1,0:T(8,128)S(1)}, f32[3,256,128]{2,1,0:T(8,128)S(1)}, u32[]{:S(2)}, u32[]{:S(2)}) collective-permute-start(f32[3,256,128]{2,1,0:T(8,128)S(1)} %constant_dynamic-slice_fusion.1), channel_id=1, source_target_pairs={{0,4},{4,0},{8,12},{12,8},{16,20},{20,16},{24,28},{28,24},{1,5},{5... | collective-permute-start | bytes 1179656 | tf_op jit(solution)/shard_map/ppermute | solution.py:395
  163.5 9.2 %collective-permute-start.30 = (f32[256,128]{1,0:T(8,128)S(1)}, f32[256,128]{1,0:T(8,128)S(1)}, u32[]{:S(2)}, u32[]{:S(2)}) collective-permute-start(f32[256,128]{1,0:T(8,128)S(1)} %broadcast_select_fusion), channel_id=1, source_target_pairs={{0,4},{4,0},{8,12},{12,8},{16,20},{20,16},{24,28},{28,24},{1,5},{5... | collective-permute-start | bytes 393224 | tf_op jit(solution)/shard_map/ppermute | solution.py:395
  168.0 6.1 %collective-permute-start.22 = (f32[256,128]{1,0:T(8,128)S(1)}, f32[256,128]{1,0:T(8,128)S(1)}, u32[]{:S(2)}, u32[]{:S(2)}) collective-permute-start(f32[256,128]{1,0:T(8,128)S(1)} %broadcast_select_fusion.1), channel_id=1, source_target_pairs={{0,4},{4,0},{8,12},{12,8},{16,20},{20,16},{24,28},{28,24},{1,5},{5... | collective-permute-start | bytes 393224 | tf_op jit(solution)/shard_map/ppermute | solution.py:395
  (49 other events, 326.1 us)

commit v3 on v2

v3 whole, which is shorter than its diff:
```python
import functools

import jax
import jax.numpy as jnp
from jax import lax
from jax.experimental import pallas as pl
from jax.experimental.pallas import tpu as pltpu
from jax.sharding import PartitionSpec as P

NB = 256
DEG = 4

penalty = 3.0
center = 4.0
half_width = 12.0

PARAMS = pltpu.CompilerParams(vmem_limit_bytes=12 * 1024 * 1024)
SCALARS = pl.BlockSpec(memory_space=pltpu.SMEM)
ANY = pl.BlockSpec(memory_space=pl.ANY)
VMEM = pl.BlockSpec(memory_space=pltpu.VMEM)
NN = (((1,), (0,)), ((), ()))
NT = (((1,), (1,)), ((), ()))


def split(value):
    high = value.astype(jnp.bfloat16)
    low = (value - high.astype(jnp.float32)).astype(jnp.bfloat16)
    return high, low


def dot(first, second, dims=NN):
    return lax.dot_general(first, second, dims, preferred_element_type=jnp.float32)


def dot3(first, second, dims=NN):
    first_high, first_low = first
    second_high, second_low = second
    return dot(first_high, second_high, dims) + (dot(first_high, second_low, dims) + dot(first_low, second_high, dims))


def picked(parts, chosen):
    return dot(parts[0], chosen) + dot(parts[1], chosen)


def one_hot(index_row, rows, offset=0):
    at = lax.broadcasted_iota(jnp.int32, (rows, index_row.shape[1]), 0) - offset
    return (at == index_row).astype(jnp.float32).astype(jnp.bfloat16)


def lead_kernel(side_ref, index_ref, basis_ref, vector_ref, traces_ref, *rest):
    cut_refs, (held, sems) = rest[:-2], rest[-2:]
    first = pltpu.make_async_copy(basis_ref.at[0], held, sems.at[0])
    first.start()
    width = cut_refs[0].shape[2]
    copies = []
    for at, out_ref in enumerate(cut_refs):
        source = vector_ref
        if vector_ref.shape[2] > width:
            start = pl.multiple_of((side_ref[0] * len(cut_refs) + at) * width, width)
            source = vector_ref.at[:, :, pl.ds(start, width)]
        copies.append(pltpu.make_async_copy(source, out_ref, sems.at[1 + at]))
        copies[-1].start()
    first.wait()
    traces_ref[...] = picked(split(held[...].T), one_hot(index_ref[0], held.shape[0]))
    for copy in copies:
        copy.wait()


def blocks_kernel(
    faces_total, core_ref, index_ref, quad_ref, pair_ref, basis_ref, applied_ref, send_ref, keep_ref, last_ref, held, acted, traces, sems
):
    count = basis_ref.shape[0]
    size = basis_ref.shape[2]
    half = size // 2
    core = core_ref[0]

    def copies(at):
        return (
            pltpu.make_async_copy(basis_ref.at[at], held.at[at], sems.at[2 * at]),
            pltpu.make_async_copy(applied_ref.at[at], acted.at[at], sems.at[2 * at + 1]),
        )

    for at in range(count):
        for copy in copies(at):
            copy.start()

    def store(element, rows, value):
        @pl.when(element // (count // 2) == core)
        def _():
            keep_ref[element % (count // 2), rows] = value

        @pl.when(element // (count // 2) != core)
        def _():
            send_ref[element % (count // 2), rows] = value

    @pl.loop(0, count)
    def _(at):
        for copy in copies(at):
            copy.wait()
        turned = held[at].T
        found = picked(split(turned), one_hot(index_ref[at], held.shape[1]))
        traces[at] = found
        width = found.shape[1] // 2
        outer, layer = found[:, :width], found[:, width:]
        total = dot3(split(turned * quad_ref[at]), split(acted[at]))
        total = total + dot3(split((2.0 * outer + layer) * (1.0 / faces_total)), split(outer), NT)
        mixed, side, diagonal = packed(0.5 * (total + total.T))
        store(at, slice(size, size + half), jnp.concatenate([mixed, side], axis=1))
        store(at, slice(size + half, None), jnp.broadcast_to(jnp.concatenate([diagonal, diagonal], axis=1), (8, size)))

    @pl.loop(0, count - 1)
    def _(at):
        following = traces[at + 1]
        width = following.shape[1] // 2
        order = one_hot(pair_ref[at], width)
        face, inside = picked(split(following[:, :width]), order), picked(split(following[:, width:]), order)
        store(at, slice(0, size), coupled(traces[at], face, inside, faces_total))

    last_ref[...] = traces[count - 1]


def coupled(own, face, inside, faces_total):
    width = own.shape[1] // 2
    outer, layer = own[:, :width], own[:, width:]
    near = split((penalty * outer + 0.5 * layer) * (-1.0 / faces_total))
    far = split(outer * (0.5 / faces_total))
    return dot3(near, split(face), NT) + dot3(far, split(inside), NT)


def last_kernel(faces_total, core_ref, pair_ref, own_ref, lead_ref, send_in, keep_in, send_ref, keep_ref, block, sem):
    width = own_ref.shape[1] // 2
    lead = split(lead_ref[...])
    face = picked(lead, one_hot(pair_ref[...], width))
    inside = picked(lead, one_hot(pair_ref[...], width, width // 2))
    block[...] = coupled(own_ref[...], face, inside, faces_total)
    at = send_ref.shape[0] - 1
    rows = pl.ds(0, block.shape[0])
    for core, ref in ((0, send_ref), (1, keep_ref)):

        @pl.when(core_ref[0] == core)
        def _():
            copy = pltpu.make_async_copy(block, ref.at[at, rows], sem)
            copy.start()
            copy.wait()


def packed(volume):
    half = volume.shape[0] // 2
    row = lax.broadcasted_iota(jnp.int32, (half, half), 0)
    column = lax.broadcasted_iota(jnp.int32, (half, half), 1)
    corner = volume[half:, half:]
    mixed = jnp.where(column >= row, volume[:half, :half], corner)
    diagonal = jnp.sum(jnp.where(column == row, corner, 0.0), axis=0, keepdims=True)
    return mixed, volume[:half, half:], diagonal


def unpacked(mixed, side, diagonal):
    half = mixed.shape[0]
    row = lax.broadcasted_iota(jnp.int32, (half, half), 0)
    column = lax.broadcasted_iota(jnp.int32, (half, half), 1)
    turned = mixed.T
    first = jnp.where(column >= row, mixed, turned)
    corner = jnp.where(column < row, mixed, jnp.where(column == row, diagonal, turned))
    top = jnp.concatenate([first, side], axis=1)
    return jnp.concatenate([top, jnp.concatenate([side.T, corner], axis=1)], axis=0)


def weights_kernel(me_ref, *refs):
    sources, (high_ref, low_ref), held, sems = refs[:6], refs[6:8], refs[8], refs[9]
    me = me_ref[0]
    size = held.shape[2]
    half = size // 2
    places = ((0, 0), (1, 0), (2, 0), (3, 0), (4, 0), (4, 1), (4, 2), (5, 0))
    away_at = (0, 1, 4, 5, 2, 3, 6, 7)
    copies = [pltpu.make_async_copy(sources[ref].at[at], held.at[n], sems.at[n]) for n, (ref, at) in enumerate(places)]
    for copy in copies:
        copy.start()
    row = lax.broadcasted_iota(jnp.int32, (size, size), 0)
    diagonal = row == lax.broadcasted_iota(jnp.int32, (size, size), 1)

    for n, away in enumerate(away_at):
        copies[n].wait()
        element = away ^ me
        volume = unpacked(held[n, size : size + half, :half], held[n, size : size + half, half:], held[n, size + half : size + half + 1, :half])
        volume = (volume - jnp.where(diagonal, center, 0.0)) * (1.0 / half_width)
        coupling = held[n, :size] * (1.0 / half_width)
        following = lax.rem(element + 1, len(away_at))
        for place, at_column, value in ((following, 0, coupling.T), (element, 1, volume), (element, 2, coupling)):
            high, low = split(value)
            high_ref[place, :, at_column * size : (at_column + 1) * size] = high
            low_ref[place, :, at_column * size : (at_column + 1) * size] = low


def held_shape(rows, columns):
    return (rows, 2 * columns) if columns % 128 == 0 else (2, rows, columns)


def hold(held, at, value):
    high, low = split(value)
    size, columns = value.shape
    rows = slice(at * size, (at + 1) * size)
    if len(held.shape) == 2:
        held[rows, :columns] = high
        held[rows, columns:] = low
    else:
        held[0, rows] = high
        held[1, rows] = low


def apply_row(high, low, held, start, columns):
    rows = pl.ds(start, high.shape[1])
    if len(held.shape) == 2:
        if columns == 128:
            both = dot(high, held[rows, :])
            total = both[:, :columns] + both[:, columns:]
        else:
            total = dot(high, held[rows, :columns]) + dot(high, held[rows, columns:])
        return total + dot(low, held[rows, :columns])
    return dot(high, held[0, rows]) + (dot(high, held[1, rows]) + dot(low, held[0, rows]))


def advance(first, result, before):
    return result if first else 2.0 * result - before


def head_kernel(first, before, high, low, head, inner, below, old, out, held):
    size, columns = head.shape
    for at, value in enumerate((below[...], head[...], inner[0])):
        hold(held, at, value)
    before_high, before_low = split((before[...] * (1.0 / half_width)).T)
    row = apply_row(
        jnp.concatenate([before_high, high[0, :, size:]], axis=1), jnp.concatenate([before_low, low[0, :, size:]], axis=1), held, 0, columns
    )
    out[...] = advance(first, row, None if first else old[...])


def tail_kernel(first, high, low, tail, inner, above, old, out, held):
    for at, value in enumerate((inner[inner.shape[0] - 1], tail[...], above[...])):
        hold(held, at, value)
    last = high.shape[0] - 1
    row = apply_row(high[last], low[last], held, 0, tail.shape[1])
    out[...] = advance(first, row, None if first else old[...])


def inner_kernel(first, high, low, head, tail, inner, old, out, held):
    count, size, columns = inner.shape
    hold(held, 0, head[...])
    for at in range(count):
        hold(held, at + 1, inner[at])
    hold(held, count + 1, tail[...])

    @pl.loop(0, count)
    def _(at):
        row = apply_row(high[at + 1], low[at + 1], held, pl.multiple_of(at * size, size), columns)
        out[at] = advance(first, row, None if first else old[at])


def arrange_kernel(chunk, chunks, at_ref, vector_ref, got_ref, head_ref, tail_ref, inner_ref, sems):
    half, _, width = got_ref.shape
    side = at_ref[0]
    targets = [head_ref] + [inner_ref.at[at] for at in range(2 * half - 2)] + [tail_ref]

    def moved(act):
        for element, target in enumerate(targets):
            own = vector_ref.at[element % half]
            if vector_ref.shape[2] > width:
                start = pl.multiple_of((at_ref[0] * chunks + chunk) * width, width)
                own = vector_ref.at[element % half, :, pl.ds(start, width)]
            for source, mine in ((own, True), (got_ref.at[element % half], False)):

                @pl.when((side == element // half) == mine)
                def _():
                    act(pltpu.make_async_copy(source, target, sems.at[element]))

    moved(lambda copy: copy.start())
    moved(lambda copy: copy.wait())


def collect_kernel(count, chunks, side_ref, *refs):
    out_ref = refs[-1]
    step = pl.program_id(0)
    side = side_ref[0]
    at_end = step == side * (count - 1)
    for chunk in range(chunks):
        head_ref, tail_ref, inner_ref, got_end_ref, got_inner_ref = refs[5 * chunk : 5 * chunk + 5]
        end = jnp.where(side == 0, head_ref[...], tail_ref[...])
        mine = jnp.where(at_end, end, inner_ref[0])
        theirs = jnp.where(at_end, got_end_ref[...], got_inner_ref[0])
        width = mine.shape[1]
        first = chunk * width
        second = (chunks + chunk) * width
        out_ref[0, :, first : first + width] = jnp.where(side == 0, mine, theirs)
        out_ref[0, :, second : second + width] = jnp.where(side == 0, theirs, mine)


def whole(shape):
    return pl.BlockSpec(shape, lambda *steps: (0,) * len(shape))


def lead_and_cut(side, index, basis, vector, chunks, width):
    points, size = basis.shape[1:]
    count = vector.shape[0]
    return pl.pallas_call(
        lead_kernel,
        in_specs=[SCALARS, VMEM, ANY, ANY],
        out_specs=[VMEM] + [VMEM] * chunks,
        out_shape=[jax.ShapeDtypeStruct((size, index.shape[2]), jnp.float32)]
        + [jax.ShapeDtypeStruct((count, size, width), jnp.float32)] * chunks,
        scratch_shapes=[pltpu.VMEM((points, size), jnp.float32), pltpu.SemaphoreType.DMA((1 + chunks,))],
        compiler_params=PARAMS,
    )(side, index, basis, vector)


def blocks(core, index, quad, pairs, basis, applied, faces_total):
    count, points, size = basis.shape
    spots = index.shape[2]
    part = jax.ShapeDtypeStruct((count // 2, size + size // 2 + 8, size), jnp.float32)
    return pl.pallas_call(
        functools.partial(blocks_kernel, faces_total),
        in_specs=[SCALARS, VMEM, VMEM, VMEM, ANY, ANY],
        out_specs=[VMEM] * 3,
        out_shape=[part, part, jax.ShapeDtypeStruct((size, spots), jnp.float32)],
        scratch_shapes=[
            pltpu.VMEM((count, points, size), jnp.float32),
            pltpu.VMEM((count, points, size), jnp.float32),
            pltpu.VMEM((count, size, spots), jnp.float32),
            pltpu.SemaphoreType.DMA((2 * count,)),
        ],
        compiler_params=PARAMS,
    )(core, index, quad, pairs, basis, applied)


def last_coupling(core, pair, own, lead, send, keep, faces_total):
    size = own.shape[0]
    return pl.pallas_call(
        functools.partial(last_kernel, faces_total),
        in_specs=[SCALARS, VMEM, VMEM, VMEM, ANY, ANY],
        out_specs=[ANY] * 2,
        out_shape=[jax.ShapeDtypeStruct(send.shape, jnp.float32)] * 2,
        input_output_aliases={4: 0, 5: 1},
        scratch_shapes=[pltpu.VMEM((size, size), jnp.float32), pltpu.SemaphoreType.DMA],
        compiler_params=PARAMS,
    )(core, pair, own, lead, send, keep)


def weights(me, *parts):
    rows, size = parts[0].shape[1:]
    return pl.pallas_call(
        weights_kernel,
        in_specs=[SCALARS] + [ANY] * 6,
        out_specs=[VMEM] * 2,
        out_shape=[jax.ShapeDtypeStruct((8, size, 3 * size), jnp.bfloat16)] * 2,
        scratch_shapes=[pltpu.VMEM((8, rows, size), jnp.float32), pltpu.SemaphoreType.DMA((8,))],
        compiler_params=PARAMS,
    )(me, *parts)


def apply_head(first, before, high, low, head, inner, below, old):
    return pl.pallas_call(
        functools.partial(head_kernel, first),
        in_specs=[VMEM] * 7,
        out_specs=VMEM,
        out_shape=jax.ShapeDtypeStruct(head.shape, jnp.float32),
        scratch_shapes=[pltpu.VMEM(held_shape(3 * head.shape[0], head.shape[1]), jnp.bfloat16)],
        compiler_params=PARAMS,
    )(before, high, low, head, inner, below, old)


def apply_tail(first, high, low, tail, inner, above, old):
    return pl.pallas_call(
        functools.partial(tail_kernel, first),
        in_specs=[VMEM] * 6,
        out_specs=VMEM,
        out_shape=jax.ShapeDtypeStruct(tail.shape, jnp.float32),
        scratch_shapes=[pltpu.VMEM(held_shape(3 * tail.shape[0], tail.shape[1]), jnp.bfloat16)],
        compiler_params=PARAMS,
    )(high, low, tail, inner, above, old)


def apply_inner(first, high, low, head, tail, inner, old):
    return pl.pallas_call(
        functools.partial(inner_kernel, first),
        in_specs=[VMEM] * 6,
        out_specs=VMEM,
        out_shape=jax.ShapeDtypeStruct(inner.shape, jnp.float32),
        scratch_shapes=[pltpu.VMEM(held_shape((inner.shape[0] + 2) * inner.shape[1], inner.shape[2]), jnp.bfloat16)],
        compiler_params=PARAMS,
    )(high, low, head, tail, inner, old)


def arranged(at, vector, got, chunk):
    half, size, columns = got.shape
    chunks = max(vector.shape[2] // 2 // columns, 1)
    return pl.pallas_call(
        functools.partial(arrange_kernel, chunk, chunks),
        in_specs=[SCALARS, ANY, ANY],
        out_specs=[VMEM] * 3,
        out_shape=[jax.ShapeDtypeStruct((size, columns), jnp.float32)] * 2
        + [jax.ShapeDtypeStruct((2 * half - 2, size, columns), jnp.float32)],
        scratch_shapes=[pltpu.SemaphoreType.DMA((2 * half,))],
        compiler_params=PARAMS,
    )(at, vector, got)


def collected(side, parts):
    size, width = parts[0][0].shape
    chunks = len(parts)
    half = parts[0][4].shape[0] + 1
    spot = lambda s, o: jnp.where(o[0] == 0, jnp.maximum(s - 1, 0), jnp.minimum(s, half - 2))
    flat = pl.BlockSpec((size, width), lambda s, o: (0, 0))
    return pl.pallas_call(
        functools.partial(collect_kernel, half, chunks),
        grid_spec=pltpu.PrefetchScalarGridSpec(
            num_scalar_prefetch=1,
            grid=(half,),
            in_specs=[
                flat,
                flat,
                pl.BlockSpec((1, size, width), lambda s, o: (o[0] * (half - 1) + spot(s, o), 0, 0)),
                flat,
                pl.BlockSpec((1, size, width), lambda s, o: (spot(s, o), 0, 0)),
            ]
            * chunks,
            out_specs=pl.BlockSpec((1, size, 2 * chunks * width), lambda s, o: (s, 0, 0)),
        ),
        out_shape=jax.ShapeDtypeStruct((half, size, 2 * chunks * width), jnp.float32),
        compiler_params=PARAMS,
    )(side, *[value for part in parts for value in part])


def flipped(value, axis, bit):
    count = lax.axis_size(axis)
    return lax.ppermute(value, axis, [(i, i ^ bit) for i in range(count)])


def shifted(value, axis, steps):
    count = lax.axis_size(axis)
    return lax.ppermute(value, axis, [(i, (i + steps) % count) for i in range(count)])


def body(basis, applied, quad, face_index, face_pairing, orbitals):
    count, points, size = basis.shape
    spots = face_index.shape[2]
    columns = orbitals.shape[1]
    chunks = 2 if columns % 512 == 0 else 1
    elems, width = lax.axis_size("elem"), lax.axis_size("pts")
    faces_total = float(spots * width)
    side = lax.axis_index("elem") % 2
    core = lax.axis_index("pts") % 2
    lane = lax.axis_index("pts") // 2 % 2
    side_at = side.reshape(1).astype(jnp.int32)
    vector = orbitals.reshape(count, size, columns)

    lead_index = face_index[:1, 0:2].reshape(1, 1, 2 * spots)
    part = columns // 2 // chunks
    own = foreign = vector
    if part % 128:
        own = lax.dynamic_slice_in_dim(vector, side * part, part, axis=2)
        foreign = lax.dynamic_slice_in_dim(vector, (1 - side) * part, part, axis=2)
    lead, *foreign = lead_and_cut(1 - side_at, lead_index, basis, foreign, chunks, part)
    lead = shifted(lead, "elem", -1)
    got = [flipped(value, "elem", 1) for value in foreign]

    index = jnp.stack([face_index[:, 0], face_index[:, 2], face_index[:, 1], face_index[:, 3]], axis=1)
    index = index.reshape(count, 1, 4 * spots)
    pairs = jnp.concatenate([jnp.full_like(face_pairing, -points), face_pairing], axis=1).reshape(count, 1, 2 * spots)
    core_at = core.reshape(1).astype(jnp.int32)
    send, keep, last = blocks(core_at, index, quad.reshape(count, 1, points), pairs, basis, applied, faces_total)
    send, keep = last_coupling(core_at, pairs[-1], last, lead, send, keep, faces_total)
    half = count // 2

    state, belows, aboves = [], [], []

    def arrange(chunk, received):
        state.append(arranged(side_at, own, received, chunk))
        belows.append(shifted(state[chunk][1], "elem", 2))
        aboves.append(shifted(state[chunk][0], "elem", -2))


    other = flipped(send, "pts", 1)
    quarter = half // 2
    pick = lambda value, at: lax.dynamic_slice_in_dim(value, at * quarter, quarter)
    send = pick(keep, 1 - lane) + pick(other, 1 - lane)
    mine = pick(keep, lane) + pick(other, lane) + flipped(send, "pts", 2)
    bit = 4
    while bit < width:
        mine = mine + flipped(mine, "pts", bit)
        bit *= 2
    got[0], mine = lax.optimization_barrier((got[0], mine))
    arrange(0, got[0])
    beside = flipped(mine, "pts", 2)
    across = flipped(mine, "elem", 1)
    belows[0], aboves[0], across = lax.optimization_barrier((belows[0], aboves[0], across))
    both = flipped(across, "pts", 2)
    near = flipped(jnp.concatenate([mine, beside, across]), "pts", 1)
    if chunks > 1:
        got[1], both = lax.optimization_barrier((got[1], both))
        arrange(1, got[1])
    far = flipped(both, "pts", 1)

    last = jnp.where(
        side == 1, jnp.where(lane == 1, mine[0, :size], beside[0, :size]), jnp.where(lane == 1, across[0, :size], both[0, :size])
    )
    flat = lambda e, p: e % elems * width + p
    odd = [(e, p) for e in range(elems) for p in range(1, width, 2)]
    before = lax.ppermute(last, ("elem", "pts"), [(flat(e, p), flat(e + 2, p)) for e, p in odd])
    before = before + lax.ppermute(before, ("elem", "pts"), [(flat(e, p), flat(e, p - 1)) for e, p in odd])

    me = (side * 4 + core * 2 + lane).reshape(1).astype(jnp.int32)
    high, low = weights(me, mine, beside, across, both, near, far)

    old = list(state)
    parts = []
    for degree in range(DEG):
        first = degree == 0
        for c in range(chunks):
            head, tail, inner = state[c]
            new_tail = apply_tail(first, high, low, tail, inner, aboves[c], old[c][1])
            new_head = apply_head(first, before, high, low, head, inner, belows[c], old[c][0])
            new_inner = apply_inner(first, high, low, head, tail, inner, old[c][2])
            old[c] = state[c]
            state[c] = new_head, new_tail, new_inner
            if degree < DEG - 1:
                belows[c] = shifted(new_tail, "elem", 2)
                aboves[c] = shifted(new_head, "elem", -2)
            else:
                foreign = lax.dynamic_slice_in_dim(new_inner, (1 - side) * (count - 1), count - 1)
                got_inner = flipped(foreign, "elem", 1)
                got_end = flipped(jnp.where(side == 0, new_tail, new_head), "elem", 1)
                parts.append((new_head, new_tail, new_inner, got_end, got_inner))
    return collected(side_at, parts).reshape(count * size, columns)


def solution(mesh):
    return jax.shard_map(
        body,
        mesh=mesh,
        in_specs=(
            P("elem", "pts", None),
            P("elem", "pts", None),
            P("elem", "pts"),
            P("elem", None, "pts"),
            P("elem", "pts"),
            P("elem", "pts"),
        ),
        out_specs=P("elem", "pts"),
        check_vma=False,
    )
```

time: 177 us -> 170 us (0.960)
  Pallas kernels: 69 us -> 60.8 us
  local copies, waits for them, and re-layouts: 15.5 us -> 21.3 us
  waiting for transfers between devices: 40.2 us -> 37.8 us
  starting transfers between devices: 46 us -> 43.8 us
    ppermute x13, waiting for transfers between devices: 21.6 us -> 35.2 us  [flipped(): return lax.ppermute(value, axis, [(i, i ^ bit) for i in range(count)])]
    ppermute x17, waiting for transfers between devices: 12.1 us -> 1.37 us  [shifted(): lax.ppermute(value, axis, [(i, (i + steps) % count) for i in range(count)])]
    ppermute x1, waiting for transfers between devices: 6.55 us -> 1.21 us  [body(): lax.ppermute(before, ('elem', 'pts'), [(flat(e, p), flat(e, p - 1)) for e...]
    ppermute x13, starting transfers between devices: 16.1 us -> 10.9 us  [flipped(): return lax.ppermute(value, axis, [(i, i ^ bit) for i in range(count)])]
    unnamed x98 -> x90, local copies, waits for them, and re-layouts: 15.2 us -> 20.2 us
    pallas_call x7 -> x6, Pallas kernels: 19.1 us -> 15.6 us  [the longest x1 6.72 us: blocks(): pl.pallas_call(functools.partial(blocks_kernel, faces_total), in_specs=[S...]
    pallas_call x8, Pallas kernels: 25.3 us -> 22.1 us  [apply_inner(): pl.pallas_call(functools.partial(inner_kernel, first), in_specs=[VMEM] *...]
    ppermute x17, starting transfers between devices: 28 us -> 31 us  [shifted(): lax.ppermute(value, axis, [(i, (i + steps) % count) for i in range(count)])]
  transfers between devices with their start and end apart: 32 -> 32, of which waited for: 11 -> 9; matrix products, arithmetic and copies ran while one was open for 2% -> 2% of each run, Pallas kernels for 33% -> 33%
where the time goes in v3:
time: 170 us; the launch traced here: 169 us
  Pallas kernels  60.8 us (36%)
  starting transfers between devices  43.8 us (26%)
  waiting for transfers between devices  37.8 us (22%)
  local copies, waits for them, and re-layouts  21.3 us (13%)
  other arithmetic  4.71 us (3%)
    ppermute x13, waiting for transfers between devices, flipped(): return lax.ppermute(value, axis, [(i, i ^ bit) for i in range(count)])  35.2 us
    ppermute x17, starting transfers between devices, shifted(): lax.ppermute(value, axis, [(i, (i + steps) % count) for i in range(count)])  31 us
    pallas_call x8, Pallas kernels, apply_inner(): pl.pallas_call(functools.partial(inner_kernel, first), in_specs=[VMEM] *...  22.1 us
    unnamed x90, local copies, waits for them, and re-layouts  20.2 us
    pallas_call x8, Pallas kernels, apply_head(): pl.pallas_call(functools.partial(head_kernel, first), in_specs=[VMEM] * 7...  10.9 us
    ppermute x13, starting transfers between devices, flipped(): return lax.ppermute(value, axis, [(i, i ^ bit) for i in range(count)])  10.9 us
    pallas_call x8, Pallas kernels, apply_tail(): pl.pallas_call(functools.partial(tail_kernel, first), in_specs=[VMEM] * 6...  10.2 us
    pallas_call x1, Pallas kernels, blocks(): pl.pallas_call(functools.partial(blocks_kernel, faces_total), in_specs=[S...  6.72 us
  transfers between devices with their start and end apart: 32, of which 9 were waited for; matrix products, arithmetic and copies ran while one was open for 2% of the time, Pallas kernels for 33%

profile of v3, /device:TPU:0, one launch (start us, length us, event | category | flops | bytes accessed | tf_op | source)
XLA Modules:
  0.0 169.1 jit_solution(6587568699910731698)
XLA Ops:
  5.6 6.1 %collective-permute-start.1 = (f32[256,128]{1,0:T(8,128)S(1)}, f32[256,128]{1,0:T(8,128)S(1)}, u32[]{:S(2)}, u32[]{:S(2)}) collective-permute-start(f32[256,128]{1,0:T(8,128)S(1)} %get-tuple-element.30), channel_id=1, source_target_pairs={{0,28},{4,0},{8,4},{12,8},{16,12},{20,16},{24,20},{28,24},{1,29},{... | collective-permute-start | bytes 393224 | tf_op jit(solution)/shard_map/ppermute | solution.py:438
  13.5 6.7 %shard_map.65 = (f32[2,392,256]{2,1,0:T(8,128)}, f32[2,392,256]{2,1,0:T(8,128)S(1)}, f32[256,256]{1,0:T(8,128)S(1)}) custom-call(s32[1]{0:T(128)} %bitcast.2.core_ref, s32[4,1,256]{2,1,0:T(1,128)S(1)} %reshape.39.index_ref, f32[4,1,512]{2,1,0:T(1,128)S(1)} %reshape.40.quad_ref, s32[4,1,128]{2,1,0:T(1,128)S(1)} %bitcast.13, f32[4,512,256]{2,1,0:T(8,128)S(1)} %copy-done.16, ...), custom_call_target="tpu_custom_call" | custom-call | tf_op jit(solution)/shard_map/pallas_call | solution.py:318
  21.7 2.5 %collective-permute-done.2 = f32[2,392,256]{2,1,0:T(8,128)S(1)} collective-permute-done((f32[2,392,256]{2,1,0:T(8,128)}, f32[2,392,256]{2,1,0:T(8,128)S(1)}, u32[]{:S(2)}, u32[]{:S(2)}) %collective-permute-start.2) | collective-permute-done | bytes 802848 | tf_op jit(solution)/shard_map/ppermute | solution.py:433
  27.8 10.0 %collective-permute-done.3 = f32[1,392,256]{2,1,0:T(8,128)} collective-permute-done((f32[1,392,256]{2,1,0:T(8,128)S(1)}, f32[1,392,256]{2,1,0:T(8,128)}, u32[]{:S(2)}, u32[]{:S(2)}) %collective-permute-start.3) | collective-permute-done | bytes 401440 | tf_op jit(solution)/shard_map/ppermute | solution.py:433
  39.0 2.8 %collective-permute-done.got_ref = f32[4,256,128]{2,1,0:T(8,128)} collective-permute-done((f32[4,256,128]{2,1,0:T(8,128)}, f32[4,256,128]{2,1,0:T(8,128)}, u32[]{:S(2)}, u32[]{:S(2)}) %collective-permute-start) | collective-permute-done | bytes 524320 | tf_op jit(solution)/shard_map/ppermute | solution.py:433
  45.5 3.8 %collective-permute-start.6 = (f32[256,128]{1,0:T(8,128)S(1)}, f32[256,128]{1,0:T(8,128)S(1)}, u32[]{:S(2)}, u32[]{:S(2)}) collective-permute-start(f32[256,128]{1,0:T(8,128)S(1)} %get-tuple-element.38.head.old), channel_id=1, source_target_pairs={{0,24},{4,28},{8,0},{12,4},{16,8},{20,12},{24,16},{28,20},{1,25},{... | collective-permute-start | bytes 393224 | tf_op jit(solution)/shard_map/ppermute | solution.py:438
  56.3 7.1 %collective-permute-done.8.got_ref = f32[4,256,128]{2,1,0:T(8,128)} collective-permute-done((f32[4,256,128]{2,1,0:T(8,128)}, f32[4,256,128]{2,1,0:T(8,128)}, u32[]{:S(2)}, u32[]{:S(2)}) %collective-permute-start.8) | collective-permute-done | bytes 524320 | tf_op jit(solution)/shard_map/ppermute | solution.py:433
  63.3 3.3 %collective-permute-done.9.refs_3_ = f32[1,392,256]{2,1,0:T(8,128)} collective-permute-done((f32[1,392,256]{2,1,0:T(8,128)S(1)}, f32[1,392,256]{2,1,0:T(8,128)}, u32[]{:S(2)}, u32[]{:S(2)}) %collective-permute-start.9) | collective-permute-done | bytes 401440 | tf_op jit(solution)/shard_map/ppermute | solution.py:433
  70.7 2.0 %shard_map.81 = (f32[256,128]{1,0:T(8,128)}, f32[256,128]{1,0:T(8,128)}, f32[6,256,128]{2,1,0:T(8,128)S(1)}) custom-call(s32[1]{0:T(128)} %bitcast.at_ref.side_ref, f32[4,256,512]{2,1,0:T(8,128)S(1)} %bitcast.12, f32[4,256,128]{2,1,0:T(8,128)} %collective-permute-done.8.got_ref), custom_call_target="tpu_custom_call" | custom-call | tf_op jit(solution)/shard_map/pallas_call | solution.py:394
  75.0 2.4 %collective-permute-start.23 = (f32[256,128]{1,0:T(8,128)}, f32[256,128]{1,0:T(8,128)}, u32[]{:S(2)}, u32[]{:S(2)}) collective-permute-start(f32[256,128]{1,0:T(8,128)} %get-tuple-element.48.head.old), channel_id=1, source_target_pairs={{0,24},{4,28},{8,0},{12,4},{16,8},{20,12},{24,16},{28,20},{1,25},{... | collective-permute-start | bytes 393224 | tf_op jit(solution)/shard_map/ppermute | solution.py:438
  83.4 2.7 %shard_map.68 = (bf16[8,256,768]{2,1,0:T(8,128)(2,1)S(1)}, bf16[8,256,768]{2,1,0:T(8,128)(2,1)S(1)}) custom-call(s32[1]{0:T(128)} %bitcast.6.me_ref, f32[1,392,256]{2,1,0:T(8,128)S(1)} %copy-done.18, f32[1,392,256]{2,1,0:T(8,128)S(1)} %copy-done.22, f32[1,392,256]{2,1,0:T(8,128)S(1)} %copy-done.20, f32[1,392,256]{2,1,0:T(8,128)} %collective-permute-done.9.refs_3_, ...), custom_call_target="tpu_custom_call" | custom-call | tf_op jit(solution)/shard_map/pallas_call | solution.py:348
  86.2 1.9 %shard_map.82.head.old = f32[256,128]{1,0:T(8,128)S(1)} custom-call(f32[256,256]{1,0:T(8,128)S(1)} %add.52.before, bf16[8,256,768]{2,1,0:T(8,128)(2,1)S(1)} %get-tuple-element.42.high, bf16[8,256,768]{2,1,0:T(8,128)(2,1)S(1)} %get-tuple-element.43.low, f32[256,128]{1,0:T(8,128)} %get-tuple-element.48.head.old, f32[6,256,128]{2,1,0:T(8,128)S(1)} %copy-done.6, ...), custom_call_target="tpu_custom_call" | custom-call | tf_op jit(solution)/shard_map/pallas_call | solution.py:359
  92.2 3.2 %collective-permute-start.15 = (f32[256,128]{1,0:T(8,128)S(1)}, f32[256,128]{1,0:T(8,128)S(1)}, u32[]{:S(2)}, u32[]{:S(2)}) collective-permute-start(f32[256,128]{1,0:T(8,128)S(1)} %shard_map.69.head.old), channel_id=1, source_target_pairs={{0,24},{4,28},{8,0},{12,4},{16,8},{20,12},{24,16},{28,20},{1,25},{... | collective-permute-start | bytes 393224 | tf_op jit(solution)/shard_map/ppermute | solution.py:438
  95.9 3.4 %shard_map.83.inner.old = f32[6,256,128]{2,1,0:T(8,128)S(1)} custom-call(bf16[8,256,768]{2,1,0:T(8,128)(2,1)S(1)} %get-tuple-element.42.high, bf16[8,256,768]{2,1,0:T(8,128)(2,1)S(1)} %get-tuple-element.43.low, f32[256,128]{1,0:T(8,128)} %get-tuple-element.48.head.old, f32[256,128]{1,0:T(8,128)} %get-tuple-element.50.tail.old, f32[6,256,128]{2,1,0:T(8,128)S(1)} %copy-done.6, ...), custom_call_target="tpu_custom_call" | custom-call | tf_op jit(solution)/shard_map/pallas_call | solution.py:381
  99.2 2.1 %shard_map.87.tail.old = f32[256,128]{1,0:T(8,128)} custom-call(bf16[8,256,768]{2,1,0:T(8,128)(2,1)S(1)} %get-tuple-element.42.high, bf16[8,256,768]{2,1,0:T(8,128)(2,1)S(1)} %get-tuple-element.43.low, f32[256,128]{1,0:T(8,128)S(1)} %shard_map.84.tail.old, f32[6,256,128]{2,1,0:T(8,128)S(1)} %shard_map.83.inner.old, ...), custom_call_target="tpu_custom_call" | custom-call | tf_op jit(solution)/shard_map/pallas_call | solution.py:370
  101.4 2.0 %shard_map.85.head.old = f32[256,128]{1,0:T(8,128)} custom-call(f32[256,256]{1,0:T(8,128)S(1)} %add.52.before, bf16[8,256,768]{2,1,0:T(8,128)(2,1)S(1)} %get-tuple-element.42.high, bf16[8,256,768]{2,1,0:T(8,128)(2,1)S(1)} %get-tuple-element.43.low, f32[256,128]{1,0:T(8,128)S(1)} %shard_map.82.head.old, f32[6,256,128]{2,1,0:T(8,128)S(1)} %shard_map.83.inner.old, ...), custom_call_target="tpu_custom_call" | custom-call | tf_op jit(solution)/shard_map/pallas_call | solution.py:359
  103.4 3.8 %collective-permute-start.27 = (f32[256,128]{1,0:T(8,128)}, f32[256,128]{1,0:T(8,128)}, u32[]{:S(2)}, u32[]{:S(2)}) collective-permute-start(f32[256,128]{1,0:T(8,128)} %shard_map.85.head.old), channel_id=1, source_target_pairs={{0,24},{4,28},{8,0},{12,4},{16,8},{20,12},{24,16},{28,20},{1,25},{... | collective-permute-start | bytes 393224 | tf_op jit(solution)/shard_map/ppermute | solution.py:438
  107.2 2.4 %shard_map.70.inner.old = f32[6,256,128]{2,1,0:T(8,128)S(1)} custom-call(bf16[8,256,768]{2,1,0:T(8,128)(2,1)S(1)} %get-tuple-element.42.high, bf16[8,256,768]{2,1,0:T(8,128)(2,1)S(1)} %get-tuple-element.43.low, f32[256,128]{1,0:T(8,128)S(1)} %get-tuple-element.38.head.old, f32[256,128]{1,0:T(8,128)S(1)} %copy-done.29, f32[6,256,128]{2,1,0:T(8,128)S(1)} %copy-done.3, ...), custom_call_target="tpu_custom_call" | custom-call | tf_op jit(solution)/shard_map/pallas_call | solution.py:381
  111.8 3.8 %collective-permute-start.17 = (f32[256,128]{1,0:T(8,128)}, f32[256,128]{1,0:T(8,128)S(1)}, u32[]{:S(2)}, u32[]{:S(2)}) collective-permute-start(f32[256,128]{1,0:T(8,128)} %shard_map.72.head.old), channel_id=1, source_target_pairs={{0,24},{4,28},{8,0},{12,4},{16,8},{20,12},{24,16},{28,20},{1,25},{... | collective-permute-start | bytes 393224 | tf_op jit(solution)/shard_map/ppermute | solution.py:438
  115.6 1.9 %copy-done.1 = bf16[8,256,768]{2,1,0:T(8,128)(2,1)S(1)} copy-done((bf16[8,256,768]{2,1,0:T(8,128)(2,1)S(1)}, bf16[8,256,768]{2,1,0:T(8,128)(2,1)}, u32[]{:S(2)}) %copy-start.1) | copy-done | bytes 3145752
  121.6 2.4 %shard_map.86.inner.old = f32[6,256,128]{2,1,0:T(8,128)S(1)} custom-call(bf16[8,256,768]{2,1,0:T(8,128)(2,1)S(1)} %get-tuple-element.42.high, bf16[8,256,768]{2,1,0:T(8,128)(2,1)S(1)} %copy-done.1, f32[256,128]{1,0:T(8,128)S(1)} %copy-done.26, f32[256,128]{1,0:T(8,128)S(1)} %copy-done.33, f32[6,256,128]{2,1,0:T(8,128)S(1)} %copy-done.9, ...), custom_call_target="tpu_custom_call" | custom-call | tf_op jit(solution)/shard_map/pallas_call | solution.py:381
  124.0 2.4 %shard_map.73.inner.old = f32[6,256,128]{2,1,0:T(8,128)S(1)} custom-call(bf16[8,256,768]{2,1,0:T(8,128)(2,1)S(1)} %get-tuple-element.42.high, bf16[8,256,768]{2,1,0:T(8,128)(2,1)S(1)} %copy-done.1, f32[256,128]{1,0:T(8,128)S(1)} %copy-done.24, f32[256,128]{1,0:T(8,128)S(1)} %copy-done.31, f32[6,256,128]{2,1,0:T(8,128)S(1)} %copy-done.12, ...), custom_call_target="tpu_custom_call" | custom-call | tf_op jit(solution)/shard_map/pallas_call | solution.py:381
  126.4 3.4 %shard_map.89.inner = f32[6,256,128]{2,1,0:T(8,128)S(1)} custom-call(bf16[8,256,768]{2,1,0:T(8,128)(2,1)S(1)} %get-tuple-element.42.high, bf16[8,256,768]{2,1,0:T(8,128)(2,1)S(1)} %copy-done.1, f32[256,128]{1,0:T(8,128)} %shard_map.85.head.old, f32[256,128]{1,0:T(8,128)} %shard_map.87.tail.old, f32[6,256,128]{2,1,0:T(8,128)S(1)} %shard_map.86.inner.old, ...), custom_call_target="tpu_custom_call" | custom-call | tf_op jit(solution)/shard_map/pallas_call | solution.py:381
  129.8 3.4 %shard_map.76.inner = f32[6,256,128]{2,1,0:T(8,128)S(1)} custom-call(bf16[8,256,768]{2,1,0:T(8,128)(2,1)S(1)} %get-tuple-element.42.high, bf16[8,256,768]{2,1,0:T(8,128)(2,1)S(1)} %copy-done.1, f32[256,128]{1,0:T(8,128)} %shard_map.72.head.old, f32[256,128]{1,0:T(8,128)} %shard_map.74.tail.old, f32[6,256,128]{2,1,0:T(8,128)S(1)} %shard_map.73.inner.old, ...), custom_call_target="tpu_custom_call" | custom-call | tf_op jit(solution)/shard_map/pallas_call | solution.py:381
  136.3 1.9 %collective-permute-start.28 = (f32[256,128]{1,0:T(8,128)S(1)}, f32[256,128]{1,0:T(8,128)S(1)}, u32[]{:S(2)}, u32[]{:S(2)}) collective-permute-start(f32[256,128]{1,0:T(8,128)S(1)} %shard_map.90.tail), channel_id=1, source_target_pairs={{0,8},{4,12},{8,16},{12,20},{16,24},{20,28},{24,0},{28,4},{1,9},{5... | collective-permute-start | bytes 393224 | tf_op jit(solution)/shard_map/ppermute | solution.py:438
  138.1 2.4 %shard_map.93.refs_7_ = f32[6,256,128]{2,1,0:T(8,128)S(1)} custom-call(bf16[8,256,768]{2,1,0:T(8,128)(2,1)S(1)} %get-tuple-element.42.high, bf16[8,256,768]{2,1,0:T(8,128)(2,1)S(1)} %copy-done.1, f32[256,128]{1,0:T(8,128)S(1)} %shard_map.88.head, f32[256,128]{1,0:T(8,128)S(1)} %shard_map.90.tail, f32[6,256,128]{2,1,0:T(8,128)S(1)} %shard_map.89.inner, ...), custom_call_target="tpu_custom_call" | custom-call | tf_op jit(solution)/shard_map/pallas_call | solution.py:381
  140.6 1.7 %collective-permute-start.31 = (f32[3,256,128]{2,1,0:T(8,128)S(1)}, f32[3,256,128]{2,1,0:T(8,128)S(1)}, u32[]{:S(2)}, u32[]{:S(2)}) collective-permute-start(f32[3,256,128]{2,1,0:T(8,128)S(1)} %constant_dynamic-slice_fusion.1), channel_id=1, source_target_pairs={{0,4},{4,0},{8,12},{12,8},{16,20},{20,16},{24,28},{28,24},{1,5},{5... | collective-permute-start | bytes 1179656 | tf_op jit(solution)/shard_map/ppermute | solution.py:433
  143.7 2.1 %collective-permute-start.19 = (f32[256,128]{1,0:T(8,128)S(1)}, f32[256,128]{1,0:T(8,128)S(1)}, u32[]{:S(2)}, u32[]{:S(2)}) collective-permute-start(f32[256,128]{1,0:T(8,128)S(1)} %shard_map.75.head), channel_id=1, source_target_pairs={{0,24},{4,28},{8,0},{12,4},{16,8},{20,12},{24,16},{28,20},{1,25},{... | collective-permute-start | bytes 393224 | tf_op jit(solution)/shard_map/ppermute | solution.py:438
  147.2 2.4 %shard_map.80.refs_2_ = f32[6,256,128]{2,1,0:T(8,128)S(1)} custom-call(bf16[8,256,768]{2,1,0:T(8,128)(2,1)S(1)} %get-tuple-element.42.high, bf16[8,256,768]{2,1,0:T(8,128)(2,1)S(1)} %copy-done.1, f32[256,128]{1,0:T(8,128)S(1)} %shard_map.75.head, f32[256,128]{1,0:T(8,128)S(1)} %shard_map.77.tail, f32[6,256,128]{2,1,0:T(8,128)S(1)} %shard_map.76.inner, ...), custom_call_target="tpu_custom_call" | custom-call | tf_op jit(solution)/shard_map/pallas_call | solution.py:381
  157.6 6.9 %collective-permute-done.30.refs_8_ = f32[256,128]{1,0:T(8,128)S(1)} collective-permute-done((f32[256,128]{1,0:T(8,128)S(1)}, f32[256,128]{1,0:T(8,128)S(1)}, u32[]{:S(2)}, u32[]{:S(2)}) %collective-permute-start.30) | collective-permute-done | bytes 131104 | tf_op jit(solution)/shard_map/ppermute | solution.py:433
  164.5 2.7 %collective-permute-done.20.refs_3_ = f32[256,128]{1,0:T(8,128)S(1)} collective-permute-done((f32[256,128]{1,0:T(8,128)S(1)}, f32[256,128]{1,0:T(8,128)S(1)}, u32[]{:S(2)}, u32[]{:S(2)}) %collective-permute-start.20) | collective-permute-done | bytes 131104 | tf_op jit(solution)/shard_map/ppermute | solution.py:433
  167.1 1.9 %shard_map.94 = f32[4,256,512]{2,1,0:T(8,128)} custom-call(s32[1]{0:T(128)} %bitcast.at_ref.side_ref, f32[256,128]{1,0:T(8,128)S(1)} %shard_map.78.refs_0_, f32[256,128]{1,0:T(8,128)S(1)} %shard_map.79.refs_1_, f32[6,256,128]{2,1,0:T(8,128)S(1)} %shard_map.80.refs_2_, f32[256,128]{1,0:T(8,128)S(1)} %collective-permute-done.20.refs_3_, ...), custom_call_target="tpu_custom_call" | custom-call | tf_op jit(solution)/shard_map/pallas_call | solution.py:411
  (170 shorter events, 61.2 us)
Async XLA Ops:
  5.6 14.7 %collective-permute-start.1 = (f32[256,128]{1,0:T(8,128)S(1)}, f32[256,128]{1,0:T(8,128)S(1)}, u32[]{:S(2)}, u32[]{:S(2)}) collective-permute-start(f32[256,128]{1,0:T(8,128)S(1)} %get-tuple-element.30), channel_id=1, source_target_pairs={{0,28},{4,0},{8,4},{12,8},{16,12},{20,16},{24,20},{28,24},{1,29},{... | collective-permute-start | bytes 393224 | tf_op jit(solution)/shard_map/ppermute | solution.py:438
  21.6 2.6 %collective-permute-start.2 = (f32[2,392,256]{2,1,0:T(8,128)}, f32[2,392,256]{2,1,0:T(8,128)S(1)}, u32[]{:S(2)}, u32[]{:S(2)}) collective-permute-start(f32[2,392,256]{2,1,0:T(8,128)} %get-tuple-element.34), channel_id=1, source_target_pairs={{0,1},{1,0},{2,3},{3,2},{4,5},{5,4},{6,7},{7,6},{8,9},{9,8},{10,11... | collective-permute-start | bytes 2408456 | tf_op jit(solution)/shard_map/ppermute | solution.py:433
  26.3 11.5 %collective-permute-start.3 = (f32[1,392,256]{2,1,0:T(8,128)S(1)}, f32[1,392,256]{2,1,0:T(8,128)}, u32[]{:S(2)}, u32[]{:S(2)}) collective-permute-start(f32[1,392,256]{2,1,0:T(8,128)S(1)} %dynamic-slice_add_fusion), channel_id=1, source_target_pairs={{0,2},{1,3},{2,0},{3,1},{4,6},{5,7},{6,4},{7,5},{8,10},{9,11},{10,... | collective-permute-start | bytes 1204232 | tf_op jit(solution)/shard_map/ppermute | solution.py:433
  27.8 14.0 %collective-permute-start = (f32[4,256,128]{2,1,0:T(8,128)}, f32[4,256,128]{2,1,0:T(8,128)}, u32[]{:S(2)}, u32[]{:S(2)}) collective-permute-start(f32[4,256,128]{2,1,0:T(8,128)} %get-tuple-element.28), channel_id=1, source_target_pairs={{0,4},{4,0},{8,12},{12,8},{16,20},{20,16},{24,28},{28,24},{1,5},{5... | collective-permute-start | bytes 1572872 | tf_op jit(solution)/shard_map/ppermute | solution.py:433
  41.8 11.8 %collective-permute-start.7 = (f32[1,392,256]{2,1,0:T(8,128)S(1)}, f32[1,392,256]{2,1,0:T(8,128)S(1)}, u32[]{:S(2)}, u32[]{:S(2)}) collective-permute-start(f32[1,392,256]{2,1,0:T(8,128)S(1)} %add_add_fusion.refs_0_), channel_id=1, source_target_pairs={{0,4},{4,0},{8,12},{12,8},{16,20},{20,16},{24,28},{28,24},{1,5},{5... | collective-permute-start | bytes 1204232 | tf_op jit(solution)/shard_map/ppermute | solution.py:433
  42.1 11.5 %collective-permute-start.4 = (f32[1,392,256]{2,1,0:T(8,128)S(1)}, f32[1,392,256]{2,1,0:T(8,128)S(1)}, u32[]{:S(2)}, u32[]{:S(2)}) collective-permute-start(f32[1,392,256]{2,1,0:T(8,128)S(1)} %add_add_fusion.refs_0_), channel_id=1, source_target_pairs={{0,2},{1,3},{2,0},{3,1},{4,6},{5,7},{6,4},{7,5},{8,10},{9,11},{10,... | collective-permute-start | bytes 1204232 | tf_op jit(solution)/shard_map/ppermute | solution.py:433
  44.8 7.5 %collective-permute-start.5 = (f32[256,128]{1,0:T(8,128)S(1)}, f32[256,128]{1,0:T(8,128)S(1)}, u32[]{:S(2)}, u32[]{:S(2)}) collective-permute-start(f32[256,128]{1,0:T(8,128)S(1)} %get-tuple-element.37.tail.old), channel_id=1, source_target_pairs={{0,8},{4,12},{8,16},{12,20},{16,24},{20,28},{24,0},{28,4},{1,9},{5... | collective-permute-start | bytes 393224 | tf_op jit(solution)/shard_map/ppermute | solution.py:438
  45.5 7.5 %collective-permute-start.6 = (f32[256,128]{1,0:T(8,128)S(1)}, f32[256,128]{1,0:T(8,128)S(1)}, u32[]{:S(2)}, u32[]{:S(2)}) collective-permute-start(f32[256,128]{1,0:T(8,128)S(1)} %get-tuple-element.38.head.old), channel_id=1, source_target_pairs={{0,24},{4,28},{8,0},{12,4},{16,8},{20,12},{24,16},{28,20},{1,25},{... | collective-permute-start | bytes 393224 | tf_op jit(solution)/shard_map/ppermute | solution.py:438
  49.3 14.0 %collective-permute-start.8 = (f32[4,256,128]{2,1,0:T(8,128)}, f32[4,256,128]{2,1,0:T(8,128)}, u32[]{:S(2)}, u32[]{:S(2)}) collective-permute-start(f32[4,256,128]{2,1,0:T(8,128)} %get-tuple-element.40), channel_id=1, source_target_pairs={{0,4},{4,0},{8,12},{12,8},{16,20},{20,16},{24,28},{28,24},{1,5},{5... | collective-permute-start | bytes 1572872 | tf_op jit(solution)/shard_map/ppermute | solution.py:433
  54.8 24.6 %collective-permute-start.12 = (f32[3,392,256]{2,1,0:T(8,128)}, f32[3,392,256]{2,1,0:T(8,128)}, u32[]{:S(2)}, u32[]{:S(2)}) collective-permute-start(f32[3,392,256]{2,1,0:T(8,128)} %pad_maximum_fusion), channel_id=1, source_target_pairs={{0,1},{1,0},{2,3},{3,2},{4,5},{5,4},{6,7},{7,6},{8,9},{9,8},{10,11... | collective-permute-start | bytes 3612680 | tf_op jit(solution)/shard_map/ppermute | solution.py:433
  54.8 11.8 %collective-permute-start.9 = (f32[1,392,256]{2,1,0:T(8,128)S(1)}, f32[1,392,256]{2,1,0:T(8,128)}, u32[]{:S(2)}, u32[]{:S(2)}) collective-permute-start(f32[1,392,256]{2,1,0:T(8,128)S(1)} %collective-permute-done.7.refs_2_), channel_id=1, source_target_pairs={{0,2},{1,3},{2,0},{3,1},{4,6},{5,7},{6,4},{7,5},{8,10},{9,11},{10,... | collective-permute-start | bytes 1204232 | tf_op jit(solution)/shard_map/ppermute | solution.py:433
  67.7 1.7 %collective-permute-start.10 = (f32[256,256]{1,0:T(8,128)S(1)}, f32[256,256]{1,0:T(8,128)S(1)}, u32[]{:S(2)}, u32[]{:S(2)}) collective-permute-start(f32[256,256]{1,0:T(8,128)S(1)} %fusion.1), channel_id=1, source_target_pairs={{1,9},{3,11},{5,13},{7,15},{9,17},{11,19},{13,21},{15,23},{17,25},... | collective-permute-start | bytes 786440 | tf_op jit(solution)/shard_map/ppermute | solution.py:506
  68.4 10.3 %collective-permute-start.13 = (f32[1,392,256]{2,1,0:T(8,128)}, f32[1,392,256]{2,1,0:T(8,128)S(1)}, u32[]{:S(2)}, u32[]{:S(2)}) collective-permute-start(f32[1,392,256]{2,1,0:T(8,128)} %collective-permute-done.9.refs_3_), channel_id=1, source_target_pairs={{0,1},{1,0},{2,3},{3,2},{4,5},{5,4},{6,7},{7,6},{8,9},{9,8},{10,11... | collective-permute-start | bytes 1204232 | tf_op jit(solution)/shard_map/ppermute | solution.py:433
  69.4 9.2 %collective-permute-start.11 = (f32[256,256]{1,0:T(8,128)S(1)}, f32[256,256]{1,0:T(8,128)S(1)}, u32[]{:S(2)}, u32[]{:S(2)}) collective-permute-start(f32[256,256]{1,0:T(8,128)S(1)} %collective-permute-done.10), channel_id=1, source_target_pairs={{1,0},{3,2},{5,4},{7,6},{9,8},{11,10},{13,12},{15,14},{17,16},{19,... | collective-permute-start | bytes 786440 | tf_op jit(solution)/shard_map/ppermute | solution.py:507
  73.6 12.6 %collective-permute-start.22 = (f32[256,128]{1,0:T(8,128)}, f32[256,128]{1,0:T(8,128)}, u32[]{:S(2)}, u32[]{:S(2)}) collective-permute-start(f32[256,128]{1,0:T(8,128)} %get-tuple-element.50.tail.old), channel_id=1, source_target_pairs={{0,8},{4,12},{8,16},{12,20},{16,24},{20,28},{24,0},{28,4},{1,9},{5... | collective-permute-start | bytes 393224 | tf_op jit(solution)/shard_map/ppermute | solution.py:438
  75.0 14.5 %collective-permute-start.23 = (f32[256,128]{1,0:T(8,128)}, f32[256,128]{1,0:T(8,128)}, u32[]{:S(2)}, u32[]{:S(2)}) collective-permute-start(f32[256,128]{1,0:T(8,128)} %get-tuple-element.48.head.old), channel_id=1, source_target_pairs={{0,24},{4,28},{8,0},{12,4},{16,8},{20,12},{24,16},{28,20},{1,25},{... | collective-permute-start | bytes 393224 | tf_op jit(solution)/shard_map/ppermute | solution.py:438
  88.2 11.1 %collective-permute-start.25 = (f32[256,128]{1,0:T(8,128)S(1)}, f32[256,128]{1,0:T(8,128)S(1)}, u32[]{:S(2)}, u32[]{:S(2)}) collective-permute-start(f32[256,128]{1,0:T(8,128)S(1)} %shard_map.82.head.old), channel_id=1, source_target_pairs={{0,24},{4,28},{8,0},{12,4},{16,8},{20,12},{24,16},{28,20},{1,25},{... | collective-permute-start | bytes 393224 | tf_op jit(solution)/shard_map/ppermute | solution.py:438
  91.0 10.4 %collective-permute-start.24 = (f32[256,128]{1,0:T(8,128)S(1)}, f32[256,128]{1,0:T(8,128)S(1)}, u32[]{:S(2)}, u32[]{:S(2)}) collective-permute-start(f32[256,128]{1,0:T(8,128)S(1)} %shard_map.84.tail.old), channel_id=1, source_target_pairs={{0,8},{4,12},{8,16},{12,20},{16,24},{20,28},{24,0},{28,4},{1,9},{5... | collective-permute-start | bytes 393224 | tf_op jit(solution)/shard_map/ppermute | solution.py:438
  92.2 17.4 %collective-permute-start.15 = (f32[256,128]{1,0:T(8,128)S(1)}, f32[256,128]{1,0:T(8,128)S(1)}, u32[]{:S(2)}, u32[]{:S(2)}) collective-permute-start(f32[256,128]{1,0:T(8,128)S(1)} %shard_map.69.head.old), channel_id=1, source_target_pairs={{0,24},{4,28},{8,0},{12,4},{16,8},{20,12},{24,16},{28,20},{1,25},{... | collective-permute-start | bytes 393224 | tf_op jit(solution)/shard_map/ppermute | solution.py:438
  95.8 14.9 %collective-permute-start.14 = (f32[256,128]{1,0:T(8,128)S(1)}, f32[256,128]{1,0:T(8,128)S(1)}, u32[]{:S(2)}, u32[]{:S(2)}) collective-permute-start(f32[256,128]{1,0:T(8,128)S(1)} %shard_map.71.tail.old), channel_id=1, source_target_pairs={{0,8},{4,12},{8,16},{12,20},{16,24},{20,28},{24,0},{28,4},{1,9},{5... | collective-permute-start | bytes 393224 | tf_op jit(solution)/shard_map/ppermute | solution.py:438
  101.4 31.8 %collective-permute-start.26 = (f32[256,128]{1,0:T(8,128)}, f32[256,128]{1,0:T(8,128)}, u32[]{:S(2)}, u32[]{:S(2)}) collective-permute-start(f32[256,128]{1,0:T(8,128)} %shard_map.87.tail.old), channel_id=1, source_target_pairs={{0,8},{4,12},{8,16},{12,20},{16,24},{20,28},{24,0},{28,4},{1,9},{5... | collective-permute-start | bytes 393224 | tf_op jit(solution)/shard_map/ppermute | solution.py:438
  103.4 31.5 %collective-permute-start.27 = (f32[256,128]{1,0:T(8,128)}, f32[256,128]{1,0:T(8,128)}, u32[]{:S(2)}, u32[]{:S(2)}) collective-permute-start(f32[256,128]{1,0:T(8,128)} %shard_map.85.head.old), channel_id=1, source_target_pairs={{0,24},{4,28},{8,0},{12,4},{16,8},{20,12},{24,16},{28,20},{1,25},{... | collective-permute-start | bytes 393224 | tf_op jit(solution)/shard_map/ppermute | solution.py:438
  110.7 31.6 %collective-permute-start.16 = (f32[256,128]{1,0:T(8,128)}, f32[256,128]{1,0:T(8,128)}, u32[]{:S(2)}, u32[]{:S(2)}) collective-permute-start(f32[256,128]{1,0:T(8,128)} %shard_map.74.tail.old), channel_id=1, source_target_pairs={{0,8},{4,12},{8,16},{12,20},{16,24},{20,28},{24,0},{28,4},{1,9},{5... | collective-permute-start | bytes 393224 | tf_op jit(solution)/shard_map/ppermute | solution.py:438
  111.8 34.0 %collective-permute-start.17 = (f32[256,128]{1,0:T(8,128)}, f32[256,128]{1,0:T(8,128)S(1)}, u32[]{:S(2)}, u32[]{:S(2)}) collective-permute-start(f32[256,128]{1,0:T(8,128)} %shard_map.72.head.old), channel_id=1, source_target_pairs={{0,24},{4,28},{8,0},{12,4},{16,8},{20,12},{24,16},{28,20},{1,25},{... | collective-permute-start | bytes 393224 | tf_op jit(solution)/shard_map/ppermute | solution.py:438
  134.6 15.0 %collective-permute-start.29 = (f32[256,128]{1,0:T(8,128)S(1)}, f32[256,128]{1,0:T(8,128)S(1)}, u32[]{:S(2)}, u32[]{:S(2)}) collective-permute-start(f32[256,128]{1,0:T(8,128)S(1)} %shard_map.88.head), channel_id=1, source_target_pairs={{0,24},{4,28},{8,0},{12,4},{16,8},{20,12},{24,16},{28,20},{1,25},{... | collective-permute-start | bytes 393224 | tf_op jit(solution)/shard_map/ppermute | solution.py:438
  136.3 15.1 %collective-permute-start.28 = (f32[256,128]{1,0:T(8,128)S(1)}, f32[256,128]{1,0:T(8,128)S(1)}, u32[]{:S(2)}, u32[]{:S(2)}) collective-permute-start(f32[256,128]{1,0:T(8,128)S(1)} %shard_map.90.tail), channel_id=1, source_target_pairs={{0,8},{4,12},{8,16},{12,20},{16,24},{20,28},{24,0},{28,4},{1,9},{5... | collective-permute-start | bytes 393224 | tf_op jit(solution)/shard_map/ppermute | solution.py:438
  140.6 26.5 %collective-permute-start.31 = (f32[3,256,128]{2,1,0:T(8,128)S(1)}, f32[3,256,128]{2,1,0:T(8,128)S(1)}, u32[]{:S(2)}, u32[]{:S(2)}) collective-permute-start(f32[3,256,128]{2,1,0:T(8,128)S(1)} %constant_dynamic-slice_fusion.1), channel_id=1, source_target_pairs={{0,4},{4,0},{8,12},{12,8},{16,20},{20,16},{24,28},{28,24},{1,5},{5... | collective-permute-start | bytes 1179656 | tf_op jit(solution)/shard_map/ppermute | solution.py:433
  143.7 10.7 %collective-permute-start.19 = (f32[256,128]{1,0:T(8,128)S(1)}, f32[256,128]{1,0:T(8,128)S(1)}, u32[]{:S(2)}, u32[]{:S(2)}) collective-permute-start(f32[256,128]{1,0:T(8,128)S(1)} %shard_map.75.head), channel_id=1, source_target_pairs={{0,24},{4,28},{8,0},{12,4},{16,8},{20,12},{24,16},{28,20},{1,25},{... | collective-permute-start | bytes 393224 | tf_op jit(solution)/shard_map/ppermute | solution.py:438
  147.1 8.7 %collective-permute-start.18 = (f32[256,128]{1,0:T(8,128)S(1)}, f32[256,128]{1,0:T(8,128)S(1)}, u32[]{:S(2)}, u32[]{:S(2)}) collective-permute-start(f32[256,128]{1,0:T(8,128)S(1)} %shard_map.77.tail), channel_id=1, source_target_pairs={{0,8},{4,12},{8,16},{12,20},{16,24},{20,28},{24,0},{28,4},{1,9},{5... | collective-permute-start | bytes 393224 | tf_op jit(solution)/shard_map/ppermute | solution.py:438
  149.6 17.5 %collective-permute-start.21 = (f32[3,256,128]{2,1,0:T(8,128)S(1)}, f32[3,256,128]{2,1,0:T(8,128)S(1)}, u32[]{:S(2)}, u32[]{:S(2)}) collective-permute-start(f32[3,256,128]{2,1,0:T(8,128)S(1)} %constant_dynamic-slice_fusion), channel_id=1, source_target_pairs={{0,4},{4,0},{8,12},{12,8},{16,20},{20,16},{24,28},{28,24},{1,5},{5... | collective-permute-start | bytes 1179656 | tf_op jit(solution)/shard_map/ppermute | solution.py:433
  152.7 11.7 %collective-permute-start.30 = (f32[256,128]{1,0:T(8,128)S(1)}, f32[256,128]{1,0:T(8,128)S(1)}, u32[]{:S(2)}, u32[]{:S(2)}) collective-permute-start(f32[256,128]{1,0:T(8,128)S(1)} %broadcast_select_fusion), channel_id=1, source_target_pairs={{0,4},{4,0},{8,12},{12,8},{16,20},{20,16},{24,28},{28,24},{1,5},{5... | collective-permute-start | bytes 393224 | tf_op jit(solution)/shard_map/ppermute | solution.py:433
  157.1 10.0 %collective-permute-start.20 = (f32[256,128]{1,0:T(8,128)S(1)}, f32[256,128]{1,0:T(8,128)S(1)}, u32[]{:S(2)}, u32[]{:S(2)}) collective-permute-start(f32[256,128]{1,0:T(8,128)S(1)} %broadcast_select_fusion.1), channel_id=1, source_target_pairs={{0,4},{4,0},{8,12},{12,8},{16,20},{20,16},{24,28},{28,24},{1,5},{5... | collective-permute-start | bytes 393224 | tf_op jit(solution)/shard_map/ppermute | solution.py:433
  (45 other events, 235.3 us)

commit v4 on v3

--- a/solution.py
+++ b/solution.py
@@ -17,6 +17,18 @@
 PARAMS = pltpu.CompilerParams(vmem_limit_bytes=12 * 1024 * 1024)
 SCALARS = pl.BlockSpec(memory_space=pltpu.SMEM)
 ANY = pl.BlockSpec(memory_space=pl.ANY)
+
+
+def near_core(shape, dtype=jnp.float32):
+    return pltpu.VMEM(shape, dtype)
+
+
+def far_off(value):
+    return pltpu.with_memory_space_constraint(value, pltpu.MemorySpace.HBM)
+
+
+def close_by(value):
+    return pltpu.with_memory_space_constraint(value, pltpu.MemorySpace.VMEM)
 VMEM = pl.BlockSpec(memory_space=pltpu.VMEM)
 NN = (((1,), (0,)), ((), ()))
 NT = (((1,), (1,)), ((), ()))
@@ -166,13 +178,12 @@
 
 
 def weights_kernel(me_ref, *refs):
-    sources, (high_ref, low_ref), held, sems = refs[:6], refs[6:8], refs[8], refs[9]
+    sources, (high_ref, low_ref), held, sems = refs[:8], refs[8:10], refs[10], refs[11]
     me = me_ref[0]
     size = held.shape[2]
     half = size // 2
-    places = ((0, 0), (1, 0), (2, 0), (3, 0), (4, 0), (4, 1), (4, 2), (5, 0))
-    away_at = (0, 1, 4, 5, 2, 3, 6, 7)
-    copies = [pltpu.make_async_copy(sources[ref].at[at], held.at[n], sems.at[n]) for n, (ref, at) in enumerate(places)]
+    away_at = (0, 2, 1, 4, 3, 6, 5, 7)
+    copies = [pltpu.make_async_copy(source.at[0], held.at[n], sems.at[n]) for n, source in enumerate(sources)]
     for copy in copies:
         copy.start()
     row = lax.broadcasted_iota(jnp.int32, (size, size), 0)
@@ -181,14 +192,34 @@
     for n, away in enumerate(away_at):
         copies[n].wait()
         element = away ^ me
-        volume = unpacked(held[n, size : size + half, :half], held[n, size : size + half, half:], held[n, size + half : size + half + 1, :half])
-        volume = (volume - jnp.where(diagonal, center, 0.0)) * (1.0 / half_width)
-        coupling = held[n, :size] * (1.0 / half_width)
         following = lax.rem(element + 1, len(away_at))
-        for place, at_column, value in ((following, 0, coupling.T), (element, 1, volume), (element, 2, coupling)):
-            high, low = split(value)
-            high_ref[place, :, at_column * size : (at_column + 1) * size] = high
-            low_ref[place, :, at_column * size : (at_column + 1) * size] = low
+        volume, coupling = scaled(held[n], diagonal)
+        for place, at, value in ((following, 0, coupling.T), (element, 1, volume), (element, 2, coupling)):
+            high_ref[place, :, at * size : (at + 1) * size], low_ref[place, :, at * size : (at + 1) * size] = split(value)
+
+
+def scaled(block, diagonal):
+    size = block.shape[1]
+    half = size // 2
+    volume = unpacked(block[size : size + half, :half], block[size : size + half, half:], block[size + half : size + half + 1, :half])
+    return (volume - jnp.where(diagonal, center, 0.0)) * (1.0 / half_width), block[:size] * (1.0 / half_width)
+
+
+def outer_kernel(core_ref, first_ref, second_ref, swapped_ref, high_in, low_in, high_ref, low_ref):
+    size = first_ref.shape[2]
+    row = lax.broadcasted_iota(jnp.int32, (size, size), 0)
+    diagonal = row == lax.broadcasted_iota(jnp.int32, (size, size), 1)
+    kept = first_ref[0] + second_ref[0]
+    core = core_ref[0]
+    prior = jnp.where(core == 1, kept[:size], swapped_ref[0, :size]) * (1.0 / half_width)
+    volume, coupling = scaled(jnp.where(core == 1, swapped_ref[0], kept), diagonal)
+    last = high_in.shape[0] - 1
+    high_ref[0, :, size:] = high_in[0, :, size:]
+    low_ref[0, :, size:] = low_in[0, :, size:]
+    high_ref[0, :, :size], low_ref[0, :, :size] = split(prior.T)
+    turned = (high_in[last, :, 2 * size :].astype(jnp.float32) + low_in[last, :, 2 * size :].astype(jnp.float32)).T
+    for at, value in enumerate((turned, volume, coupling)):
+        high_ref[1, :, at * size : (at + 1) * size], low_ref[1, :, at * size : (at + 1) * size] = split(value)
 
 
 def held_shape(rows, columns):
@@ -223,48 +254,56 @@
     return result if first else 2.0 * result - before
 
 
-def head_kernel(first, before, high, low, head, inner, below, old, out, held):
-    size, columns = head.shape
-    for at, value in enumerate((below[...], head[...], inner[0])):
-        hold(held, at, value)
-    before_high, before_low = split((before[...] * (1.0 / half_width)).T)
-    row = apply_row(
-        jnp.concatenate([before_high, high[0, :, size:]], axis=1), jnp.concatenate([before_low, low[0, :, size:]], axis=1), held, 0, columns
-    )
-    out[...] = advance(first, row, None if first else old[...])
-
-
-def tail_kernel(first, high, low, tail, inner, above, old, out, held):
-    for at, value in enumerate((inner[inner.shape[0] - 1], tail[...], above[...])):
+def edge_kernel(first, up, high, low, high_outer, low_outer, inner, halo, old, out, held):
+    size, columns = inner.shape[1:]
+    count = inner.shape[0]
+    local = (inner[count - 2], inner[count - 1]) if up else (inner[0], inner[1])
+    beyond = (halo[0], halo[1])
+    for at, value in enumerate(local + beyond if up else beyond + local):
         hold(held, at, value)
     last = high.shape[0] - 1
-    row = apply_row(high[last], low[last], held, 0, tail.shape[1])
-    out[...] = advance(first, row, None if first else old[...])
-
-
-def inner_kernel(first, high, low, head, tail, inner, old, out, held):
+    rows = ((high[last], low[last]), (high_outer[1], low_outer[1])) if up else ((high_outer[0], low_outer[0]), (high[1], low[1]))
+    for at, (part_high, part_low) in enumerate(rows):
+        row = apply_row(part_high, part_low, held, at * size, columns)
+        out[at] = advance(first, row, None if first else old[at])
+
+
+def inner_kernel(first, up, high, low, edge, inner, old, out, held):
     count, size, columns = inner.shape
-    hold(held, 0, head[...])
+    for at in range(2):
+        hold(held, at if up else count + at, edge[at])
     for at in range(count):
-        hold(held, at + 1, inner[at])
-    hold(held, count + 1, tail[...])
+        hold(held, at + 2 if up else at, inner[at])
 
     @pl.loop(0, count)
     def _(at):
-        row = apply_row(high[at + 1], low[at + 1], held, pl.multiple_of(at * size, size), columns)
+        place = at + (1 if up else 2)
+        row = apply_row(high[place], low[place], held, pl.multiple_of(at * size, size), columns)
         out[at] = advance(first, row, None if first else old[at])
 
 
-def arrange_kernel(chunk, chunks, at_ref, vector_ref, got_ref, head_ref, tail_ref, inner_ref, sems):
+def fold_kernel(lane_ref, keep_ref, other_ref, send_ref, stay_ref):
+    lane = lane_ref[0]
+    half = keep_ref.shape[0] // 2
+    for at in range(half):
+        send_ref[at] = keep_ref[(1 - lane) * half + at] + other_ref[(1 - lane) * half + at]
+        stay_ref[at] = keep_ref[lane * half + at] + other_ref[lane * half + at]
+
+
+def sum_kernel(first_ref, second_ref, out_ref):
+    out_ref[...] = first_ref[...] + second_ref[...]
+
+
+def arrange_kernel(chunk, chunks, side_ref, vector_ref, got_ref, edge_ref, inner_ref, sems):
     half, _, width = got_ref.shape
-    side = at_ref[0]
-    targets = [head_ref] + [inner_ref.at[at] for at in range(2 * half - 2)] + [tail_ref]
+    side = side_ref[0]
+    targets = [edge_ref.at[0], edge_ref.at[1]] + [inner_ref.at[at] for at in range(2 * half - 2)]
 
     def moved(act):
         for element, target in enumerate(targets):
             own = vector_ref.at[element % half]
             if vector_ref.shape[2] > width:
-                start = pl.multiple_of((at_ref[0] * chunks + chunk) * width, width)
+                start = pl.multiple_of((side * chunks + chunk) * width, width)
                 own = vector_ref.at[element % half, :, pl.ds(start, width)]
             for source, mine in ((own, True), (got_ref.at[element % half], False)):
 
@@ -276,25 +315,49 @@
     moved(lambda copy: copy.wait())
 
 
-def collect_kernel(count, chunks, side_ref, *refs):
-    out_ref = refs[-1]
-    step = pl.program_id(0)
-    side = side_ref[0]
-    at_end = step == side * (count - 1)
+def place_pairs(out_ref, sems, side, chunks, chunk, width, pairs):
+    def moved(act):
+        for at, (wanted, source, element, foreign) in enumerate(pairs):
+
+            @pl.when(side == wanted)
+            def _():
+                part = 1 - side if foreign else side
+                start = pl.multiple_of((part * chunks + chunk) * width, width)
+                act(pltpu.make_async_copy(source, out_ref.at[pl.ds(element, 2), :, pl.ds(start, width)], sems.at[chunk, at]))
+
+    return moved
+
+
+def collect_kernel(chunks, side_ref, *refs):
+    sources, out_ref, sems = refs[: 3 * chunks], refs[-2], refs[-1]
+    acts = []
     for chunk in range(chunks):
-        head_ref, tail_ref, inner_ref, got_end_ref, got_inner_ref = refs[5 * chunk : 5 * chunk + 5]
-        end = jnp.where(side == 0, head_ref[...], tail_ref[...])
-        mine = jnp.where(at_end, end, inner_ref[0])
-        theirs = jnp.where(at_end, got_end_ref[...], got_inner_ref[0])
-        width = mine.shape[1]
-        first = chunk * width
-        second = (chunks + chunk) * width
-        out_ref[0, :, first : first + width] = jnp.where(side == 0, mine, theirs)
-        out_ref[0, :, second : second + width] = jnp.where(side == 0, theirs, mine)
-
-
-def whole(shape):
-    return pl.BlockSpec(shape, lambda *steps: (0,) * len(shape))
+        edge, inner, near = sources[3 * chunk : 3 * chunk + 3]
+        pairs = (
+            (0, edge, 0, False),
+            (0, inner.at[pl.ds(0, 2)], 2, False),
+            (0, near, 2, True),
+            (1, inner.at[pl.ds(2, 2)], 0, False),
+            (1, inner.at[pl.ds(4, 2)], 2, False),
+            (1, near, 0, True),
+        )
+        acts.append(place_pairs(out_ref, sems, side_ref[0], chunks, chunk, edge.shape[2], pairs))
+    for act in acts:
+        act(lambda copy: copy.start())
+    for act in acts:
+        act(lambda copy: copy.wait())
+
+
+def finish_kernel(chunks, side_ref, *refs):
+    sources, out_ref, sems = refs[:chunks], refs[-2], refs[-1]
+    acts = []
+    for chunk, far in enumerate(sources):
+        pairs = ((0, far, 0, True), (1, far, 2, True))
+        acts.append(place_pairs(out_ref, sems, side_ref[0], chunks, chunk, far.shape[2], pairs))
+    for act in acts:
+        act(lambda copy: copy.start())
+    for act in acts:
+        act(lambda copy: copy.wait())
 
 
 def lead_and_cut(side, index, basis, vector, chunks, width):
@@ -308,18 +371,18 @@
         + [jax.ShapeDtypeStruct((count, size, width), jnp.float32)] * chunks,
         scratch_shapes=[pltpu.VMEM((points, size), jnp.float32), pltpu.SemaphoreType.DMA((1 + chunks,))],
         compiler_params=PARAMS,
-    )(side, index, basis, vector)
+    )(side, index, far_off(basis), far_off(vector))
 
 
 def blocks(core, index, quad, pairs, basis, applied, faces_total):
     count, points, size = basis.shape
     spots = index.shape[2]
-    part = jax.ShapeDtypeStruct((count // 2, size + size // 2 + 8, size), jnp.float32)
+    part = near_core((count // 2, size + size // 2 + 8, size))
     return pl.pallas_call(
         functools.partial(blocks_kernel, faces_total),
         in_specs=[SCALARS, VMEM, VMEM, VMEM, ANY, ANY],
         out_specs=[VMEM] * 3,
-        out_shape=[part, part, jax.ShapeDtypeStruct((size, spots), jnp.float32)],
+        out_shape=[part, part, near_core((size, spots))],
         scratch_shapes=[
             pltpu.VMEM((count, points, size), jnp.float32),
             pltpu.VMEM((count, points, size), jnp.float32),
@@ -327,7 +390,7 @@
             pltpu.SemaphoreType.DMA((2 * count,)),
         ],
         compiler_params=PARAMS,
-    )(core, index, quad, pairs, basis, applied)
+    )(core, index, quad, pairs, far_off(basis), far_off(applied))
 
 
 def last_coupling(core, pair, own, lead, send, keep, faces_total):
@@ -336,7 +399,7 @@
         functools.partial(last_kernel, faces_total),
         in_specs=[SCALARS, VMEM, VMEM, VMEM, ANY, ANY],
         out_specs=[ANY] * 2,
-        out_shape=[jax.ShapeDtypeStruct(send.shape, jnp.float32)] * 2,
+        out_shape=[near_core(send.shape)] * 2,
         input_output_aliases={4: 0, 5: 1},
         scratch_shapes=[pltpu.VMEM((size, size), jnp.float32), pltpu.SemaphoreType.DMA],
         compiler_params=PARAMS,
@@ -347,85 +410,104 @@
     rows, size = parts[0].shape[1:]
     return pl.pallas_call(
         weights_kernel,
-        in_specs=[SCALARS] + [ANY] * 6,
+        in_specs=[SCALARS] + [ANY] * 8,
         out_specs=[VMEM] * 2,
-        out_shape=[jax.ShapeDtypeStruct((8, size, 3 * size), jnp.bfloat16)] * 2,
+        out_shape=[near_core((8, size, 3 * size), jnp.bfloat16)] * 2,
         scratch_shapes=[pltpu.VMEM((8, rows, size), jnp.float32), pltpu.SemaphoreType.DMA((8,))],
         compiler_params=PARAMS,
     )(me, *parts)
 
 
-def apply_head(first, before, high, low, head, inner, below, old):
-    return pl.pallas_call(
-        functools.partial(head_kernel, first),
+def outer_weights(core, first, second, swapped, high, low):
+    size = first.shape[2]
+    return pl.pallas_call(
+        outer_kernel,
+        in_specs=[SCALARS] + [VMEM] * 5,
+        out_specs=[VMEM] * 2,
+        out_shape=[near_core((2, size, 3 * size), jnp.bfloat16)] * 2,
+        compiler_params=PARAMS,
+    )(core, first, second, swapped, high, low)
+
+
+def apply_edge(first, up, high, low, high_outer, low_outer, inner, halo, old):
+    _, size, columns = inner.shape
+    return pl.pallas_call(
+        functools.partial(edge_kernel, first, up),
         in_specs=[VMEM] * 7,
         out_specs=VMEM,
-        out_shape=jax.ShapeDtypeStruct(head.shape, jnp.float32),
-        scratch_shapes=[pltpu.VMEM(held_shape(3 * head.shape[0], head.shape[1]), jnp.bfloat16)],
-        compiler_params=PARAMS,
-    )(before, high, low, head, inner, below, old)
-
-
-def apply_tail(first, high, low, tail, inner, above, old):
-    return pl.pallas_call(
-        functools.partial(tail_kernel, first),
-        in_specs=[VMEM] * 6,
+        out_shape=near_core(halo.shape),
+        scratch_shapes=[pltpu.VMEM(held_shape(4 * size, columns), jnp.bfloat16)],
+        compiler_params=PARAMS,
+    )(high, low, high_outer, low_outer, inner, close_by(halo), old)
+
+
+def apply_inner(first, up, high, low, edge, inner, old):
+    count, size, columns = inner.shape
+    return pl.pallas_call(
+        functools.partial(inner_kernel, first, up),
+        in_specs=[VMEM] * 5,
         out_specs=VMEM,
-        out_shape=jax.ShapeDtypeStruct(tail.shape, jnp.float32),
-        scratch_shapes=[pltpu.VMEM(held_shape(3 * tail.shape[0], tail.shape[1]), jnp.bfloat16)],
-        compiler_params=PARAMS,
-    )(high, low, tail, inner, above, old)
-
-
-def apply_inner(first, high, low, head, tail, inner, old):
-    return pl.pallas_call(
-        functools.partial(inner_kernel, first),
-        in_specs=[VMEM] * 6,
-        out_specs=VMEM,
-        out_shape=jax.ShapeDtypeStruct(inner.shape, jnp.float32),
-        scratch_shapes=[pltpu.VMEM(held_shape((inner.shape[0] + 2) * inner.shape[1], inner.shape[2]), jnp.bfloat16)],
-        compiler_params=PARAMS,
-    )(high, low, head, tail, inner, old)
-
-
-def arranged(at, vector, got, chunk):
+        out_shape=near_core(inner.shape),
+        scratch_shapes=[pltpu.VMEM(held_shape((count + 2) * size, columns), jnp.bfloat16)],
+        compiler_params=PARAMS,
+    )(high, low, edge, inner, old)
+
+
+def folded(lane, keep, other):
+    shape = (keep.shape[0] // 2, *keep.shape[1:])
+    return pl.pallas_call(
+        fold_kernel,
+        in_specs=[SCALARS, VMEM, VMEM],
+        out_specs=[VMEM] * 2,
+        out_shape=[near_core(shape)] * 2,
+        compiler_params=PARAMS,
+    )(lane, keep, close_by(other))
+
+
+def added(first, second):
+    return pl.pallas_call(
+        sum_kernel, in_specs=[VMEM] * 2, out_specs=VMEM, out_shape=near_core(first.shape), compiler_params=PARAMS
+    )(first, close_by(second))
+
+
+def arranged(side, vector, got, chunk):
     half, size, columns = got.shape
     chunks = max(vector.shape[2] // 2 // columns, 1)
     return pl.pallas_call(
         functools.partial(arrange_kernel, chunk, chunks),
         in_specs=[SCALARS, ANY, ANY],
-        out_specs=[VMEM] * 3,
-        out_shape=[jax.ShapeDtypeStruct((size, columns), jnp.float32)] * 2
-        + [jax.ShapeDtypeStruct((2 * half - 2, size, columns), jnp.float32)],
+        out_specs=[VMEM] * 2,
+        out_shape=[near_core((2, size, columns)), near_core((2 * half - 2, size, columns))],
         scratch_shapes=[pltpu.SemaphoreType.DMA((2 * half,))],
         compiler_params=PARAMS,
-    )(at, vector, got)
+    )(side, far_off(vector), got)
 
 
 def collected(side, parts):
-    size, width = parts[0][0].shape
+    count = 4
+    _, size, width = parts[0][0].shape
     chunks = len(parts)
-    half = parts[0][4].shape[0] + 1
-    spot = lambda s, o: jnp.where(o[0] == 0, jnp.maximum(s - 1, 0), jnp.minimum(s, half - 2))
-    flat = pl.BlockSpec((size, width), lambda s, o: (0, 0))
-    return pl.pallas_call(
-        functools.partial(collect_kernel, half, chunks),
-        grid_spec=pltpu.PrefetchScalarGridSpec(
-            num_scalar_prefetch=1,
-            grid=(half,),
-            in_specs=[
-                flat,
-                flat,
-                pl.BlockSpec((1, size, width), lambda s, o: (o[0] * (half - 1) + spot(s, o), 0, 0)),
-                flat,
-                pl.BlockSpec((1, size, width), lambda s, o: (spot(s, o), 0, 0)),
-            ]
-            * chunks,
-            out_specs=pl.BlockSpec((1, size, 2 * chunks * width), lambda s, o: (s, 0, 0)),
-        ),
-        out_shape=jax.ShapeDtypeStruct((half, size, 2 * chunks * width), jnp.float32),
+    return pl.pallas_call(
+        functools.partial(collect_kernel, chunks),
+        in_specs=[SCALARS] + [ANY] * (3 * chunks),
+        out_specs=ANY,
+        out_shape=jax.ShapeDtypeStruct((count, size, 2 * chunks * width), jnp.float32),
+        scratch_shapes=[pltpu.SemaphoreType.DMA((chunks, 6))],
         compiler_params=PARAMS,
     )(side, *[value for part in parts for value in part])
+
+
+def finished(side, parts, result):
+    chunks = len(parts)
+    return pl.pallas_call(
+        functools.partial(finish_kernel, chunks),
+        in_specs=[SCALARS] + [ANY] * (chunks + 1),
+        out_specs=ANY,
+        out_shape=jax.ShapeDtypeStruct(result.shape, jnp.float32),
+        input_output_aliases={1 + chunks: 0},
+        scratch_shapes=[pltpu.SemaphoreType.DMA((chunks, 2))],
+        compiler_params=PARAMS,
+    )(side, *parts, result)
 
 
 def flipped(value, axis, bit):
@@ -469,66 +551,73 @@
     send, keep = last_coupling(core_at, pairs[-1], last, lead, send, keep, faces_total)
     half = count // 2
 
-    state, belows, aboves = [], [], []
-
-    def arrange(chunk, received):
-        state.append(arranged(side_at, own, received, chunk))
-        belows.append(shifted(state[chunk][1], "elem", 2))
-        aboves.append(shifted(state[chunk][0], "elem", -2))
-
-
-    other = flipped(send, "pts", 1)
-    quarter = half // 2
-    pick = lambda value, at: lax.dynamic_slice_in_dim(value, at * quarter, quarter)
-    send = pick(keep, 1 - lane) + pick(other, 1 - lane)
-    mine = pick(keep, lane) + pick(other, lane) + flipped(send, "pts", 2)
+    lane_at = lane.reshape(1).astype(jnp.int32)
+    send, stay = folded(lane_at, keep, flipped(send, "pts", 1))
+    mine = added(stay, flipped(send, "pts", 2))
     bit = 4
     while bit < width:
         mine = mine + flipped(mine, "pts", bit)
         bit *= 2
     got[0], mine = lax.optimization_barrier((got[0], mine))
-    arrange(0, got[0])
+    state, halos = [], []
+
+    def arrange(chunk):
+        state.append(arranged(side_at, own, got[chunk], chunk))
+        halos.append(shifted(state[chunk][0], "elem", -2))
+
+    arrange(0)
     beside = flipped(mine, "pts", 2)
     across = flipped(mine, "elem", 1)
-    belows[0], aboves[0], across = lax.optimization_barrier((belows[0], aboves[0], across))
+    mine_near = flipped(mine, "pts", 1)
+    halos[0], across = lax.optimization_barrier((halos[0], across))
     both = flipped(across, "pts", 2)
-    near = flipped(jnp.concatenate([mine, beside, across]), "pts", 1)
+    beside_near = flipped(beside, "pts", 1)
+    across_near = flipped(across, "pts", 1)
+
+    last = jnp.where(lane == core, mine, beside)
+    flat = lambda e, p: e % elems * width + p
+    holds = [(e, p) for e in range(elems) for p in range(width) if e % 2 == p % 2]
+    outer = lax.ppermute(last, ("elem", "pts"), [(flat(e, p), flat(e + (2 if p % 2 else -2), p)) for e, p in holds])
+    outer_side = lax.ppermute(outer, ("elem", "pts"), [(flat(e, p), flat(e ^ 1, p)) for e, p in holds])
+    outer_near = flipped(outer + outer_side, "pts", 1)
+
     if chunks > 1:
         got[1], both = lax.optimization_barrier((got[1], both))
-        arrange(1, got[1])
-    far = flipped(both, "pts", 1)
-
-    last = jnp.where(
-        side == 1, jnp.where(lane == 1, mine[0, :size], beside[0, :size]), jnp.where(lane == 1, across[0, :size], both[0, :size])
-    )
-    flat = lambda e, p: e % elems * width + p
-    odd = [(e, p) for e in range(elems) for p in range(1, width, 2)]
-    before = lax.ppermute(last, ("elem", "pts"), [(flat(e, p), flat(e + 2, p)) for e, p in odd])
-    before = before + lax.ppermute(before, ("elem", "pts"), [(flat(e, p), flat(e, p - 1)) for e, p in odd])
+        arrange(1)
+    both_near = flipped(both, "pts", 1)
 
     me = (side * 4 + core * 2 + lane).reshape(1).astype(jnp.int32)
-    high, low = weights(me, mine, beside, across, both, near, far)
+    high, low = weights(me, mine, mine_near, beside, across, beside_near, across_near, both, both_near)
+    high_outer, low_outer = outer_weights(core_at, outer, outer_side, outer_near, high, low)
 
     old = list(state)
-    parts = []
+    near, far = [], []
     for degree in range(DEG):
-        first = degree == 0
+        first, up = degree == 0, degree % 2 == 0
         for c in range(chunks):
-            head, tail, inner = state[c]
-            new_tail = apply_tail(first, high, low, tail, inner, aboves[c], old[c][1])
-            new_head = apply_head(first, before, high, low, head, inner, belows[c], old[c][0])
-            new_inner = apply_inner(first, high, low, head, tail, inner, old[c][2])
+            edge, inner = state[c]
+            new_inner = apply_inner(first, up, high, low, edge, inner, old[c][1])
+            if degree == DEG - 1:
+                near.append(flipped(jnp.where(side == 0, new_inner[2:4], new_inner[:2]), "elem", 1))
+                near[c], halos[c] = lax.optimization_barrier((near[c], halos[c]))
+            new_edge = apply_edge(first, up, high, low, high_outer, low_outer, inner, halos[c], old[c][0])
             old[c] = state[c]
-            state[c] = new_head, new_tail, new_inner
+            state[c] = new_edge, new_inner
             if degree < DEG - 1:
-                belows[c] = shifted(new_tail, "elem", 2)
-                aboves[c] = shifted(new_head, "elem", -2)
+                halos[c] = shifted(new_edge, "elem", 2 if up else -2)
             else:
-                foreign = lax.dynamic_slice_in_dim(new_inner, (1 - side) * (count - 1), count - 1)
-                got_inner = flipped(foreign, "elem", 1)
-                got_end = flipped(jnp.where(side == 0, new_tail, new_head), "elem", 1)
-                parts.append((new_head, new_tail, new_inner, got_end, got_inner))
-    return collected(side_at, parts).reshape(count * size, columns)
+                far.append(flipped(jnp.where(side == 0, new_inner[4:], new_edge), "elem", 1))
+    if part % 128:
+        (edge, inner), near, far = state[0], near[0], far[0]
+        lower = jnp.concatenate([edge, inner[:2]])
+        mine = jnp.where(side == 0, lower, inner[2:])
+        theirs = jnp.where(side == 0, jnp.concatenate([far, near]), jnp.concatenate([near, far]))
+        swap = lambda first, second: jnp.concatenate([first, second], axis=2)
+        result = jnp.where(side == 0, swap(mine, theirs), swap(theirs, mine))
+    else:
+        result = collected(side_at, [(*state[c], near[c]) for c in range(chunks)])
+        result = finished(side_at, far, result)
+    return result.reshape(count * size, columns)
 
 
 def solution(mesh):

time: 170 us -> 152 us (0.89)
  starting transfers between devices: 43.8 us -> 30.8 us
  waiting for transfers between devices: 37.8 us -> 49.4 us
  Pallas kernels: 60.8 us -> 51.2 us
  other arithmetic: 4.71 us -> 1.08 us
  local copies, waits for them, and re-layouts: 21.3 us -> 18.3 us
    ppermute x17 -> x9, starting transfers between devices: 31 us -> 11.6 us  [shifted(): lax.ppermute(value, axis, [(i, (i + steps) % count) for i in range(count)])]
    ppermute x17 -> x9, waiting for transfers between devices: 1.37 us -> 15.4 us  [shifted(): lax.ppermute(value, axis, [(i, (i + steps) % count) for i in range(count)])]
    pallas_call x26 -> x22, Pallas kernels: 47.9 us -> 38.4 us  [the longest x8 21.2 us: apply_inner(): pl.pallas_call(functools.partial(inner_kernel, first, up), in_specs=[VMEM...]
    ppermute x2, starting transfers between devices: 1.96 us -> 5.97 us  [the longest x1 3.62 us: body(): lax.ppermute(outer, ('elem', 'pts'), [(flat(e, p), flat(e ^ 1, p)) for e,...]
    ppermute x13 -> x16, waiting for transfers between devices: 35.2 us -> 32.1 us  [flipped(): return lax.ppermute(value, axis, [(i, i ^ bit) for i in range(count)])]
    unnamed x90 -> x86, local copies, waits for them, and re-layouts: 20.2 us -> 17.2 us
    ppermute x13 -> x16, starting transfers between devices: 10.9 us -> 13.2 us  [flipped(): return lax.ppermute(value, axis, [(i, i ^ bit) for i in range(count)])]
  transfers between devices with their start and end apart: 32 -> 27, of which waited for: 9 -> 12; matrix products, arithmetic and copies ran while one was open for 2% -> 1% of each run, Pallas kernels for 33% -> 31%
where the time goes in v4:
time: 152 us; the launch traced here: 151 us
  Pallas kernels  51.2 us (34%)
  waiting for transfers between devices  49.4 us (32%)
  starting transfers between devices  30.8 us (20%)
  local copies, waits for them, and re-layouts  18.3 us (12%)
    ppermute x16, waiting for transfers between devices, flipped(): return lax.ppermute(value, axis, [(i, i ^ bit) for i in range(count)])  32.1 us
    pallas_call x8, Pallas kernels, apply_inner(): pl.pallas_call(functools.partial(inner_kernel, first, up), in_specs=[VMEM...  21.2 us
    unnamed x86, local copies, waits for them, and re-layouts  17.2 us
    ppermute x9, waiting for transfers between devices, shifted(): lax.ppermute(value, axis, [(i, (i + steps) % count) for i in range(count)])  15.4 us
    ppermute x16, starting transfers between devices, flipped(): return lax.ppermute(value, axis, [(i, i ^ bit) for i in range(count)])  13.2 us
    ppermute x9, starting transfers between devices, shifted(): lax.ppermute(value, axis, [(i, (i + steps) % count) for i in range(count)])  11.6 us
    pallas_call x8, Pallas kernels, apply_edge(): pl.pallas_call(functools.partial(edge_kernel, first, up), in_specs=[VMEM]...  10.3 us
    pallas_call x1, Pallas kernels, blocks(): pl.pallas_call(functools.partial(blocks_kernel, faces_total), in_specs=[S...  6.76 us
  transfers between devices with their start and end apart: 27, of which 12 were waited for; matrix products, arithmetic and copies ran while one was open for 1% of the time, Pallas kernels for 31%

profile of v4, /device:TPU:0, one launch (start us, length us, event | category | flops | bytes accessed | tf_op | source)
XLA Modules:
  0.0 151.4 jit_solution(10749802317128932987)
XLA Ops:
  0.8 2.3 %shard_map.64 = (f32[256,128]{1,0:T(8,128)S(1)}, f32[4,256,128]{2,1,0:T(8,128)}, f32[4,256,128]{2,1,0:T(8,128)S(1)}) custom-call(s32[1]{0:T(128)S(6)} %sub.8.side_ref, s32[1,1,128]{2,1,0:T(1,128)S(1)} %reshape.34.index_ref, f32[4,512,256]{2,1,0:T(8,128)} %basis_ref.3, f32[4,256,512]{2,1,0:T(8,128)} %bitcast.10), custom_call_target="tpu_custom_call" | custom-call | tf_op jit(solution)/shard_map/pallas_call | solution.py:366
  3.9 6.0 %collective-permute-start.1 = (f32[256,128]{1,0:T(8,128)S(1)}, f32[256,128]{1,0:T(8,128)S(1)}, u32[]{:S(2)}, u32[]{:S(2)}) collective-permute-start(f32[256,128]{1,0:T(8,128)S(1)} %get-tuple-element.35), channel_id=1, source_target_pairs={{0,28},{4,0},{8,4},{12,8},{16,12},{20,16},{24,20},{28,24},{1,29},{... | collective-permute-start | bytes 393224 | tf_op jit(solution)/shard_map/ppermute | solution.py:520
  10.2 6.8 %shard_map.65 = (f32[2,392,256]{2,1,0:T(8,128)S(1)}, f32[2,392,256]{2,1,0:T(8,128)S(1)}, f32[256,256]{1,0:T(8,128)S(1)}) custom-call(s32[1]{0:T(128)} %bitcast.4.core_ref, s32[4,1,256]{2,1,0:T(1,128)S(1)} %reshape.38.index_ref, f32[4,1,512]{2,1,0:T(1,128)S(1)} %reshape.39.quad_ref, s32[4,1,128]{2,1,0:T(1,128)S(1)} %bitcast.9, f32[4,512,256]{2,1,0:T(8,128)} %basis_ref.3, ...), custom_call_target="tpu_custom_call" | custom-call | tf_op jit(solution)/shard_map/pallas_call | solution.py:381
  17.8 2.2 %collective-permute-done.2.other_ref = f32[2,392,256]{2,1,0:T(8,128)S(1)} collective-permute-done((f32[2,392,256]{2,1,0:T(8,128)S(1)}, f32[2,392,256]{2,1,0:T(8,128)S(1)}, u32[]{:S(2)}, u32[]{:S(2)}) %collective-permute-start.2) | collective-permute-done | bytes 802848 | tf_op jit(solution)/shard_map/ppermute | solution.py:515
  20.1 1.6 %collective-permute-start.3 = (f32[1,392,256]{2,1,0:T(8,128)S(1)}, f32[1,392,256]{2,1,0:T(8,128)S(1)}, u32[]{:S(2)}, u32[]{:S(2)}) collective-permute-start(f32[1,392,256]{2,1,0:T(8,128)S(1)} %get-tuple-element.41), channel_id=1, source_target_pairs={{0,2},{1,3},{2,0},{3,1},{4,6},{5,7},{6,4},{7,5},{8,10},{9,11},{10,... | collective-permute-start | bytes 1204232 | tf_op jit(solution)/shard_map/ppermute | solution.py:515
  21.7 9.8 %collective-permute-done.3.second_ref = f32[1,392,256]{2,1,0:T(8,128)S(1)} collective-permute-done((f32[1,392,256]{2,1,0:T(8,128)S(1)}, f32[1,392,256]{2,1,0:T(8,128)S(1)}, u32[]{:S(2)}, u32[]{:S(2)}) %collective-permute-start.3) | collective-permute-done | bytes 401440 | tf_op jit(solution)/shard_map/ppermute | solution.py:515
  34.0 9.1 %collective-permute-done.5.refs_2_ = f32[1,392,256]{2,1,0:T(8,128)S(1)} collective-permute-done((f32[1,392,256]{2,1,0:T(8,128)S(1)}, f32[1,392,256]{2,1,0:T(8,128)S(1)}, u32[]{:S(2)}, u32[]{:S(2)}) %collective-permute-start.5) | collective-permute-done | bytes 401440 | tf_op jit(solution)/shard_map/ppermute | solution.py:515
  43.2 2.4 %collective-permute-start.13 = (f32[1,392,256]{2,1,0:T(8,128)S(1)}, f32[1,392,256]{2,1,0:T(8,128)S(1)}, u32[]{:S(2)}, u32[]{:S(2)}) collective-permute-start(f32[1,392,256]{2,1,0:T(8,128)S(1)} %broadcast_select_fusion), channel_id=1, source_target_pairs={{0,24},{2,26},{5,13},{7,15},{8,0},{10,2},{13,21},{15,23},{16,8},{1... | collective-permute-start | bytes 1204232 | tf_op jit(solution)/shard_map/ppermute | solution.py:580
  48.1 9.2 %collective-permute-done.6.halo = f32[2,256,128]{2,1,0:T(8,128)S(1)} collective-permute-done((f32[2,256,128]{2,1,0:T(8,128)S(1)}, f32[2,256,128]{2,1,0:T(8,128)S(1)}, u32[]{:S(2)}, u32[]{:S(2)}) %collective-permute-start.6) | collective-permute-done | bytes 262176 | tf_op jit(solution)/shard_map/ppermute | solution.py:520
  59.5 3.6 %collective-permute-start.14 = (f32[1,392,256]{2,1,0:T(8,128)S(1)}, f32[1,392,256]{2,1,0:T(8,128)S(1)}, u32[]{:S(2)}, u32[]{:S(2)}) collective-permute-start(f32[1,392,256]{2,1,0:T(8,128)S(1)} %collective-permute-done.13.first_ref), channel_id=1, source_target_pairs={{0,4},{2,6},{5,1},{7,3},{8,12},{10,14},{13,9},{15,11},{16,20},{18,... | collective-permute-start | bytes 1204232 | tf_op jit(solution)/shard_map/ppermute | solution.py:581
  66.6 1.8 %collective-permute-done.14.second_ref = f32[1,392,256]{2,1,0:T(8,128)S(1)} collective-permute-done((f32[1,392,256]{2,1,0:T(8,128)S(1)}, f32[1,392,256]{2,1,0:T(8,128)S(1)}, u32[]{:S(2)}, u32[]{:S(2)}) %collective-permute-start.14) | collective-permute-done | bytes 401440 | tf_op jit(solution)/shard_map/ppermute | solution.py:581
  69.4 1.9 %shard_map.80 = (f32[2,256,128]{2,1,0:T(8,128)}, f32[6,256,128]{2,1,0:T(8,128)S(1)}) custom-call(s32[1]{0:T(128)} %bitcast.side_ref, f32[4,256,512]{2,1,0:T(8,128)} %bitcast.12, f32[4,256,128]{2,1,0:T(8,128)S(1)} %collective-permute-done.10.got_ref), custom_call_target="tpu_custom_call" | custom-call | tf_op jit(solution)/shard_map/pallas_call | solution.py:476
  79.7 3.0 %shard_map.70 = (bf16[8,256,768]{2,1,0:T(8,128)(2,1)S(1)}, bf16[8,256,768]{2,1,0:T(8,128)(2,1)S(1)}) custom-call(s32[1]{0:T(128)} %bitcast.1.me_ref, f32[1,392,256]{2,1,0:T(8,128)S(1)} %shard_map.68.refs_0_, f32[1,392,256]{2,1,0:T(8,128)S(1)} %copy-done.34, f32[1,392,256]{2,1,0:T(8,128)S(1)} %copy-done.24, f32[1,392,256]{2,1,0:T(8,128)S(1)} %copy-done.30, ...), custom_call_target="tpu_custom_call" | custom-call | tf_op jit(solution)/shard_map/pallas_call | solution.py:411
  82.8 1.8 %shard_map.71 = (bf16[2,256,768]{2,1,0:T(8,128)(2,1)S(1)}, bf16[2,256,768]{2,1,0:T(8,128)(2,1)S(1)}) custom-call(s32[1]{0:T(128)} %bitcast.4.core_ref, f32[1,392,256]{2,1,0:T(8,128)S(1)} %copy-done.26, f32[1,392,256]{2,1,0:T(8,128)S(1)} %copy-done.28, f32[1,392,256]{2,1,0:T(8,128)} %collective-permute-done.15.swapped_ref, ...), custom_call_target="tpu_custom_call" | custom-call | tf_op jit(solution)/shard_map/pallas_call | solution.py:423
  87.0 1.6 %shard_map.81.edge.old = f32[2,256,128]{2,1,0:T(8,128)S(1)} custom-call(bf16[8,256,768]{2,1,0:T(8,128)(2,1)S(1)} %get-tuple-element.48.high_in.high, bf16[8,256,768]{2,1,0:T(8,128)(2,1)S(1)} %get-tuple-element.49.low_in.low, bf16[2,256,768]{2,1,0:T(8,128)(2,1)S(1)} %get-tuple-element.50.high_outer, bf16[2,256,768]{2,1,0:T(8,128)(2,1)S(1)} %get-tuple-element.51.low_outer, ...), custom_call_target="tpu_custom_call" | custom-call | tf_op jit(solution)/shard_map/pallas_call | solution.py:434
  89.2 2.4 %shard_map.73.inner.old = f32[6,256,128]{2,1,0:T(8,128)S(1)} custom-call(bf16[8,256,768]{2,1,0:T(8,128)(2,1)S(1)} %get-tuple-element.48.high_in.high, bf16[8,256,768]{2,1,0:T(8,128)(2,1)S(1)} %get-tuple-element.49.low_in.low, f32[2,256,128]{2,1,0:T(8,128)S(1)} %copy-done.18, f32[6,256,128]{2,1,0:T(8,128)S(1)} %copy-done.7, f32[6,256,128]{2,1,0:T(8,128)S(1)} %copy-done.7), custom_call_target="tpu_custom_call" | custom-call | tf_op jit(solution)/shard_map/pallas_call | solution.py:446
  91.6 5.3 %collective-permute-done.16.halo = f32[2,256,128]{2,1,0:T(8,128)S(1)} collective-permute-done((f32[2,256,128]{2,1,0:T(8,128)S(1)}, f32[2,256,128]{2,1,0:T(8,128)S(1)}, u32[]{:S(2)}, u32[]{:S(2)}) %collective-permute-start.16) | collective-permute-done | bytes 262176 | tf_op jit(solution)/shard_map/ppermute | solution.py:520
  98.2 3.3 %shard_map.82.inner.old = f32[6,256,128]{2,1,0:T(8,128)S(1)} custom-call(bf16[8,256,768]{2,1,0:T(8,128)(2,1)S(1)} %get-tuple-element.48.high_in.high, bf16[8,256,768]{2,1,0:T(8,128)(2,1)S(1)} %get-tuple-element.49.low_in.low, f32[2,256,128]{2,1,0:T(8,128)} %get-tuple-element.57.old.edge, f32[6,256,128]{2,1,0:T(8,128)S(1)} %copy-done.10, ...), custom_call_target="tpu_custom_call" | custom-call | tf_op jit(solution)/shard_map/pallas_call | solution.py:446
  102.5 1.5 %shard_map.84.edge.old = f32[2,256,128]{2,1,0:T(8,128)S(1)} custom-call(bf16[8,256,768]{2,1,0:T(8,128)(2,1)S(1)} %get-tuple-element.48.high_in.high, bf16[8,256,768]{2,1,0:T(8,128)(2,1)S(1)} %get-tuple-element.49.low_in.low, bf16[2,256,768]{2,1,0:T(8,128)(2,1)S(1)} %get-tuple-element.50.high_outer, bf16[2,256,768]{2,1,0:T(8,128)(2,1)S(1)} %get-tuple-element.51.low_outer, ...), custom_call_target="tpu_custom_call" | custom-call | tf_op jit(solution)/shard_map/pallas_call | solution.py:434
  104.4 1.9 %copy-done.1 = bf16[8,256,768]{2,1,0:T(8,128)(2,1)S(1)} copy-done((bf16[8,256,768]{2,1,0:T(8,128)(2,1)S(1)}, bf16[8,256,768]{2,1,0:T(8,128)(2,1)}, u32[]{:S(2)}) %copy-start.1) | copy-done | bytes 3145752
  109.5 2.4 %shard_map.74.inner.old = f32[6,256,128]{2,1,0:T(8,128)S(1)} custom-call(bf16[8,256,768]{2,1,0:T(8,128)(2,1)S(1)} %get-tuple-element.48.high_in.high, bf16[8,256,768]{2,1,0:T(8,128)(2,1)S(1)} %copy-done.1, f32[2,256,128]{2,1,0:T(8,128)S(1)} %copy-done.22, f32[6,256,128]{2,1,0:T(8,128)S(1)} %copy-done.15, f32[6,256,128]{2,1,0:T(8,128)S(1)} %copy-done.8), custom_call_target="tpu_custom_call" | custom-call | tf_op jit(solution)/shard_map/pallas_call | solution.py:446
  111.9 3.5 %shard_map.77.inner = f32[6,256,128]{2,1,0:T(8,128)S(1)} custom-call(bf16[8,256,768]{2,1,0:T(8,128)(2,1)S(1)} %get-tuple-element.48.high_in.high, bf16[8,256,768]{2,1,0:T(8,128)(2,1)S(1)} %copy-done.1, f32[2,256,128]{2,1,0:T(8,128)} %shard_map.75.edge.old, f32[6,256,128]{2,1,0:T(8,128)S(1)} %shard_map.74.inner.old, f32[6,256,128]{2,1,0:T(8,128)S(1)} %copy-done.16), custom_call_target="tpu_custom_call" | custom-call | tf_op jit(solution)/shard_map/pallas_call | solution.py:446
  117.0 2.4 %shard_map.78.refs_1_ = f32[6,256,128]{2,1,0:T(8,128)S(1)} custom-call(bf16[8,256,768]{2,1,0:T(8,128)(2,1)S(1)} %get-tuple-element.48.high_in.high, bf16[8,256,768]{2,1,0:T(8,128)(2,1)S(1)} %copy-done.1, f32[2,256,128]{2,1,0:T(8,128)S(1)} %shard_map.76.edge, f32[6,256,128]{2,1,0:T(8,128)S(1)} %shard_map.77.inner, f32[6,256,128]{2,1,0:T(8,128)S(1)} %shard_map.74.inner.old), custom_call_target="tpu_custom_call" | custom-call | tf_op jit(solution)/shard_map/pallas_call | solution.py:446
  119.4 4.2 %collective-permute-start.18 = (f32[2,256,128]{2,1,0:T(8,128)S(1)}, f32[2,256,128]{2,1,0:T(8,128)S(1)}, u32[]{:S(2)}, u32[]{:S(2)}) collective-permute-start(f32[2,256,128]{2,1,0:T(8,128)S(1)} %slice_select_fusion.2), channel_id=1, source_target_pairs={{0,4},{4,0},{8,12},{12,8},{16,20},{20,16},{24,28},{28,24},{1,5},{5... | collective-permute-start | bytes 786440 | tf_op jit(solution)/shard_map/ppermute | solution.py:515
  124.7 2.4 %shard_map.83.inner.old = f32[6,256,128]{2,1,0:T(8,128)S(1)} custom-call(bf16[8,256,768]{2,1,0:T(8,128)(2,1)S(1)} %get-tuple-element.48.high_in.high, bf16[8,256,768]{2,1,0:T(8,128)(2,1)S(1)} %copy-done.1, f32[2,256,128]{2,1,0:T(8,128)S(1)} %copy-done.20, f32[6,256,128]{2,1,0:T(8,128)S(1)} %copy-done.13, f32[6,256,128]{2,1,0:T(8,128)S(1)} %copy-done.11), custom_call_target="tpu_custom_call" | custom-call | tf_op jit(solution)/shard_map/pallas_call | solution.py:446
  127.1 2.4 %shard_map.86.inner = f32[6,256,128]{2,1,0:T(8,128)S(1)} custom-call(bf16[8,256,768]{2,1,0:T(8,128)(2,1)S(1)} %get-tuple-element.48.high_in.high, bf16[8,256,768]{2,1,0:T(8,128)(2,1)S(1)} %copy-done.1, f32[2,256,128]{2,1,0:T(8,128)S(1)} %shard_map.84.edge.old, f32[6,256,128]{2,1,0:T(8,128)S(1)} %shard_map.83.inner.old, f32[6,256,128]{2,1,0:T(8,128)S(1)} %copy-done.13), custom_call_target="tpu_custom_call" | custom-call | tf_op jit(solution)/shard_map/pallas_call | solution.py:446
  131.0 2.4 %shard_map.87.refs_4_ = f32[6,256,128]{2,1,0:T(8,128)S(1)} custom-call(bf16[8,256,768]{2,1,0:T(8,128)(2,1)S(1)} %get-tuple-element.48.high_in.high, bf16[8,256,768]{2,1,0:T(8,128)(2,1)S(1)} %copy-done.1, f32[2,256,128]{2,1,0:T(8,128)S(1)} %shard_map.85.edge, f32[6,256,128]{2,1,0:T(8,128)S(1)} %shard_map.86.inner, f32[6,256,128]{2,1,0:T(8,128)S(1)} %shard_map.83.inner.old), custom_call_target="tpu_custom_call" | custom-call | tf_op jit(solution)/shard_map/pallas_call | solution.py:446
  134.9 1.5 %shard_map.79.refs_0_ = f32[2,256,128]{2,1,0:T(8,128)S(1)} custom-call(bf16[8,256,768]{2,1,0:T(8,128)(2,1)S(1)} %get-tuple-element.48.high_in.high, bf16[8,256,768]{2,1,0:T(8,128)(2,1)S(1)} %copy-done.1, bf16[2,256,768]{2,1,0:T(8,128)(2,1)S(1)} %copy-done.3, bf16[2,256,768]{2,1,0:T(8,128)(2,1)S(1)} %copy-done.5, f32[6,256,128]{2,1,0:T(8,128)S(1)} %shard_map.77.inner, ...), custom_call_target="tpu_custom_call" | custom-call | tf_op jit(solution)/shard_map/pallas_call | solution.py:434
  136.5 2.0 %collective-permute-start.20 = (f32[2,256,128]{2,1,0:T(8,128)S(1)}, f32[2,256,128]{2,1,0:T(8,128)S(1)}, u32[]{:S(2)}, u32[]{:S(2)}) collective-permute-start(f32[2,256,128]{2,1,0:T(8,128)S(1)} %slice_select_fusion.3), channel_id=1, source_target_pairs={{0,4},{4,0},{8,12},{12,8},{16,20},{20,16},{24,28},{28,24},{1,5},{5... | collective-permute-start | bytes 786440 | tf_op jit(solution)/shard_map/ppermute | solution.py:515
  138.5 4.1 %collective-permute-done.24.refs_5_ = f32[2,256,128]{2,1,0:T(8,128)S(1)} collective-permute-done((f32[2,256,128]{2,1,0:T(8,128)S(1)}, f32[2,256,128]{2,1,0:T(8,128)S(1)}, u32[]{:S(2)}, u32[]{:S(2)}) %collective-permute-start.24) | collective-permute-done | bytes 262176 | tf_op jit(solution)/shard_map/ppermute | solution.py:515
  145.7 2.0 %collective-permute-done.20.refs_0_ = f32[2,256,128]{2,1,0:T(8,128)S(1)} collective-permute-done((f32[2,256,128]{2,1,0:T(8,128)S(1)}, f32[2,256,128]{2,1,0:T(8,128)S(1)}, u32[]{:S(2)}, u32[]{:S(2)}) %collective-permute-start.20) | collective-permute-done | bytes 262176 | tf_op jit(solution)/shard_map/ppermute | solution.py:515
  147.7 2.8 %collective-permute-done.26.refs_1_ = f32[2,256,128]{2,1,0:T(8,128)S(1)} collective-permute-done((f32[2,256,128]{2,1,0:T(8,128)S(1)}, f32[2,256,128]{2,1,0:T(8,128)S(1)}, u32[]{:S(2)}, u32[]{:S(2)}) %collective-permute-start.26) | collective-permute-done | bytes 262176 | tf_op jit(solution)/shard_map/ppermute | solution.py:515
  (149 shorter events, 41.1 us)
Async XLA Ops:
  3.9 13.1 %collective-permute-start.1 = (f32[256,128]{1,0:T(8,128)S(1)}, f32[256,128]{1,0:T(8,128)S(1)}, u32[]{:S(2)}, u32[]{:S(2)}) collective-permute-start(f32[256,128]{1,0:T(8,128)S(1)} %get-tuple-element.35), channel_id=1, source_target_pairs={{0,28},{4,0},{8,4},{12,8},{16,12},{20,16},{24,20},{28,24},{1,29},{... | collective-permute-start | bytes 393224 | tf_op jit(solution)/shard_map/ppermute | solution.py:520
  17.6 2.4 %collective-permute-start.2 = (f32[2,392,256]{2,1,0:T(8,128)S(1)}, f32[2,392,256]{2,1,0:T(8,128)S(1)}, u32[]{:S(2)}, u32[]{:S(2)}) collective-permute-start(f32[2,392,256]{2,1,0:T(8,128)S(1)} %get-tuple-element.39), channel_id=1, source_target_pairs={{0,1},{1,0},{2,3},{3,2},{4,5},{5,4},{6,7},{7,6},{8,9},{9,8},{10,11... | collective-permute-start | bytes 2408456 | tf_op jit(solution)/shard_map/ppermute | solution.py:515
  17.7 14.6 %collective-permute-start = (f32[4,256,128]{2,1,0:T(8,128)}, f32[4,256,128]{2,1,0:T(8,128)S(1)}, u32[]{:S(2)}, u32[]{:S(2)}) collective-permute-start(f32[4,256,128]{2,1,0:T(8,128)} %get-tuple-element.33), channel_id=1, source_target_pairs={{0,4},{4,0},{8,12},{12,8},{16,20},{20,16},{24,28},{28,24},{1,5},{5... | collective-permute-start | bytes 1572872 | tf_op jit(solution)/shard_map/ppermute | solution.py:515
  20.1 11.4 %collective-permute-start.3 = (f32[1,392,256]{2,1,0:T(8,128)S(1)}, f32[1,392,256]{2,1,0:T(8,128)S(1)}, u32[]{:S(2)}, u32[]{:S(2)}) collective-permute-start(f32[1,392,256]{2,1,0:T(8,128)S(1)} %get-tuple-element.41), channel_id=1, source_target_pairs={{0,2},{1,3},{2,0},{3,1},{4,6},{5,7},{6,4},{7,5},{8,10},{9,11},{10,... | collective-permute-start | bytes 1204232 | tf_op jit(solution)/shard_map/ppermute | solution.py:515
  32.3 10.9 %collective-permute-start.5 = (f32[1,392,256]{2,1,0:T(8,128)S(1)}, f32[1,392,256]{2,1,0:T(8,128)S(1)}, u32[]{:S(2)}, u32[]{:S(2)}) collective-permute-start(f32[1,392,256]{2,1,0:T(8,128)S(1)} %shard_map.68.refs_0_), channel_id=1, source_target_pairs={{0,2},{1,3},{2,0},{3,1},{4,6},{5,7},{6,4},{7,5},{8,10},{9,11},{10,... | collective-permute-start | bytes 1204232 | tf_op jit(solution)/shard_map/ppermute | solution.py:515
  33.8 24.2 %collective-permute-start.7 = (f32[1,392,256]{2,1,0:T(8,128)S(1)}, f32[1,392,256]{2,1,0:T(8,128)S(1)}, u32[]{:S(2)}, u32[]{:S(2)}) collective-permute-start(f32[1,392,256]{2,1,0:T(8,128)S(1)} %shard_map.68.refs_0_), channel_id=1, source_target_pairs={{0,4},{4,0},{8,12},{12,8},{16,20},{20,16},{24,28},{28,24},{1,5},{5... | collective-permute-start | bytes 1204232 | tf_op jit(solution)/shard_map/ppermute | solution.py:515
  43.1 26.2 %copy-start.23 = (f32[1,392,256]{2,1,0:T(8,128)}, f32[1,392,256]{2,1,0:T(8,128)S(1)}, u32[]{:S(2)}) copy-start(f32[1,392,256]{2,1,0:T(8,128)S(1)} %collective-permute-done.5.refs_2_) | copy-start | bytes 1204228
  43.2 16.3 %collective-permute-start.13 = (f32[1,392,256]{2,1,0:T(8,128)S(1)}, f32[1,392,256]{2,1,0:T(8,128)S(1)}, u32[]{:S(2)}, u32[]{:S(2)}) collective-permute-start(f32[1,392,256]{2,1,0:T(8,128)S(1)} %broadcast_select_fusion), channel_id=1, source_target_pairs={{0,24},{2,26},{5,13},{7,15},{8,0},{10,2},{13,21},{15,23},{16,8},{1... | collective-permute-start | bytes 1204232 | tf_op jit(solution)/shard_map/ppermute | solution.py:580
  47.6 21.7 %copy-start.17 = (f32[2,256,128]{2,1,0:T(8,128)}, f32[2,256,128]{2,1,0:T(8,128)S(1)}, u32[]{:S(2)}) copy-start(f32[2,256,128]{2,1,0:T(8,128)S(1)} %get-tuple-element.44.old.edge) | copy-start | bytes 786436
  47.6 9.6 %collective-permute-start.6 = (f32[2,256,128]{2,1,0:T(8,128)S(1)}, f32[2,256,128]{2,1,0:T(8,128)S(1)}, u32[]{:S(2)}, u32[]{:S(2)}) collective-permute-start(f32[2,256,128]{2,1,0:T(8,128)S(1)} %get-tuple-element.44.old.edge), channel_id=1, source_target_pairs={{0,24},{4,28},{8,0},{12,4},{16,8},{20,12},{24,16},{28,20},{1,25},{... | collective-permute-start | bytes 786440 | tf_op jit(solution)/shard_map/ppermute | solution.py:520
  48.1 16.3 %collective-permute-start.10 = (f32[4,256,128]{2,1,0:T(8,128)}, f32[4,256,128]{2,1,0:T(8,128)S(1)}, u32[]{:S(2)}, u32[]{:S(2)}) collective-permute-start(f32[4,256,128]{2,1,0:T(8,128)} %copy-done.39), channel_id=1, source_target_pairs={{0,4},{4,0},{8,12},{12,8},{16,20},{20,16},{24,28},{28,24},{1,5},{5... | collective-permute-start | bytes 1572872 | tf_op jit(solution)/shard_map/ppermute | solution.py:515
  58.0 7.9 %collective-permute-start.11 = (f32[1,392,256]{2,1,0:T(8,128)S(1)}, f32[1,392,256]{2,1,0:T(8,128)S(1)}, u32[]{:S(2)}, u32[]{:S(2)}) collective-permute-start(f32[1,392,256]{2,1,0:T(8,128)S(1)} %collective-permute-done.7.refs_3_), channel_id=1, source_target_pairs={{0,2},{1,3},{2,0},{3,1},{4,6},{5,7},{6,4},{7,5},{8,10},{9,11},{10,... | collective-permute-start | bytes 1204232 | tf_op jit(solution)/shard_map/ppermute | solution.py:515
  59.5 9.0 %collective-permute-start.14 = (f32[1,392,256]{2,1,0:T(8,128)S(1)}, f32[1,392,256]{2,1,0:T(8,128)S(1)}, u32[]{:S(2)}, u32[]{:S(2)}) collective-permute-start(f32[1,392,256]{2,1,0:T(8,128)S(1)} %collective-permute-done.13.first_ref), channel_id=1, source_target_pairs={{0,4},{2,6},{5,1},{7,3},{8,12},{10,14},{13,9},{15,11},{16,20},{18,... | collective-permute-start | bytes 1204232 | tf_op jit(solution)/shard_map/ppermute | solution.py:581
  63.1 9.1 %collective-permute-start.4 = (f32[1,392,256]{2,1,0:T(8,128)S(1)}, f32[1,392,256]{2,1,0:T(8,128)S(1)}, u32[]{:S(2)}, u32[]{:S(2)}) collective-permute-start(f32[1,392,256]{2,1,0:T(8,128)S(1)} %shard_map.68.refs_0_), channel_id=1, source_target_pairs={{0,1},{1,0},{2,3},{3,2},{4,5},{5,4},{6,7},{7,6},{8,9},{9,8},{10,11... | collective-permute-start | bytes 1204232 | tf_op jit(solution)/shard_map/ppermute | solution.py:515
  63.2 10.7 %collective-permute-start.9 = (f32[1,392,256]{2,1,0:T(8,128)S(1)}, f32[1,392,256]{2,1,0:T(8,128)S(1)}, u32[]{:S(2)}, u32[]{:S(2)}) collective-permute-start(f32[1,392,256]{2,1,0:T(8,128)S(1)} %collective-permute-done.7.refs_3_), channel_id=1, source_target_pairs={{0,1},{1,0},{2,3},{3,2},{4,5},{5,4},{6,7},{7,6},{8,9},{9,8},{10,11... | collective-permute-start | bytes 1204232 | tf_op jit(solution)/shard_map/ppermute | solution.py:515
  64.4 9.5 %collective-permute-start.8 = (f32[1,392,256]{2,1,0:T(8,128)S(1)}, f32[1,392,256]{2,1,0:T(8,128)}, u32[]{:S(2)}, u32[]{:S(2)}) collective-permute-start(f32[1,392,256]{2,1,0:T(8,128)S(1)} %collective-permute-done.5.refs_2_), channel_id=1, source_target_pairs={{0,1},{1,0},{2,3},{3,2},{4,5},{5,4},{6,7},{7,6},{8,9},{9,8},{10,11... | collective-permute-start | bytes 1204232 | tf_op jit(solution)/shard_map/ppermute | solution.py:515
  65.8 8.8 %collective-permute-start.12 = (f32[1,392,256]{2,1,0:T(8,128)S(1)}, f32[1,392,256]{2,1,0:T(8,128)}, u32[]{:S(2)}, u32[]{:S(2)}) collective-permute-start(f32[1,392,256]{2,1,0:T(8,128)S(1)} %collective-permute-done.11.refs_6_), channel_id=1, source_target_pairs={{0,1},{1,0},{2,3},{3,2},{4,5},{5,4},{6,7},{7,6},{8,9},{9,8},{10,11... | collective-permute-start | bytes 1204232 | tf_op jit(solution)/shard_map/ppermute | solution.py:515
  69.3 13.4 %collective-permute-start.15 = (f32[1,392,256]{2,1,0:T(8,128)}, f32[1,392,256]{2,1,0:T(8,128)}, u32[]{:S(2)}, u32[]{:S(2)}) collective-permute-start(f32[1,392,256]{2,1,0:T(8,128)} %add.27), channel_id=1, source_target_pairs={{0,1},{1,0},{2,3},{3,2},{4,5},{5,4},{6,7},{7,6},{8,9},{9,8},{10,11... | collective-permute-start | bytes 1204232 | tf_op jit(solution)/shard_map/ppermute | solution.py:515
  73.0 14.0 %collective-permute-start.21 = (f32[2,256,128]{2,1,0:T(8,128)}, f32[2,256,128]{2,1,0:T(8,128)}, u32[]{:S(2)}, u32[]{:S(2)}) collective-permute-start(f32[2,256,128]{2,1,0:T(8,128)} %get-tuple-element.57.old.edge), channel_id=1, source_target_pairs={{0,24},{4,28},{8,0},{12,4},{16,8},{20,12},{24,16},{28,20},{1,25},{... | collective-permute-start | bytes 786440 | tf_op jit(solution)/shard_map/ppermute | solution.py:520
  82.7 19.8 %copy-start = (bf16[8,256,768]{2,1,0:T(8,128)(2,1)}, bf16[8,256,768]{2,1,0:T(8,128)(2,1)S(1)}, u32[]{:S(2)}) copy-start(bf16[8,256,768]{2,1,0:T(8,128)(2,1)S(1)} %get-tuple-element.49.low_in.low) | copy-start | bytes 9437188
  84.5 18.0 %copy-start.2 = (bf16[2,256,768]{2,1,0:T(8,128)(2,1)}, bf16[2,256,768]{2,1,0:T(8,128)(2,1)S(1)}, u32[]{:S(2)}) copy-start(bf16[2,256,768]{2,1,0:T(8,128)(2,1)S(1)} %get-tuple-element.50.high_outer) | copy-start | bytes 2359300
  84.5 18.0 %copy-start.4 = (bf16[2,256,768]{2,1,0:T(8,128)(2,1)}, bf16[2,256,768]{2,1,0:T(8,128)(2,1)S(1)}, u32[]{:S(2)}) copy-start(bf16[2,256,768]{2,1,0:T(8,128)(2,1)S(1)} %get-tuple-element.51.low_outer) | copy-start | bytes 2359300
  85.8 11.1 %collective-permute-start.16 = (f32[2,256,128]{2,1,0:T(8,128)S(1)}, f32[2,256,128]{2,1,0:T(8,128)S(1)}, u32[]{:S(2)}, u32[]{:S(2)}) collective-permute-start(f32[2,256,128]{2,1,0:T(8,128)S(1)} %shard_map.72.edge.old), channel_id=1, source_target_pairs={{0,8},{4,12},{8,16},{12,20},{16,24},{20,28},{24,0},{28,4},{1,9},{5... | collective-permute-start | bytes 786440 | tf_op jit(solution)/shard_map/ppermute | solution.py:520
  88.7 13.9 %collective-permute-start.22 = (f32[2,256,128]{2,1,0:T(8,128)S(1)}, f32[2,256,128]{2,1,0:T(8,128)S(1)}, u32[]{:S(2)}, u32[]{:S(2)}) collective-permute-start(f32[2,256,128]{2,1,0:T(8,128)S(1)} %shard_map.81.edge.old), channel_id=1, source_target_pairs={{0,8},{4,12},{8,16},{12,20},{16,24},{20,28},{24,0},{28,4},{1,9},{5... | collective-permute-start | bytes 786440 | tf_op jit(solution)/shard_map/ppermute | solution.py:520
  98.2 17.1 %collective-permute-start.17 = (f32[2,256,128]{2,1,0:T(8,128)}, f32[2,256,128]{2,1,0:T(8,128)}, u32[]{:S(2)}, u32[]{:S(2)}) collective-permute-start(f32[2,256,128]{2,1,0:T(8,128)} %shard_map.75.edge.old), channel_id=1, source_target_pairs={{0,24},{4,28},{8,0},{12,4},{16,8},{20,12},{24,16},{28,20},{1,25},{... | collective-permute-start | bytes 786440 | tf_op jit(solution)/shard_map/ppermute | solution.py:520
  104.1 25.4 %collective-permute-start.23 = (f32[2,256,128]{2,1,0:T(8,128)S(1)}, f32[2,256,128]{2,1,0:T(8,128)}, u32[]{:S(2)}, u32[]{:S(2)}) collective-permute-start(f32[2,256,128]{2,1,0:T(8,128)S(1)} %shard_map.84.edge.old), channel_id=1, source_target_pairs={{0,24},{4,28},{8,0},{12,4},{16,8},{20,12},{24,16},{28,20},{1,25},{... | collective-permute-start | bytes 786440 | tf_op jit(solution)/shard_map/ppermute | solution.py:520
  119.4 15.5 %collective-permute-start.18 = (f32[2,256,128]{2,1,0:T(8,128)S(1)}, f32[2,256,128]{2,1,0:T(8,128)S(1)}, u32[]{:S(2)}, u32[]{:S(2)}) collective-permute-start(f32[2,256,128]{2,1,0:T(8,128)S(1)} %slice_select_fusion.2), channel_id=1, source_target_pairs={{0,4},{4,0},{8,12},{12,8},{16,20},{20,16},{24,28},{28,24},{1,5},{5... | collective-permute-start | bytes 786440 | tf_op jit(solution)/shard_map/ppermute | solution.py:515
  123.6 11.2 %collective-permute-start.19 = (f32[2,256,128]{2,1,0:T(8,128)S(1)}, f32[2,256,128]{2,1,0:T(8,128)S(1)}, u32[]{:S(2)}, u32[]{:S(2)}) collective-permute-start(f32[2,256,128]{2,1,0:T(8,128)S(1)} %shard_map.76.edge), channel_id=1, source_target_pairs={{0,8},{4,12},{8,16},{12,20},{16,24},{20,28},{24,0},{28,4},{1,9},{5... | collective-permute-start | bytes 786440 | tf_op jit(solution)/shard_map/ppermute | solution.py:520
  133.5 9.1 %collective-permute-start.24 = (f32[2,256,128]{2,1,0:T(8,128)S(1)}, f32[2,256,128]{2,1,0:T(8,128)S(1)}, u32[]{:S(2)}, u32[]{:S(2)}) collective-permute-start(f32[2,256,128]{2,1,0:T(8,128)S(1)} %slice_select_fusion), channel_id=1, source_target_pairs={{0,4},{4,0},{8,12},{12,8},{16,20},{20,16},{24,28},{28,24},{1,5},{5... | collective-permute-start | bytes 786440 | tf_op jit(solution)/shard_map/ppermute | solution.py:515
  133.6 9.0 %collective-permute-start.25 = (f32[2,256,128]{2,1,0:T(8,128)S(1)}, f32[2,256,128]{2,1,0:T(8,128)S(1)}, u32[]{:S(2)}, u32[]{:S(2)}) collective-permute-start(f32[2,256,128]{2,1,0:T(8,128)S(1)} %shard_map.85.edge), channel_id=1, source_target_pairs={{0,8},{4,12},{8,16},{12,20},{16,24},{20,28},{24,0},{28,4},{1,9},{5... | collective-permute-start | bytes 786440 | tf_op jit(solution)/shard_map/ppermute | solution.py:520
  136.5 11.2 %collective-permute-start.20 = (f32[2,256,128]{2,1,0:T(8,128)S(1)}, f32[2,256,128]{2,1,0:T(8,128)S(1)}, u32[]{:S(2)}, u32[]{:S(2)}) collective-permute-start(f32[2,256,128]{2,1,0:T(8,128)S(1)} %slice_select_fusion.3), channel_id=1, source_target_pairs={{0,4},{4,0},{8,12},{12,8},{16,20},{20,16},{24,28},{28,24},{1,5},{5... | collective-permute-start | bytes 786440 | tf_op jit(solution)/shard_map/ppermute | solution.py:515
  143.2 7.2 %collective-permute-start.26 = (f32[2,256,128]{2,1,0:T(8,128)S(1)}, f32[2,256,128]{2,1,0:T(8,128)S(1)}, u32[]{:S(2)}, u32[]{:S(2)}) collective-permute-start(f32[2,256,128]{2,1,0:T(8,128)S(1)} %slice_select_fusion.1), channel_id=1, source_target_pairs={{0,4},{4,0},{8,12},{12,8},{16,20},{20,16},{24,28},{28,24},{1,5},{5... | collective-permute-start | bytes 786440 | tf_op jit(solution)/shard_map/ppermute | solution.py:515
  (38 other events, 122.7 us)

commit v5 on v4

--- a/solution.py
+++ b/solution.py
@@ -63,13 +63,15 @@
     cut_refs, (held, sems) = rest[:-2], rest[-2:]
     first = pltpu.make_async_copy(basis_ref.at[0], held, sems.at[0])
     first.start()
-    width = cut_refs[0].shape[2]
+    half = cut_refs[-1].shape[2]
     copies = []
     for at, out_ref in enumerate(cut_refs):
-        source = vector_ref
-        if vector_ref.shape[2] > width:
-            start = pl.multiple_of((side_ref[0] * len(cut_refs) + at) * width, width)
-            source = vector_ref.at[:, :, pl.ds(start, width)]
+        width = out_ref.shape[2]
+        element = 0 if at < len(cut_refs) - 1 else 2
+        source = vector_ref.at[pl.ds(element, 2)]
+        if vector_ref.shape[2] > half:
+            first_column = pl.multiple_of(side_ref[0] * half, half) + (at * width if element == 0 else 0)
+            source = vector_ref.at[pl.ds(element, 2), :, pl.ds(pl.multiple_of(first_column, width), width)]
         copies.append(pltpu.make_async_copy(source, out_ref, sems.at[1 + at]))
         copies[-1].start()
     first.wait()
@@ -254,10 +256,11 @@
     return result if first else 2.0 * result - before
 
 
-def edge_kernel(first, up, high, low, high_outer, low_outer, inner, halo, old, out, held):
-    size, columns = inner.shape[1:]
-    count = inner.shape[0]
-    local = (inner[count - 2], inner[count - 1]) if up else (inner[0], inner[1])
+def edge_kernel(first, up, lane, high, low, high_outer, low_outer, inner, halo, old, out, held):
+    count, size, _ = inner.shape
+    columns = halo.shape[2]
+    lanes = slice(lane, lane + columns)
+    local = (inner[count - 2, :, lanes], inner[count - 1, :, lanes]) if up else (inner[0, :, lanes], inner[1, :, lanes])
     beyond = (halo[0], halo[1])
     for at, value in enumerate(local + beyond if up else beyond + local):
         hold(held, at, value)
@@ -268,18 +271,20 @@
         out[at] = advance(first, row, None if first else old[at])
 
 
-def inner_kernel(first, up, high, low, edge, inner, old, out, held):
-    count, size, columns = inner.shape
+def inner_kernel(first, up, lane, high, low, inner, old, *refs):
+    edges, out, held = refs[:-2], refs[-2], refs[-1]
+    count, size, columns = out.shape
+    lanes = slice(lane, lane + columns)
     for at in range(2):
-        hold(held, at if up else count + at, edge[at])
+        hold(held, at if up else count + at, jnp.concatenate([edge[at] for edge in edges], axis=1))
     for at in range(count):
-        hold(held, at + 2 if up else at, inner[at])
+        hold(held, at + 2 if up else at, inner[at, :, lanes])
 
     @pl.loop(0, count)
     def _(at):
         place = at + (1 if up else 2)
         row = apply_row(high[place], low[place], held, pl.multiple_of(at * size, size), columns)
-        out[at] = advance(first, row, None if first else old[at])
+        out[at] = advance(first, row, None if first else old[at, :, lanes])
 
 
 def fold_kernel(lane_ref, keep_ref, other_ref, send_ref, stay_ref):
@@ -294,25 +299,45 @@
     out_ref[...] = first_ref[...] + second_ref[...]
 
 
-def arrange_kernel(chunk, chunks, side_ref, vector_ref, got_ref, edge_ref, inner_ref, sems):
-    half, _, width = got_ref.shape
-    side = side_ref[0]
-    targets = [edge_ref.at[0], edge_ref.at[1]] + [inner_ref.at[at] for at in range(2 * half - 2)]
-
+def copy_pairs(side, pairs, sems):
     def moved(act):
-        for element, target in enumerate(targets):
-            own = vector_ref.at[element % half]
-            if vector_ref.shape[2] > width:
-                start = pl.multiple_of((side * chunks + chunk) * width, width)
-                own = vector_ref.at[element % half, :, pl.ds(start, width)]
-            for source, mine in ((own, True), (got_ref.at[element % half], False)):
-
-                @pl.when((side == element // half) == mine)
-                def _():
-                    act(pltpu.make_async_copy(source, target, sems.at[element]))
+        for at, (wanted, source, target) in enumerate(pairs):
+
+            @pl.when(side == wanted)
+            def _():
+                act(pltpu.make_async_copy(source, target, sems.at[at]))
 
     moved(lambda copy: copy.start())
     moved(lambda copy: copy.wait())
+
+
+def own_columns(vector_ref, side, element, count, half, lane, width):
+    if vector_ref.shape[2] == half:
+        return vector_ref.at[pl.ds(element, count)]
+    start = pl.multiple_of(pl.multiple_of(side * half, half) + lane, width)
+    return vector_ref.at[pl.ds(element, count), :, pl.ds(start, width)]
+
+
+def arrange_edge_kernel(half, lane, side_ref, vector_ref, got_ref, edge_ref, sems):
+    own = own_columns(vector_ref, side_ref[0], 0, 2, half, lane, got_ref.shape[2])
+    copy_pairs(side_ref[0], ((0, own, edge_ref), (1, got_ref, edge_ref)), sems)
+
+
+def arrange_inner_kernel(chunks, side_ref, vector_ref, *refs):
+    first, (second, inner_ref, sems) = refs[:chunks], refs[chunks:]
+    half = second.shape[2]
+    width = half // chunks
+    own = lambda element, count: own_columns(vector_ref, side_ref[0], element, count, half, 0, half)
+    pairs = [
+        (0, own(2, 2), inner_ref.at[pl.ds(0, 2)]),
+        (0, second, inner_ref.at[pl.ds(4, 2)]),
+        (1, second, inner_ref.at[pl.ds(0, 2)]),
+        (1, own(0, 4), inner_ref.at[pl.ds(2, 4)]),
+    ]
+    for at, got in enumerate(first):
+        target = inner_ref.at[pl.ds(2, 2)] if chunks == 1 else inner_ref.at[pl.ds(2, 2), :, pl.ds(at * width, width)]
+        pairs.append((0, got, target))
+    copy_pairs(side_ref[0], pairs, sems)
 
 
 def place_pairs(out_ref, sems, side, chunks, chunk, width, pairs):
@@ -360,16 +385,15 @@
         act(lambda copy: copy.wait())
 
 
-def lead_and_cut(side, index, basis, vector, chunks, width):
+def lead_and_cut(side, index, basis, vector, chunks, half):
     points, size = basis.shape[1:]
-    count = vector.shape[0]
+    cuts = [jax.ShapeDtypeStruct((2, size, half // chunks), jnp.float32)] * chunks
     return pl.pallas_call(
         lead_kernel,
         in_specs=[SCALARS, VMEM, ANY, ANY],
-        out_specs=[VMEM] + [VMEM] * chunks,
-        out_shape=[jax.ShapeDtypeStruct((size, index.shape[2]), jnp.float32)]
-        + [jax.ShapeDtypeStruct((count, size, width), jnp.float32)] * chunks,
-        scratch_shapes=[pltpu.VMEM((points, size), jnp.float32), pltpu.SemaphoreType.DMA((1 + chunks,))],
+        out_specs=[VMEM] * (2 + chunks),
+        out_shape=[jax.ShapeDtypeStruct((size, index.shape[2]), jnp.float32), *cuts, jax.ShapeDtypeStruct((2, size, half), jnp.float32)],
+        scratch_shapes=[pltpu.VMEM((points, size), jnp.float32), pltpu.SemaphoreType.DMA((2 + chunks,))],
         compiler_params=PARAMS,
     )(side, index, far_off(basis), far_off(vector))
 
@@ -415,7 +439,7 @@
         out_shape=[near_core((8, size, 3 * size), jnp.bfloat16)] * 2,
         scratch_shapes=[pltpu.VMEM((8, rows, size), jnp.float32), pltpu.SemaphoreType.DMA((8,))],
         compiler_params=PARAMS,
-    )(me, *parts)
+    )(me, *[far_off(part) for part in parts])
 
 
 def outer_weights(core, first, second, swapped, high, low):
@@ -429,28 +453,31 @@
     )(core, first, second, swapped, high, low)
 
 
-def apply_edge(first, up, high, low, high_outer, low_outer, inner, halo, old):
-    _, size, columns = inner.shape
-    return pl.pallas_call(
-        functools.partial(edge_kernel, first, up),
+def apply_edge(first, up, lane, high, low, high_outer, low_outer, inner, halo, old):
+    size, columns = halo.shape[1:]
+    return pl.pallas_call(
+        functools.partial(edge_kernel, first, up, lane),
         in_specs=[VMEM] * 7,
         out_specs=VMEM,
         out_shape=near_core(halo.shape),
+        input_output_aliases={} if first else {6: 0},
         scratch_shapes=[pltpu.VMEM(held_shape(4 * size, columns), jnp.bfloat16)],
         compiler_params=PARAMS,
     )(high, low, high_outer, low_outer, inner, close_by(halo), old)
 
 
-def apply_inner(first, up, high, low, edge, inner, old):
+def apply_inner(first, up, lane, high, low, edges, inner, old):
     count, size, columns = inner.shape
-    return pl.pallas_call(
-        functools.partial(inner_kernel, first, up),
-        in_specs=[VMEM] * 5,
+    width = sum(edge.shape[2] for edge in edges)
+    return pl.pallas_call(
+        functools.partial(inner_kernel, first, up, lane),
+        in_specs=[VMEM] * (4 + len(edges)),
         out_specs=VMEM,
-        out_shape=near_core(inner.shape),
-        scratch_shapes=[pltpu.VMEM(held_shape((count + 2) * size, columns), jnp.bfloat16)],
-        compiler_params=PARAMS,
-    )(high, low, edge, inner, old)
+        out_shape=near_core((count, size, width)),
+        input_output_aliases={} if first or width < columns else {3: 0},
+        scratch_shapes=[pltpu.VMEM(held_shape((count + 2) * size, width), jnp.bfloat16)],
+        compiler_params=PARAMS,
+    )(high, low, inner, old, *edges)
 
 
 def folded(lane, keep, other):
@@ -470,17 +497,28 @@
     )(first, close_by(second))
 
 
-def arranged(side, vector, got, chunk):
-    half, size, columns = got.shape
-    chunks = max(vector.shape[2] // 2 // columns, 1)
-    return pl.pallas_call(
-        functools.partial(arrange_kernel, chunk, chunks),
+def arranged_edge(side, vector, got, half, lane):
+    return pl.pallas_call(
+        functools.partial(arrange_edge_kernel, half, lane),
         in_specs=[SCALARS, ANY, ANY],
-        out_specs=[VMEM] * 2,
-        out_shape=[near_core((2, size, columns)), near_core((2 * half - 2, size, columns))],
-        scratch_shapes=[pltpu.SemaphoreType.DMA((2 * half,))],
+        out_specs=VMEM,
+        out_shape=near_core(got.shape),
+        scratch_shapes=[pltpu.SemaphoreType.DMA((2,))],
         compiler_params=PARAMS,
     )(side, far_off(vector), got)
+
+
+def arranged_inner(side, vector, first, second):
+    _, size, half = second.shape
+    chunks = len(first)
+    return pl.pallas_call(
+        functools.partial(arrange_inner_kernel, chunks),
+        in_specs=[SCALARS] + [ANY] * (2 + chunks),
+        out_specs=VMEM,
+        out_shape=near_core((6, size, half)),
+        scratch_shapes=[pltpu.SemaphoreType.DMA((4 + chunks,))],
+        compiler_params=PARAMS,
+    )(side, far_off(vector), *first, second)
 
 
 def collected(side, parts):
@@ -534,12 +572,13 @@
     vector = orbitals.reshape(count, size, columns)
 
     lead_index = face_index[:1, 0:2].reshape(1, 1, 2 * spots)
-    part = columns // 2 // chunks
+    wide = columns // 2
+    part = wide // chunks
     own = foreign = vector
     if part % 128:
         own = lax.dynamic_slice_in_dim(vector, side * part, part, axis=2)
         foreign = lax.dynamic_slice_in_dim(vector, (1 - side) * part, part, axis=2)
-    lead, *foreign = lead_and_cut(1 - side_at, lead_index, basis, foreign, chunks, part)
+    lead, *foreign = lead_and_cut(1 - side_at, lead_index, basis, foreign, chunks, wide)
     lead = shifted(lead, "elem", -1)
     got = [flipped(value, "elem", 1) for value in foreign]
 
@@ -558,18 +597,14 @@
     while bit < width:
         mine = mine + flipped(mine, "pts", bit)
         bit *= 2
-    got[0], mine = lax.optimization_barrier((got[0], mine))
-    state, halos = [], []
-
-    def arrange(chunk):
-        state.append(arranged(side_at, own, got[chunk], chunk))
-        halos.append(shifted(state[chunk][0], "elem", -2))
-
-    arrange(0)
+    edges, halos = [], []
+    for chunk in range(chunks):
+        edges.append(arranged_edge(side_at, own, got[chunk], wide, chunk * part))
+        halos.append(shifted(edges[chunk], "elem", -2))
+    halos[0], got[chunks - 1], mine = lax.optimization_barrier((halos[0], got[chunks - 1], mine))
     beside = flipped(mine, "pts", 2)
     across = flipped(mine, "elem", 1)
     mine_near = flipped(mine, "pts", 1)
-    halos[0], across = lax.optimization_barrier((halos[0], across))
     both = flipped(across, "pts", 2)
     beside_near = flipped(beside, "pts", 1)
     across_near = flipped(across, "pts", 1)
@@ -581,41 +616,43 @@
     outer_side = lax.ppermute(outer, ("elem", "pts"), [(flat(e, p), flat(e ^ 1, p)) for e, p in holds])
     outer_near = flipped(outer + outer_side, "pts", 1)
 
-    if chunks > 1:
-        got[1], both = lax.optimization_barrier((got[1], both))
-        arrange(1)
+    halos[-1], got[-1], both = lax.optimization_barrier((halos[-1], got[-1], both))
+    inner = arranged_inner(side_at, own, got[:-1], got[-1])
     both_near = flipped(both, "pts", 1)
 
     me = (side * 4 + core * 2 + lane).reshape(1).astype(jnp.int32)
     high, low = weights(me, mine, mine_near, beside, across, beside_near, across_near, both, both_near)
     high_outer, low_outer = outer_weights(core_at, outer, outer_side, outer_near, high, low)
 
-    old = list(state)
-    near, far = [], []
+    old_edges, old_inner = list(edges), inner
+    near, far, parts = [], [], []
     for degree in range(DEG):
-        first, up = degree == 0, degree % 2 == 0
+        first, up, final = degree == 0, degree % 2 == 0, degree == DEG - 1
+        if not final:
+            new_inner = apply_inner(first, up, 0, high, low, edges, inner, old_inner)
+        new_edges = []
         for c in range(chunks):
-            edge, inner = state[c]
-            new_inner = apply_inner(first, up, high, low, edge, inner, old[c][1])
-            if degree == DEG - 1:
-                near.append(flipped(jnp.where(side == 0, new_inner[2:4], new_inner[:2]), "elem", 1))
-                near[c], halos[c] = lax.optimization_barrier((near[c], halos[c]))
-            new_edge = apply_edge(first, up, high, low, high_outer, low_outer, inner, halos[c], old[c][0])
-            old[c] = state[c]
-            state[c] = new_edge, new_inner
-            if degree < DEG - 1:
-                halos[c] = shifted(new_edge, "elem", 2 if up else -2)
+            if final:
+                parts.append(apply_inner(first, up, c * part, high, low, edges[c : c + 1], inner, old_inner))
+                near.append(flipped(jnp.where(side == 0, parts[c][2:4], parts[c][:2]), "elem", 1))
+            new_edges.append(apply_edge(first, up, c * part, high, low, high_outer, low_outer, inner, halos[c], old_edges[c]))
+            if final:
+                send = jnp.where(side == 0, parts[c][4:], new_edges[c])
+                near[c], send = lax.optimization_barrier((near[c], send))
+                far.append(flipped(send, "elem", 1))
             else:
-                far.append(flipped(jnp.where(side == 0, new_inner[4:], new_edge), "elem", 1))
+                halos[c] = shifted(new_edges[c], "elem", 2 if up else -2)
+        old_edges, edges = edges, new_edges
+        old_inner, inner = inner, new_inner
     if part % 128:
-        (edge, inner), near, far = state[0], near[0], far[0]
+        edge, inner, near, far = edges[0], parts[0], near[0], far[0]
         lower = jnp.concatenate([edge, inner[:2]])
         mine = jnp.where(side == 0, lower, inner[2:])
         theirs = jnp.where(side == 0, jnp.concatenate([far, near]), jnp.concatenate([near, far]))
         swap = lambda first, second: jnp.concatenate([first, second], axis=2)
         result = jnp.where(side == 0, swap(mine, theirs), swap(theirs, mine))
     else:
-        result = collected(side_at, [(*state[c], near[c]) for c in range(chunks)])
+        result = collected(side_at, [(edges[c], parts[c], near[c]) for c in range(chunks)])
         result = finished(side_at, far, result)
     return result.reshape(count * size, columns)
 

time: 152 us -> 157 us (1.033)
  waiting for transfers between devices: 49.4 us -> 58.8 us
  local copies, waits for them, and re-layouts: 18.3 us -> 10.4 us
  starting transfers between devices: 30.8 us -> 35.5 us
  Pallas kernels: 51.2 us -> 49.1 us
    ppermute x9, starting transfers between devices: 11.6 us -> 21.2 us  [shifted(): lax.ppermute(value, axis, [(i, (i + steps) % count) for i in range(count)])]
    unnamed x86 -> x66, local copies, waits for them, and re-layouts: 17.2 us -> 9.43 us
    ppermute x16 -> x17, waiting for transfers between devices: 32.1 us -> 38.3 us  [flipped(): return lax.ppermute(value, axis, [(i, i ^ bit) for i in range(count)])]
    ppermute x1, waiting for transfers between devices: 0.01 us -> 5.75 us  [body(): lax.ppermute(last, ('elem', 'pts'), [(flat(e, p), flat(e + (2 if p % 2 el...]
    ppermute x16 -> x17, starting transfers between devices: 13.2 us -> 8.88 us  [flipped(): return lax.ppermute(value, axis, [(i, i ^ bit) for i in range(count)])]
    ppermute x1, starting transfers between devices: 3.62 us -> 1.3 us  [body(): lax.ppermute(outer, ('elem', 'pts'), [(flat(e, p), flat(e ^ 1, p)) for e,...]
    ppermute x1, waiting for transfers between devices: 1.83 us -> 0.01 us  [body(): lax.ppermute(outer, ('elem', 'pts'), [(flat(e, p), flat(e ^ 1, p)) for e,...]
    ppermute x1, starting transfers between devices: 2.36 us -> 4.15 us  [body(): lax.ppermute(last, ('elem', 'pts'), [(flat(e, p), flat(e + (2 if p % 2 el...]
  transfers between devices with their start and end apart: 27 -> 28, of which waited for: 12 -> 15; matrix products, arithmetic and copies ran while one was open for 1% -> 1% of each run, Pallas kernels for 31% -> 27%
where the time goes in v5:
time: 157 us; the launch traced here: 156 us
  waiting for transfers between devices  58.8 us (37%)
  Pallas kernels  49.1 us (31%)
  starting transfers between devices  35.5 us (23%)
  local copies, waits for them, and re-layouts  10.4 us (7%)
    ppermute x17, waiting for transfers between devices, flipped(): return lax.ppermute(value, axis, [(i, i ^ bit) for i in range(count)])  38.3 us
    ppermute x9, starting transfers between devices, shifted(): lax.ppermute(value, axis, [(i, (i + steps) % count) for i in range(count)])  21.2 us
    pallas_call x5, Pallas kernels, apply_inner(): pl.pallas_call(functools.partial(inner_kernel, first, up, lane), in_specs...  17.8 us
    ppermute x9, waiting for transfers between devices, shifted(): lax.ppermute(value, axis, [(i, (i + steps) % count) for i in range(count)])  14.8 us
    pallas_call x8, Pallas kernels, apply_edge(): pl.pallas_call(functools.partial(edge_kernel, first, up, lane), in_specs=...  11.9 us
    unnamed x66, local copies, waits for them, and re-layouts  9.43 us
    ppermute x17, starting transfers between devices, flipped(): return lax.ppermute(value, axis, [(i, i ^ bit) for i in range(count)])  8.88 us
    pallas_call x1, Pallas kernels, blocks(): pl.pallas_call(functools.partial(blocks_kernel, faces_total), in_specs=[S...  6.77 us
  transfers between devices with their start and end apart: 28, of which 15 were waited for; matrix products, arithmetic and copies ran while one was open for 1% of the time, Pallas kernels for 27%

profile of v5, /device:TPU:0, one launch (start us, length us, event | category | flops | bytes accessed | tf_op | source)
XLA Modules:
  0.0 155.8 jit_solution(6679508086011193194)
XLA Ops:
  0.8 2.2 %shard_map.64 = (f32[256,128]{1,0:T(8,128)S(1)}, f32[2,256,128]{2,1,0:T(8,128)S(1)}, f32[2,256,128]{2,1,0:T(8,128)}, f32[2,256,256]{2,1,0:T(8,128)S(1)}) custom-call(s32[1]{0:T(128)S(6)} %sub.8.side_ref, s32[1,1,128]{2,1,0:T(1,128)S(1)} %reshape.35.index_ref, f32[4,512,256]{2,1,0:T(8,128)} %basis_ref.3, f32[4,256,512]{2,1,0:T(8,128)} %bitcast.10), custom_call_target="tpu_custom_call" | custom-call | tf_op jit(solution)/shard_map/pallas_call | solution.py:391
  3.8 6.0 %collective-permute-start.3 = (f32[256,128]{1,0:T(8,128)S(1)}, f32[256,128]{1,0:T(8,128)S(1)}, u32[]{:S(2)}, u32[]{:S(2)}) collective-permute-start(f32[256,128]{1,0:T(8,128)S(1)} %get-tuple-element.33), channel_id=1, source_target_pairs={{0,28},{4,0},{8,4},{12,8},{16,12},{20,16},{24,20},{28,24},{1,29},{... | collective-permute-start | bytes 393224 | tf_op jit(solution)/shard_map/ppermute | solution.py:558
  10.0 6.8 %shard_map.66 = (f32[2,392,256]{2,1,0:T(8,128)S(1)}, f32[2,392,256]{2,1,0:T(8,128)S(1)}, f32[256,256]{1,0:T(8,128)S(1)}) custom-call(s32[1]{0:T(128)} %bitcast.4.core_ref, s32[4,1,256]{2,1,0:T(1,128)S(1)} %reshape.38.index_ref, f32[4,1,512]{2,1,0:T(1,128)S(1)} %reshape.39.quad_ref, s32[4,1,128]{2,1,0:T(1,128)S(1)} %bitcast.9, f32[4,512,256]{2,1,0:T(8,128)} %basis_ref.3, ...), custom_call_target="tpu_custom_call" | custom-call | tf_op jit(solution)/shard_map/pallas_call | solution.py:405
  17.7 2.2 %collective-permute-done.4.other_ref = f32[2,392,256]{2,1,0:T(8,128)S(1)} collective-permute-done((f32[2,392,256]{2,1,0:T(8,128)S(1)}, f32[2,392,256]{2,1,0:T(8,128)S(1)}, u32[]{:S(2)}, u32[]{:S(2)}) %collective-permute-start.4) | collective-permute-done | bytes 802848 | tf_op jit(solution)/shard_map/ppermute | solution.py:553
  21.6 5.2 %collective-permute-done.got_ref.refs_0_ = f32[2,256,128]{2,1,0:T(8,128)S(1)} collective-permute-done((f32[2,256,128]{2,1,0:T(8,128)S(1)}, f32[2,256,128]{2,1,0:T(8,128)S(1)}, u32[]{:S(2)}, u32[]{:S(2)}) %collective-permute-start) | collective-permute-done | bytes 262176 | tf_op jit(solution)/shard_map/ppermute | solution.py:553
  28.3 3.2 %collective-permute-done.5.second_ref = f32[1,392,256]{2,1,0:T(8,128)S(1)} collective-permute-done((f32[1,392,256]{2,1,0:T(8,128)S(1)}, f32[1,392,256]{2,1,0:T(8,128)S(1)}, u32[]{:S(2)}, u32[]{:S(2)}) %collective-permute-start.5) | collective-permute-done | bytes 401440 | tf_op jit(solution)/shard_map/ppermute | solution.py:553
  31.9 3.3 %collective-permute-done.1.halo = f32[2,256,128]{2,1,0:T(8,128)S(1)} collective-permute-done((f32[2,256,128]{2,1,0:T(8,128)S(1)}, f32[2,256,128]{2,1,0:T(8,128)S(1)}, u32[]{:S(2)}, u32[]{:S(2)}) %collective-permute-start.1) | collective-permute-done | bytes 262176 | tf_op jit(solution)/shard_map/ppermute | solution.py:558
  36.7 8.1 %collective-permute-done.7.refs_2_ = f32[1,392,256]{2,1,0:T(8,128)} collective-permute-done((f32[1,392,256]{2,1,0:T(8,128)S(1)}, f32[1,392,256]{2,1,0:T(8,128)}, u32[]{:S(2)}, u32[]{:S(2)}) %collective-permute-start.7) | collective-permute-done | bytes 401440 | tf_op jit(solution)/shard_map/ppermute | solution.py:553
  44.9 4.2 %collective-permute-start.15 = (f32[1,392,256]{2,1,0:T(8,128)S(1)}, f32[1,392,256]{2,1,0:T(8,128)S(1)}, u32[]{:S(2)}, u32[]{:S(2)}) collective-permute-start(f32[1,392,256]{2,1,0:T(8,128)S(1)} %broadcast_select_fusion), channel_id=1, source_target_pairs={{0,24},{2,26},{5,13},{7,15},{8,0},{10,2},{13,21},{15,23},{16,8},{1... | collective-permute-start | bytes 1204232 | tf_op jit(solution)/shard_map/ppermute | solution.py:615
  49.1 2.5 %collective-permute-start.13 = (f32[1,392,256]{2,1,0:T(8,128)}, f32[1,392,256]{2,1,0:T(8,128)}, u32[]{:S(2)}, u32[]{:S(2)}) collective-permute-start(f32[1,392,256]{2,1,0:T(8,128)} %collective-permute-done.8.refs_3_), channel_id=1, source_target_pairs={{0,2},{1,3},{2,0},{3,1},{4,6},{5,7},{6,4},{7,5},{8,10},{9,11},{10,... | collective-permute-start | bytes 1204232 | tf_op jit(solution)/shard_map/ppermute | solution.py:553
  51.7 5.7 %collective-permute-done.15.first_ref = f32[1,392,256]{2,1,0:T(8,128)S(1)} collective-permute-done((f32[1,392,256]{2,1,0:T(8,128)S(1)}, f32[1,392,256]{2,1,0:T(8,128)S(1)}, u32[]{:S(2)}, u32[]{:S(2)}) %collective-permute-start.15) | collective-permute-done | bytes 401440 | tf_op jit(solution)/shard_map/ppermute | solution.py:615
  59.7 4.1 %collective-permute-start.11 = (f32[2,256,128]{2,1,0:T(8,128)S(1)}, f32[2,256,128]{2,1,0:T(8,128)S(1)}, u32[]{:S(2)}, u32[]{:S(2)}) collective-permute-start(f32[2,256,128]{2,1,0:T(8,128)S(1)} %shard_map.70.refs_1_.old), channel_id=1, source_target_pairs={{0,24},{4,28},{8,0},{12,4},{16,8},{20,12},{24,16},{28,20},{1,25},{... | collective-permute-start | bytes 786440 | tf_op jit(solution)/shard_map/ppermute | solution.py:558
  64.5 3.2 %collective-permute-done.11.halo = f32[2,256,128]{2,1,0:T(8,128)S(1)} collective-permute-done((f32[2,256,128]{2,1,0:T(8,128)S(1)}, f32[2,256,128]{2,1,0:T(8,128)S(1)}, u32[]{:S(2)}, u32[]{:S(2)}) %collective-permute-start.11) | collective-permute-done | bytes 262176 | tf_op jit(solution)/shard_map/ppermute | solution.py:558
  71.6 2.8 %shard_map.71 = (bf16[8,256,768]{2,1,0:T(8,128)(2,1)S(1)}, bf16[8,256,768]{2,1,0:T(8,128)(2,1)S(1)}) custom-call(s32[1]{0:T(128)} %bitcast.1.me_ref, f32[1,392,256]{2,1,0:T(8,128)} %copy-done.18, f32[1,392,256]{2,1,0:T(8,128)} %collective-permute-done.6.refs_1_, f32[1,392,256]{2,1,0:T(8,128)} %collective-permute-done.7.refs_2_, ...), custom_call_target="tpu_custom_call" | custom-call | tf_op jit(solution)/shard_map/pallas_call | solution.py:435
  74.5 1.7 %shard_map.74 = (bf16[2,256,768]{2,1,0:T(8,128)(2,1)S(1)}, bf16[2,256,768]{2,1,0:T(8,128)(2,1)S(1)}) custom-call(s32[1]{0:T(128)} %bitcast.4.core_ref, f32[1,392,256]{2,1,0:T(8,128)S(1)} %copy-done.20, f32[1,392,256]{2,1,0:T(8,128)S(1)} %copy-done.22, f32[1,392,256]{2,1,0:T(8,128)} %collective-permute-done.17.swapped_ref, ...), custom_call_target="tpu_custom_call" | custom-call | tf_op jit(solution)/shard_map/pallas_call | solution.py:447
  80.6 3.2 %shard_map.73.inner.old = f32[6,256,256]{2,1,0:T(8,128)S(1)} custom-call(bf16[8,256,768]{2,1,0:T(8,128)(2,1)S(1)} %get-tuple-element.43.high.high_in, bf16[8,256,768]{2,1,0:T(8,128)(2,1)S(1)} %get-tuple-element.44.low.low_in, f32[6,256,256]{2,1,0:T(8,128)S(1)} %shard_map.72.inner.old, f32[6,256,256]{2,1,0:T(8,128)S(1)} %shard_map.72.inner.old, ...), custom_call_target="tpu_custom_call" | custom-call | tf_op jit(solution)/shard_map/pallas_call | solution.py:472
  83.9 5.4 %collective-permute-done.19.halo = f32[2,256,128]{2,1,0:T(8,128)S(1)} collective-permute-done((f32[2,256,128]{2,1,0:T(8,128)}, f32[2,256,128]{2,1,0:T(8,128)S(1)}, u32[]{:S(2)}, u32[]{:S(2)}) %collective-permute-start.19) | collective-permute-done | bytes 262176 | tf_op jit(solution)/shard_map/ppermute | solution.py:558
  89.8 2.1 %collective-permute-start.24 = (f32[2,256,128]{2,1,0:T(8,128)S(1)}, f32[2,256,128]{2,1,0:T(8,128)S(1)}, u32[]{:S(2)}, u32[]{:S(2)}) collective-permute-start(f32[2,256,128]{2,1,0:T(8,128)S(1)} %shard_map.79.refs_1_.old), channel_id=1, source_target_pairs={{0,24},{4,28},{8,0},{12,4},{16,8},{20,12},{24,16},{28,20},{1,25},{... | collective-permute-start | bytes 786440 | tf_op jit(solution)/shard_map/ppermute | solution.py:558
  92.0 2.9 %collective-permute-done.18.halo = f32[2,256,128]{2,1,0:T(8,128)S(1)} collective-permute-done((f32[2,256,128]{2,1,0:T(8,128)}, f32[2,256,128]{2,1,0:T(8,128)S(1)}, u32[]{:S(2)}, u32[]{:S(2)}) %collective-permute-start.18) | collective-permute-done | bytes 262176 | tf_op jit(solution)/shard_map/ppermute | solution.py:558
  95.5 6.8 %collective-permute-start.20 = (f32[2,256,128]{2,1,0:T(8,128)S(1)}, f32[2,256,128]{2,1,0:T(8,128)S(1)}, u32[]{:S(2)}, u32[]{:S(2)}) collective-permute-start(f32[2,256,128]{2,1,0:T(8,128)S(1)} %shard_map.78.refs_0_.old), channel_id=1, source_target_pairs={{0,24},{4,28},{8,0},{12,4},{16,8},{20,12},{24,16},{28,20},{1,25},{... | collective-permute-start | bytes 786440 | tf_op jit(solution)/shard_map/ppermute | solution.py:558
  102.4 4.3 %shard_map.77.inner.old = f32[6,256,256]{2,1,0:T(8,128)S(1)} custom-call(bf16[8,256,768]{2,1,0:T(8,128)(2,1)S(1)} %get-tuple-element.43.high.high_in, bf16[8,256,768]{2,1,0:T(8,128)(2,1)S(1)} %get-tuple-element.44.low.low_in, f32[6,256,256]{2,1,0:T(8,128)S(1)} %shard_map.73.inner.old, ...), custom_call_target="tpu_custom_call", output_to_operand_aliasing={{}: (3, {})} | custom-call | tf_op jit(solution)/shard_map/pallas_call | solution.py:472
  106.7 2.5 %shard_map.84.refs_0_ = f32[2,256,128]{2,1,0:T(8,128)} custom-call(bf16[8,256,768]{2,1,0:T(8,128)(2,1)S(1)} %get-tuple-element.43.high.high_in, bf16[8,256,768]{2,1,0:T(8,128)(2,1)S(1)} %get-tuple-element.44.low.low_in, bf16[2,256,768]{2,1,0:T(8,128)(2,1)S(1)} %get-tuple-element.47.high_outer, ...), custom_call_target="tpu_custom_call", output_to_operand_aliasing={{}: (6, {})} | custom-call | tf_op jit(solution)/shard_map/pallas_call | solution.py:458
  109.2 2.3 %shard_map.81.refs_0_ = f32[2,256,128]{2,1,0:T(8,128)} custom-call(bf16[8,256,768]{2,1,0:T(8,128)(2,1)S(1)} %get-tuple-element.43.high.high_in, bf16[8,256,768]{2,1,0:T(8,128)(2,1)S(1)} %get-tuple-element.44.low.low_in, bf16[2,256,768]{2,1,0:T(8,128)(2,1)S(1)} %get-tuple-element.47.high_outer, ...), custom_call_target="tpu_custom_call", output_to_operand_aliasing={{}: (6, {})} | custom-call | tf_op jit(solution)/shard_map/pallas_call | solution.py:458
  111.5 1.9 %copy-done.1 = bf16[8,256,768]{2,1,0:T(8,128)(2,1)S(1)} copy-done((bf16[8,256,768]{2,1,0:T(8,128)(2,1)S(1)}, bf16[8,256,768]{2,1,0:T(8,128)(2,1)}, u32[]{:S(2)}) %copy-start.1) | copy-done | bytes 3145752
  117.2 3.2 %shard_map.80.inner = f32[6,256,256]{2,1,0:T(8,128)S(1)} custom-call(bf16[8,256,768]{2,1,0:T(8,128)(2,1)S(1)} %get-tuple-element.43.high.high_in, bf16[8,256,768]{2,1,0:T(8,128)(2,1)S(1)} %copy-done.1, f32[6,256,256]{2,1,0:T(8,128)S(1)} %copy-done.4, f32[6,256,256]{2,1,0:T(8,128)S(1)} %copy-done.6, ...), custom_call_target="tpu_custom_call", output_to_operand_aliasing={{}: (3, {})} | custom-call | tf_op jit(solution)/shard_map/pallas_call | solution.py:472
  120.4 3.5 %shard_map.82.refs_1_ = f32[6,256,128]{2,1,0:T(8,128)S(1)} custom-call(bf16[8,256,768]{2,1,0:T(8,128)(2,1)S(1)} %get-tuple-element.43.high.high_in, bf16[8,256,768]{2,1,0:T(8,128)(2,1)S(1)} %copy-done.1, f32[6,256,256]{2,1,0:T(8,128)S(1)} %shard_map.80.inner, f32[6,256,256]{2,1,0:T(8,128)S(1)} %copy-done.4, f32[2,256,128]{2,1,0:T(8,128)} %shard_map.81.refs_0_), custom_call_target="tpu_custom_call" | custom-call | tf_op jit(solution)/shard_map/pallas_call | solution.py:472
  124.0 3.5 %shard_map.85.refs_4_ = f32[6,256,128]{2,1,0:T(8,128)S(1)} custom-call(bf16[8,256,768]{2,1,0:T(8,128)(2,1)S(1)} %get-tuple-element.43.high.high_in, bf16[8,256,768]{2,1,0:T(8,128)(2,1)S(1)} %copy-done.1, f32[6,256,256]{2,1,0:T(8,128)S(1)} %shard_map.80.inner, f32[6,256,256]{2,1,0:T(8,128)S(1)} %copy-done.4, f32[2,256,128]{2,1,0:T(8,128)} %shard_map.84.refs_0_), custom_call_target="tpu_custom_call" | custom-call | tf_op jit(solution)/shard_map/pallas_call | solution.py:472
  132.5 2.0 %collective-permute-start.21 = (f32[2,256,128]{2,1,0:T(8,128)S(1)}, f32[2,256,128]{2,1,0:T(8,128)S(1)}, u32[]{:S(2)}, u32[]{:S(2)}) collective-permute-start(f32[2,256,128]{2,1,0:T(8,128)S(1)} %get-tuple-element.58), channel_id=1, source_target_pairs={{0,4},{4,0},{8,12},{12,8},{16,20},{20,16},{24,28},{28,24},{1,5},{5... | collective-permute-start | bytes 786440 | tf_op jit(solution)/shard_map/ppermute | solution.py:553
  134.5 5.5 %collective-permute-done.25.refs_5_ = f32[2,256,128]{2,1,0:T(8,128)S(1)} collective-permute-done((f32[2,256,128]{2,1,0:T(8,128)S(1)}, f32[2,256,128]{2,1,0:T(8,128)S(1)}, u32[]{:S(2)}, u32[]{:S(2)}) %collective-permute-start.25) | collective-permute-done | bytes 262176 | tf_op jit(solution)/shard_map/ppermute | solution.py:553
  140.0 5.6 %collective-permute-done.21.refs_2_ = f32[2,256,128]{2,1,0:T(8,128)S(1)} collective-permute-done((f32[2,256,128]{2,1,0:T(8,128)S(1)}, f32[2,256,128]{2,1,0:T(8,128)S(1)}, u32[]{:S(2)}, u32[]{:S(2)}) %collective-permute-start.21) | collective-permute-done | bytes 262176 | tf_op jit(solution)/shard_map/ppermute | solution.py:553
  146.9 4.4 %collective-permute-done.27.refs_1_ = f32[2,256,128]{2,1,0:T(8,128)S(1)} collective-permute-done((f32[2,256,128]{2,1,0:T(8,128)S(1)}, f32[2,256,128]{2,1,0:T(8,128)S(1)}, u32[]{:S(2)}, u32[]{:S(2)}) %collective-permute-start.27) | collective-permute-done | bytes 262176 | tf_op jit(solution)/shard_map/ppermute | solution.py:553
  151.2 3.6 %collective-permute-done.23.refs_0_ = f32[2,256,128]{2,1,0:T(8,128)S(1)} collective-permute-done((f32[2,256,128]{2,1,0:T(8,128)S(1)}, f32[2,256,128]{2,1,0:T(8,128)S(1)}, u32[]{:S(2)}, u32[]{:S(2)}) %collective-permute-start.23) | collective-permute-done | bytes 262176 | tf_op jit(solution)/shard_map/ppermute | solution.py:553
  (127 shorter events, 31.0 us)
Async XLA Ops:
  3.8 13.1 %collective-permute-start.3 = (f32[256,128]{1,0:T(8,128)S(1)}, f32[256,128]{1,0:T(8,128)S(1)}, u32[]{:S(2)}, u32[]{:S(2)}) collective-permute-start(f32[256,128]{1,0:T(8,128)S(1)} %get-tuple-element.33), channel_id=1, source_target_pairs={{0,28},{4,0},{8,4},{12,8},{16,12},{20,16},{24,20},{28,24},{1,29},{... | collective-permute-start | bytes 393224 | tf_op jit(solution)/shard_map/ppermute | solution.py:558
  17.5 2.4 %collective-permute-start.4 = (f32[2,392,256]{2,1,0:T(8,128)S(1)}, f32[2,392,256]{2,1,0:T(8,128)S(1)}, u32[]{:S(2)}, u32[]{:S(2)}) collective-permute-start(f32[2,392,256]{2,1,0:T(8,128)S(1)} %get-tuple-element.37), channel_id=1, source_target_pairs={{0,1},{1,0},{2,3},{3,2},{4,5},{5,4},{6,7},{7,6},{8,9},{9,8},{10,11... | collective-permute-start | bytes 2408456 | tf_op jit(solution)/shard_map/ppermute | solution.py:553
  17.6 9.2 %collective-permute-start = (f32[2,256,128]{2,1,0:T(8,128)S(1)}, f32[2,256,128]{2,1,0:T(8,128)S(1)}, u32[]{:S(2)}, u32[]{:S(2)}) collective-permute-start(f32[2,256,128]{2,1,0:T(8,128)S(1)} %get-tuple-element.30), channel_id=1, source_target_pairs={{0,4},{4,0},{8,12},{12,8},{16,20},{20,16},{24,28},{28,24},{1,5},{5... | collective-permute-start | bytes 786440 | tf_op jit(solution)/shard_map/ppermute | solution.py:553
  20.0 11.4 %collective-permute-start.5 = (f32[1,392,256]{2,1,0:T(8,128)S(1)}, f32[1,392,256]{2,1,0:T(8,128)S(1)}, u32[]{:S(2)}, u32[]{:S(2)}) collective-permute-start(f32[1,392,256]{2,1,0:T(8,128)S(1)} %get-tuple-element.39), channel_id=1, source_target_pairs={{0,2},{1,3},{2,0},{3,1},{4,6},{5,7},{6,4},{7,5},{8,10},{9,11},{10,... | collective-permute-start | bytes 1204232 | tf_op jit(solution)/shard_map/ppermute | solution.py:553
  21.6 10.4 %collective-permute-start.2 = (f32[2,256,128]{2,1,0:T(8,128)}, f32[2,256,128]{2,1,0:T(8,128)S(1)}, u32[]{:S(2)}, u32[]{:S(2)}) collective-permute-start(f32[2,256,128]{2,1,0:T(8,128)} %get-tuple-element.31), channel_id=1, source_target_pairs={{0,4},{4,0},{8,12},{12,8},{16,20},{20,16},{24,28},{28,24},{1,5},{5... | collective-permute-start | bytes 786440 | tf_op jit(solution)/shard_map/ppermute | solution.py:553
  27.8 7.5 %collective-permute-start.1 = (f32[2,256,128]{2,1,0:T(8,128)S(1)}, f32[2,256,128]{2,1,0:T(8,128)S(1)}, u32[]{:S(2)}, u32[]{:S(2)}) collective-permute-start(f32[2,256,128]{2,1,0:T(8,128)S(1)} %shard_map.65.refs_0_.old), channel_id=1, source_target_pairs={{0,24},{4,28},{8,0},{12,4},{16,8},{20,12},{24,16},{28,20},{1,25},{... | collective-permute-start | bytes 786440 | tf_op jit(solution)/shard_map/ppermute | solution.py:558
  31.5 37.8 %copy-start.18 = (f32[1,392,256]{2,1,0:T(8,128)}, f32[1,392,256]{2,1,0:T(8,128)S(1)}, u32[]{:S(2)}) copy-start(f32[1,392,256]{2,1,0:T(8,128)S(1)} %shard_map.69.refs_0_) | copy-start | bytes 1204228
  35.2 9.6 %collective-permute-start.7 = (f32[1,392,256]{2,1,0:T(8,128)S(1)}, f32[1,392,256]{2,1,0:T(8,128)}, u32[]{:S(2)}, u32[]{:S(2)}) collective-permute-start(f32[1,392,256]{2,1,0:T(8,128)S(1)} %shard_map.69.refs_0_), channel_id=1, source_target_pairs={{0,2},{1,3},{2,0},{3,1},{4,6},{5,7},{6,4},{7,5},{8,10},{9,11},{10,... | collective-permute-start | bytes 1204232 | tf_op jit(solution)/shard_map/ppermute | solution.py:553
  36.7 12.4 %collective-permute-start.8 = (f32[1,392,256]{2,1,0:T(8,128)S(1)}, f32[1,392,256]{2,1,0:T(8,128)}, u32[]{:S(2)}, u32[]{:S(2)}) collective-permute-start(f32[1,392,256]{2,1,0:T(8,128)S(1)} %shard_map.69.refs_0_), channel_id=1, source_target_pairs={{0,4},{4,0},{8,12},{12,8},{16,20},{20,16},{24,28},{28,24},{1,5},{5... | collective-permute-start | bytes 1204232 | tf_op jit(solution)/shard_map/ppermute | solution.py:553
  44.9 12.6 %collective-permute-start.15 = (f32[1,392,256]{2,1,0:T(8,128)S(1)}, f32[1,392,256]{2,1,0:T(8,128)S(1)}, u32[]{:S(2)}, u32[]{:S(2)}) collective-permute-start(f32[1,392,256]{2,1,0:T(8,128)S(1)} %broadcast_select_fusion), channel_id=1, source_target_pairs={{0,24},{2,26},{5,13},{7,15},{8,0},{10,2},{13,21},{15,23},{16,8},{1... | collective-permute-start | bytes 1204232 | tf_op jit(solution)/shard_map/ppermute | solution.py:615
  49.1 18.7 %collective-permute-start.12 = (f32[2,256,256]{2,1,0:T(8,128)S(1)}, f32[2,256,256]{2,1,0:T(8,128)S(1)}, u32[]{:S(2)}, u32[]{:S(2)}) collective-permute-start(f32[2,256,256]{2,1,0:T(8,128)S(1)} %copy-done.28), channel_id=1, source_target_pairs={{0,4},{4,0},{8,12},{12,8},{16,20},{20,16},{24,28},{28,24},{1,5},{5... | collective-permute-start | bytes 1572872 | tf_op jit(solution)/shard_map/ppermute | solution.py:553
  49.1 19.1 %collective-permute-start.13 = (f32[1,392,256]{2,1,0:T(8,128)}, f32[1,392,256]{2,1,0:T(8,128)}, u32[]{:S(2)}, u32[]{:S(2)}) collective-permute-start(f32[1,392,256]{2,1,0:T(8,128)} %collective-permute-done.8.refs_3_), channel_id=1, source_target_pairs={{0,2},{1,3},{2,0},{3,1},{4,6},{5,7},{6,4},{7,5},{8,10},{9,11},{10,... | collective-permute-start | bytes 1204232 | tf_op jit(solution)/shard_map/ppermute | solution.py:553
  57.4 10.9 %collective-permute-start.16 = (f32[1,392,256]{2,1,0:T(8,128)S(1)}, f32[1,392,256]{2,1,0:T(8,128)S(1)}, u32[]{:S(2)}, u32[]{:S(2)}) collective-permute-start(f32[1,392,256]{2,1,0:T(8,128)S(1)} %collective-permute-done.15.first_ref), channel_id=1, source_target_pairs={{0,4},{2,6},{5,1},{7,3},{8,12},{10,14},{13,9},{15,11},{16,20},{18,... | collective-permute-start | bytes 1204232 | tf_op jit(solution)/shard_map/ppermute | solution.py:616
  59.7 8.0 %collective-permute-start.11 = (f32[2,256,128]{2,1,0:T(8,128)S(1)}, f32[2,256,128]{2,1,0:T(8,128)S(1)}, u32[]{:S(2)}, u32[]{:S(2)}) collective-permute-start(f32[2,256,128]{2,1,0:T(8,128)S(1)} %shard_map.70.refs_1_.old), channel_id=1, source_target_pairs={{0,24},{4,28},{8,0},{12,4},{16,8},{20,12},{24,16},{28,20},{1,25},{... | collective-permute-start | bytes 786440 | tf_op jit(solution)/shard_map/ppermute | solution.py:558
  64.5 6.3 %collective-permute-start.6 = (f32[1,392,256]{2,1,0:T(8,128)S(1)}, f32[1,392,256]{2,1,0:T(8,128)}, u32[]{:S(2)}, u32[]{:S(2)}) collective-permute-start(f32[1,392,256]{2,1,0:T(8,128)S(1)} %shard_map.69.refs_0_), channel_id=1, source_target_pairs={{0,1},{1,0},{2,3},{3,2},{4,5},{5,4},{6,7},{7,6},{8,9},{9,8},{10,11... | collective-permute-start | bytes 1204232 | tf_op jit(solution)/shard_map/ppermute | solution.py:553
  67.7 3.1 %collective-permute-start.10 = (f32[1,392,256]{2,1,0:T(8,128)}, f32[1,392,256]{2,1,0:T(8,128)}, u32[]{:S(2)}, u32[]{:S(2)}) collective-permute-start(f32[1,392,256]{2,1,0:T(8,128)} %collective-permute-done.8.refs_3_), channel_id=1, source_target_pairs={{0,1},{1,0},{2,3},{3,2},{4,5},{5,4},{6,7},{7,6},{8,9},{9,8},{10,11... | collective-permute-start | bytes 1204232 | tf_op jit(solution)/shard_map/ppermute | solution.py:553
  67.7 3.1 %collective-permute-start.9 = (f32[1,392,256]{2,1,0:T(8,128)}, f32[1,392,256]{2,1,0:T(8,128)S(1)}, u32[]{:S(2)}, u32[]{:S(2)}) collective-permute-start(f32[1,392,256]{2,1,0:T(8,128)} %collective-permute-done.7.refs_2_), channel_id=1, source_target_pairs={{0,1},{1,0},{2,3},{3,2},{4,5},{5,4},{6,7},{7,6},{8,9},{9,8},{10,11... | collective-permute-start | bytes 1204232 | tf_op jit(solution)/shard_map/ppermute | solution.py:553
  68.2 2.7 %collective-permute-start.14 = (f32[1,392,256]{2,1,0:T(8,128)}, f32[1,392,256]{2,1,0:T(8,128)}, u32[]{:S(2)}, u32[]{:S(2)}) collective-permute-start(f32[1,392,256]{2,1,0:T(8,128)} %collective-permute-done.13.refs_6_), channel_id=1, source_target_pairs={{0,1},{1,0},{2,3},{3,2},{4,5},{5,4},{6,7},{7,6},{8,9},{9,8},{10,11... | collective-permute-start | bytes 1204232 | tf_op jit(solution)/shard_map/ppermute | solution.py:553
  69.2 5.2 %collective-permute-start.17 = (f32[1,392,256]{2,1,0:T(8,128)}, f32[1,392,256]{2,1,0:T(8,128)}, u32[]{:S(2)}, u32[]{:S(2)}) collective-permute-start(f32[1,392,256]{2,1,0:T(8,128)} %add.27), channel_id=1, source_target_pairs={{0,1},{1,0},{2,3},{3,2},{4,5},{5,4},{6,7},{7,6},{8,9},{9,8},{10,11... | collective-permute-start | bytes 1204232 | tf_op jit(solution)/shard_map/ppermute | solution.py:553
  74.4 34.7 %copy-start = (bf16[8,256,768]{2,1,0:T(8,128)(2,1)}, bf16[8,256,768]{2,1,0:T(8,128)(2,1)S(1)}, u32[]{:S(2)}) copy-start(bf16[8,256,768]{2,1,0:T(8,128)(2,1)S(1)} %get-tuple-element.44.low.low_in) | copy-start | bytes 9437188
  76.2 32.9 %copy-start.9 = (bf16[2,256,768]{2,1,0:T(8,128)(2,1)}, bf16[2,256,768]{2,1,0:T(8,128)(2,1)S(1)}, u32[]{:S(2)}) copy-start(bf16[2,256,768]{2,1,0:T(8,128)(2,1)S(1)} %get-tuple-element.47.high_outer) | copy-start | bytes 2359300
  76.3 32.9 %copy-start.11 = (bf16[2,256,768]{2,1,0:T(8,128)(2,1)}, bf16[2,256,768]{2,1,0:T(8,128)(2,1)S(1)}, u32[]{:S(2)}) copy-start(bf16[2,256,768]{2,1,0:T(8,128)(2,1)S(1)} %get-tuple-element.48.low_outer) | copy-start | bytes 2359300
  77.6 11.6 %collective-permute-start.19 = (f32[2,256,128]{2,1,0:T(8,128)}, f32[2,256,128]{2,1,0:T(8,128)S(1)}, u32[]{:S(2)}, u32[]{:S(2)}) collective-permute-start(f32[2,256,128]{2,1,0:T(8,128)} %shard_map.76.refs_1_.old), channel_id=1, source_target_pairs={{0,8},{4,12},{8,16},{12,20},{16,24},{20,28},{24,0},{28,4},{1,9},{5... | collective-permute-start | bytes 786440 | tf_op jit(solution)/shard_map/ppermute | solution.py:558
  79.0 15.9 %collective-permute-start.18 = (f32[2,256,128]{2,1,0:T(8,128)}, f32[2,256,128]{2,1,0:T(8,128)S(1)}, u32[]{:S(2)}, u32[]{:S(2)}) collective-permute-start(f32[2,256,128]{2,1,0:T(8,128)} %shard_map.75.refs_0_.old), channel_id=1, source_target_pairs={{0,8},{4,12},{8,16},{12,20},{16,24},{20,28},{24,0},{28,4},{1,9},{5... | collective-permute-start | bytes 786440 | tf_op jit(solution)/shard_map/ppermute | solution.py:558
  89.8 16.8 %collective-permute-start.24 = (f32[2,256,128]{2,1,0:T(8,128)S(1)}, f32[2,256,128]{2,1,0:T(8,128)S(1)}, u32[]{:S(2)}, u32[]{:S(2)}) collective-permute-start(f32[2,256,128]{2,1,0:T(8,128)S(1)} %shard_map.79.refs_1_.old), channel_id=1, source_target_pairs={{0,24},{4,28},{8,0},{12,4},{16,8},{20,12},{24,16},{28,20},{1,25},{... | collective-permute-start | bytes 786440 | tf_op jit(solution)/shard_map/ppermute | solution.py:558
  95.5 13.7 %collective-permute-start.20 = (f32[2,256,128]{2,1,0:T(8,128)S(1)}, f32[2,256,128]{2,1,0:T(8,128)S(1)}, u32[]{:S(2)}, u32[]{:S(2)}) collective-permute-start(f32[2,256,128]{2,1,0:T(8,128)S(1)} %shard_map.78.refs_0_.old), channel_id=1, source_target_pairs={{0,24},{4,28},{8,0},{12,4},{16,8},{20,12},{24,16},{28,20},{1,25},{... | collective-permute-start | bytes 786440 | tf_op jit(solution)/shard_map/ppermute | solution.py:558
  109.2 18.3 %collective-permute-start.26 = (f32[2,256,128]{2,1,0:T(8,128)}, f32[2,256,128]{2,1,0:T(8,128)}, u32[]{:S(2)}, u32[]{:S(2)}) collective-permute-start(f32[2,256,128]{2,1,0:T(8,128)} %shard_map.84.refs_0_), channel_id=1, source_target_pairs={{0,8},{4,12},{8,16},{12,20},{16,24},{20,28},{24,0},{28,4},{1,9},{5... | collective-permute-start | bytes 786440 | tf_op jit(solution)/shard_map/ppermute | solution.py:558
  111.5 19.3 %collective-permute-start.22 = (f32[2,256,128]{2,1,0:T(8,128)}, f32[2,256,128]{2,1,0:T(8,128)}, u32[]{:S(2)}, u32[]{:S(2)}) collective-permute-start(f32[2,256,128]{2,1,0:T(8,128)} %shard_map.81.refs_0_), channel_id=1, source_target_pairs={{0,8},{4,12},{8,16},{12,20},{16,24},{20,28},{24,0},{28,4},{1,9},{5... | collective-permute-start | bytes 786440 | tf_op jit(solution)/shard_map/ppermute | solution.py:558
  130.7 9.3 %collective-permute-start.25 = (f32[2,256,128]{2,1,0:T(8,128)S(1)}, f32[2,256,128]{2,1,0:T(8,128)S(1)}, u32[]{:S(2)}, u32[]{:S(2)}) collective-permute-start(f32[2,256,128]{2,1,0:T(8,128)S(1)} %get-tuple-element.56), channel_id=1, source_target_pairs={{0,4},{4,0},{8,12},{12,8},{16,20},{20,16},{24,28},{28,24},{1,5},{5... | collective-permute-start | bytes 786440 | tf_op jit(solution)/shard_map/ppermute | solution.py:553
  132.5 13.1 %collective-permute-start.21 = (f32[2,256,128]{2,1,0:T(8,128)S(1)}, f32[2,256,128]{2,1,0:T(8,128)S(1)}, u32[]{:S(2)}, u32[]{:S(2)}) collective-permute-start(f32[2,256,128]{2,1,0:T(8,128)S(1)} %get-tuple-element.58), channel_id=1, source_target_pairs={{0,4},{4,0},{8,12},{12,8},{16,20},{20,16},{24,28},{28,24},{1,5},{5... | collective-permute-start | bytes 786440 | tf_op jit(solution)/shard_map/ppermute | solution.py:553
  140.0 11.2 %collective-permute-start.27 = (f32[2,256,128]{2,1,0:T(8,128)S(1)}, f32[2,256,128]{2,1,0:T(8,128)S(1)}, u32[]{:S(2)}, u32[]{:S(2)}) collective-permute-start(f32[2,256,128]{2,1,0:T(8,128)S(1)} %get-tuple-element.52), channel_id=1, source_target_pairs={{0,4},{4,0},{8,12},{12,8},{16,20},{20,16},{24,28},{28,24},{1,5},{5... | collective-permute-start | bytes 786440 | tf_op jit(solution)/shard_map/ppermute | solution.py:553
  145.6 9.2 %collective-permute-start.23 = (f32[2,256,128]{2,1,0:T(8,128)S(1)}, f32[2,256,128]{2,1,0:T(8,128)S(1)}, u32[]{:S(2)}, u32[]{:S(2)}) collective-permute-start(f32[2,256,128]{2,1,0:T(8,128)S(1)} %get-tuple-element.51), channel_id=1, source_target_pairs={{0,4},{4,0},{8,12},{12,8},{16,20},{20,16},{24,28},{28,24},{1,5},{5... | collective-permute-start | bytes 786440 | tf_op jit(solution)/shard_map/ppermute | solution.py:553
  (29 other events, 151.9 us)

commit v6 on v5

v6 whole, which is shorter than its diff:
```python
import functools

import jax
import jax.numpy as jnp
from jax import lax
from jax.experimental import pallas as pl
from jax.experimental.pallas import tpu as pltpu
from jax.sharding import PartitionSpec as P

NB = 256
DEG = 4

penalty = 3.0
center = 4.0
half_width = 12.0

PARAMS = pltpu.CompilerParams(vmem_limit_bytes=12 * 1024 * 1024)
SCALARS = pl.BlockSpec(memory_space=pltpu.SMEM)
ANY = pl.BlockSpec(memory_space=pl.ANY)


def near_core(shape, dtype=jnp.float32):
    return pltpu.VMEM(shape, dtype)


def far_off(value):
    return pltpu.with_memory_space_constraint(value, pltpu.MemorySpace.HBM)


def close_by(value):
    return pltpu.with_memory_space_constraint(value, pltpu.MemorySpace.VMEM)
VMEM = pl.BlockSpec(memory_space=pltpu.VMEM)
NN = (((1,), (0,)), ((), ()))
NT = (((1,), (1,)), ((), ()))


def split(value):
    high = value.astype(jnp.bfloat16)
    low = (value - high.astype(jnp.float32)).astype(jnp.bfloat16)
    return high, low


def dot(first, second, dims=NN):
    return lax.dot_general(first, second, dims, preferred_element_type=jnp.float32)


def dot3(first, second, dims=NN):
    first_high, first_low = first
    second_high, second_low = second
    return dot(first_high, second_high, dims) + (dot(first_high, second_low, dims) + dot(first_low, second_high, dims))


def picked(parts, chosen):
    return dot(parts[0], chosen) + dot(parts[1], chosen)


def one_hot(index_row, rows, offset=0):
    at = lax.broadcasted_iota(jnp.int32, (rows, index_row.shape[1]), 0) - offset
    return (at == index_row).astype(jnp.float32).astype(jnp.bfloat16)


def lead_kernel(at_ref, index_ref, basis_ref, vector_ref, traces_ref, *rest):
    cut_refs, (held, sems) = rest[:-2], rest[-2:]
    first = pltpu.make_async_copy(basis_ref.at[0], held, sems.at[0])
    first.start()
    copies = []
    for at, out_ref in enumerate(cut_refs):
        source = own_columns(vector_ref, 1 - at_ref[0], 2 * at, out_ref.shape[2])
        copies.append(pltpu.make_async_copy(source, out_ref, sems.at[1 + at]))
        copies[-1].start()
    first.wait()
    traces_ref[...] = picked(split(held[...].T), one_hot(index_ref[0], held.shape[0]))
    for copy in copies:
        copy.wait()


def blocks_kernel(
    faces_total, at_ref, index_ref, quad_ref, pair_ref, basis_ref, applied_ref, send_ref, keep_ref, last_ref, held, acted, traces, sems
):
    count = basis_ref.shape[0]
    size = basis_ref.shape[2]
    half = size // 2
    core = at_ref[1]

    def copies(at):
        return (
            pltpu.make_async_copy(basis_ref.at[at], held.at[at], sems.at[2 * at]),
            pltpu.make_async_copy(applied_ref.at[at], acted.at[at], sems.at[2 * at + 1]),
        )

    for at in range(count):
        for copy in copies(at):
            copy.start()

    def store(element, rows, value):
        @pl.when(element // (count // 2) == core)
        def _():
            keep_ref[element % (count // 2), rows] = value

        @pl.when(element // (count // 2) != core)
        def _():
            send_ref[element % (count // 2), rows] = value

    @pl.loop(0, count)
    def _(at):
        for copy in copies(at):
            copy.wait()
        turned = held[at].T
        found = picked(split(turned), one_hot(index_ref[at], held.shape[1]))
        traces[at] = found
        width = found.shape[1] // 2
        outer, layer = found[:, :width], found[:, width:]
        total = dot3(split(turned * quad_ref[at]), split(acted[at]))
        total = total + dot3(split((2.0 * outer + layer) * (1.0 / faces_total)), split(outer), NT)
        mixed, side, diagonal = packed(0.5 * (total + total.T))
        store(at, slice(size, size + half), jnp.concatenate([mixed, side], axis=1))
        store(at, slice(size + half, None), jnp.broadcast_to(jnp.concatenate([diagonal, diagonal], axis=1), (8, size)))

    @pl.loop(0, count - 1)
    def _(at):
        following = traces[at + 1]
        width = following.shape[1] // 2
        order = one_hot(pair_ref[at], width)
        face, inside = picked(split(following[:, :width]), order), picked(split(following[:, width:]), order)
        store(at, slice(0, size), coupled(traces[at], face, inside, faces_total))

    last_ref[...] = traces[count - 1]


def coupled(own, face, inside, faces_total):
    width = own.shape[1] // 2
    outer, layer = own[:, :width], own[:, width:]
    near = split((penalty * outer + 0.5 * layer) * (-1.0 / faces_total))
    far = split(outer * (0.5 / faces_total))
    return dot3(near, split(face), NT) + dot3(far, split(inside), NT)


def last_kernel(faces_total, at_ref, pair_ref, own_ref, lead_ref, send_in, keep_in, send_ref, keep_ref, block, sem):
    width = own_ref.shape[1] // 2
    lead = split(lead_ref[...])
    face = picked(lead, one_hot(pair_ref[...], width))
    inside = picked(lead, one_hot(pair_ref[...], width, width // 2))
    block[...] = coupled(own_ref[...], face, inside, faces_total)
    at = send_ref.shape[0] - 1
    rows = pl.ds(0, block.shape[0])
    for core, ref in ((0, send_ref), (1, keep_ref)):

        @pl.when(at_ref[1] == core)
        def _():
            copy = pltpu.make_async_copy(block, ref.at[at, rows], sem)
            copy.start()
            copy.wait()


def packed(volume):
    half = volume.shape[0] // 2
    row = lax.broadcasted_iota(jnp.int32, (half, half), 0)
    column = lax.broadcasted_iota(jnp.int32, (half, half), 1)
    corner = volume[half:, half:]
    mixed = jnp.where(column >= row, volume[:half, :half], corner)
    diagonal = jnp.sum(jnp.where(column == row, corner, 0.0), axis=0, keepdims=True)
    return mixed, volume[:half, half:], diagonal


def unpacked(mixed, side, diagonal):
    half = mixed.shape[0]
    row = lax.broadcasted_iota(jnp.int32, (half, half), 0)
    column = lax.broadcasted_iota(jnp.int32, (half, half), 1)
    turned = mixed.T
    first = jnp.where(column >= row, mixed, turned)
    corner = jnp.where(column < row, mixed, jnp.where(column == row, diagonal, turned))
    top = jnp.concatenate([first, side], axis=1)
    return jnp.concatenate([top, jnp.concatenate([side.T, corner], axis=1)], axis=0)


def weights_kernel(at_ref, *refs):
    sources, (high_ref, low_ref), held, sems = refs[:8], refs[8:10], refs[10], refs[11]
    me = at_ref[3]
    size = held.shape[2]
    half = size // 2
    away_at = (0, 2, 1, 4, 3, 6, 5, 7)
    copies = [pltpu.make_async_copy(source.at[0], held.at[n], sems.at[n]) for n, source in enumerate(sources)]
    for copy in copies:
        copy.start()
    row = lax.broadcasted_iota(jnp.int32, (size, size), 0)
    diagonal = row == lax.broadcasted_iota(jnp.int32, (size, size), 1)

    for n, away in enumerate(away_at):
        copies[n].wait()
        element = away ^ me
        following = lax.rem(element + 1, len(away_at))
        volume, coupling = scaled(held[n], diagonal)
        for place, at, value in ((following, 0, coupling.T), (element, 1, volume), (element, 2, coupling)):
            high_ref[place, :, at * size : (at + 1) * size], low_ref[place, :, at * size : (at + 1) * size] = split(value)


def scaled(block, diagonal):
    size = block.shape[1]
    half = size // 2
    volume = unpacked(block[size : size + half, :half], block[size : size + half, half:], block[size + half : size + half + 1, :half])
    return (volume - jnp.where(diagonal, center, 0.0)) * (1.0 / half_width), block[:size] * (1.0 / half_width)


def outer_kernel(at_ref, kept_ref, swapped_ref, high_in, low_in, high_ref, low_ref):
    size = kept_ref.shape[2]
    rows = kept_ref.shape[1] - size
    row = lax.broadcasted_iota(jnp.int32, (size, size), 0)
    diagonal = row == lax.broadcasted_iota(jnp.int32, (size, size), 1)
    lower = at_ref[1] == 1
    below = jnp.where(lower, kept_ref[0], swapped_ref[0])
    volume, coupling = scaled(below[:rows], diagonal)
    turned = coupling.T
    for at, value in enumerate(((below[rows:] * (1.0 / half_width)).T, volume, coupling)):
        high_ref[0, :, at * size : (at + 1) * size], low_ref[0, :, at * size : (at + 1) * size] = split(value)
    high_ref[1, :, :size], low_ref[1, :, :size] = split(turned)
    high_ref[1, :, size:] = high_in[0, :, size:]
    low_ref[1, :, size:] = low_in[0, :, size:]
    volume, coupling = scaled(jnp.where(lower, swapped_ref[0, :rows], kept_ref[0, :rows]), diagonal)
    last = high_in.shape[0] - 1
    turned = (high_in[last, :, 2 * size :].astype(jnp.float32) + low_in[last, :, 2 * size :].astype(jnp.float32)).T
    for at, value in enumerate((turned, volume, coupling)):
        high_ref[2, :, at * size : (at + 1) * size], low_ref[2, :, at * size : (at + 1) * size] = split(value)


def held_shape(rows, columns):
    return (rows, 2 * columns) if columns % 128 == 0 else (2, rows, columns)


def hold(held, at, value):
    high, low = split(value)
    size, columns = value.shape
    rows = slice(at * size, (at + 1) * size)
    if len(held.shape) == 2:
        held[rows, :columns] = high
        held[rows, columns:] = low
    else:
        held[0, rows] = high
        held[1, rows] = low


def apply_row(high, low, held, start, columns):
    rows = pl.ds(start, high.shape[1])
    if len(held.shape) == 2:
        if columns == 128:
            both = dot(high, held[rows, :])
            total = both[:, :columns] + both[:, columns:]
        else:
            total = dot(high, held[rows, :columns]) + dot(high, held[rows, columns:])
        return total + dot(low, held[rows, :columns])
    return dot(high, held[0, rows]) + (dot(high, held[1, rows]) + dot(low, held[0, rows]))


def hold_all(held, values):
    for at, value in enumerate(values):
        hold(held, at, value)


def first_kernel(high, low, y0, above, y1, held):
    count, size, columns = y0.shape
    hold_all(held, [y0[at] for at in range(count)] + [above[0]])

    @pl.loop(0, count - 1)
    def _(at):
        y1[at] = apply_row(high[at + 1], low[at + 1], held, pl.multiple_of(at * size, size), columns)


def second_kernel(chunks, high, low, outer_high, outer_low, y0, below, above, y1, y1_ends, *refs):
    outs, held = refs[:-1], refs[-1]
    count, size, columns = y0.shape
    row = lambda weight, start: apply_row(*weight, held, start * size, columns)
    outer = lambda at: (outer_high[at], outer_low[at])
    main = lambda at: (high[at], low[at])
    hold_all(held, (below[0], below[1], y0[0], y0[1], y0[count - 1], above[0], above[1]))
    y1_ends[0] = row(outer(0), 0)
    y1_ends[1] = row(outer(1), 1)
    y1_ends[2] = row(outer(2), 4)
    hold_all(held, (y1_ends[0], y1_ends[1], y1[0], y1[1], y1[count - 4], y1[count - 3], y1[count - 2], y1_ends[2]))
    width = columns // chunks
    for out_at, at, weight, start, element in (
        (0, 0, outer(1), 0, 0),
        (0, 1, main(1), 1, 1),
        (1, 0, main(count - 2), 4, count - 2),
        (1, 1, main(count - 1), 5, count - 1),
    ):
        value = 2.0 * row(weight, start) - y0[element]
        for chunk in range(chunks):
            outs[out_at * chunks + chunk][at] = value[:, chunk * width : (chunk + 1) * width]


def middle_kernel(chunks, at_ref, high, low, y0, y1, *refs):
    ends, (y3_kept, y4, send, held, y2, y3) = refs[: 2 * chunks], refs[2 * chunks :]
    count, size, columns = y0.shape
    row = lambda place, at: apply_row(high[place], low[place], held, pl.multiple_of(at * size, size), columns)
    hold_all(held, [y1[at] for at in range(count - 2)])

    @pl.loop(0, count - 4)
    def _(at):
        y2[at] = 2.0 * row(at + 2, at) - y0[at + 2]

    joined = lambda group, at: jnp.concatenate([end[at] for end in ends[group * chunks : (group + 1) * chunks]], axis=1)
    hold_all(held, [joined(0, 0), joined(0, 1)] + [y2[at] for at in range(count - 4)] + [joined(1, 0), joined(1, 1)])

    @pl.loop(0, count - 2)
    def _(at):
        y3[at] = 2.0 * row(at + 1, at) - y1[at]

    hold_all(held, [y3[at] for at in range(count - 2)])

    @pl.loop(0, count - 4)
    def _(at):
        y4[at] = 2.0 * row(at + 2, at) - y2[at]

    send[...] = y4[pl.ds((1 - at_ref[0]) * 2, 2)]
    for at, place in enumerate((0, 1, count - 4, count - 3)):
        y3_kept[at] = y3[place]


def last_rows_kernel(
    lane, at_ref, high, low, outer_high, outer_low, y1, y1_ends, y3, y2_low, y2_high, below, above, y4_low, y4_high, send, held
):
    size, columns = below.shape[1:]
    count = high.shape[0]
    lanes = slice(lane, lane + columns)
    row = lambda weight, start: apply_row(*weight, held, start * size, columns)
    outer = lambda at: (outer_high[at], outer_low[at])
    main = lambda at: (high[at], low[at])
    hold_all(held, (below[0], below[1], y2_low[0], y2_low[1], y2_high[0], y2_high[1], above[0], above[1]))
    lower = 2.0 * row(outer(0), 0) - y1_ends[0, :, lanes]
    low_own = 2.0 * row(outer(1), 1) - y1_ends[1, :, lanes]
    high_own = 2.0 * row(main(count - 1), 4) - y1[count - 2, :, lanes]
    upper = 2.0 * row(outer(2), 5) - y1_ends[2, :, lanes]
    hold_all(held, (lower, low_own, y3[0, :, lanes], y3[1, :, lanes], y3[2, :, lanes], y3[3, :, lanes], high_own, upper))
    y4_low[0] = 2.0 * row(outer(1), 0) - y2_low[0]
    y4_low[1] = 2.0 * row(main(1), 1) - y2_low[1]
    y4_high[0] = 2.0 * row(main(count - 2), 4) - y2_high[0]
    y4_high[1] = 2.0 * row(main(count - 1), 5) - y2_high[1]
    send[...] = jnp.where(at_ref[0] == 0, y4_high[...], y4_low[...])


def fold_kernel(at_ref, keep_ref, other_ref, send_ref, stay_ref):
    lane = at_ref[2]
    half = keep_ref.shape[0] // 2
    for at in range(half):
        send_ref[at] = keep_ref[(1 - lane) * half + at] + other_ref[(1 - lane) * half + at]
        stay_ref[at] = keep_ref[lane * half + at] + other_ref[lane * half + at]


def outer_block_kernel(at_ref, mine_ref, beside_ref, out_ref, sems):
    rows, size = mine_ref.shape[1:]

    def moved(act):
        for wanted, outer, other in ((True, mine_ref, beside_ref), (False, beside_ref, mine_ref)):

            @pl.when((at_ref[1] == at_ref[2]) == wanted)
            def _():
                act(pltpu.make_async_copy(outer.at[0], out_ref.at[0, pl.ds(0, rows)], sems.at[0]))
                act(pltpu.make_async_copy(other.at[0, pl.ds(0, size)], out_ref.at[0, pl.ds(rows, size)], sems.at[1]))

    moved(lambda copy: copy.start())
    moved(lambda copy: copy.wait())


def sum_kernel(first_ref, second_ref, out_ref):
    out_ref[...] = first_ref[...] + second_ref[...]


def copy_pairs(side, pairs, sems):
    def moved(act):
        for at, (wanted, source, target) in enumerate(pairs):

            @pl.when(side == wanted)
            def _():
                act(pltpu.make_async_copy(source, target, sems.at[at]))

    moved(lambda copy: copy.start())
    moved(lambda copy: copy.wait())


def own_columns(vector_ref, half, element, width, count=2):
    if vector_ref.shape[2] == width:
        return vector_ref.at[pl.ds(element, count)]
    return vector_ref.at[pl.ds(element, count), :, pl.ds(pl.multiple_of(half * width, width), width)]


def arrange_pair_kernel(element, wanted, at_ref, vector_ref, got_ref, out_ref, sems):
    own = own_columns(vector_ref, at_ref[0], element, got_ref.shape[2])
    copy_pairs(at_ref[0], ((wanted, own, out_ref), (1 - wanted, got_ref, out_ref)), sems)


def arrange_kernel(at_ref, vector_ref, first_ref, second_ref, out_ref, sems):
    own = own_columns(vector_ref, at_ref[0], 0, first_ref.shape[2], 4)
    pairs = []
    for side in range(2):
        pairs.append((side, own, out_ref.at[pl.ds(4 * side, 4)]))
        pairs.append((side, first_ref, out_ref.at[pl.ds(4 - 4 * side, 2)]))
        pairs.append((side, second_ref, out_ref.at[pl.ds(6 - 4 * side, 2)]))
    copy_pairs(at_ref[0], pairs, sems)


def place_pairs(out_ref, sems, side, chunks, chunk, width, pairs):
    def moved(act):
        for at, (wanted, source, element, foreign) in enumerate(pairs):

            @pl.when(side == wanted)
            def _():
                part = 1 - side if foreign else side
                start = pl.multiple_of((part * chunks + chunk) * width, width)
                act(pltpu.make_async_copy(source, out_ref.at[pl.ds(element, 2), :, pl.ds(start, width)], sems.at[chunk, at]))

    return moved


def collect_kernel(at_ref, y4, near, out_ref, sems):
    pairs = (
        (0, y4.at[pl.ds(0, 2)], 2, False),
        (0, near, 2, True),
        (1, y4.at[pl.ds(2, 2)], 0, False),
        (1, near, 0, True),
    )
    act = place_pairs(out_ref, sems, at_ref[0], 1, 0, near.shape[2], pairs)
    act(lambda copy: copy.start())
    act(lambda copy: copy.wait())


def finish_kernel(chunks, at_ref, *refs):
    sources, out_ref, sems = refs[: 3 * chunks], refs[-2], refs[-1]
    acts = []
    for chunk in range(chunks):
        y4_low, y4_high, far = sources[3 * chunk : 3 * chunk + 3]
        pairs = ((0, y4_low, 0, False), (0, far, 0, True), (1, y4_high, 2, False), (1, far, 2, True))
        acts.append(place_pairs(out_ref, sems, at_ref[0], chunks, chunk, far.shape[2], pairs))
    for act in acts:
        act(lambda copy: copy.start())
    for act in acts:
        act(lambda copy: copy.wait())


def lead_and_cut(at, index, basis, vector, half):
    points, size = basis.shape[1:]
    return pl.pallas_call(
        lead_kernel,
        in_specs=[SCALARS, VMEM, ANY, ANY],
        out_specs=[VMEM] * 3,
        out_shape=[near_core((size, index.shape[2]))] + [near_core((2, size, half))] * 2,
        scratch_shapes=[pltpu.VMEM((points, size), jnp.float32), pltpu.SemaphoreType.DMA((3,))],
        compiler_params=PARAMS,
    )(at, index, far_off(basis), far_off(vector))


def blocks(core, index, quad, pairs, basis, applied, faces_total):
    count, points, size = basis.shape
    spots = index.shape[2]
    part = near_core((count // 2, size + size // 2 + 8, size))
    return pl.pallas_call(
        functools.partial(blocks_kernel, faces_total),
        in_specs=[SCALARS, VMEM, VMEM, VMEM, ANY, ANY],
        out_specs=[VMEM] * 3,
        out_shape=[part, part, near_core((size, spots))],
        scratch_shapes=[
            pltpu.VMEM((count, points, size), jnp.float32),
            pltpu.VMEM((count, points, size), jnp.float32),
            pltpu.VMEM((count, size, spots), jnp.float32),
            pltpu.SemaphoreType.DMA((2 * count,)),
        ],
        compiler_params=PARAMS,
    )(core, index, quad, pairs, far_off(basis), far_off(applied))


def last_coupling(core, pair, own, lead, send, keep, faces_total):
    size = own.shape[0]
    return pl.pallas_call(
        functools.partial(last_kernel, faces_total),
        in_specs=[SCALARS, VMEM, VMEM, VMEM, ANY, ANY],
        out_specs=[ANY] * 2,
        out_shape=[near_core(send.shape)] * 2,
        input_output_aliases={4: 0, 5: 1},
        scratch_shapes=[pltpu.VMEM((size, size), jnp.float32), pltpu.SemaphoreType.DMA],
        compiler_params=PARAMS,
    )(core, pair, own, lead, send, keep)


def weights(me, *parts):
    rows, size = parts[0].shape[1:]
    return pl.pallas_call(
        weights_kernel,
        in_specs=[SCALARS] + [ANY] * 8,
        out_specs=[VMEM] * 2,
        out_shape=[near_core((8, size, 3 * size), jnp.bfloat16)] * 2,
        scratch_shapes=[pltpu.VMEM((8, rows, size), jnp.float32), pltpu.SemaphoreType.DMA((8,))],
        compiler_params=PARAMS,
    )(me, *[far_off(part) for part in parts])


def outer_weights(at, kept, swapped, high, low):
    size = kept.shape[2]
    return pl.pallas_call(
        outer_kernel,
        in_specs=[SCALARS] + [VMEM] * 4,
        out_specs=[VMEM] * 2,
        out_shape=[near_core((3, size, 3 * size), jnp.bfloat16)] * 2,
        compiler_params=PARAMS,
    )(at, kept, swapped, high, low)


def first_rows(high, low, y0, above):
    count, size, columns = y0.shape
    return pl.pallas_call(
        first_kernel,
        in_specs=[VMEM] * 4,
        out_specs=VMEM,
        out_shape=near_core((count - 1, size, columns)),
        scratch_shapes=[pltpu.VMEM(held_shape((count + 1) * size, columns), jnp.bfloat16)],
        compiler_params=PARAMS,
    )(high, low, y0, above)


def second_rows(chunks, high, low, outer_high, outer_low, y0, below, above, y1):
    count, size, columns = y0.shape
    return pl.pallas_call(
        functools.partial(second_kernel, chunks),
        in_specs=[VMEM] * 8,
        out_specs=[VMEM] * (1 + 2 * chunks),
        out_shape=[near_core((3, size, columns))] + [near_core((2, size, columns // chunks))] * (2 * chunks),
        scratch_shapes=[pltpu.VMEM(held_shape(8 * size, columns), jnp.bfloat16)],
        compiler_params=PARAMS,
    )(high, low, outer_high, outer_low, y0, close_by(below), close_by(above), y1)


def middle_rows(at, chunks, high, low, y0, y1, ends):
    count, size, columns = y0.shape
    return pl.pallas_call(
        functools.partial(middle_kernel, chunks),
        in_specs=[SCALARS] + [VMEM] * (4 + 2 * chunks),
        out_specs=[VMEM] * 3,
        out_shape=[near_core((4, size, columns)), near_core((count - 4, size, columns)), near_core((2, size, columns))],
        scratch_shapes=[
            pltpu.VMEM(held_shape(count * size, columns), jnp.bfloat16),
            pltpu.VMEM((count - 4, size, columns), jnp.float32),
            pltpu.VMEM((count - 2, size, columns), jnp.float32),
        ],
        compiler_params=PARAMS,
    )(at, high, low, y0, y1, *ends)


def last_rows(at, lane, high, low, outer_high, outer_low, y1, y1_ends, y3, y2_low, y2_high, below, above):
    size, columns = below.shape[1:]
    return pl.pallas_call(
        functools.partial(last_rows_kernel, lane),
        in_specs=[SCALARS] + [VMEM] * 11,
        out_specs=[VMEM] * 3,
        out_shape=[near_core(below.shape)] * 3,
        scratch_shapes=[pltpu.VMEM(held_shape(8 * size, columns), jnp.bfloat16)],
        compiler_params=PARAMS,
    )(at, high, low, outer_high, outer_low, y1, y1_ends, y3, y2_low, y2_high, close_by(below), close_by(above))


def folded(lane, keep, other):
    shape = (keep.shape[0] // 2, *keep.shape[1:])
    return pl.pallas_call(
        fold_kernel,
        in_specs=[SCALARS, VMEM, VMEM],
        out_specs=[VMEM] * 2,
        out_shape=[near_core(shape)] * 2,
        compiler_params=PARAMS,
    )(lane, keep, close_by(other))


def outer_block(at, mine, beside):
    return pl.pallas_call(
        outer_block_kernel,
        in_specs=[SCALARS, ANY, ANY],
        out_specs=VMEM,
        out_shape=near_core((1, mine.shape[1] + mine.shape[2], mine.shape[2])),
        scratch_shapes=[pltpu.SemaphoreType.DMA((2,))],
        compiler_params=PARAMS,
    )(at, mine, beside)


def added(first, second):
    return pl.pallas_call(
        sum_kernel, in_specs=[VMEM] * 2, out_specs=VMEM, out_shape=near_core(first.shape), compiler_params=PARAMS
    )(first, close_by(second))


def arranged_pair(at, element, wanted, vector, got):
    return pl.pallas_call(
        functools.partial(arrange_pair_kernel, element, wanted),
        in_specs=[SCALARS, ANY, ANY],
        out_specs=VMEM,
        out_shape=near_core(got.shape),
        scratch_shapes=[pltpu.SemaphoreType.DMA((2,))],
        compiler_params=PARAMS,
    )(at, far_off(vector), got)


def arranged(at, vector, first, second):
    return pl.pallas_call(
        arrange_kernel,
        in_specs=[SCALARS, ANY, ANY, ANY],
        out_specs=VMEM,
        out_shape=near_core((8, *first.shape[1:])),
        scratch_shapes=[pltpu.SemaphoreType.DMA((6,))],
        compiler_params=PARAMS,
    )(at, far_off(vector), first, second)


def collected(at, y4, near):
    _, size, columns = near.shape
    return pl.pallas_call(
        collect_kernel,
        in_specs=[SCALARS, ANY, ANY],
        out_specs=ANY,
        out_shape=jax.ShapeDtypeStruct((4, size, 2 * columns), jnp.float32),
        scratch_shapes=[pltpu.SemaphoreType.DMA((1, 4))],
        compiler_params=PARAMS,
    )(at, y4, near)


def finished(at, parts, result):
    chunks = len(parts)
    return pl.pallas_call(
        functools.partial(finish_kernel, chunks),
        in_specs=[SCALARS] + [ANY] * (3 * chunks + 1),
        out_specs=ANY,
        out_shape=jax.ShapeDtypeStruct(result.shape, jnp.float32),
        input_output_aliases={1 + 3 * chunks: 0},
        scratch_shapes=[pltpu.SemaphoreType.DMA((chunks, 4))],
        compiler_params=PARAMS,
    )(at, *[value for part in parts for value in part], result)


def flipped(value, axis, bit):
    count = lax.axis_size(axis)
    return lax.ppermute(value, axis, [(i, i ^ bit) for i in range(count)])


def shifted(value, axis, steps):
    count = lax.axis_size(axis)
    return lax.ppermute(value, axis, [(i, (i + steps) % count) for i in range(count)])


def body(basis, applied, quad, face_index, face_pairing, orbitals):
    count, points, size = basis.shape
    spots = face_index.shape[2]
    columns = orbitals.shape[1]
    chunks = 2 if columns % 512 == 0 else 1
    elems, width = lax.axis_size("elem"), lax.axis_size("pts")
    faces_total = float(spots * width)
    side = lax.axis_index("elem") % 2
    core = lax.axis_index("pts") % 2
    lane = lax.axis_index("pts") // 2 % 2
    vector = orbitals.reshape(count, size, columns)
    at = jnp.stack([side, core, lane, side * 4 + core * 2 + lane]).astype(jnp.int32)

    lead_index = face_index[:1, 0:2].reshape(1, 1, 2 * spots)
    index = jnp.stack([face_index[:, 0], face_index[:, 2], face_index[:, 1], face_index[:, 3]], axis=1)
    index = index.reshape(count, 1, 4 * spots)
    pairs = jnp.concatenate([jnp.full_like(face_pairing, -points), face_pairing], axis=1).reshape(count, 1, 2 * spots)
    quad = quad.reshape(count, 1, points)
    last_pair = pairs[-1]
    vector, at, lead_index, index, pairs, last_pair, quad = lax.optimization_barrier(
        (vector, at, lead_index, index, pairs, last_pair, quad)
    )
    wide = columns // 2
    part = wide // chunks
    own = foreign = vector
    if part % 128:
        own = lax.dynamic_slice_in_dim(vector, side * part, part, axis=2)
        foreign = lax.dynamic_slice_in_dim(vector, (1 - side) * part, part, axis=2)
    lead, first, second = lead_and_cut(at, lead_index, basis, foreign, wide)
    lead = shifted(lead, "elem", -1)
    first, second = flipped(first, "elem", 1), flipped(second, "elem", 1)

    send, keep, last = blocks(at, index, quad, pairs, basis, applied, faces_total)
    send, keep = last_coupling(at, last_pair, last, lead, send, keep, faces_total)
    send, stay = folded(at, keep, flipped(send, "pts", 1))
    mine = added(stay, flipped(send, "pts", 2))
    bit = 4
    while bit < width:
        mine = mine + flipped(mine, "pts", bit)
        bit *= 2
    first, mine = lax.optimization_barrier((first, mine))
    above = shifted(arranged_pair(at, 0, 0, own, first), "elem", -2)
    beside = flipped(mine, "pts", 2)
    across = flipped(mine, "elem", 1)
    beside, across = lax.optimization_barrier((beside, across))
    mine_near = flipped(mine, "pts", 1)
    both = flipped(across, "pts", 2)
    beside_near = flipped(beside, "pts", 1)
    across_near = flipped(across, "pts", 1)

    last = outer_block(at, mine, beside)
    flat = lambda e, p: e % elems * width + p
    holds = [(e, p) for e in range(elems) for p in range(width) if e % 2 == p % 2]
    outer = lax.ppermute(last, ("elem", "pts"), [(flat(e, p), flat(e + (2 if p % 2 else -2), p)) for e, p in holds])
    outer = added(outer, lax.ppermute(outer, ("elem", "pts"), [(flat(e, p), flat(e ^ 1, p)) for e, p in holds]))
    outer_near = flipped(outer, "pts", 1)

    above, second, both = lax.optimization_barrier((above, second, both))
    below = shifted(arranged_pair(at, 2, 1, own, second), "elem", 2)
    y0 = arranged(at, own, first, second)
    both_near = flipped(both, "pts", 1)

    high, low = weights(at, mine, mine_near, beside, across, beside_near, across_near, both, both_near)
    high_outer, low_outer = outer_weights(at, outer, outer_near, high, low)

    y1 = first_rows(high, low, y0, above)
    y1_ends, *ends = second_rows(chunks, high, low, high_outer, low_outer, y0, below, above, y1)
    belows = [shifted(value, "elem", 2) for value in ends[chunks:]]
    aboves = [shifted(value, "elem", -2) for value in ends[:chunks]]
    y3, y4, near = middle_rows(at, chunks, high, low, y0, y1, ends)
    near = flipped(near, "elem", 1)
    parts = []
    for c in range(chunks):
        y4_low, y4_high, far = last_rows(
            at, c * part, high, low, high_outer, low_outer, y1, y1_ends, y3, ends[c], ends[chunks + c], belows[c], aboves[c]
        )
        parts.append((y4_low, y4_high, flipped(far, "elem", 1)))
    if part % 128:
        y4_low, y4_high, far = parts[0]
        mine = jnp.where(side == 0, jnp.concatenate([y4_low, y4[:2]]), jnp.concatenate([y4[2:], y4_high]))
        theirs = jnp.where(side == 0, jnp.concatenate([far, near]), jnp.concatenate([near, far]))
        swap = lambda first, second: jnp.concatenate([first, second], axis=2)
        result = jnp.where(side == 0, swap(mine, theirs), swap(theirs, mine))
    else:
        result = finished(at, parts, collected(at, y4, near))
    return result.reshape(count * size, columns)


def solution(mesh):
    return jax.shard_map(
        body,
        mesh=mesh,
        in_specs=(
            P("elem", "pts", None),
            P("elem", "pts", None),
            P("elem", "pts"),
            P("elem", None, "pts"),
            P("elem", "pts"),
            P("elem", "pts"),
        ),
        out_specs=P("elem", "pts"),
        check_vma=False,
    )
```

time: 157 us -> 138 us (0.88)
  starting transfers between devices: 35.5 us -> 28 us
  Pallas kernels: 49.1 us -> 43 us
  local copies, waits for them, and re-layouts: 10.4 us -> 5.46 us
    pallas_call x18 -> x11, Pallas kernels: 35.7 us -> 26.8 us  [the longest x1 8.14 us: middle_rows(): pl.pallas_call(functools.partial(middle_kernel, chunks), in_specs=[SCALAR...]
    ppermute x1, waiting for transfers between devices: 0.01 us -> 8.14 us  [body(): lax.ppermute(outer, ('elem', 'pts'), [(flat(e, p), flat(e ^ 1, p)) for e,...]
    unnamed x66 -> x16, local copies, waits for them, and re-layouts: 9.43 us -> 1.54 us
    ppermute x9 -> x7, waiting for transfers between devices: 14.8 us -> 8.31 us  [shifted(): lax.ppermute(value, axis, [(i, (i + steps) % count) for i in range(count)])]
    ppermute x9 -> x7, starting transfers between devices: 21.2 us -> 16.1 us  [shifted(): lax.ppermute(value, axis, [(i, (i + steps) % count) for i in range(count)])]
    ppermute x17 -> x15, waiting for transfers between devices: 38.3 us -> 33.7 us  [flipped(): return lax.ppermute(value, axis, [(i, i ^ bit) for i in range(count)])]
    ppermute x1, waiting for transfers between devices: 5.75 us -> 10.2 us  [body(): lax.ppermute(last, ('elem', 'pts'), [(flat(e, p), flat(e + (2 if p % 2 el...]
    ppermute x1, starting transfers between devices: 4.15 us -> 2.36 us  [body(): lax.ppermute(last, ('elem', 'pts'), [(flat(e, p), flat(e + (2 if p % 2 el...]
  transfers between devices with their start and end apart: 28 -> 24, of which waited for: 15 -> 13; matrix products, arithmetic and copies ran while one was open for 1% -> 0% of each run, Pallas kernels for 27% -> 25%
where the time goes in v6:
time: 138 us; the launch traced here: 137 us
  waiting for transfers between devices  60.3 us (44%)
  Pallas kernels  43 us (31%)
  starting transfers between devices  28 us (20%)
  local copies, waits for them, and re-layouts  5.46 us (4%)
    ppermute x15, waiting for transfers between devices, flipped(): return lax.ppermute(value, axis, [(i, i ^ bit) for i in range(count)])  33.7 us
    ppermute x7, starting transfers between devices, shifted(): lax.ppermute(value, axis, [(i, (i + steps) % count) for i in range(count)])  16.1 us
    ppermute x1, waiting for transfers between devices, body(): lax.ppermute(last, ('elem', 'pts'), [(flat(e, p), flat(e + (2 if p % 2 el...  10.2 us
    ppermute x7, waiting for transfers between devices, shifted(): lax.ppermute(value, axis, [(i, (i + steps) % count) for i in range(count)])  8.31 us
    ppermute x15, starting transfers between devices, flipped(): return lax.ppermute(value, axis, [(i, i ^ bit) for i in range(count)])  8.25 us
    ppermute x1, waiting for transfers between devices, body(): lax.ppermute(outer, ('elem', 'pts'), [(flat(e, p), flat(e ^ 1, p)) for e,...  8.14 us
    pallas_call x1, Pallas kernels, middle_rows(): pl.pallas_call(functools.partial(middle_kernel, chunks), in_specs=[SCALAR...  8.14 us
    pallas_call x1, Pallas kernels, blocks(): pl.pallas_call(functools.partial(blocks_kernel, faces_total), in_specs=[S...  7.3 us
  transfers between devices with their start and end apart: 24, of which 13 were waited for; matrix products, arithmetic and copies ran while one was open for 0% of the time, Pallas kernels for 25%

profile of v6, /device:TPU:0, one launch (start us, length us, event | category | flops | bytes accessed | tf_op | source)
XLA Modules:
  0.0 137.3 jit_solution(5880943145382168883)
XLA Ops:
  4.0 2.0 %shard_map.64 = (f32[256,128]{1,0:T(8,128)S(1)}, f32[2,256,256]{2,1,0:T(8,128)S(1)}, f32[2,256,256]{2,1,0:T(8,128)S(1)}) custom-call(s32[4]{0:T(128)S(1)} %pad_add_fusion.1.at_ref, s32[1,1,128]{2,1,0:T(1,128)S(1)} %reshape.21.index_ref, f32[4,512,256]{2,1,0:T(8,128)} %basis_ref.3, f32[4,256,512]{2,1,0:T(8,128)} %bitcast.10), custom_call_target="tpu_custom_call" | custom-call | tf_op jit(solution)/shard_map/pallas_call | solution.py:440
  6.0 6.1 %collective-permute-start.1 = (f32[256,128]{1,0:T(8,128)S(1)}, f32[256,128]{1,0:T(8,128)S(1)}, u32[]{:S(2)}, u32[]{:S(2)}) collective-permute-start(f32[256,128]{1,0:T(8,128)S(1)} %get-tuple-element.56), channel_id=1, source_target_pairs={{0,28},{4,0},{8,4},{12,8},{16,12},{20,16},{24,20},{28,24},{1,29},{... | collective-permute-start | bytes 393224 | tf_op jit(solution)/shard_map/ppermute | solution.py:639
  12.1 7.3 %shard_map.65 = (f32[2,392,256]{2,1,0:T(8,128)S(1)}, f32[2,392,256]{2,1,0:T(8,128)S(1)}, f32[256,256]{1,0:T(8,128)S(1)}) custom-call(s32[4]{0:T(128)S(1)} %pad_add_fusion.1.at_ref, s32[4,1,256]{2,1,0:T(1,128)S(1)} %reshape.22.index_ref, f32[4,1,512]{2,1,0:T(1,128)S(1)} %reshape.24.quad_ref, s32[4,1,128]{2,1,0:T(1,128)S(1)} %bitcast.9, ...), custom_call_target="tpu_custom_call" | custom-call | tf_op jit(solution)/shard_map/pallas_call | solution.py:454
  20.8 2.2 %collective-permute-done.2.other_ref = f32[2,392,256]{2,1,0:T(8,128)S(1)} collective-permute-done((f32[2,392,256]{2,1,0:T(8,128)S(1)}, f32[2,392,256]{2,1,0:T(8,128)S(1)}, u32[]{:S(2)}, u32[]{:S(2)}) %collective-permute-start.2) | collective-permute-done | bytes 802848 | tf_op jit(solution)/shard_map/ppermute | solution.py:634
  23.6 1.6 %collective-permute-start.3 = (f32[1,392,256]{2,1,0:T(8,128)S(1)}, f32[1,392,256]{2,1,0:T(8,128)S(1)}, u32[]{:S(2)}, u32[]{:S(2)}) collective-permute-start(f32[1,392,256]{2,1,0:T(8,128)S(1)} %get-tuple-element.62), channel_id=1, source_target_pairs={{0,2},{1,3},{2,0},{3,1},{4,6},{5,7},{6,4},{7,5},{8,10},{9,11},{10,... | collective-permute-start | bytes 1204232 | tf_op jit(solution)/shard_map/ppermute | solution.py:634
  25.2 9.8 %collective-permute-done.3.second_ref = f32[1,392,256]{2,1,0:T(8,128)S(1)} collective-permute-done((f32[1,392,256]{2,1,0:T(8,128)S(1)}, f32[1,392,256]{2,1,0:T(8,128)S(1)}, u32[]{:S(2)}, u32[]{:S(2)}) %collective-permute-start.3) | collective-permute-done | bytes 401440 | tf_op jit(solution)/shard_map/ppermute | solution.py:634
  35.1 1.6 %collective-permute-start.5 = (f32[1,392,256]{2,1,0:T(8,128)S(1)}, f32[1,392,256]{2,1,0:T(8,128)S(1)}, u32[]{:S(2)}, u32[]{:S(2)}) collective-permute-start(f32[1,392,256]{2,1,0:T(8,128)S(1)} %shard_map.68.refs_0_.mine_ref), channel_id=1, source_target_pairs={{0,2},{1,3},{2,0},{3,1},{4,6},{5,7},{6,4},{7,5},{8,10},{9,11},{10,... | collective-permute-start | bytes 1204232 | tf_op jit(solution)/shard_map/ppermute | solution.py:634
  36.8 9.1 %collective-permute-done.5.refs_2_.beside_ref = f32[1,392,256]{2,1,0:T(8,128)S(1)} collective-permute-done((f32[1,392,256]{2,1,0:T(8,128)S(1)}, f32[1,392,256]{2,1,0:T(8,128)S(1)}, u32[]{:S(2)}, u32[]{:S(2)}) %collective-permute-start.5) | collective-permute-done | bytes 401440 | tf_op jit(solution)/shard_map/ppermute | solution.py:634
  45.9 1.2 collective-permute-done.6.refs_3_
  47.9 2.4 %collective-permute-start.13 = (f32[1,648,256]{2,1,0:T(8,128)S(1)}, f32[1,648,256]{2,1,0:T(8,128)S(1)}, u32[]{:S(2)}, u32[]{:S(2)}) collective-permute-start(f32[1,648,256]{2,1,0:T(8,128)S(1)} %shard_map.71), channel_id=1, source_target_pairs={{0,24},{2,26},{5,13},{7,15},{8,0},{10,2},{13,21},{15,23},{16,8},{1... | collective-permute-start | bytes 1990664 | tf_op jit(solution)/shard_map/ppermute | solution.py:695
  50.3 10.2 %collective-permute-done.13.first_ref = f32[1,648,256]{2,1,0:T(8,128)S(1)} collective-permute-done((f32[1,648,256]{2,1,0:T(8,128)S(1)}, f32[1,648,256]{2,1,0:T(8,128)S(1)}, u32[]{:S(2)}, u32[]{:S(2)}) %collective-permute-start.13) | collective-permute-done | bytes 663584 | tf_op jit(solution)/shard_map/ppermute | solution.py:695
  60.5 1.3 collective-permute-start.14
  61.9 1.6 %shard_map.69 = f32[2,256,256]{2,1,0:T(8,128)S(1)} custom-call(s32[4]{0:T(128)S(1)} %pad_add_fusion.1.at_ref, f32[4,256,512]{2,1,0:T(8,128)} %bitcast.11, f32[2,256,256]{2,1,0:T(8,128)S(1)} %collective-permute-done.got_ref.first_ref), custom_call_target="tpu_custom_call" | custom-call | tf_op jit(solution)/shard_map/pallas_call | solution.py:586
  63.5 2.3 %collective-permute-start.9 = (f32[2,256,256]{2,1,0:T(8,128)S(1)}, f32[2,256,256]{2,1,0:T(8,128)S(1)}, u32[]{:S(2)}, u32[]{:S(2)}) collective-permute-start(f32[2,256,256]{2,1,0:T(8,128)S(1)} %shard_map.69), channel_id=1, source_target_pairs={{0,24},{4,28},{8,0},{12,4},{16,8},{20,12},{24,16},{28,20},{1,25},{... | collective-permute-start | bytes 1572872 | tf_op jit(solution)/shard_map/ppermute | solution.py:639
  66.3 8.1 %collective-permute-done.14.second_ref = f32[1,648,256]{2,1,0:T(8,128)S(1)} collective-permute-done((f32[1,648,256]{2,1,0:T(8,128)S(1)}, f32[1,648,256]{2,1,0:T(8,128)S(1)}, u32[]{:S(2)}, u32[]{:S(2)}) %collective-permute-start.14) | collective-permute-done | bytes 663584 | tf_op jit(solution)/shard_map/ppermute | solution.py:696
  74.6 5.5 %collective-permute-done.10.second_ref.got_ref = f32[2,256,256]{2,1,0:T(8,128)S(1)} collective-permute-done((f32[2,256,256]{2,1,0:T(8,128)S(1)}, f32[2,256,256]{2,1,0:T(8,128)S(1)}, u32[]{:S(2)}, u32[]{:S(2)}) %collective-permute-start.10) | collective-permute-done | bytes 524320 | tf_op jit(solution)/shard_map/ppermute | solution.py:634
  81.8 1.8 %shard_map.74.y0 = f32[8,256,256]{2,1,0:T(8,128)S(1)} custom-call(s32[4]{0:T(128)S(1)} %pad_add_fusion.1.at_ref, f32[4,256,512]{2,1,0:T(8,128)} %bitcast.13, f32[2,256,256]{2,1,0:T(8,128)S(1)} %collective-permute-done.got_ref.first_ref, f32[2,256,256]{2,1,0:T(8,128)S(1)} %collective-permute-done.10.second_ref.got_ref), custom_call_target="tpu_custom_call" | custom-call | tf_op jit(solution)/shard_map/pallas_call | solution.py:597
  85.3 3.4 %shard_map.70 = (bf16[8,256,768]{2,1,0:T(8,128)(2,1)S(1)}, bf16[8,256,768]{2,1,0:T(8,128)(2,1)S(1)}) custom-call(s32[4]{0:T(128)S(1)} %pad_add_fusion.1.at_ref, f32[1,392,256]{2,1,0:T(8,128)} %copy-done, f32[1,392,256]{2,1,0:T(8,128)} %copy-done.4, f32[1,392,256]{2,1,0:T(8,128)} %copy-done.1, f32[1,392,256]{2,1,0:T(8,128)} %copy-done.2, ...), custom_call_target="tpu_custom_call" | custom-call | tf_op jit(solution)/shard_map/pallas_call | solution.py:484
  88.7 3.8 %shard_map.75.y1 = f32[7,256,256]{2,1,0:T(8,128)S(1)} custom-call(bf16[8,256,768]{2,1,0:T(8,128)(2,1)S(1)} %get-tuple-element.69.high_in.high, bf16[8,256,768]{2,1,0:T(8,128)(2,1)S(1)} %get-tuple-element.70.low_in.low, f32[8,256,256]{2,1,0:T(8,128)S(1)} %shard_map.74.y0, f32[2,256,256]{2,1,0:T(8,128)S(1)} %collective-permute-done.9.above), custom_call_target="tpu_custom_call" | custom-call | tf_op jit(solution)/shard_map/pallas_call | solution.py:507
  93.5 3.3 %collective-permute-done.16.below = f32[2,256,256]{2,1,0:T(8,128)S(1)} collective-permute-done((f32[2,256,256]{2,1,0:T(8,128)S(1)}, f32[2,256,256]{2,1,0:T(8,128)S(1)}, u32[]{:S(2)}, u32[]{:S(2)}) %collective-permute-start.16) | collective-permute-done | bytes 524320 | tf_op jit(solution)/shard_map/ppermute | solution.py:639
  96.8 2.5 %shard_map.77 = (f32[3,256,256]{2,1,0:T(8,128)S(1)}, f32[2,256,128]{2,1,0:T(8,128)S(1)}, f32[2,256,128]{2,1,0:T(8,128)S(1)}, f32[2,256,128]{2,1,0:T(8,128)S(1)}, f32[2,256,128]{2,1,0:T(8,128)S(1)}) custom-call(bf16[8,256,768]{2,1,0:T(8,128)(2,1)S(1)} %get-tuple-element.69.high_in.high, bf16[8,256,768]{2,1,0:T(8,128)(2,1)S(1)} %get-tuple-element.70.low_in.low, ...), custom_call_target="tpu_custom_call" | custom-call | tf_op jit(solution)/shard_map/pallas_call | solution.py:519
  99.4 3.8 %collective-permute-start.18 = (f32[2,256,128]{2,1,0:T(8,128)S(1)}, f32[2,256,128]{2,1,0:T(8,128)S(1)}, u32[]{:S(2)}, u32[]{:S(2)}) collective-permute-start(f32[2,256,128]{2,1,0:T(8,128)S(1)} %get-tuple-element.76.refs_0_.y2_low), channel_id=1, source_target_pairs={{0,24},{4,28},{8,0},{12,4},{16,8},{20,12},{24,16},{28,20},{1,25},{... | collective-permute-start | bytes 786440 | tf_op jit(solution)/shard_map/ppermute | solution.py:639
  103.2 8.1 %shard_map.78 = (f32[4,256,256]{2,1,0:T(8,128)S(1)}, f32[4,256,256]{2,1,0:T(8,128)S(1)}, f32[2,256,256]{2,1,0:T(8,128)S(1)}) custom-call(s32[4]{0:T(128)S(1)} %pad_add_fusion.1.at_ref, bf16[8,256,768]{2,1,0:T(8,128)(2,1)S(1)} %get-tuple-element.69.high_in.high, bf16[8,256,768]{2,1,0:T(8,128)(2,1)S(1)} %get-tuple-element.70.low_in.low, ...), custom_call_target="tpu_custom_call" | custom-call | tf_op jit(solution)/shard_map/pallas_call | solution.py:531
  112.3 3.8 %collective-permute-start.21 = (f32[2,256,128]{2,1,0:T(8,128)S(1)}, f32[2,256,128]{2,1,0:T(8,128)S(1)}, u32[]{:S(2)}, u32[]{:S(2)}) collective-permute-start(f32[2,256,128]{2,1,0:T(8,128)S(1)} %get-tuple-element.77.refs_1_.y2_low), channel_id=1, source_target_pairs={{0,24},{4,28},{8,0},{12,4},{16,8},{20,12},{24,16},{28,20},{1,25},{... | collective-permute-start | bytes 786440 | tf_op jit(solution)/shard_map/ppermute | solution.py:639
  116.1 2.5 %shard_map.79 = (f32[2,256,128]{2,1,0:T(8,128)S(1)}, f32[2,256,128]{2,1,0:T(8,128)S(1)}, f32[2,256,128]{2,1,0:T(8,128)S(1)}) custom-call(s32[4]{0:T(128)S(1)} %pad_add_fusion.1.at_ref, bf16[8,256,768]{2,1,0:T(8,128)(2,1)S(1)} %get-tuple-element.69.high_in.high, bf16[8,256,768]{2,1,0:T(8,128)(2,1)S(1)} %get-tuple-element.70.low_in.low, ...), custom_call_target="tpu_custom_call" | custom-call | tf_op jit(solution)/shard_map/pallas_call | solution.py:547
  118.5 1.3 collective-permute-start.19
  119.8 1.9 %collective-permute-done.20.below = f32[2,256,128]{2,1,0:T(8,128)S(1)} collective-permute-done((f32[2,256,128]{2,1,0:T(8,128)S(1)}, f32[2,256,128]{2,1,0:T(8,128)S(1)}, u32[]{:S(2)}, u32[]{:S(2)}) %collective-permute-start.20) | collective-permute-done | bytes 262176 | tf_op jit(solution)/shard_map/ppermute | solution.py:639
  121.7 3.1 %collective-permute-done.21.above = f32[2,256,128]{2,1,0:T(8,128)S(1)} collective-permute-done((f32[2,256,128]{2,1,0:T(8,128)S(1)}, f32[2,256,128]{2,1,0:T(8,128)S(1)}, u32[]{:S(2)}, u32[]{:S(2)}) %collective-permute-start.21) | collective-permute-done | bytes 262176 | tf_op jit(solution)/shard_map/ppermute | solution.py:639
  124.8 2.5 %shard_map.80 = (f32[2,256,128]{2,1,0:T(8,128)S(1)}, f32[2,256,128]{2,1,0:T(8,128)S(1)}, f32[2,256,128]{2,1,0:T(8,128)S(1)}) custom-call(s32[4]{0:T(128)S(1)} %pad_add_fusion.1.at_ref, bf16[8,256,768]{2,1,0:T(8,128)(2,1)S(1)} %get-tuple-element.69.high_in.high, bf16[8,256,768]{2,1,0:T(8,128)(2,1)S(1)} %get-tuple-element.70.low_in.low, ...), custom_call_target="tpu_custom_call" | custom-call | tf_op jit(solution)/shard_map/pallas_call | solution.py:547
  128.3 1.5 %shard_map.81.refs_6_ = f32[4,256,512]{2,1,0:T(8,128)} custom-call(s32[4]{0:T(128)S(1)} %pad_add_fusion.1.at_ref, f32[4,256,256]{2,1,0:T(8,128)S(1)} %get-tuple-element.87.y4, f32[2,256,256]{2,1,0:T(8,128)S(1)} %collective-permute-done.23.near), custom_call_target="tpu_custom_call" | custom-call | tf_op jit(solution)/shard_map/pallas_call | solution.py:609
  131.0 4.6 %collective-permute-done.22.refs_5_ = f32[2,256,128]{2,1,0:T(8,128)S(1)} collective-permute-done((f32[2,256,128]{2,1,0:T(8,128)S(1)}, f32[2,256,128]{2,1,0:T(8,128)S(1)}, u32[]{:S(2)}, u32[]{:S(2)}) %collective-permute-start.22) | collective-permute-done | bytes 262176 | tf_op jit(solution)/shard_map/ppermute | solution.py:634
  135.6 1.6 %shard_map.82 = f32[4,256,512]{2,1,0:T(8,128)} custom-call(s32[4]{0:T(128)S(1)} %pad_add_fusion.1.at_ref, f32[2,256,128]{2,1,0:T(8,128)S(1)} %get-tuple-element.81.refs_0_, f32[2,256,128]{2,1,0:T(8,128)S(1)} %get-tuple-element.82.refs_1_, f32[2,256,128]{2,1,0:T(8,128)S(1)} %collective-permute-done.19.refs_2_, ...), custom_call_target="tpu_custom_call", output_to_operand_aliasing={{}: (7, {})} | custom-call | tf_op jit(solution)/shard_map/pallas_call | solution.py:621
  (60 shorter events, 15.2 us)
Async XLA Ops:
  6.0 13.4 %collective-permute-start.1 = (f32[256,128]{1,0:T(8,128)S(1)}, f32[256,128]{1,0:T(8,128)S(1)}, u32[]{:S(2)}, u32[]{:S(2)}) collective-permute-start(f32[256,128]{1,0:T(8,128)S(1)} %get-tuple-element.56), channel_id=1, source_target_pairs={{0,28},{4,0},{8,4},{12,8},{16,12},{20,16},{24,20},{28,24},{1,29},{... | collective-permute-start | bytes 393224 | tf_op jit(solution)/shard_map/ppermute | solution.py:639
  20.6 2.4 %collective-permute-start.2 = (f32[2,392,256]{2,1,0:T(8,128)S(1)}, f32[2,392,256]{2,1,0:T(8,128)S(1)}, u32[]{:S(2)}, u32[]{:S(2)}) collective-permute-start(f32[2,392,256]{2,1,0:T(8,128)S(1)} %get-tuple-element.60), channel_id=1, source_target_pairs={{0,1},{1,0},{2,3},{3,2},{4,5},{5,4},{6,7},{7,6},{8,9},{9,8},{10,11... | collective-permute-start | bytes 2408456 | tf_op jit(solution)/shard_map/ppermute | solution.py:634
  20.7 14.4 %collective-permute-start = (f32[2,256,256]{2,1,0:T(8,128)S(1)}, f32[2,256,256]{2,1,0:T(8,128)S(1)}, u32[]{:S(2)}, u32[]{:S(2)}) collective-permute-start(f32[2,256,256]{2,1,0:T(8,128)S(1)} %get-tuple-element.50), channel_id=1, source_target_pairs={{0,4},{4,0},{8,12},{12,8},{16,20},{20,16},{24,28},{28,24},{1,5},{5... | collective-permute-start | bytes 1572872 | tf_op jit(solution)/shard_map/ppermute | solution.py:634
  23.6 11.4 %collective-permute-start.3 = (f32[1,392,256]{2,1,0:T(8,128)S(1)}, f32[1,392,256]{2,1,0:T(8,128)S(1)}, u32[]{:S(2)}, u32[]{:S(2)}) collective-permute-start(f32[1,392,256]{2,1,0:T(8,128)S(1)} %get-tuple-element.62), channel_id=1, source_target_pairs={{0,2},{1,3},{2,0},{3,1},{4,6},{5,7},{6,4},{7,5},{8,10},{9,11},{10,... | collective-permute-start | bytes 1204232 | tf_op jit(solution)/shard_map/ppermute | solution.py:634
  35.1 31.3 %copy-start = (f32[1,392,256]{2,1,0:T(8,128)}, f32[1,392,256]{2,1,0:T(8,128)S(1)}, u32[]{:S(2)}) copy-start(f32[1,392,256]{2,1,0:T(8,128)S(1)} %shard_map.68.refs_0_.mine_ref) | copy-start | bytes 1204228
  35.1 10.8 %collective-permute-start.5 = (f32[1,392,256]{2,1,0:T(8,128)S(1)}, f32[1,392,256]{2,1,0:T(8,128)S(1)}, u32[]{:S(2)}, u32[]{:S(2)}) collective-permute-start(f32[1,392,256]{2,1,0:T(8,128)S(1)} %shard_map.68.refs_0_.mine_ref), channel_id=1, source_target_pairs={{0,2},{1,3},{2,0},{3,1},{4,6},{5,7},{6,4},{7,5},{8,10},{9,11},{10,... | collective-permute-start | bytes 1204232 | tf_op jit(solution)/shard_map/ppermute | solution.py:634
  36.6 10.4 %collective-permute-start.6 = (f32[1,392,256]{2,1,0:T(8,128)S(1)}, f32[1,392,256]{2,1,0:T(8,128)S(1)}, u32[]{:S(2)}, u32[]{:S(2)}) collective-permute-start(f32[1,392,256]{2,1,0:T(8,128)S(1)} %shard_map.68.refs_0_.mine_ref), channel_id=1, source_target_pairs={{0,4},{4,0},{8,12},{12,8},{16,20},{20,16},{24,28},{28,24},{1,5},{5... | collective-permute-start | bytes 1204232 | tf_op jit(solution)/shard_map/ppermute | solution.py:634
  45.9 34.9 %copy-start.1 = (f32[1,392,256]{2,1,0:T(8,128)}, f32[1,392,256]{2,1,0:T(8,128)S(1)}, u32[]{:S(2)}) copy-start(f32[1,392,256]{2,1,0:T(8,128)S(1)} %collective-permute-done.5.refs_2_.beside_ref) | copy-start | bytes 1204228
  47.1 34.2 %copy-start.2 = (f32[1,392,256]{2,1,0:T(8,128)}, f32[1,392,256]{2,1,0:T(8,128)S(1)}, u32[]{:S(2)}) copy-start(f32[1,392,256]{2,1,0:T(8,128)S(1)} %collective-permute-done.6.refs_3_) | copy-start | bytes 1204228
  47.9 12.6 %collective-permute-start.13 = (f32[1,648,256]{2,1,0:T(8,128)S(1)}, f32[1,648,256]{2,1,0:T(8,128)S(1)}, u32[]{:S(2)}, u32[]{:S(2)}) collective-permute-start(f32[1,648,256]{2,1,0:T(8,128)S(1)} %shard_map.71), channel_id=1, source_target_pairs={{0,24},{2,26},{5,13},{7,15},{8,0},{10,2},{13,21},{15,23},{16,8},{1... | collective-permute-start | bytes 1990664 | tf_op jit(solution)/shard_map/ppermute | solution.py:695
  60.5 14.0 %collective-permute-start.14 = (f32[1,648,256]{2,1,0:T(8,128)S(1)}, f32[1,648,256]{2,1,0:T(8,128)S(1)}, u32[]{:S(2)}, u32[]{:S(2)}) collective-permute-start(f32[1,648,256]{2,1,0:T(8,128)S(1)} %collective-permute-done.13.first_ref), channel_id=1, source_target_pairs={{0,4},{2,6},{5,1},{7,3},{8,12},{10,14},{13,9},{15,11},{16,20},{18,... | collective-permute-start | bytes 1990664 | tf_op jit(solution)/shard_map/ppermute | solution.py:696
  61.8 18.3 %collective-permute-start.10 = (f32[2,256,256]{2,1,0:T(8,128)S(1)}, f32[2,256,256]{2,1,0:T(8,128)S(1)}, u32[]{:S(2)}, u32[]{:S(2)}) collective-permute-start(f32[2,256,256]{2,1,0:T(8,128)S(1)} %get-tuple-element.67), channel_id=1, source_target_pairs={{0,4},{4,0},{8,12},{12,8},{16,20},{20,16},{24,28},{28,24},{1,5},{5... | collective-permute-start | bytes 1572872 | tf_op jit(solution)/shard_map/ppermute | solution.py:634
  63.5 16.6 %collective-permute-start.9 = (f32[2,256,256]{2,1,0:T(8,128)S(1)}, f32[2,256,256]{2,1,0:T(8,128)S(1)}, u32[]{:S(2)}, u32[]{:S(2)}) collective-permute-start(f32[2,256,256]{2,1,0:T(8,128)S(1)} %shard_map.69), channel_id=1, source_target_pairs={{0,24},{4,28},{8,0},{12,4},{16,8},{20,12},{24,16},{28,20},{1,25},{... | collective-permute-start | bytes 1572872 | tf_op jit(solution)/shard_map/ppermute | solution.py:639
  65.8 14.3 %collective-permute-start.11 = (f32[1,392,256]{2,1,0:T(8,128)S(1)}, f32[1,392,256]{2,1,0:T(8,128)S(1)}, u32[]{:S(2)}, u32[]{:S(2)}) collective-permute-start(f32[1,392,256]{2,1,0:T(8,128)S(1)} %collective-permute-done.6.refs_3_), channel_id=1, source_target_pairs={{0,2},{1,3},{2,0},{3,1},{4,6},{5,7},{6,4},{7,5},{8,10},{9,11},{10,... | collective-permute-start | bytes 1204232 | tf_op jit(solution)/shard_map/ppermute | solution.py:634
  66.3 15.1 %collective-permute-start.4 = (f32[1,392,256]{2,1,0:T(8,128)S(1)}, f32[1,392,256]{2,1,0:T(8,128)S(1)}, u32[]{:S(2)}, u32[]{:S(2)}) collective-permute-start(f32[1,392,256]{2,1,0:T(8,128)S(1)} %shard_map.68.refs_0_.mine_ref), channel_id=1, source_target_pairs={{0,1},{1,0},{2,3},{3,2},{4,5},{5,4},{6,7},{7,6},{8,9},{9,8},{10,11... | collective-permute-start | bytes 1204232 | tf_op jit(solution)/shard_map/ppermute | solution.py:634
  74.5 17.9 %collective-permute-start.15 = (f32[1,648,256]{2,1,0:T(8,128)S(1)}, f32[1,648,256]{2,1,0:T(8,128)S(1)}, u32[]{:S(2)}, u32[]{:S(2)}) collective-permute-start(f32[1,648,256]{2,1,0:T(8,128)S(1)} %shard_map.72.kept_ref), channel_id=1, source_target_pairs={{0,1},{1,0},{2,3},{3,2},{4,5},{5,4},{6,7},{7,6},{8,9},{9,8},{10,11... | collective-permute-start | bytes 1990664 | tf_op jit(solution)/shard_map/ppermute | solution.py:634
  80.1 3.5 %copy-start.3 = (f32[1,392,256]{2,1,0:T(8,128)}, f32[1,392,256]{2,1,0:T(8,128)S(1)}, u32[]{:S(2)}) copy-start(f32[1,392,256]{2,1,0:T(8,128)S(1)} %collective-permute-done.11.refs_6_) | copy-start | bytes 1204228
  80.7 16.1 %collective-permute-start.16 = (f32[2,256,256]{2,1,0:T(8,128)S(1)}, f32[2,256,256]{2,1,0:T(8,128)S(1)}, u32[]{:S(2)}, u32[]{:S(2)}) collective-permute-start(f32[2,256,256]{2,1,0:T(8,128)S(1)} %shard_map.76), channel_id=1, source_target_pairs={{0,8},{4,12},{8,16},{12,20},{16,24},{20,28},{24,0},{28,4},{1,9},{5... | collective-permute-start | bytes 1572872 | tf_op jit(solution)/shard_map/ppermute | solution.py:639
  80.8 2.9 %collective-permute-start.7 = (f32[1,392,256]{2,1,0:T(8,128)S(1)}, f32[1,392,256]{2,1,0:T(8,128)S(1)}, u32[]{:S(2)}, u32[]{:S(2)}) collective-permute-start(f32[1,392,256]{2,1,0:T(8,128)S(1)} %collective-permute-done.5.refs_2_.beside_ref), channel_id=1, source_target_pairs={{0,1},{1,0},{2,3},{3,2},{4,5},{5,4},{6,7},{7,6},{8,9},{9,8},{10,11... | collective-permute-start | bytes 1204232 | tf_op jit(solution)/shard_map/ppermute | solution.py:634
  81.3 2.4 %collective-permute-start.8 = (f32[1,392,256]{2,1,0:T(8,128)S(1)}, f32[1,392,256]{2,1,0:T(8,128)S(1)}, u32[]{:S(2)}, u32[]{:S(2)}) collective-permute-start(f32[1,392,256]{2,1,0:T(8,128)S(1)} %collective-permute-done.6.refs_3_), channel_id=1, source_target_pairs={{0,1},{1,0},{2,3},{3,2},{4,5},{5,4},{6,7},{7,6},{8,9},{9,8},{10,11... | collective-permute-start | bytes 1204232 | tf_op jit(solution)/shard_map/ppermute | solution.py:634
  81.4 2.3 %copy-start.4 = (f32[1,392,256]{2,1,0:T(8,128)}, f32[1,392,256]{2,1,0:T(8,128)S(1)}, u32[]{:S(2)}) copy-start(f32[1,392,256]{2,1,0:T(8,128)S(1)} %collective-permute-done.4.refs_1_) | copy-start | bytes 1204228
  81.4 2.4 %collective-permute-start.12 = (f32[1,392,256]{2,1,0:T(8,128)S(1)}, f32[1,392,256]{2,1,0:T(8,128)S(1)}, u32[]{:S(2)}, u32[]{:S(2)}) collective-permute-start(f32[1,392,256]{2,1,0:T(8,128)S(1)} %collective-permute-done.11.refs_6_), channel_id=1, source_target_pairs={{0,1},{1,0},{2,3},{3,2},{4,5},{5,4},{6,7},{7,6},{8,9},{9,8},{10,11... | collective-permute-start | bytes 1204232 | tf_op jit(solution)/shard_map/ppermute | solution.py:634
  83.7 0.8 copy-start.5
  83.7 0.9 copy-start.6
  84.5 0.8 copy-start.7
  99.3 16.7 %collective-permute-start.17 = (f32[2,256,128]{2,1,0:T(8,128)S(1)}, f32[2,256,128]{2,1,0:T(8,128)S(1)}, u32[]{:S(2)}, u32[]{:S(2)}) collective-permute-start(f32[2,256,128]{2,1,0:T(8,128)S(1)} %get-tuple-element.78.refs_2_.y2_high), channel_id=1, source_target_pairs={{0,8},{4,12},{8,16},{12,20},{16,24},{20,28},{24,0},{28,4},{1,9},{5... | collective-permute-start | bytes 786440 | tf_op jit(solution)/shard_map/ppermute | solution.py:639
  99.4 16.7 %collective-permute-start.18 = (f32[2,256,128]{2,1,0:T(8,128)S(1)}, f32[2,256,128]{2,1,0:T(8,128)S(1)}, u32[]{:S(2)}, u32[]{:S(2)}) collective-permute-start(f32[2,256,128]{2,1,0:T(8,128)S(1)} %get-tuple-element.76.refs_0_.y2_low), channel_id=1, source_target_pairs={{0,24},{4,28},{8,0},{12,4},{16,8},{20,12},{24,16},{28,20},{1,25},{... | collective-permute-start | bytes 786440 | tf_op jit(solution)/shard_map/ppermute | solution.py:639
  103.2 18.5 %collective-permute-start.20 = (f32[2,256,128]{2,1,0:T(8,128)S(1)}, f32[2,256,128]{2,1,0:T(8,128)S(1)}, u32[]{:S(2)}, u32[]{:S(2)}) collective-permute-start(f32[2,256,128]{2,1,0:T(8,128)S(1)} %get-tuple-element.79.refs_3_.y2_high), channel_id=1, source_target_pairs={{0,8},{4,12},{8,16},{12,20},{16,24},{20,28},{24,0},{28,4},{1,9},{5... | collective-permute-start | bytes 786440 | tf_op jit(solution)/shard_map/ppermute | solution.py:639
  111.4 16.9 %collective-permute-start.23 = (f32[2,256,256]{2,1,0:T(8,128)S(1)}, f32[2,256,256]{2,1,0:T(8,128)S(1)}, u32[]{:S(2)}, u32[]{:S(2)}) collective-permute-start(f32[2,256,256]{2,1,0:T(8,128)S(1)} %get-tuple-element.88), channel_id=1, source_target_pairs={{0,4},{4,0},{8,12},{12,8},{16,20},{20,16},{24,28},{28,24},{1,5},{5... | collective-permute-start | bytes 1572872 | tf_op jit(solution)/shard_map/ppermute | solution.py:634
  112.3 12.5 %collective-permute-start.21 = (f32[2,256,128]{2,1,0:T(8,128)S(1)}, f32[2,256,128]{2,1,0:T(8,128)S(1)}, u32[]{:S(2)}, u32[]{:S(2)}) collective-permute-start(f32[2,256,128]{2,1,0:T(8,128)S(1)} %get-tuple-element.77.refs_1_.y2_low), channel_id=1, source_target_pairs={{0,24},{4,28},{8,0},{12,4},{16,8},{20,12},{24,16},{28,20},{1,25},{... | collective-permute-start | bytes 786440 | tf_op jit(solution)/shard_map/ppermute | solution.py:639
  118.5 12.4 %collective-permute-start.19 = (f32[2,256,128]{2,1,0:T(8,128)S(1)}, f32[2,256,128]{2,1,0:T(8,128)S(1)}, u32[]{:S(2)}, u32[]{:S(2)}) collective-permute-start(f32[2,256,128]{2,1,0:T(8,128)S(1)} %get-tuple-element.83), channel_id=1, source_target_pairs={{0,4},{4,0},{8,12},{12,8},{16,20},{20,16},{24,28},{28,24},{1,5},{5... | collective-permute-start | bytes 786440 | tf_op jit(solution)/shard_map/ppermute | solution.py:634
  127.3 8.3 %collective-permute-start.22 = (f32[2,256,128]{2,1,0:T(8,128)S(1)}, f32[2,256,128]{2,1,0:T(8,128)S(1)}, u32[]{:S(2)}, u32[]{:S(2)}) collective-permute-start(f32[2,256,128]{2,1,0:T(8,128)S(1)} %get-tuple-element.86), channel_id=1, source_target_pairs={{0,4},{4,0},{8,12},{12,8},{16,20},{20,16},{24,28},{28,24},{1,5},{5... | collective-permute-start | bytes 786440 | tf_op jit(solution)/shard_map/ppermute | solution.py:634

commit v7 on v6

--- a/solution.py
+++ b/solution.py
@@ -65,11 +65,13 @@
     first.start()
     copies = []
     for at, out_ref in enumerate(cut_refs):
-        source = own_columns(vector_ref, 1 - at_ref[0], 2 * at, out_ref.shape[2])
+        chunks = len(cut_refs) // 2
+        source = own_columns(vector_ref, (1 - at_ref[0]) * chunks + at % chunks, 2 * (at // chunks), out_ref.shape[2])
         copies.append(pltpu.make_async_copy(source, out_ref, sems.at[1 + at]))
         copies[-1].start()
     first.wait()
-    traces_ref[...] = picked(split(held[...].T), one_hot(index_ref[0], held.shape[0]))
+    rows = jnp.concatenate([index_ref[0, 0:1], index_ref[0, 1:2]], axis=1)
+    traces_ref[...] = picked(split(held[...].T), one_hot(rows, held.shape[0]))
     for copy in copies:
         copy.wait()
 
@@ -106,11 +108,12 @@
         for copy in copies(at):
             copy.wait()
         turned = held[at].T
-        found = picked(split(turned), one_hot(index_ref[at], held.shape[1]))
+        rows = jnp.concatenate([index_ref[at, place : place + 1] for place in (0, 2, 1, 3)], axis=1)
+        found = picked(split(turned), one_hot(rows, held.shape[1]))
         traces[at] = found
         width = found.shape[1] // 2
         outer, layer = found[:, :width], found[:, width:]
-        total = dot3(split(turned * quad_ref[at]), split(acted[at]))
+        total = dot3(split(turned * quad_ref[pl.ds(at, 1)]), split(acted[at]))
         total = total + dot3(split((2.0 * outer + layer) * (1.0 / faces_total)), split(outer), NT)
         mixed, side, diagonal = packed(0.5 * (total + total.T))
         store(at, slice(size, size + half), jnp.concatenate([mixed, side], axis=1))
@@ -120,11 +123,15 @@
     def _(at):
         following = traces[at + 1]
         width = following.shape[1] // 2
-        order = one_hot(pair_ref[at], width)
+        order = one_hot(paired(pair_ref[pl.ds(at, 1)]), width)
         face, inside = picked(split(following[:, :width]), order), picked(split(following[:, width:]), order)
         store(at, slice(0, size), coupled(traces[at], face, inside, faces_total))
 
     last_ref[...] = traces[count - 1]
+
+
+def paired(row):
+    return jnp.concatenate([jnp.full_like(row, -2 * row.shape[1] - 1), row], axis=1)
 
 
 def coupled(own, face, inside, faces_total):
@@ -138,8 +145,9 @@
 def last_kernel(faces_total, at_ref, pair_ref, own_ref, lead_ref, send_in, keep_in, send_ref, keep_ref, block, sem):
     width = own_ref.shape[1] // 2
     lead = split(lead_ref[...])
-    face = picked(lead, one_hot(pair_ref[...], width))
-    inside = picked(lead, one_hot(pair_ref[...], width, width // 2))
+    order = paired(pair_ref[pl.ds(pair_ref.shape[0] - 1, 1)])
+    face = picked(lead, one_hot(order, width))
+    inside = picked(lead, one_hot(order, width, width // 2))
     block[...] = coupled(own_ref[...], face, inside, faces_total)
     at = send_ref.shape[0] - 1
     rows = pl.ds(0, block.shape[0])
@@ -382,18 +390,29 @@
     return vector_ref.at[pl.ds(element, count), :, pl.ds(pl.multiple_of(half * width, width), width)]
 
 
-def arrange_pair_kernel(element, wanted, at_ref, vector_ref, got_ref, out_ref, sems):
-    own = own_columns(vector_ref, at_ref[0], element, got_ref.shape[2])
-    copy_pairs(at_ref[0], ((wanted, own, out_ref), (1 - wanted, got_ref, out_ref)), sems)
-
-
-def arrange_kernel(at_ref, vector_ref, first_ref, second_ref, out_ref, sems):
-    own = own_columns(vector_ref, at_ref[0], 0, first_ref.shape[2], 4)
+def chunk_of(ref, element, chunk, width):
+    rows = pl.ds(element, 2)
+    return ref.at[rows] if ref.shape[2] == width else ref.at[rows, :, pl.ds(chunk * width, width)]
+
+
+def arrange_pair_kernel(element, wanted, at_ref, vector_ref, *refs):
+    got_refs, (out_ref, sems) = refs[:-2], refs[-2:]
+    pairs = [(wanted, own_columns(vector_ref, at_ref[0], element, out_ref.shape[2]), out_ref)]
+    for chunk, got_ref in enumerate(got_refs):
+        pairs.append((1 - wanted, got_ref, chunk_of(out_ref, 0, chunk, got_ref.shape[2])))
+    copy_pairs(at_ref[0], pairs, sems)
+
+
+def arrange_kernel(at_ref, vector_ref, *refs):
+    got_refs, (out_ref, sems) = refs[:-2], refs[-2:]
+    own = own_columns(vector_ref, at_ref[0], 0, out_ref.shape[2], 4)
+    chunks = len(got_refs) // 2
     pairs = []
     for side in range(2):
         pairs.append((side, own, out_ref.at[pl.ds(4 * side, 4)]))
-        pairs.append((side, first_ref, out_ref.at[pl.ds(4 - 4 * side, 2)]))
-        pairs.append((side, second_ref, out_ref.at[pl.ds(6 - 4 * side, 2)]))
+        for at, got_ref in enumerate(got_refs):
+            element = 4 - 4 * side + 2 * (at // chunks)
+            pairs.append((side, got_ref, chunk_of(out_ref, element, at % chunks, got_ref.shape[2])))
     copy_pairs(at_ref[0], pairs, sems)
 
 
@@ -435,21 +454,21 @@
         act(lambda copy: copy.wait())
 
 
-def lead_and_cut(at, index, basis, vector, half):
+def lead_and_cut(at, index, basis, vector, half, chunks):
     points, size = basis.shape[1:]
     return pl.pallas_call(
         lead_kernel,
         in_specs=[SCALARS, VMEM, ANY, ANY],
-        out_specs=[VMEM] * 3,
-        out_shape=[near_core((size, index.shape[2]))] + [near_core((2, size, half))] * 2,
-        scratch_shapes=[pltpu.VMEM((points, size), jnp.float32), pltpu.SemaphoreType.DMA((3,))],
+        out_specs=[VMEM] * (1 + 2 * chunks),
+        out_shape=[near_core((size, 2 * index.shape[2]))] + [near_core((2, size, half // chunks))] * (2 * chunks),
+        scratch_shapes=[pltpu.VMEM((points, size), jnp.float32), pltpu.SemaphoreType.DMA((1 + 2 * chunks,))],
         compiler_params=PARAMS,
     )(at, index, far_off(basis), far_off(vector))
 
 
 def blocks(core, index, quad, pairs, basis, applied, faces_total):
     count, points, size = basis.shape
-    spots = index.shape[2]
+    spots = 4 * index.shape[2]
     part = near_core((count // 2, size + size // 2 + 8, size))
     return pl.pallas_call(
         functools.partial(blocks_kernel, faces_total),
@@ -583,25 +602,27 @@
 
 
 def arranged_pair(at, element, wanted, vector, got):
+    _, size, width = got[0].shape
     return pl.pallas_call(
         functools.partial(arrange_pair_kernel, element, wanted),
-        in_specs=[SCALARS, ANY, ANY],
+        in_specs=[SCALARS] + [ANY] * (1 + len(got)),
         out_specs=VMEM,
-        out_shape=near_core(got.shape),
-        scratch_shapes=[pltpu.SemaphoreType.DMA((2,))],
-        compiler_params=PARAMS,
-    )(at, far_off(vector), got)
-
-
-def arranged(at, vector, first, second):
+        out_shape=near_core((2, size, width * len(got))),
+        scratch_shapes=[pltpu.SemaphoreType.DMA((1 + len(got),))],
+        compiler_params=PARAMS,
+    )(at, far_off(vector), *got)
+
+
+def arranged(at, vector, got):
+    _, size, width = got[0].shape
     return pl.pallas_call(
         arrange_kernel,
-        in_specs=[SCALARS, ANY, ANY, ANY],
+        in_specs=[SCALARS] + [ANY] * (1 + len(got)),
         out_specs=VMEM,
-        out_shape=near_core((8, *first.shape[1:])),
-        scratch_shapes=[pltpu.SemaphoreType.DMA((6,))],
-        compiler_params=PARAMS,
-    )(at, far_off(vector), first, second)
+        out_shape=near_core((8, size, width * len(got) // 2)),
+        scratch_shapes=[pltpu.SemaphoreType.DMA((2 + 2 * len(got),))],
+        compiler_params=PARAMS,
+    )(at, far_off(vector), *got)
 
 
 def collected(at, y4, near):
@@ -652,38 +673,33 @@
     vector = orbitals.reshape(count, size, columns)
     at = jnp.stack([side, core, lane, side * 4 + core * 2 + lane]).astype(jnp.int32)
 
-    lead_index = face_index[:1, 0:2].reshape(1, 1, 2 * spots)
-    index = jnp.stack([face_index[:, 0], face_index[:, 2], face_index[:, 1], face_index[:, 3]], axis=1)
-    index = index.reshape(count, 1, 4 * spots)
-    pairs = jnp.concatenate([jnp.full_like(face_pairing, -points), face_pairing], axis=1).reshape(count, 1, 2 * spots)
-    quad = quad.reshape(count, 1, points)
-    last_pair = pairs[-1]
-    vector, at, lead_index, index, pairs, last_pair, quad = lax.optimization_barrier(
-        (vector, at, lead_index, index, pairs, last_pair, quad)
-    )
+    vector, at = lax.optimization_barrier((vector, at))
     wide = columns // 2
     part = wide // chunks
     own = foreign = vector
     if part % 128:
         own = lax.dynamic_slice_in_dim(vector, side * part, part, axis=2)
         foreign = lax.dynamic_slice_in_dim(vector, (1 - side) * part, part, axis=2)
-    lead, first, second = lead_and_cut(at, lead_index, basis, foreign, wide)
+    lead, *got = lead_and_cut(at, face_index, basis, foreign, wide, chunks)
     lead = shifted(lead, "elem", -1)
-    first, second = flipped(first, "elem", 1), flipped(second, "elem", 1)
-
-    send, keep, last = blocks(at, index, quad, pairs, basis, applied, faces_total)
-    send, keep = last_coupling(at, last_pair, last, lead, send, keep, faces_total)
+    got = [flipped(value, "elem", 1) for value in got]
+
+    send, keep, last = blocks(at, face_index, quad, face_pairing, basis, applied, faces_total)
+    send, keep = last_coupling(at, face_pairing, last, lead, send, keep, faces_total)
+    got[0], send = lax.optimization_barrier((got[0], send))
     send, stay = folded(at, keep, flipped(send, "pts", 1))
-    mine = added(stay, flipped(send, "pts", 2))
+    received = flipped(send, "pts", 2)
+    pair_low = arranged_pair(at, 0, 0, own, got[:chunks])
+    pair_low, received = lax.optimization_barrier((pair_low, received))
+    mine = added(stay, received)
     bit = 4
     while bit < width:
         mine = mine + flipped(mine, "pts", bit)
         bit *= 2
-    first, mine = lax.optimization_barrier((first, mine))
-    above = shifted(arranged_pair(at, 0, 0, own, first), "elem", -2)
+    above = shifted(pair_low, "elem", -2)
     beside = flipped(mine, "pts", 2)
     across = flipped(mine, "elem", 1)
-    beside, across = lax.optimization_barrier((beside, across))
+    above, beside, across = lax.optimization_barrier((above, beside, across))
     mine_near = flipped(mine, "pts", 1)
     both = flipped(across, "pts", 2)
     beside_near = flipped(beside, "pts", 1)
@@ -693,18 +709,19 @@
     flat = lambda e, p: e % elems * width + p
     holds = [(e, p) for e in range(elems) for p in range(width) if e % 2 == p % 2]
     outer = lax.ppermute(last, ("elem", "pts"), [(flat(e, p), flat(e + (2 if p % 2 else -2), p)) for e, p in holds])
-    outer = added(outer, lax.ppermute(outer, ("elem", "pts"), [(flat(e, p), flat(e ^ 1, p)) for e, p in holds]))
-    outer_near = flipped(outer, "pts", 1)
-
-    above, second, both = lax.optimization_barrier((above, second, both))
-    below = shifted(arranged_pair(at, 2, 1, own, second), "elem", 2)
-    y0 = arranged(at, own, first, second)
+    passed = lax.ppermute(outer, ("elem", "pts"), [(flat(e, p), flat(e ^ 1, p)) for e, p in holds])
+    got[chunks:], both = lax.optimization_barrier((got[chunks:], both))
+
+    below = shifted(arranged_pair(at, 2, 1, own, got[chunks:]), "elem", 2)
+    y0 = arranged(at, own, got)
     both_near = flipped(both, "pts", 1)
 
     high, low = weights(at, mine, mine_near, beside, across, beside_near, across_near, both, both_near)
-    high_outer, low_outer = outer_weights(at, outer, outer_near, high, low)
 
     y1 = first_rows(high, low, y0, above)
+    below, y1, passed = lax.optimization_barrier((below, y1, passed))
+    outer = added(outer, passed)
+    high_outer, low_outer = outer_weights(at, outer, flipped(outer, "pts", 1), high, low)
     y1_ends, *ends = second_rows(chunks, high, low, high_outer, low_outer, y0, below, above, y1)
     belows = [shifted(value, "elem", 2) for value in ends[chunks:]]
     aboves = [shifted(value, "elem", -2) for value in ends[:chunks]]

time: 138 us -> 129 us (0.935)
  waiting for transfers between devices: 60.3 us -> 48.9 us
  starting transfers between devices: 28 us -> 33.5 us
  local copies, waits for them, and re-layouts: 5.46 us -> 2 us
    ppermute x1, waiting for transfers between devices: 8.14 us -> 0.01 us  [body(): lax.ppermute(outer, ('elem', 'pts'), [(flat(e, p), flat(e ^ 1, p)) for e,...]
    ppermute x1, waiting for transfers between devices: 10.2 us -> 4.58 us  [body(): lax.ppermute(last, ('elem', 'pts'), [(flat(e, p), flat(e + (2 if p % 2 el...]
    ppermute x15 -> x17, starting transfers between devices: 8.25 us -> 13.8 us  [flipped(): return lax.ppermute(value, axis, [(i, i ^ bit) for i in range(count)])]
    ppermute x7, starting transfers between devices: 16.1 us -> 13 us  [shifted(): lax.ppermute(value, axis, [(i, (i + steps) % count) for i in range(count)])]
    ppermute x1, starting transfers between devices: 2.36 us -> 5.27 us  [body(): lax.ppermute(last, ('elem', 'pts'), [(flat(e, p), flat(e + (2 if p % 2 el...]
    slice x3 -> x0, local copies, waits for them, and re-layouts: 2.29 us -> none  [the longest x1 0.85 us: body(): face_index[:, 0]]
    reshape x4 -> x0, local copies, waits for them, and re-layouts: 1.63 us -> none  [the longest x1 0.76 us: body(): jnp.concatenate([jnp.full_like(face_pairing, -points), face_pairing], axi...]
    ppermute x15 -> x17, waiting for transfers between devices: 33.7 us -> 34.7 us  [flipped(): return lax.ppermute(value, axis, [(i, i ^ bit) for i in range(count)])]
  transfers between devices with their start and end apart: 24 -> 26, of which waited for: 13 -> 14; matrix products, arithmetic and copies ran while one was open for 0% -> 0% of each run, Pallas kernels for 25% -> 27%
where the time goes in v7:
time: 129 us; the launch traced here: 128 us
  waiting for transfers between devices  48.9 us (38%)
  Pallas kernels  43.5 us (34%)
  starting transfers between devices  33.5 us (26%)
  local copies, waits for them, and re-layouts  2 us (2%)
    ppermute x17, waiting for transfers between devices, flipped(): return lax.ppermute(value, axis, [(i, i ^ bit) for i in range(count)])  34.7 us
    ppermute x17, starting transfers between devices, flipped(): return lax.ppermute(value, axis, [(i, i ^ bit) for i in range(count)])  13.8 us
    ppermute x7, starting transfers between devices, shifted(): lax.ppermute(value, axis, [(i, (i + steps) % count) for i in range(count)])  13 us
    ppermute x7, waiting for transfers between devices, shifted(): lax.ppermute(value, axis, [(i, (i + steps) % count) for i in range(count)])  9.59 us
    pallas_call x1, Pallas kernels, middle_rows(): pl.pallas_call(functools.partial(middle_kernel, chunks), in_specs=[SCALAR...  8.14 us
    pallas_call x1, Pallas kernels, blocks(): pl.pallas_call(functools.partial(blocks_kernel, faces_total), in_specs=[S...  7.62 us
    ppermute x1, starting transfers between devices, body(): lax.ppermute(last, ('elem', 'pts'), [(flat(e, p), flat(e + (2 if p % 2 el...  5.27 us
    pallas_call x2, Pallas kernels, last_rows(): pl.pallas_call(functools.partial(last_rows_kernel, lane), in_specs=[SCALA...  4.95 us
  transfers between devices with their start and end apart: 26, of which 14 were waited for; matrix products, arithmetic and copies ran while one was open for 0% of the time, Pallas kernels for 27%

profile of v7, /device:TPU:0, one launch (start us, length us, event | category | flops | bytes accessed | tf_op | source)
XLA Modules:
  0.0 128.4 jit_solution(9094117664492190063)
XLA Ops:
  0.8 2.1 %shard_map.65 = (f32[256,128]{1,0:T(8,128)S(1)}, f32[2,256,128]{2,1,0:T(8,128)S(1)}, f32[2,256,128]{2,1,0:T(8,128)S(1)}, f32[2,256,128]{2,1,0:T(8,128)S(1)}, f32[2,256,128]{2,1,0:T(8,128)S(1)}) custom-call(s32[4]{0:T(128)S(1)} %pad_add_fusion.at_ref, s32[4,4,64]{2,1,0:T(4,128)S(1)} %copy-done.2, f32[4,512,256]{2,1,0:T(8,128)} %basis_ref.3, ...), custom_call_target="tpu_custom_call" | custom-call | tf_op jit(solution)/shard_map/pallas_call | solution.py:459
  2.8 3.0 %collective-permute-start.1 = (f32[2,256,128]{2,1,0:T(8,128)S(1)}, f32[2,256,128]{2,1,0:T(8,128)S(1)}, u32[]{:S(2)}, u32[]{:S(2)}) collective-permute-start(f32[2,256,128]{2,1,0:T(8,128)S(1)} %get-tuple-element.57), channel_id=1, source_target_pairs={{0,4},{4,0},{8,12},{12,8},{16,20},{20,16},{24,28},{28,24},{1,5},{5... | collective-permute-start | bytes 786440 | tf_op jit(solution)/shard_map/ppermute | solution.py:655
  5.9 3.5 %collective-permute-start = (f32[256,128]{1,0:T(8,128)S(1)}, f32[256,128]{1,0:T(8,128)S(1)}, u32[]{:S(2)}, u32[]{:S(2)}) collective-permute-start(f32[256,128]{1,0:T(8,128)S(1)} %get-tuple-element.53), channel_id=1, source_target_pairs={{0,28},{4,0},{8,4},{12,8},{16,12},{20,16},{24,20},{28,24},{1,29},{... | collective-permute-start | bytes 393224 | tf_op jit(solution)/shard_map/ppermute | solution.py:660
  9.4 7.6 %shard_map.64 = (f32[2,392,256]{2,1,0:T(8,128)S(1)}, f32[2,392,256]{2,1,0:T(8,128)S(1)}, f32[256,256]{1,0:T(8,128)S(1)}) custom-call(s32[4]{0:T(128)S(1)} %pad_add_fusion.at_ref, s32[4,4,64]{2,1,0:T(4,128)S(1)} %copy-done.2, f32[4,512]{1,0:T(4,128)S(1)} %copy-done.3, s32[4,64]{1,0:T(4,128)S(1)} %copy-done.4, f32[4,512,256]{2,1,0:T(8,128)} %basis_ref.3, ...), custom_call_target="tpu_custom_call" | custom-call | tf_op jit(solution)/shard_map/pallas_call | solution.py:473
  18.4 2.3 %collective-permute-done.2.other_ref = f32[2,392,256]{2,1,0:T(8,128)S(1)} collective-permute-done((f32[2,392,256]{2,1,0:T(8,128)S(1)}, f32[2,392,256]{2,1,0:T(8,128)S(1)}, u32[]{:S(2)}, u32[]{:S(2)}) %collective-permute-start.2) | collective-permute-done | bytes 802848 | tf_op jit(solution)/shard_map/ppermute | solution.py:655
  21.3 1.6 %collective-permute-start.4 = (f32[1,392,256]{2,1,0:T(8,128)S(1)}, f32[1,392,256]{2,1,0:T(8,128)S(1)}, u32[]{:S(2)}, u32[]{:S(2)}) collective-permute-start(f32[1,392,256]{2,1,0:T(8,128)S(1)} %get-tuple-element.63), channel_id=1, source_target_pairs={{0,2},{1,3},{2,0},{3,1},{4,6},{5,7},{6,4},{7,5},{8,10},{9,11},{10,... | collective-permute-start | bytes 1204232 | tf_op jit(solution)/shard_map/ppermute | solution.py:655
  22.9 8.1 %collective-permute-done.3.refs_1_ = f32[2,256,128]{2,1,0:T(8,128)S(1)} collective-permute-done((f32[2,256,128]{2,1,0:T(8,128)S(1)}, f32[2,256,128]{2,1,0:T(8,128)S(1)}, u32[]{:S(2)}, u32[]{:S(2)}) %collective-permute-start.3) | collective-permute-done | bytes 262176 | tf_op jit(solution)/shard_map/ppermute | solution.py:655
  30.9 1.6 %shard_map.68 = f32[2,256,256]{2,1,0:T(8,128)S(1)} custom-call(s32[4]{0:T(128)S(1)} %pad_add_fusion.at_ref, f32[4,256,512]{2,1,0:T(8,128)} %bitcast.7, f32[2,256,128]{2,1,0:T(8,128)S(1)} %collective-permute-done.1.refs_0_, f32[2,256,128]{2,1,0:T(8,128)S(1)} %collective-permute-done.3.refs_1_), custom_call_target="tpu_custom_call" | custom-call | tf_op jit(solution)/shard_map/pallas_call | solution.py:606
  32.7 1.8 %collective-permute-start.6 = (f32[2,256,256]{2,1,0:T(8,128)S(1)}, f32[2,256,256]{2,1,0:T(8,128)S(1)}, u32[]{:S(2)}, u32[]{:S(2)}) collective-permute-start(f32[2,256,256]{2,1,0:T(8,128)S(1)} %shard_map.68), channel_id=1, source_target_pairs={{0,24},{4,28},{8,0},{12,4},{16,8},{20,12},{24,16},{28,20},{1,25},{... | collective-permute-start | bytes 1572872 | tf_op jit(solution)/shard_map/ppermute | solution.py:660
  34.5 1.6 %collective-permute-start.7 = (f32[1,392,256]{2,1,0:T(8,128)S(1)}, f32[1,392,256]{2,1,0:T(8,128)S(1)}, u32[]{:S(2)}, u32[]{:S(2)}) collective-permute-start(f32[1,392,256]{2,1,0:T(8,128)S(1)} %shard_map.69.refs_0_.mine_ref), channel_id=1, source_target_pairs={{0,2},{1,3},{2,0},{3,1},{4,6},{5,7},{6,4},{7,5},{8,10},{9,11},{10,... | collective-permute-start | bytes 1204232 | tf_op jit(solution)/shard_map/ppermute | solution.py:655
  36.4 8.4 %collective-permute-done.7.refs_2_.beside_ref = f32[1,392,256]{2,1,0:T(8,128)S(1)} collective-permute-done((f32[1,392,256]{2,1,0:T(8,128)S(1)}, f32[1,392,256]{2,1,0:T(8,128)S(1)}, u32[]{:S(2)}, u32[]{:S(2)}) %collective-permute-start.7) | collective-permute-done | bytes 401440 | tf_op jit(solution)/shard_map/ppermute | solution.py:655
  46.8 5.3 %collective-permute-start.15 = (f32[1,648,256]{2,1,0:T(8,128)S(1)}, f32[1,648,256]{2,1,0:T(8,128)S(1)}, u32[]{:S(2)}, u32[]{:S(2)}) collective-permute-start(f32[1,648,256]{2,1,0:T(8,128)S(1)} %shard_map.71), channel_id=1, source_target_pairs={{0,24},{2,26},{5,13},{7,15},{8,0},{10,2},{13,21},{15,23},{16,8},{1... | collective-permute-start | bytes 1990664 | tf_op jit(solution)/shard_map/ppermute | solution.py:711
  52.1 1.6 %collective-permute-start.13 = (f32[1,392,256]{2,1,0:T(8,128)S(1)}, f32[1,392,256]{2,1,0:T(8,128)S(1)}, u32[]{:S(2)}, u32[]{:S(2)}) collective-permute-start(f32[1,392,256]{2,1,0:T(8,128)S(1)} %collective-permute-done.8.refs_3_), channel_id=1, source_target_pairs={{0,2},{1,3},{2,0},{3,1},{4,6},{5,7},{6,4},{7,5},{8,10},{9,11},{10,... | collective-permute-start | bytes 1204232 | tf_op jit(solution)/shard_map/ppermute | solution.py:655
  53.7 2.0 %collective-permute-start.12 = (f32[2,256,128]{2,1,0:T(8,128)S(1)}, f32[2,256,128]{2,1,0:T(8,128)S(1)}, u32[]{:S(2)}, u32[]{:S(2)}) collective-permute-start(f32[2,256,128]{2,1,0:T(8,128)S(1)} %get-tuple-element.69), channel_id=1, source_target_pairs={{0,4},{4,0},{8,12},{12,8},{16,20},{20,16},{24,28},{28,24},{1,5},{5... | collective-permute-start | bytes 786440 | tf_op jit(solution)/shard_map/ppermute | solution.py:655
  55.7 4.6 %collective-permute-done.15.first_ref = f32[1,648,256]{2,1,0:T(8,128)S(1)} collective-permute-done((f32[1,648,256]{2,1,0:T(8,128)S(1)}, f32[1,648,256]{2,1,0:T(8,128)S(1)}, u32[]{:S(2)}, u32[]{:S(2)}) %collective-permute-start.15) | collective-permute-done | bytes 663584 | tf_op jit(solution)/shard_map/ppermute | solution.py:711
  62.8 5.6 %collective-permute-done.12.refs_1_.refs_3_ = f32[2,256,128]{2,1,0:T(8,128)S(1)} collective-permute-done((f32[2,256,128]{2,1,0:T(8,128)S(1)}, f32[2,256,128]{2,1,0:T(8,128)S(1)}, u32[]{:S(2)}, u32[]{:S(2)}) %collective-permute-start.12) | collective-permute-done | bytes 262176 | tf_op jit(solution)/shard_map/ppermute | solution.py:655
  69.8 1.9 %shard_map.73.y0 = f32[8,256,256]{2,1,0:T(8,128)S(1)} custom-call(s32[4]{0:T(128)S(1)} %pad_add_fusion.at_ref, f32[4,256,512]{2,1,0:T(8,128)} %bitcast.9, f32[2,256,128]{2,1,0:T(8,128)S(1)} %collective-permute-done.1.refs_0_, f32[2,256,128]{2,1,0:T(8,128)S(1)} %collective-permute-done.3.refs_1_, f32[2,256,128]{2,1,0:T(8,128)S(1)} %collective-permute-done.11.refs_0_.refs_2_, ...), custom_call_target="tpu_custom_call" | custom-call | tf_op jit(solution)/shard_map/pallas_call | solution.py:618
  73.4 3.4 %shard_map.70 = (bf16[8,256,768]{2,1,0:T(8,128)(2,1)S(1)}, bf16[8,256,768]{2,1,0:T(8,128)(2,1)S(1)}) custom-call(s32[4]{0:T(128)S(1)} %pad_add_fusion.at_ref, f32[1,392,256]{2,1,0:T(8,128)} %copy-done, f32[1,392,256]{2,1,0:T(8,128)} %copy-done.7, f32[1,392,256]{2,1,0:T(8,128)} %copy-done.1, f32[1,392,256]{2,1,0:T(8,128)} %copy-done.5, ...), custom_call_target="tpu_custom_call" | custom-call | tf_op jit(solution)/shard_map/pallas_call | solution.py:503
  76.7 3.8 %shard_map.74.y1 = f32[7,256,256]{2,1,0:T(8,128)S(1)} custom-call(bf16[8,256,768]{2,1,0:T(8,128)(2,1)S(1)} %get-tuple-element.71.high.high_in, bf16[8,256,768]{2,1,0:T(8,128)(2,1)S(1)} %get-tuple-element.72.low.low_in, f32[8,256,256]{2,1,0:T(8,128)S(1)} %shard_map.73.y0, f32[2,256,256]{2,1,0:T(8,128)S(1)} %collective-permute-done.6.above), custom_call_target="tpu_custom_call" | custom-call | tf_op jit(solution)/shard_map/pallas_call | solution.py:526
  80.5 3.6 %collective-permute-done.16.below = f32[2,256,256]{2,1,0:T(8,128)S(1)} collective-permute-done((f32[2,256,256]{2,1,0:T(8,128)S(1)}, f32[2,256,256]{2,1,0:T(8,128)S(1)}, u32[]{:S(2)}, u32[]{:S(2)}) %collective-permute-start.16) | collective-permute-done | bytes 524320 | tf_op jit(solution)/shard_map/ppermute | solution.py:660
  84.3 2.1 %collective-permute-done.18.swapped_ref = f32[1,648,256]{2,1,0:T(8,128)S(1)} collective-permute-done((f32[1,648,256]{2,1,0:T(8,128)S(1)}, f32[1,648,256]{2,1,0:T(8,128)S(1)}, u32[]{:S(2)}, u32[]{:S(2)}) %collective-permute-start.18) | collective-permute-done | bytes 663584 | tf_op jit(solution)/shard_map/ppermute | solution.py:655
  87.4 2.5 %shard_map.77 = (f32[3,256,256]{2,1,0:T(8,128)S(1)}, f32[2,256,128]{2,1,0:T(8,128)S(1)}, f32[2,256,128]{2,1,0:T(8,128)S(1)}, f32[2,256,128]{2,1,0:T(8,128)S(1)}, f32[2,256,128]{2,1,0:T(8,128)S(1)}) custom-call(bf16[8,256,768]{2,1,0:T(8,128)(2,1)S(1)} %get-tuple-element.71.high.high_in, bf16[8,256,768]{2,1,0:T(8,128)(2,1)S(1)} %get-tuple-element.72.low.low_in, ...), custom_call_target="tpu_custom_call" | custom-call | tf_op jit(solution)/shard_map/pallas_call | solution.py:538
  90.0 3.8 %collective-permute-start.20 = (f32[2,256,128]{2,1,0:T(8,128)S(1)}, f32[2,256,128]{2,1,0:T(8,128)S(1)}, u32[]{:S(2)}, u32[]{:S(2)}) collective-permute-start(f32[2,256,128]{2,1,0:T(8,128)S(1)} %get-tuple-element.82.refs_0_.y2_low), channel_id=1, source_target_pairs={{0,24},{4,28},{8,0},{12,4},{16,8},{20,12},{24,16},{28,20},{1,25},{... | collective-permute-start | bytes 786440 | tf_op jit(solution)/shard_map/ppermute | solution.py:660
  93.8 8.1 %shard_map.78 = (f32[4,256,256]{2,1,0:T(8,128)S(1)}, f32[4,256,256]{2,1,0:T(8,128)S(1)}, f32[2,256,256]{2,1,0:T(8,128)S(1)}) custom-call(s32[4]{0:T(128)S(1)} %pad_add_fusion.at_ref, bf16[8,256,768]{2,1,0:T(8,128)(2,1)S(1)} %get-tuple-element.71.high.high_in, bf16[8,256,768]{2,1,0:T(8,128)(2,1)S(1)} %get-tuple-element.72.low.low_in, ...), custom_call_target="tpu_custom_call" | custom-call | tf_op jit(solution)/shard_map/pallas_call | solution.py:550
  102.0 1.6 %collective-permute-start.25 = (f32[2,256,256]{2,1,0:T(8,128)S(1)}, f32[2,256,256]{2,1,0:T(8,128)S(1)}, u32[]{:S(2)}, u32[]{:S(2)}) collective-permute-start(f32[2,256,256]{2,1,0:T(8,128)S(1)} %get-tuple-element.94), channel_id=1, source_target_pairs={{0,4},{4,0},{8,12},{12,8},{16,20},{20,16},{24,28},{28,24},{1,5},{5... | collective-permute-start | bytes 1572872 | tf_op jit(solution)/shard_map/ppermute | solution.py:655
  103.5 3.8 %collective-permute-start.23 = (f32[2,256,128]{2,1,0:T(8,128)S(1)}, f32[2,256,128]{2,1,0:T(8,128)S(1)}, u32[]{:S(2)}, u32[]{:S(2)}) collective-permute-start(f32[2,256,128]{2,1,0:T(8,128)S(1)} %get-tuple-element.83.refs_1_.y2_low), channel_id=1, source_target_pairs={{0,24},{4,28},{8,0},{12,4},{16,8},{20,12},{24,16},{28,20},{1,25},{... | collective-permute-start | bytes 786440 | tf_op jit(solution)/shard_map/ppermute | solution.py:660
  107.4 2.5 %shard_map.79 = (f32[2,256,128]{2,1,0:T(8,128)S(1)}, f32[2,256,128]{2,1,0:T(8,128)S(1)}, f32[2,256,128]{2,1,0:T(8,128)S(1)}) custom-call(s32[4]{0:T(128)S(1)} %pad_add_fusion.at_ref, bf16[8,256,768]{2,1,0:T(8,128)(2,1)S(1)} %get-tuple-element.71.high.high_in, bf16[8,256,768]{2,1,0:T(8,128)(2,1)S(1)} %get-tuple-element.72.low.low_in, ...), custom_call_target="tpu_custom_call" | custom-call | tf_op jit(solution)/shard_map/pallas_call | solution.py:566
  110.4 1.8 %collective-permute-done.22.below = f32[2,256,128]{2,1,0:T(8,128)S(1)} collective-permute-done((f32[2,256,128]{2,1,0:T(8,128)S(1)}, f32[2,256,128]{2,1,0:T(8,128)S(1)}, u32[]{:S(2)}, u32[]{:S(2)}) %collective-permute-start.22) | collective-permute-done | bytes 262176 | tf_op jit(solution)/shard_map/ppermute | solution.py:660
  112.3 4.2 %collective-permute-done.23.above = f32[2,256,128]{2,1,0:T(8,128)S(1)} collective-permute-done((f32[2,256,128]{2,1,0:T(8,128)S(1)}, f32[2,256,128]{2,1,0:T(8,128)S(1)}, u32[]{:S(2)}, u32[]{:S(2)}) %collective-permute-start.23) | collective-permute-done | bytes 262176 | tf_op jit(solution)/shard_map/ppermute | solution.py:660
  116.5 2.5 %shard_map.80 = (f32[2,256,128]{2,1,0:T(8,128)S(1)}, f32[2,256,128]{2,1,0:T(8,128)S(1)}, f32[2,256,128]{2,1,0:T(8,128)S(1)}) custom-call(s32[4]{0:T(128)S(1)} %pad_add_fusion.at_ref, bf16[8,256,768]{2,1,0:T(8,128)(2,1)S(1)} %get-tuple-element.71.high.high_in, bf16[8,256,768]{2,1,0:T(8,128)(2,1)S(1)} %get-tuple-element.72.low.low_in, ...), custom_call_target="tpu_custom_call" | custom-call | tf_op jit(solution)/shard_map/pallas_call | solution.py:566
  121.3 5.4 %collective-permute-done.24.refs_5_ = f32[2,256,128]{2,1,0:T(8,128)S(1)} collective-permute-done((f32[2,256,128]{2,1,0:T(8,128)S(1)}, f32[2,256,128]{2,1,0:T(8,128)S(1)}, u32[]{:S(2)}, u32[]{:S(2)}) %collective-permute-start.24) | collective-permute-done | bytes 262176 | tf_op jit(solution)/shard_map/ppermute | solution.py:655
  126.7 1.6 %shard_map.82 = f32[4,256,512]{2,1,0:T(8,128)} custom-call(s32[4]{0:T(128)S(1)} %pad_add_fusion.at_ref, f32[2,256,128]{2,1,0:T(8,128)S(1)} %get-tuple-element.87.refs_0_, f32[2,256,128]{2,1,0:T(8,128)S(1)} %get-tuple-element.88.refs_1_, f32[2,256,128]{2,1,0:T(8,128)S(1)} %collective-permute-done.21.refs_2_, ...), custom_call_target="tpu_custom_call", output_to_operand_aliasing={{}: (7, {})} | custom-call | tf_op jit(solution)/shard_map/pallas_call | solution.py:642
  (62 shorter events, 15.0 us)
Async XLA Ops:
  0.8 8.6 %copy-start.3 = (f32[4,512]{1,0:T(4,128)S(1)}, f32[4,512]{1,0:T(4,128)}, u32[]{:S(2)}) copy-start(f32[4,512]{1,0:T(4,128)} %quad_ref.1) | copy-start | bytes 24580
  0.8 8.6 %copy-start.4 = (s32[4,64]{1,0:T(4,128)S(1)}, s32[4,64]{1,0:T(4,128)}, u32[]{:S(2)}) copy-start(s32[4,64]{1,0:T(4,128)} %pair_ref.3) | copy-start | bytes 3076
  2.8 15.5 %collective-permute-start.1 = (f32[2,256,128]{2,1,0:T(8,128)S(1)}, f32[2,256,128]{2,1,0:T(8,128)S(1)}, u32[]{:S(2)}, u32[]{:S(2)}) collective-permute-start(f32[2,256,128]{2,1,0:T(8,128)S(1)} %get-tuple-element.57), channel_id=1, source_target_pairs={{0,4},{4,0},{8,12},{12,8},{16,20},{20,16},{24,28},{28,24},{1,5},{5... | collective-permute-start | bytes 786440 | tf_op jit(solution)/shard_map/ppermute | solution.py:655
  5.9 11.2 %collective-permute-start = (f32[256,128]{1,0:T(8,128)S(1)}, f32[256,128]{1,0:T(8,128)S(1)}, u32[]{:S(2)}, u32[]{:S(2)}) collective-permute-start(f32[256,128]{1,0:T(8,128)S(1)} %get-tuple-element.53), channel_id=1, source_target_pairs={{0,28},{4,0},{8,4},{12,8},{16,12},{20,16},{24,20},{28,24},{1,29},{... | collective-permute-start | bytes 393224 | tf_op jit(solution)/shard_map/ppermute | solution.py:660
  18.3 2.4 %collective-permute-start.2 = (f32[2,392,256]{2,1,0:T(8,128)S(1)}, f32[2,392,256]{2,1,0:T(8,128)S(1)}, u32[]{:S(2)}, u32[]{:S(2)}) collective-permute-start(f32[2,392,256]{2,1,0:T(8,128)S(1)} %get-tuple-element.59), channel_id=1, source_target_pairs={{0,1},{1,0},{2,3},{3,2},{4,5},{5,4},{6,7},{7,6},{8,9},{9,8},{10,11... | collective-permute-start | bytes 2408456 | tf_op jit(solution)/shard_map/ppermute | solution.py:655
  21.3 11.4 %collective-permute-start.4 = (f32[1,392,256]{2,1,0:T(8,128)S(1)}, f32[1,392,256]{2,1,0:T(8,128)S(1)}, u32[]{:S(2)}, u32[]{:S(2)}) collective-permute-start(f32[1,392,256]{2,1,0:T(8,128)S(1)} %get-tuple-element.63), channel_id=1, source_target_pairs={{0,2},{1,3},{2,0},{3,1},{4,6},{5,7},{6,4},{7,5},{8,10},{9,11},{10,... | collective-permute-start | bytes 1204232 | tf_op jit(solution)/shard_map/ppermute | solution.py:655
  22.9 8.1 %collective-permute-start.3 = (f32[2,256,128]{2,1,0:T(8,128)S(1)}, f32[2,256,128]{2,1,0:T(8,128)S(1)}, u32[]{:S(2)}, u32[]{:S(2)}) collective-permute-start(f32[2,256,128]{2,1,0:T(8,128)S(1)} %get-tuple-element.62), channel_id=1, source_target_pairs={{0,4},{4,0},{8,12},{12,8},{16,20},{20,16},{24,28},{28,24},{1,5},{5... | collective-permute-start | bytes 786440 | tf_op jit(solution)/shard_map/ppermute | solution.py:655
  32.7 13.3 %collective-permute-start.6 = (f32[2,256,256]{2,1,0:T(8,128)S(1)}, f32[2,256,256]{2,1,0:T(8,128)S(1)}, u32[]{:S(2)}, u32[]{:S(2)}) collective-permute-start(f32[2,256,256]{2,1,0:T(8,128)S(1)} %shard_map.68), channel_id=1, source_target_pairs={{0,24},{4,28},{8,0},{12,4},{16,8},{20,12},{24,16},{28,20},{1,25},{... | collective-permute-start | bytes 1572872 | tf_op jit(solution)/shard_map/ppermute | solution.py:660
  34.5 34.5 %copy-start = (f32[1,392,256]{2,1,0:T(8,128)}, f32[1,392,256]{2,1,0:T(8,128)S(1)}, u32[]{:S(2)}) copy-start(f32[1,392,256]{2,1,0:T(8,128)S(1)} %shard_map.69.refs_0_.mine_ref) | copy-start | bytes 1204228
  34.5 10.3 %collective-permute-start.7 = (f32[1,392,256]{2,1,0:T(8,128)S(1)}, f32[1,392,256]{2,1,0:T(8,128)S(1)}, u32[]{:S(2)}, u32[]{:S(2)}) collective-permute-start(f32[1,392,256]{2,1,0:T(8,128)S(1)} %shard_map.69.refs_0_.mine_ref), channel_id=1, source_target_pairs={{0,2},{1,3},{2,0},{3,1},{4,6},{5,7},{6,4},{7,5},{8,10},{9,11},{10,... | collective-permute-start | bytes 1204232 | tf_op jit(solution)/shard_map/ppermute | solution.py:655
  36.1 9.9 %collective-permute-start.8 = (f32[1,392,256]{2,1,0:T(8,128)S(1)}, f32[1,392,256]{2,1,0:T(8,128)S(1)}, u32[]{:S(2)}, u32[]{:S(2)}) collective-permute-start(f32[1,392,256]{2,1,0:T(8,128)S(1)} %shard_map.69.refs_0_.mine_ref), channel_id=1, source_target_pairs={{0,4},{4,0},{8,12},{12,8},{16,20},{20,16},{24,28},{28,24},{1,5},{5... | collective-permute-start | bytes 1204232 | tf_op jit(solution)/shard_map/ppermute | solution.py:655
  44.8 24.3 %copy-start.1 = (f32[1,392,256]{2,1,0:T(8,128)}, f32[1,392,256]{2,1,0:T(8,128)S(1)}, u32[]{:S(2)}) copy-start(f32[1,392,256]{2,1,0:T(8,128)S(1)} %collective-permute-done.7.refs_2_.beside_ref) | copy-start | bytes 1204228
  46.0 23.2 %copy-start.5 = (f32[1,392,256]{2,1,0:T(8,128)}, f32[1,392,256]{2,1,0:T(8,128)S(1)}, u32[]{:S(2)}) copy-start(f32[1,392,256]{2,1,0:T(8,128)S(1)} %collective-permute-done.8.refs_3_) | copy-start | bytes 1204228
  46.8 13.4 %collective-permute-start.15 = (f32[1,648,256]{2,1,0:T(8,128)S(1)}, f32[1,648,256]{2,1,0:T(8,128)S(1)}, u32[]{:S(2)}, u32[]{:S(2)}) collective-permute-start(f32[1,648,256]{2,1,0:T(8,128)S(1)} %shard_map.71), channel_id=1, source_target_pairs={{0,24},{2,26},{5,13},{7,15},{8,0},{10,2},{13,21},{15,23},{16,8},{1... | collective-permute-start | bytes 1990664 | tf_op jit(solution)/shard_map/ppermute | solution.py:711
  52.1 16.3 %collective-permute-start.13 = (f32[1,392,256]{2,1,0:T(8,128)S(1)}, f32[1,392,256]{2,1,0:T(8,128)S(1)}, u32[]{:S(2)}, u32[]{:S(2)}) collective-permute-start(f32[1,392,256]{2,1,0:T(8,128)S(1)} %collective-permute-done.8.refs_3_), channel_id=1, source_target_pairs={{0,2},{1,3},{2,0},{3,1},{4,6},{5,7},{6,4},{7,5},{8,10},{9,11},{10,... | collective-permute-start | bytes 1204232 | tf_op jit(solution)/shard_map/ppermute | solution.py:655
  53.7 16.0 %collective-permute-start.5 = (f32[1,392,256]{2,1,0:T(8,128)S(1)}, f32[1,392,256]{2,1,0:T(8,128)S(1)}, u32[]{:S(2)}, u32[]{:S(2)}) collective-permute-start(f32[1,392,256]{2,1,0:T(8,128)S(1)} %shard_map.69.refs_0_.mine_ref), channel_id=1, source_target_pairs={{0,1},{1,0},{2,3},{3,2},{4,5},{5,4},{6,7},{7,6},{8,9},{9,8},{10,11... | collective-permute-start | bytes 1204232 | tf_op jit(solution)/shard_map/ppermute | solution.py:655
  53.7 9.1 %collective-permute-start.11 = (f32[2,256,128]{2,1,0:T(8,128)S(1)}, f32[2,256,128]{2,1,0:T(8,128)S(1)}, u32[]{:S(2)}, u32[]{:S(2)}) collective-permute-start(f32[2,256,128]{2,1,0:T(8,128)S(1)} %get-tuple-element.68), channel_id=1, source_target_pairs={{0,4},{4,0},{8,12},{12,8},{16,20},{20,16},{24,28},{28,24},{1,5},{5... | collective-permute-start | bytes 786440 | tf_op jit(solution)/shard_map/ppermute | solution.py:655
  53.7 14.7 %collective-permute-start.12 = (f32[2,256,128]{2,1,0:T(8,128)S(1)}, f32[2,256,128]{2,1,0:T(8,128)S(1)}, u32[]{:S(2)}, u32[]{:S(2)}) collective-permute-start(f32[2,256,128]{2,1,0:T(8,128)S(1)} %get-tuple-element.69), channel_id=1, source_target_pairs={{0,4},{4,0},{8,12},{12,8},{16,20},{20,16},{24,28},{28,24},{1,5},{5... | collective-permute-start | bytes 786440 | tf_op jit(solution)/shard_map/ppermute | solution.py:655
  60.3 23.8 %collective-permute-start.17 = (f32[1,648,256]{2,1,0:T(8,128)S(1)}, f32[1,648,256]{2,1,0:T(8,128)S(1)}, u32[]{:S(2)}, u32[]{:S(2)}) collective-permute-start(f32[1,648,256]{2,1,0:T(8,128)S(1)} %collective-permute-done.15.first_ref), channel_id=1, source_target_pairs={{0,4},{2,6},{5,1},{7,3},{8,12},{10,14},{13,9},{15,11},{16,20},{18,... | collective-permute-start | bytes 1990664 | tf_op jit(solution)/shard_map/ppermute | solution.py:712
  68.4 3.3 %copy-start.6 = (f32[1,392,256]{2,1,0:T(8,128)}, f32[1,392,256]{2,1,0:T(8,128)S(1)}, u32[]{:S(2)}) copy-start(f32[1,392,256]{2,1,0:T(8,128)S(1)} %collective-permute-done.13.refs_6_) | copy-start | bytes 1204228
  69.0 15.0 %collective-permute-start.16 = (f32[2,256,256]{2,1,0:T(8,128)S(1)}, f32[2,256,256]{2,1,0:T(8,128)S(1)}, u32[]{:S(2)}, u32[]{:S(2)}) collective-permute-start(f32[2,256,256]{2,1,0:T(8,128)S(1)} %shard_map.72), channel_id=1, source_target_pairs={{0,8},{4,12},{8,16},{12,20},{16,24},{20,28},{24,0},{28,4},{1,9},{5... | collective-permute-start | bytes 1572872 | tf_op jit(solution)/shard_map/ppermute | solution.py:660
  69.1 2.6 %collective-permute-start.9 = (f32[1,392,256]{2,1,0:T(8,128)S(1)}, f32[1,392,256]{2,1,0:T(8,128)S(1)}, u32[]{:S(2)}, u32[]{:S(2)}) collective-permute-start(f32[1,392,256]{2,1,0:T(8,128)S(1)} %collective-permute-done.7.refs_2_.beside_ref), channel_id=1, source_target_pairs={{0,1},{1,0},{2,3},{3,2},{4,5},{5,4},{6,7},{7,6},{8,9},{9,8},{10,11... | collective-permute-start | bytes 1204232 | tf_op jit(solution)/shard_map/ppermute | solution.py:655
  69.2 2.5 %collective-permute-start.10 = (f32[1,392,256]{2,1,0:T(8,128)S(1)}, f32[1,392,256]{2,1,0:T(8,128)S(1)}, u32[]{:S(2)}, u32[]{:S(2)}) collective-permute-start(f32[1,392,256]{2,1,0:T(8,128)S(1)} %collective-permute-done.8.refs_3_), channel_id=1, source_target_pairs={{0,1},{1,0},{2,3},{3,2},{4,5},{5,4},{6,7},{7,6},{8,9},{9,8},{10,11... | collective-permute-start | bytes 1204232 | tf_op jit(solution)/shard_map/ppermute | solution.py:655
  69.7 2.4 %collective-permute-start.14 = (f32[1,392,256]{2,1,0:T(8,128)S(1)}, f32[1,392,256]{2,1,0:T(8,128)S(1)}, u32[]{:S(2)}, u32[]{:S(2)}) collective-permute-start(f32[1,392,256]{2,1,0:T(8,128)S(1)} %collective-permute-done.13.refs_6_), channel_id=1, source_target_pairs={{0,1},{1,0},{2,3},{3,2},{4,5},{5,4},{6,7},{7,6},{8,9},{9,8},{10,11... | collective-permute-start | bytes 1204232 | tf_op jit(solution)/shard_map/ppermute | solution.py:655
  84.2 2.2 %collective-permute-start.18 = (f32[1,648,256]{2,1,0:T(8,128)S(1)}, f32[1,648,256]{2,1,0:T(8,128)S(1)}, u32[]{:S(2)}, u32[]{:S(2)}) collective-permute-start(f32[1,648,256]{2,1,0:T(8,128)S(1)} %shard_map.75.kept_ref), channel_id=1, source_target_pairs={{0,1},{1,0},{2,3},{3,2},{4,5},{5,4},{6,7},{7,6},{8,9},{9,8},{10,11... | collective-permute-start | bytes 1990664 | tf_op jit(solution)/shard_map/ppermute | solution.py:655
  90.0 17.4 %collective-permute-start.19 = (f32[2,256,128]{2,1,0:T(8,128)S(1)}, f32[2,256,128]{2,1,0:T(8,128)S(1)}, u32[]{:S(2)}, u32[]{:S(2)}) collective-permute-start(f32[2,256,128]{2,1,0:T(8,128)S(1)} %get-tuple-element.84.refs_2_.y2_high), channel_id=1, source_target_pairs={{0,8},{4,12},{8,16},{12,20},{16,24},{20,28},{24,0},{28,4},{1,9},{5... | collective-permute-start | bytes 786440 | tf_op jit(solution)/shard_map/ppermute | solution.py:660
  90.0 17.3 %collective-permute-start.20 = (f32[2,256,128]{2,1,0:T(8,128)S(1)}, f32[2,256,128]{2,1,0:T(8,128)S(1)}, u32[]{:S(2)}, u32[]{:S(2)}) collective-permute-start(f32[2,256,128]{2,1,0:T(8,128)S(1)} %get-tuple-element.82.refs_0_.y2_low), channel_id=1, source_target_pairs={{0,24},{4,28},{8,0},{12,4},{16,8},{20,12},{24,16},{28,20},{1,25},{... | collective-permute-start | bytes 786440 | tf_op jit(solution)/shard_map/ppermute | solution.py:660
  93.8 18.5 %collective-permute-start.22 = (f32[2,256,128]{2,1,0:T(8,128)S(1)}, f32[2,256,128]{2,1,0:T(8,128)S(1)}, u32[]{:S(2)}, u32[]{:S(2)}) collective-permute-start(f32[2,256,128]{2,1,0:T(8,128)S(1)} %get-tuple-element.85.refs_3_.y2_high), channel_id=1, source_target_pairs={{0,8},{4,12},{8,16},{12,20},{16,24},{20,28},{24,0},{28,4},{1,9},{5... | collective-permute-start | bytes 786440 | tf_op jit(solution)/shard_map/ppermute | solution.py:660
  102.0 17.8 %collective-permute-start.25 = (f32[2,256,256]{2,1,0:T(8,128)S(1)}, f32[2,256,256]{2,1,0:T(8,128)S(1)}, u32[]{:S(2)}, u32[]{:S(2)}) collective-permute-start(f32[2,256,256]{2,1,0:T(8,128)S(1)} %get-tuple-element.94), channel_id=1, source_target_pairs={{0,4},{4,0},{8,12},{12,8},{16,20},{20,16},{24,28},{28,24},{1,5},{5... | collective-permute-start | bytes 1572872 | tf_op jit(solution)/shard_map/ppermute | solution.py:655
  103.5 12.9 %collective-permute-start.23 = (f32[2,256,128]{2,1,0:T(8,128)S(1)}, f32[2,256,128]{2,1,0:T(8,128)S(1)}, u32[]{:S(2)}, u32[]{:S(2)}) collective-permute-start(f32[2,256,128]{2,1,0:T(8,128)S(1)} %get-tuple-element.83.refs_1_.y2_low), channel_id=1, source_target_pairs={{0,24},{4,28},{8,0},{12,4},{16,8},{20,12},{24,16},{28,20},{1,25},{... | collective-permute-start | bytes 786440 | tf_op jit(solution)/shard_map/ppermute | solution.py:660
  109.8 11.5 %collective-permute-start.21 = (f32[2,256,128]{2,1,0:T(8,128)S(1)}, f32[2,256,128]{2,1,0:T(8,128)S(1)}, u32[]{:S(2)}, u32[]{:S(2)}) collective-permute-start(f32[2,256,128]{2,1,0:T(8,128)S(1)} %get-tuple-element.89), channel_id=1, source_target_pairs={{0,4},{4,0},{8,12},{12,8},{16,20},{20,16},{24,28},{28,24},{1,5},{5... | collective-permute-start | bytes 786440 | tf_op jit(solution)/shard_map/ppermute | solution.py:655
  119.0 7.7 %collective-permute-start.24 = (f32[2,256,128]{2,1,0:T(8,128)S(1)}, f32[2,256,128]{2,1,0:T(8,128)S(1)}, u32[]{:S(2)}, u32[]{:S(2)}) collective-permute-start(f32[2,256,128]{2,1,0:T(8,128)S(1)} %get-tuple-element.92), channel_id=1, source_target_pairs={{0,4},{4,0},{8,12},{12,8},{16,20},{20,16},{24,28},{28,24},{1,5},{5... | collective-permute-start | bytes 786440 | tf_op jit(solution)/shard_map/ppermute | solution.py:655
  (5 other events, 5.1 us)

commit v8 on v7

--- a/solution.py
+++ b/solution.py
@@ -181,25 +181,51 @@
     return jnp.concatenate([top, jnp.concatenate([side.T, corner], axis=1)], axis=0)
 
 
-def weights_kernel(at_ref, *refs):
-    sources, (high_ref, low_ref), held, sems = refs[:8], refs[8:10], refs[10], refs[11]
-    me = at_ref[3]
+def weights_kernel(aways, at_ref, *refs):
+    sources, (high_ref, low_ref), held, sems = refs[: len(aways)], refs[-4:-2], refs[-2], refs[-1]
     size = held.shape[2]
-    half = size // 2
-    away_at = (0, 2, 1, 4, 3, 6, 5, 7)
     copies = [pltpu.make_async_copy(source.at[0], held.at[n], sems.at[n]) for n, source in enumerate(sources)]
     for copy in copies:
         copy.start()
-    row = lax.broadcasted_iota(jnp.int32, (size, size), 0)
-    diagonal = row == lax.broadcasted_iota(jnp.int32, (size, size), 1)
-
-    for n, away in enumerate(away_at):
+    diagonal = diagonal_of(size)
+    for n, away in enumerate(aways):
         copies[n].wait()
-        element = away ^ me
-        following = lax.rem(element + 1, len(away_at))
+        element = away ^ at_ref[3]
+        following = lax.rem(element + 1, high_ref.shape[0])
         volume, coupling = scaled(held[n], diagonal)
         for place, at, value in ((following, 0, coupling.T), (element, 1, volume), (element, 2, coupling)):
             high_ref[place, :, at * size : (at + 1) * size], low_ref[place, :, at * size : (at + 1) * size] = split(value)
+
+
+def late_weights_kernel(aways, at_ref, *refs):
+    count = len(aways)
+    sources, targets = refs[:count], refs[count + 2 : count + 4]
+    held, built, sems, out_sems = refs[count + 4 :]
+    size = held.shape[2]
+    copies = [pltpu.make_async_copy(source.at[0], held.at[n], sems.at[n]) for n, source in enumerate(sources)]
+    for copy in copies:
+        copy.start()
+    diagonal = diagonal_of(size)
+    stores = []
+    for n, away in enumerate(aways):
+        copies[n].wait()
+        element = away ^ at_ref[3]
+        following = lax.rem(element + 1, targets[0].shape[0])
+        volume, coupling = scaled(held[n], diagonal)
+        for at, value in enumerate((coupling.T, volume, coupling)):
+            built[n, 0, :, at * size : (at + 1) * size], built[n, 1, :, at * size : (at + 1) * size] = split(value)
+        for part, target in enumerate(targets):
+            for at, (place, first, last) in enumerate(((following, 0, 1), (element, 1, 3))):
+                columns = pl.ds(first * size, (last - first) * size)
+                store = pltpu.make_async_copy(built.at[n, part, :, columns], target.at[place, :, columns], out_sems.at[n, part, at])
+                store.start()
+                stores.append(store)
+    for store in stores:
+        store.wait()
+
+
+def diagonal_of(size):
+    return lax.broadcasted_iota(jnp.int32, (size, size), 0) == lax.broadcasted_iota(jnp.int32, (size, size), 1)
 
 
 def scaled(block, diagonal):
@@ -267,7 +293,7 @@
     count, size, columns = y0.shape
     hold_all(held, [y0[at] for at in range(count)] + [above[0]])
 
-    @pl.loop(0, count - 1)
+    @pl.loop(0, count - 1, unroll=7)
     def _(at):
         y1[at] = apply_row(high[at + 1], low[at + 1], held, pl.multiple_of(at * size, size), columns)
 
@@ -301,20 +327,20 @@
     row = lambda place, at: apply_row(high[place], low[place], held, pl.multiple_of(at * size, size), columns)
     hold_all(held, [y1[at] for at in range(count - 2)])
 
-    @pl.loop(0, count - 4)
+    @pl.loop(0, count - 4, unroll=4)
     def _(at):
         y2[at] = 2.0 * row(at + 2, at) - y0[at + 2]
 
     joined = lambda group, at: jnp.concatenate([end[at] for end in ends[group * chunks : (group + 1) * chunks]], axis=1)
     hold_all(held, [joined(0, 0), joined(0, 1)] + [y2[at] for at in range(count - 4)] + [joined(1, 0), joined(1, 1)])
 
-    @pl.loop(0, count - 2)
+    @pl.loop(0, count - 2, unroll=6)
     def _(at):
         y3[at] = 2.0 * row(at + 1, at) - y1[at]
 
     hold_all(held, [y3[at] for at in range(count - 2)])
 
-    @pl.loop(0, count - 4)
+    @pl.loop(0, count - 4, unroll=4)
     def _(at):
         y4[at] = 2.0 * row(at + 2, at) - y2[at]
 
@@ -498,16 +524,37 @@
     )(core, pair, own, lead, send, keep)
 
 
-def weights(me, *parts):
-    rows, size = parts[0].shape[1:]
-    return pl.pallas_call(
-        weights_kernel,
-        in_specs=[SCALARS] + [ANY] * 8,
+def weights(at, pieces):
+    aways = tuple(pieces)
+    rows, size = pieces[aways[0]].shape[1:]
+    return pl.pallas_call(
+        functools.partial(weights_kernel, aways),
+        in_specs=[SCALARS] + [ANY] * len(aways),
         out_specs=[VMEM] * 2,
         out_shape=[near_core((8, size, 3 * size), jnp.bfloat16)] * 2,
-        scratch_shapes=[pltpu.VMEM((8, rows, size), jnp.float32), pltpu.SemaphoreType.DMA((8,))],
-        compiler_params=PARAMS,
-    )(me, *[far_off(part) for part in parts])
+        scratch_shapes=[pltpu.VMEM((len(aways), rows, size), jnp.float32), pltpu.SemaphoreType.DMA((len(aways),))],
+        compiler_params=PARAMS,
+    )(at, *pieces.values())
+
+
+def late_weights(at, pieces, high, low):
+    aways = tuple(pieces)
+    count = len(aways)
+    rows, size = pieces[aways[0]].shape[1:]
+    return pl.pallas_call(
+        functools.partial(late_weights_kernel, aways),
+        in_specs=[SCALARS] + [ANY] * (count + 2),
+        out_specs=[ANY] * 2,
+        out_shape=[near_core(high.shape, jnp.bfloat16)] * 2,
+        input_output_aliases={1 + count: 0, 2 + count: 1},
+        scratch_shapes=[
+            pltpu.VMEM((count, rows, size), jnp.float32),
+            pltpu.VMEM((count, 2, size, 3 * size), jnp.bfloat16),
+            pltpu.SemaphoreType.DMA((count,)),
+            pltpu.SemaphoreType.DMA((count, 2, 2)),
+        ],
+        compiler_params=PARAMS,
+    )(at, *pieces.values(), high, low)
 
 
 def outer_weights(at, kept, swapped, high, low):
@@ -699,7 +746,7 @@
     above = shifted(pair_low, "elem", -2)
     beside = flipped(mine, "pts", 2)
     across = flipped(mine, "elem", 1)
-    above, beside, across = lax.optimization_barrier((above, beside, across))
+    above, beside, across, got[chunks] = lax.optimization_barrier((above, beside, across, got[chunks]))
     mine_near = flipped(mine, "pts", 1)
     both = flipped(across, "pts", 2)
     beside_near = flipped(beside, "pts", 1)
@@ -716,7 +763,8 @@
     y0 = arranged(at, own, got)
     both_near = flipped(both, "pts", 1)
 
-    high, low = weights(at, mine, mine_near, beside, across, beside_near, across_near, both, both_near)
+    high, low = weights(at, {0: mine, 2: mine_near, 1: beside, 4: across, 3: beside_near, 6: across_near})
+    high, low = late_weights(at, {5: both, 7: both_near}, high, low)
 
     y1 = first_rows(high, low, y0, above)
     below, y1, passed = lax.optimization_barrier((below, y1, passed))

time: 129 us -> 124 us (0.961)
  Pallas kernels: 43.5 us -> 40.4 us
  local copies, waits for them, and re-layouts: 2 us -> 0.71 us
    ppermute x1, waiting for transfers between devices: 4.58 us -> 9.59 us  [body(): lax.ppermute(last, ('elem', 'pts'), [(flat(e, p), flat(e + (2 if p % 2 el...]
    ppermute x17, waiting for transfers between devices: 34.7 us -> 30.4 us  [flipped(): return lax.ppermute(value, axis, [(i, i ^ bit) for i in range(count)])]
    pallas_call x1, Pallas kernels: 8.14 us -> 5.2 us  [middle_rows(): pl.pallas_call(functools.partial(middle_kernel, chunks), in_specs=[SCALAR...]
    ppermute x1, starting transfers between devices: 5.27 us -> 2.36 us  [body(): lax.ppermute(last, ('elem', 'pts'), [(flat(e, p), flat(e + (2 if p % 2 el...]
    ppermute x17, starting transfers between devices: 13.8 us -> 16.2 us  [flipped(): return lax.ppermute(value, axis, [(i, i ^ bit) for i in range(count)])]
    pallas_call x1, Pallas kernels: 3.77 us -> 2.33 us  [first_rows(): pl.pallas_call(first_kernel, in_specs=[VMEM] * 4, out_specs=VMEM, out_sha...]
    unnamed x22 -> x6, local copies, waits for them, and re-layouts: 2 us -> 0.71 us
    pallas_call x1 -> x2, Pallas kernels: 3.36 us -> 4.65 us  [the longest x1 3.11 us: weights(): pl.pallas_call(functools.partial(weights_kernel, aways), in_specs=[SCALAR...]
  transfers between devices with their start and end apart: 26 -> 26, of which waited for: 14 -> 10; matrix products, arithmetic and copies ran while one was open for 0% -> 0% of each run, Pallas kernels for 27% -> 26%
where the time goes in v8:
time: 124 us
  waiting for transfers between devices  49 us (40%)
  Pallas kernels  40.4 us (33%)
  starting transfers between devices  33.2 us (27%)
    ppermute x17, waiting for transfers between devices, flipped(): return lax.ppermute(value, axis, [(i, i ^ bit) for i in range(count)])  30.4 us
    ppermute x17, starting transfers between devices, flipped(): return lax.ppermute(value, axis, [(i, i ^ bit) for i in range(count)])  16.2 us
    ppermute x7, starting transfers between devices, shifted(): lax.ppermute(value, axis, [(i, (i + steps) % count) for i in range(count)])  13.3 us
    ppermute x1, waiting for transfers between devices, body(): lax.ppermute(last, ('elem', 'pts'), [(flat(e, p), flat(e + (2 if p % 2 el...  9.59 us
    ppermute x7, waiting for transfers between devices, shifted(): lax.ppermute(value, axis, [(i, (i + steps) % count) for i in range(count)])  9.02 us
    pallas_call x1, Pallas kernels, blocks(): pl.pallas_call(functools.partial(blocks_kernel, faces_total), in_specs=[S...  7.62 us
    pallas_call x1, Pallas kernels, middle_rows(): pl.pallas_call(functools.partial(middle_kernel, chunks), in_specs=[SCALAR...  5.2 us
    pallas_call x2, Pallas kernels, last_rows(): pl.pallas_call(functools.partial(last_rows_kernel, lane), in_specs=[SCALA...  4.95 us
  transfers between devices with their start and end apart: 26, of which 10 were waited for; matrix products, arithmetic and copies ran while one was open for 0% of the time, Pallas kernels for 26%

profile of v8, /device:TPU:0, one launch (start us, length us, event | category | flops | bytes accessed | tf_op | source)
XLA Modules:
  0.0 123.8 jit_solution(12180158429299080158)
XLA Ops:
  0.8 2.1 %shard_map.64 = (f32[256,128]{1,0:T(8,128)S(1)}, f32[2,256,128]{2,1,0:T(8,128)S(1)}, f32[2,256,128]{2,1,0:T(8,128)S(1)}, f32[2,256,128]{2,1,0:T(8,128)S(1)}, f32[2,256,128]{2,1,0:T(8,128)S(1)}) custom-call(s32[4]{0:T(128)S(1)} %pad_add_fusion.at_ref, s32[4,4,64]{2,1,0:T(4,128)S(1)} %copy-done, f32[4,512,256]{2,1,0:T(8,128)} %basis_ref.3, f32[4,256,512]{2,1,0:T(8,128)} %bitcast.6), custom_call_target="tpu_custom_call" | custom-call | tf_op jit(solution)/shard_map/pallas_call | solution.py:485
  2.8 3.0 %collective-permute-start = (f32[2,256,128]{2,1,0:T(8,128)S(1)}, f32[2,256,128]{2,1,0:T(8,128)S(1)}, u32[]{:S(2)}, u32[]{:S(2)}) collective-permute-start(f32[2,256,128]{2,1,0:T(8,128)S(1)} %get-tuple-element.55), channel_id=1, source_target_pairs={{0,4},{4,0},{8,12},{12,8},{16,20},{20,16},{24,28},{28,24},{1,5},{5... | collective-permute-start | bytes 786440 | tf_op jit(solution)/shard_map/ppermute | solution.py:702
  5.9 3.5 %collective-permute-start.1 = (f32[256,128]{1,0:T(8,128)S(1)}, f32[256,128]{1,0:T(8,128)S(1)}, u32[]{:S(2)}, u32[]{:S(2)}) collective-permute-start(f32[256,128]{1,0:T(8,128)S(1)} %get-tuple-element.57), channel_id=1, source_target_pairs={{0,28},{4,0},{8,4},{12,8},{16,12},{20,16},{24,20},{28,24},{1,29},{... | collective-permute-start | bytes 393224 | tf_op jit(solution)/shard_map/ppermute | solution.py:707
  9.4 7.6 %shard_map.65 = (f32[2,392,256]{2,1,0:T(8,128)S(1)}, f32[2,392,256]{2,1,0:T(8,128)S(1)}, f32[256,256]{1,0:T(8,128)S(1)}) custom-call(s32[4]{0:T(128)S(1)} %pad_add_fusion.at_ref, s32[4,4,64]{2,1,0:T(4,128)S(1)} %copy-done, f32[4,512]{1,0:T(4,128)S(1)} %copy-done.1, s32[4,64]{1,0:T(4,128)S(1)} %copy-done.2, f32[4,512,256]{2,1,0:T(8,128)} %basis_ref.3, ...), custom_call_target="tpu_custom_call" | custom-call | tf_op jit(solution)/shard_map/pallas_call | solution.py:499
  18.4 2.3 %collective-permute-done.3.other_ref = f32[2,392,256]{2,1,0:T(8,128)S(1)} collective-permute-done((f32[2,392,256]{2,1,0:T(8,128)S(1)}, f32[2,392,256]{2,1,0:T(8,128)S(1)}, u32[]{:S(2)}, u32[]{:S(2)}) %collective-permute-start.3) | collective-permute-done | bytes 802848 | tf_op jit(solution)/shard_map/ppermute | solution.py:702
  21.3 1.6 %collective-permute-start.4 = (f32[1,392,256]{2,1,0:T(8,128)S(1)}, f32[1,392,256]{2,1,0:T(8,128)S(1)}, u32[]{:S(2)}, u32[]{:S(2)}) collective-permute-start(f32[1,392,256]{2,1,0:T(8,128)S(1)} %get-tuple-element.65), channel_id=1, source_target_pairs={{0,2},{1,3},{2,0},{3,1},{4,6},{5,7},{6,4},{7,5},{8,10},{9,11},{10,... | collective-permute-start | bytes 1204232 | tf_op jit(solution)/shard_map/ppermute | solution.py:702
  22.9 8.1 %collective-permute-done.2.refs_1_ = f32[2,256,128]{2,1,0:T(8,128)S(1)} collective-permute-done((f32[2,256,128]{2,1,0:T(8,128)S(1)}, f32[2,256,128]{2,1,0:T(8,128)S(1)}, u32[]{:S(2)}, u32[]{:S(2)}) %collective-permute-start.2) | collective-permute-done | bytes 262176 | tf_op jit(solution)/shard_map/ppermute | solution.py:702
  30.9 1.6 %shard_map.67 = f32[2,256,256]{2,1,0:T(8,128)S(1)} custom-call(s32[4]{0:T(128)S(1)} %pad_add_fusion.at_ref, f32[4,256,512]{2,1,0:T(8,128)} %bitcast.7, f32[2,256,128]{2,1,0:T(8,128)S(1)} %collective-permute-done.refs_0_, f32[2,256,128]{2,1,0:T(8,128)S(1)} %collective-permute-done.2.refs_1_), custom_call_target="tpu_custom_call" | custom-call | tf_op jit(solution)/shard_map/pallas_call | solution.py:653
  32.7 1.8 %collective-permute-start.5 = (f32[2,256,256]{2,1,0:T(8,128)S(1)}, f32[2,256,256]{2,1,0:T(8,128)S(1)}, u32[]{:S(2)}, u32[]{:S(2)}) collective-permute-start(f32[2,256,256]{2,1,0:T(8,128)S(1)} %shard_map.67), channel_id=1, source_target_pairs={{0,24},{4,28},{8,0},{12,4},{16,8},{20,12},{24,16},{28,20},{1,25},{... | collective-permute-start | bytes 1572872 | tf_op jit(solution)/shard_map/ppermute | solution.py:707
  34.5 1.6 %collective-permute-start.6 = (f32[1,392,256]{2,1,0:T(8,128)S(1)}, f32[1,392,256]{2,1,0:T(8,128)S(1)}, u32[]{:S(2)}, u32[]{:S(2)}) collective-permute-start(f32[1,392,256]{2,1,0:T(8,128)S(1)} %shard_map.69.refs_0_.mine_ref), channel_id=1, source_target_pairs={{0,2},{1,3},{2,0},{3,1},{4,6},{5,7},{6,4},{7,5},{8,10},{9,11},{10,... | collective-permute-start | bytes 1204232 | tf_op jit(solution)/shard_map/ppermute | solution.py:702
  36.4 1.7 %collective-permute-start.8 = (f32[2,256,128]{2,1,0:T(8,128)S(1)}, f32[2,256,128]{2,1,0:T(8,128)S(1)}, u32[]{:S(2)}, u32[]{:S(2)}) collective-permute-start(f32[2,256,128]{2,1,0:T(8,128)S(1)} %get-tuple-element.69), channel_id=1, source_target_pairs={{0,4},{4,0},{8,12},{12,8},{16,20},{20,16},{24,28},{28,24},{1,5},{5... | collective-permute-start | bytes 786440 | tf_op jit(solution)/shard_map/ppermute | solution.py:702
  38.1 13.5 %collective-permute-done.8.refs_0_.refs_2_ = f32[2,256,128]{2,1,0:T(8,128)S(1)} collective-permute-done((f32[2,256,128]{2,1,0:T(8,128)S(1)}, f32[2,256,128]{2,1,0:T(8,128)S(1)}, u32[]{:S(2)}, u32[]{:S(2)}) %collective-permute-start.8) | collective-permute-done | bytes 262176 | tf_op jit(solution)/shard_map/ppermute | solution.py:702
  52.5 2.4 %collective-permute-start.15 = (f32[1,648,256]{2,1,0:T(8,128)S(1)}, f32[1,648,256]{2,1,0:T(8,128)S(1)}, u32[]{:S(2)}, u32[]{:S(2)}) collective-permute-start(f32[1,648,256]{2,1,0:T(8,128)S(1)} %shard_map.72), channel_id=1, source_target_pairs={{0,24},{2,26},{5,13},{7,15},{8,0},{10,2},{13,21},{15,23},{16,8},{1... | collective-permute-start | bytes 1990664 | tf_op jit(solution)/shard_map/ppermute | solution.py:758
  55.4 9.6 %collective-permute-done.15.first_ref = f32[1,648,256]{2,1,0:T(8,128)S(1)} collective-permute-done((f32[1,648,256]{2,1,0:T(8,128)S(1)}, f32[1,648,256]{2,1,0:T(8,128)S(1)}, u32[]{:S(2)}, u32[]{:S(2)}) %collective-permute-start.15) | collective-permute-done | bytes 663584 | tf_op jit(solution)/shard_map/ppermute | solution.py:758
  67.8 1.9 %shard_map.74.y0 = f32[8,256,256]{2,1,0:T(8,128)S(1)} custom-call(s32[4]{0:T(128)S(1)} %pad_add_fusion.at_ref, f32[4,256,512]{2,1,0:T(8,128)} %bitcast.9, f32[2,256,128]{2,1,0:T(8,128)S(1)} %collective-permute-done.refs_0_, f32[2,256,128]{2,1,0:T(8,128)S(1)} %collective-permute-done.2.refs_1_, f32[2,256,128]{2,1,0:T(8,128)S(1)} %collective-permute-done.8.refs_0_.refs_2_, ...), custom_call_target="tpu_custom_call" | custom-call | tf_op jit(solution)/shard_map/pallas_call | solution.py:665
  69.7 3.1 %shard_map.70 = (bf16[8,256,768]{2,1,0:T(8,128)(2,1)S(1)}, bf16[8,256,768]{2,1,0:T(8,128)(2,1)S(1)}) custom-call(s32[4]{0:T(128)S(1)} %pad_add_fusion.at_ref, f32[1,392,256]{2,1,0:T(8,128)S(1)} %shard_map.69.refs_0_.mine_ref, f32[1,392,256]{2,1,0:T(8,128)S(1)} %collective-permute-done.12.refs_1_, ...), custom_call_target="tpu_custom_call" | custom-call | tf_op jit(solution)/shard_map/pallas_call | solution.py:530
  74.4 2.3 %shard_map.75.y1 = f32[7,256,256]{2,1,0:T(8,128)S(1)} custom-call(bf16[8,256,768]{2,1,0:T(8,128)(2,1)S(1)} %get-tuple-element.77.high.high_in, bf16[8,256,768]{2,1,0:T(8,128)(2,1)S(1)} %get-tuple-element.78.low.low_in, f32[8,256,256]{2,1,0:T(8,128)S(1)} %shard_map.74.y0, f32[2,256,256]{2,1,0:T(8,128)S(1)} %collective-permute-done.5.above), custom_call_target="tpu_custom_call" | custom-call | tf_op jit(solution)/shard_map/pallas_call | solution.py:573
  76.8 3.4 %collective-permute-done.16.below = f32[2,256,256]{2,1,0:T(8,128)S(1)} collective-permute-done((f32[2,256,256]{2,1,0:T(8,128)S(1)}, f32[2,256,256]{2,1,0:T(8,128)S(1)}, u32[]{:S(2)}, u32[]{:S(2)}) %collective-permute-start.16) | collective-permute-done | bytes 524320 | tf_op jit(solution)/shard_map/ppermute | solution.py:707
  80.3 2.1 %collective-permute-done.18.swapped_ref = f32[1,648,256]{2,1,0:T(8,128)S(1)} collective-permute-done((f32[1,648,256]{2,1,0:T(8,128)S(1)}, f32[1,648,256]{2,1,0:T(8,128)S(1)}, u32[]{:S(2)}, u32[]{:S(2)}) %collective-permute-start.18) | collective-permute-done | bytes 663584 | tf_op jit(solution)/shard_map/ppermute | solution.py:702
  83.5 2.5 %shard_map.78 = (f32[3,256,256]{2,1,0:T(8,128)S(1)}, f32[2,256,128]{2,1,0:T(8,128)S(1)}, f32[2,256,128]{2,1,0:T(8,128)S(1)}, f32[2,256,128]{2,1,0:T(8,128)S(1)}, f32[2,256,128]{2,1,0:T(8,128)S(1)}) custom-call(bf16[8,256,768]{2,1,0:T(8,128)(2,1)S(1)} %get-tuple-element.77.high.high_in, bf16[8,256,768]{2,1,0:T(8,128)(2,1)S(1)} %get-tuple-element.78.low.low_in, ...), custom_call_target="tpu_custom_call" | custom-call | tf_op jit(solution)/shard_map/pallas_call | solution.py:585
  86.1 3.8 %collective-permute-start.20 = (f32[2,256,128]{2,1,0:T(8,128)S(1)}, f32[2,256,128]{2,1,0:T(8,128)S(1)}, u32[]{:S(2)}, u32[]{:S(2)}) collective-permute-start(f32[2,256,128]{2,1,0:T(8,128)S(1)} %get-tuple-element.88.refs_0_.y2_low), channel_id=1, source_target_pairs={{0,24},{4,28},{8,0},{12,4},{16,8},{20,12},{24,16},{28,20},{1,25},{... | collective-permute-start | bytes 786440 | tf_op jit(solution)/shard_map/ppermute | solution.py:707
  89.9 5.2 %shard_map.79 = (f32[4,256,256]{2,1,0:T(8,128)S(1)}, f32[4,256,256]{2,1,0:T(8,128)S(1)}, f32[2,256,256]{2,1,0:T(8,128)S(1)}) custom-call(s32[4]{0:T(128)S(1)} %pad_add_fusion.at_ref, bf16[8,256,768]{2,1,0:T(8,128)(2,1)S(1)} %get-tuple-element.77.high.high_in, bf16[8,256,768]{2,1,0:T(8,128)(2,1)S(1)} %get-tuple-element.78.low.low_in, ...), custom_call_target="tpu_custom_call" | custom-call | tf_op jit(solution)/shard_map/pallas_call | solution.py:597
  95.1 2.4 %collective-permute-start.25 = (f32[2,256,256]{2,1,0:T(8,128)S(1)}, f32[2,256,256]{2,1,0:T(8,128)S(1)}, u32[]{:S(2)}, u32[]{:S(2)}) collective-permute-start(f32[2,256,256]{2,1,0:T(8,128)S(1)} %get-tuple-element.100), channel_id=1, source_target_pairs={{0,4},{4,0},{8,12},{12,8},{16,20},{20,16},{24,28},{28,24},{1,5},{5... | collective-permute-start | bytes 1572872 | tf_op jit(solution)/shard_map/ppermute | solution.py:702
  97.5 3.8 %collective-permute-start.23 = (f32[2,256,128]{2,1,0:T(8,128)S(1)}, f32[2,256,128]{2,1,0:T(8,128)S(1)}, u32[]{:S(2)}, u32[]{:S(2)}) collective-permute-start(f32[2,256,128]{2,1,0:T(8,128)S(1)} %get-tuple-element.89.refs_1_.y2_low), channel_id=1, source_target_pairs={{0,24},{4,28},{8,0},{12,4},{16,8},{20,12},{24,16},{28,20},{1,25},{... | collective-permute-start | bytes 786440 | tf_op jit(solution)/shard_map/ppermute | solution.py:707
  101.3 2.5 %shard_map.80 = (f32[2,256,128]{2,1,0:T(8,128)S(1)}, f32[2,256,128]{2,1,0:T(8,128)S(1)}, f32[2,256,128]{2,1,0:T(8,128)S(1)}) custom-call(s32[4]{0:T(128)S(1)} %pad_add_fusion.at_ref, bf16[8,256,768]{2,1,0:T(8,128)(2,1)S(1)} %get-tuple-element.77.high.high_in, bf16[8,256,768]{2,1,0:T(8,128)(2,1)S(1)} %get-tuple-element.78.low.low_in, ...), custom_call_target="tpu_custom_call" | custom-call | tf_op jit(solution)/shard_map/pallas_call | solution.py:613
  103.8 2.0 %collective-permute-start.21 = (f32[2,256,128]{2,1,0:T(8,128)S(1)}, f32[2,256,128]{2,1,0:T(8,128)S(1)}, u32[]{:S(2)}, u32[]{:S(2)}) collective-permute-start(f32[2,256,128]{2,1,0:T(8,128)S(1)} %get-tuple-element.95), channel_id=1, source_target_pairs={{0,4},{4,0},{8,12},{12,8},{16,20},{20,16},{24,28},{28,24},{1,5},{5... | collective-permute-start | bytes 786440 | tf_op jit(solution)/shard_map/ppermute | solution.py:702
  105.8 2.6 %collective-permute-done.22.below = f32[2,256,128]{2,1,0:T(8,128)S(1)} collective-permute-done((f32[2,256,128]{2,1,0:T(8,128)S(1)}, f32[2,256,128]{2,1,0:T(8,128)S(1)}, u32[]{:S(2)}, u32[]{:S(2)}) %collective-permute-start.22) | collective-permute-done | bytes 262176 | tf_op jit(solution)/shard_map/ppermute | solution.py:707
  108.4 3.0 %collective-permute-done.23.above = f32[2,256,128]{2,1,0:T(8,128)S(1)} collective-permute-done((f32[2,256,128]{2,1,0:T(8,128)S(1)}, f32[2,256,128]{2,1,0:T(8,128)S(1)}, u32[]{:S(2)}, u32[]{:S(2)}) %collective-permute-start.23) | collective-permute-done | bytes 262176 | tf_op jit(solution)/shard_map/ppermute | solution.py:707
  111.4 2.5 %shard_map.81 = (f32[2,256,128]{2,1,0:T(8,128)S(1)}, f32[2,256,128]{2,1,0:T(8,128)S(1)}, f32[2,256,128]{2,1,0:T(8,128)S(1)}) custom-call(s32[4]{0:T(128)S(1)} %pad_add_fusion.at_ref, bf16[8,256,768]{2,1,0:T(8,128)(2,1)S(1)} %get-tuple-element.77.high.high_in, bf16[8,256,768]{2,1,0:T(8,128)(2,1)S(1)} %get-tuple-element.78.low.low_in, ...), custom_call_target="tpu_custom_call" | custom-call | tf_op jit(solution)/shard_map/pallas_call | solution.py:613
  113.9 2.4 %collective-permute-start.24 = (f32[2,256,128]{2,1,0:T(8,128)S(1)}, f32[2,256,128]{2,1,0:T(8,128)S(1)}, u32[]{:S(2)}, u32[]{:S(2)}) collective-permute-start(f32[2,256,128]{2,1,0:T(8,128)S(1)} %get-tuple-element.98), channel_id=1, source_target_pairs={{0,4},{4,0},{8,12},{12,8},{16,20},{20,16},{24,28},{28,24},{1,5},{5... | collective-permute-start | bytes 786440 | tf_op jit(solution)/shard_map/ppermute | solution.py:702
  117.8 4.2 %collective-permute-done.24.refs_5_ = f32[2,256,128]{2,1,0:T(8,128)S(1)} collective-permute-done((f32[2,256,128]{2,1,0:T(8,128)S(1)}, f32[2,256,128]{2,1,0:T(8,128)S(1)}, u32[]{:S(2)}, u32[]{:S(2)}) %collective-permute-start.24) | collective-permute-done | bytes 262176 | tf_op jit(solution)/shard_map/ppermute | solution.py:702
  122.0 1.6 %shard_map.83 = f32[4,256,512]{2,1,0:T(8,128)} custom-call(s32[4]{0:T(128)S(1)} %pad_add_fusion.at_ref, f32[2,256,128]{2,1,0:T(8,128)S(1)} %get-tuple-element.93.refs_0_, f32[2,256,128]{2,1,0:T(8,128)S(1)} %get-tuple-element.94.refs_1_, f32[2,256,128]{2,1,0:T(8,128)S(1)} %collective-permute-done.21.refs_2_, ...), custom_call_target="tpu_custom_call", output_to_operand_aliasing={{}: (7, {})} | custom-call | tf_op jit(solution)/shard_map/pallas_call | solution.py:689
  (47 shorter events, 11.8 us)
Async XLA Ops:
  0.1 0.7 copy-start
  0.8 8.6 %copy-start.1 = (f32[4,512]{1,0:T(4,128)S(1)}, f32[4,512]{1,0:T(4,128)}, u32[]{:S(2)}) copy-start(f32[4,512]{1,0:T(4,128)} %quad_ref.1) | copy-start | bytes 24580
  0.8 8.6 %copy-start.2 = (s32[4,64]{1,0:T(4,128)S(1)}, s32[4,64]{1,0:T(4,128)}, u32[]{:S(2)}) copy-start(s32[4,64]{1,0:T(4,128)} %pair_ref.3) | copy-start | bytes 3076
  2.8 15.5 %collective-permute-start = (f32[2,256,128]{2,1,0:T(8,128)S(1)}, f32[2,256,128]{2,1,0:T(8,128)S(1)}, u32[]{:S(2)}, u32[]{:S(2)}) collective-permute-start(f32[2,256,128]{2,1,0:T(8,128)S(1)} %get-tuple-element.55), channel_id=1, source_target_pairs={{0,4},{4,0},{8,12},{12,8},{16,20},{20,16},{24,28},{28,24},{1,5},{5... | collective-permute-start | bytes 786440 | tf_op jit(solution)/shard_map/ppermute | solution.py:702
  5.9 11.2 %collective-permute-start.1 = (f32[256,128]{1,0:T(8,128)S(1)}, f32[256,128]{1,0:T(8,128)S(1)}, u32[]{:S(2)}, u32[]{:S(2)}) collective-permute-start(f32[256,128]{1,0:T(8,128)S(1)} %get-tuple-element.57), channel_id=1, source_target_pairs={{0,28},{4,0},{8,4},{12,8},{16,12},{20,16},{24,20},{28,24},{1,29},{... | collective-permute-start | bytes 393224 | tf_op jit(solution)/shard_map/ppermute | solution.py:707
  18.3 2.4 %collective-permute-start.3 = (f32[2,392,256]{2,1,0:T(8,128)S(1)}, f32[2,392,256]{2,1,0:T(8,128)S(1)}, u32[]{:S(2)}, u32[]{:S(2)}) collective-permute-start(f32[2,392,256]{2,1,0:T(8,128)S(1)} %get-tuple-element.64), channel_id=1, source_target_pairs={{0,1},{1,0},{2,3},{3,2},{4,5},{5,4},{6,7},{7,6},{8,9},{9,8},{10,11... | collective-permute-start | bytes 2408456 | tf_op jit(solution)/shard_map/ppermute | solution.py:702
  21.3 11.4 %collective-permute-start.4 = (f32[1,392,256]{2,1,0:T(8,128)S(1)}, f32[1,392,256]{2,1,0:T(8,128)S(1)}, u32[]{:S(2)}, u32[]{:S(2)}) collective-permute-start(f32[1,392,256]{2,1,0:T(8,128)S(1)} %get-tuple-element.65), channel_id=1, source_target_pairs={{0,2},{1,3},{2,0},{3,1},{4,6},{5,7},{6,4},{7,5},{8,10},{9,11},{10,... | collective-permute-start | bytes 1204232 | tf_op jit(solution)/shard_map/ppermute | solution.py:702
  22.9 8.1 %collective-permute-start.2 = (f32[2,256,128]{2,1,0:T(8,128)S(1)}, f32[2,256,128]{2,1,0:T(8,128)S(1)}, u32[]{:S(2)}, u32[]{:S(2)}) collective-permute-start(f32[2,256,128]{2,1,0:T(8,128)S(1)} %get-tuple-element.62), channel_id=1, source_target_pairs={{0,4},{4,0},{8,12},{12,8},{16,20},{20,16},{24,28},{28,24},{1,5},{5... | collective-permute-start | bytes 786440 | tf_op jit(solution)/shard_map/ppermute | solution.py:702
  32.7 18.9 %collective-permute-start.5 = (f32[2,256,256]{2,1,0:T(8,128)S(1)}, f32[2,256,256]{2,1,0:T(8,128)S(1)}, u32[]{:S(2)}, u32[]{:S(2)}) collective-permute-start(f32[2,256,256]{2,1,0:T(8,128)S(1)} %shard_map.67), channel_id=1, source_target_pairs={{0,24},{4,28},{8,0},{12,4},{16,8},{20,12},{24,16},{28,20},{1,25},{... | collective-permute-start | bytes 1572872 | tf_op jit(solution)/shard_map/ppermute | solution.py:707
  34.5 17.1 %collective-permute-start.6 = (f32[1,392,256]{2,1,0:T(8,128)S(1)}, f32[1,392,256]{2,1,0:T(8,128)S(1)}, u32[]{:S(2)}, u32[]{:S(2)}) collective-permute-start(f32[1,392,256]{2,1,0:T(8,128)S(1)} %shard_map.69.refs_0_.mine_ref), channel_id=1, source_target_pairs={{0,2},{1,3},{2,0},{3,1},{4,6},{5,7},{6,4},{7,5},{8,10},{9,11},{10,... | collective-permute-start | bytes 1204232 | tf_op jit(solution)/shard_map/ppermute | solution.py:702
  36.1 15.6 %collective-permute-start.7 = (f32[1,392,256]{2,1,0:T(8,128)S(1)}, f32[1,392,256]{2,1,0:T(8,128)S(1)}, u32[]{:S(2)}, u32[]{:S(2)}) collective-permute-start(f32[1,392,256]{2,1,0:T(8,128)S(1)} %shard_map.69.refs_0_.mine_ref), channel_id=1, source_target_pairs={{0,4},{4,0},{8,12},{12,8},{16,20},{20,16},{24,28},{28,24},{1,5},{5... | collective-permute-start | bytes 1204232 | tf_op jit(solution)/shard_map/ppermute | solution.py:702
  36.4 15.2 %collective-permute-start.8 = (f32[2,256,128]{2,1,0:T(8,128)S(1)}, f32[2,256,128]{2,1,0:T(8,128)S(1)}, u32[]{:S(2)}, u32[]{:S(2)}) collective-permute-start(f32[2,256,128]{2,1,0:T(8,128)S(1)} %get-tuple-element.69), channel_id=1, source_target_pairs={{0,4},{4,0},{8,12},{12,8},{16,20},{20,16},{24,28},{28,24},{1,5},{5... | collective-permute-start | bytes 786440 | tf_op jit(solution)/shard_map/ppermute | solution.py:702
  52.5 12.6 %collective-permute-start.15 = (f32[1,648,256]{2,1,0:T(8,128)S(1)}, f32[1,648,256]{2,1,0:T(8,128)S(1)}, u32[]{:S(2)}, u32[]{:S(2)}) collective-permute-start(f32[1,648,256]{2,1,0:T(8,128)S(1)} %shard_map.72), channel_id=1, source_target_pairs={{0,24},{2,26},{5,13},{7,15},{8,0},{10,2},{13,21},{15,23},{16,8},{1... | collective-permute-start | bytes 1990664 | tf_op jit(solution)/shard_map/ppermute | solution.py:758
  54.8 11.5 %collective-permute-start.10 = (f32[1,392,256]{2,1,0:T(8,128)S(1)}, f32[1,392,256]{2,1,0:T(8,128)S(1)}, u32[]{:S(2)}, u32[]{:S(2)}) collective-permute-start(f32[1,392,256]{2,1,0:T(8,128)S(1)} %collective-permute-done.7.refs_3_), channel_id=1, source_target_pairs={{0,2},{1,3},{2,0},{3,1},{4,6},{5,7},{6,4},{7,5},{8,10},{9,11},{10,... | collective-permute-start | bytes 1204232 | tf_op jit(solution)/shard_map/ppermute | solution.py:702
  55.4 12.4 %collective-permute-start.12 = (f32[1,392,256]{2,1,0:T(8,128)S(1)}, f32[1,392,256]{2,1,0:T(8,128)S(1)}, u32[]{:S(2)}, u32[]{:S(2)}) collective-permute-start(f32[1,392,256]{2,1,0:T(8,128)S(1)} %shard_map.69.refs_0_.mine_ref), channel_id=1, source_target_pairs={{0,1},{1,0},{2,3},{3,2},{4,5},{5,4},{6,7},{7,6},{8,9},{9,8},{10,11... | collective-permute-start | bytes 1204232 | tf_op jit(solution)/shard_map/ppermute | solution.py:702
  55.4 10.9 %collective-permute-start.9 = (f32[2,256,128]{2,1,0:T(8,128)S(1)}, f32[2,256,128]{2,1,0:T(8,128)S(1)}, u32[]{:S(2)}, u32[]{:S(2)}) collective-permute-start(f32[2,256,128]{2,1,0:T(8,128)S(1)} %get-tuple-element.71), channel_id=1, source_target_pairs={{0,4},{4,0},{8,12},{12,8},{16,20},{20,16},{24,28},{28,24},{1,5},{5... | collective-permute-start | bytes 786440 | tf_op jit(solution)/shard_map/ppermute | solution.py:702
  65.0 15.2 %collective-permute-start.17 = (f32[1,648,256]{2,1,0:T(8,128)S(1)}, f32[1,648,256]{2,1,0:T(8,128)S(1)}, u32[]{:S(2)}, u32[]{:S(2)}) collective-permute-start(f32[1,648,256]{2,1,0:T(8,128)S(1)} %collective-permute-done.15.first_ref), channel_id=1, source_target_pairs={{0,4},{2,6},{5,1},{7,3},{8,12},{10,14},{13,9},{15,11},{16,20},{18,... | collective-permute-start | bytes 1990664 | tf_op jit(solution)/shard_map/ppermute | solution.py:759
  67.0 13.2 %collective-permute-start.16 = (f32[2,256,256]{2,1,0:T(8,128)S(1)}, f32[2,256,256]{2,1,0:T(8,128)S(1)}, u32[]{:S(2)}, u32[]{:S(2)}) collective-permute-start(f32[2,256,256]{2,1,0:T(8,128)S(1)} %shard_map.73), channel_id=1, source_target_pairs={{0,8},{4,12},{8,16},{12,20},{16,24},{20,28},{24,0},{28,4},{1,9},{5... | collective-permute-start | bytes 1572872 | tf_op jit(solution)/shard_map/ppermute | solution.py:707
  67.3 2.4 %collective-permute-start.13 = (f32[1,392,256]{2,1,0:T(8,128)S(1)}, f32[1,392,256]{2,1,0:T(8,128)S(1)}, u32[]{:S(2)}, u32[]{:S(2)}) collective-permute-start(f32[1,392,256]{2,1,0:T(8,128)S(1)} %collective-permute-done.6.refs_2_.beside_ref), channel_id=1, source_target_pairs={{0,1},{1,0},{2,3},{3,2},{4,5},{5,4},{6,7},{7,6},{8,9},{9,8},{10,11... | collective-permute-start | bytes 1204232 | tf_op jit(solution)/shard_map/ppermute | solution.py:702
  67.3 2.4 %collective-permute-start.14 = (f32[1,392,256]{2,1,0:T(8,128)S(1)}, f32[1,392,256]{2,1,0:T(8,128)S(1)}, u32[]{:S(2)}, u32[]{:S(2)}) collective-permute-start(f32[1,392,256]{2,1,0:T(8,128)S(1)} %collective-permute-done.7.refs_3_), channel_id=1, source_target_pairs={{0,1},{1,0},{2,3},{3,2},{4,5},{5,4},{6,7},{7,6},{8,9},{9,8},{10,11... | collective-permute-start | bytes 1204232 | tf_op jit(solution)/shard_map/ppermute | solution.py:702
  67.8 5.0 %collective-permute-start.11 = (f32[1,392,256]{2,1,0:T(8,128)S(1)}, f32[1,392,256]{2,1,0:T(8,128)S(1)}, u32[]{:S(2)}, u32[]{:S(2)}) collective-permute-start(f32[1,392,256]{2,1,0:T(8,128)S(1)} %collective-permute-done.10.refs_0_), channel_id=1, source_target_pairs={{0,1},{1,0},{2,3},{3,2},{4,5},{5,4},{6,7},{7,6},{8,9},{9,8},{10,11... | collective-permute-start | bytes 1204232 | tf_op jit(solution)/shard_map/ppermute | solution.py:702
  80.3 2.2 %collective-permute-start.18 = (f32[1,648,256]{2,1,0:T(8,128)S(1)}, f32[1,648,256]{2,1,0:T(8,128)S(1)}, u32[]{:S(2)}, u32[]{:S(2)}) collective-permute-start(f32[1,648,256]{2,1,0:T(8,128)S(1)} %shard_map.76.kept_ref), channel_id=1, source_target_pairs={{0,1},{1,0},{2,3},{3,2},{4,5},{5,4},{6,7},{7,6},{8,9},{9,8},{10,11... | collective-permute-start | bytes 1990664 | tf_op jit(solution)/shard_map/ppermute | solution.py:702
  86.0 15.3 %collective-permute-start.19 = (f32[2,256,128]{2,1,0:T(8,128)S(1)}, f32[2,256,128]{2,1,0:T(8,128)S(1)}, u32[]{:S(2)}, u32[]{:S(2)}) collective-permute-start(f32[2,256,128]{2,1,0:T(8,128)S(1)} %get-tuple-element.90.refs_2_.y2_high), channel_id=1, source_target_pairs={{0,8},{4,12},{8,16},{12,20},{16,24},{20,28},{24,0},{28,4},{1,9},{5... | collective-permute-start | bytes 786440 | tf_op jit(solution)/shard_map/ppermute | solution.py:707
  86.1 15.2 %collective-permute-start.20 = (f32[2,256,128]{2,1,0:T(8,128)S(1)}, f32[2,256,128]{2,1,0:T(8,128)S(1)}, u32[]{:S(2)}, u32[]{:S(2)}) collective-permute-start(f32[2,256,128]{2,1,0:T(8,128)S(1)} %get-tuple-element.88.refs_0_.y2_low), channel_id=1, source_target_pairs={{0,24},{4,28},{8,0},{12,4},{16,8},{20,12},{24,16},{28,20},{1,25},{... | collective-permute-start | bytes 786440 | tf_op jit(solution)/shard_map/ppermute | solution.py:707
  89.9 18.5 %collective-permute-start.22 = (f32[2,256,128]{2,1,0:T(8,128)S(1)}, f32[2,256,128]{2,1,0:T(8,128)S(1)}, u32[]{:S(2)}, u32[]{:S(2)}) collective-permute-start(f32[2,256,128]{2,1,0:T(8,128)S(1)} %get-tuple-element.91.refs_3_.y2_high), channel_id=1, source_target_pairs={{0,8},{4,12},{8,16},{12,20},{16,24},{20,28},{24,0},{28,4},{1,9},{5... | collective-permute-start | bytes 786440 | tf_op jit(solution)/shard_map/ppermute | solution.py:707
  95.1 21.1 %collective-permute-start.25 = (f32[2,256,256]{2,1,0:T(8,128)S(1)}, f32[2,256,256]{2,1,0:T(8,128)S(1)}, u32[]{:S(2)}, u32[]{:S(2)}) collective-permute-start(f32[2,256,256]{2,1,0:T(8,128)S(1)} %get-tuple-element.100), channel_id=1, source_target_pairs={{0,4},{4,0},{8,12},{12,8},{16,20},{20,16},{24,28},{28,24},{1,5},{5... | collective-permute-start | bytes 1572872 | tf_op jit(solution)/shard_map/ppermute | solution.py:702
  97.5 13.9 %collective-permute-start.23 = (f32[2,256,128]{2,1,0:T(8,128)S(1)}, f32[2,256,128]{2,1,0:T(8,128)S(1)}, u32[]{:S(2)}, u32[]{:S(2)}) collective-permute-start(f32[2,256,128]{2,1,0:T(8,128)S(1)} %get-tuple-element.89.refs_1_.y2_low), channel_id=1, source_target_pairs={{0,24},{4,28},{8,0},{12,4},{16,8},{20,12},{24,16},{28,20},{1,25},{... | collective-permute-start | bytes 786440 | tf_op jit(solution)/shard_map/ppermute | solution.py:707
  103.8 14.0 %collective-permute-start.21 = (f32[2,256,128]{2,1,0:T(8,128)S(1)}, f32[2,256,128]{2,1,0:T(8,128)S(1)}, u32[]{:S(2)}, u32[]{:S(2)}) collective-permute-start(f32[2,256,128]{2,1,0:T(8,128)S(1)} %get-tuple-element.95), channel_id=1, source_target_pairs={{0,4},{4,0},{8,12},{12,8},{16,20},{20,16},{24,28},{28,24},{1,5},{5... | collective-permute-start | bytes 786440 | tf_op jit(solution)/shard_map/ppermute | solution.py:702
  113.9 8.2 %collective-permute-start.24 = (f32[2,256,128]{2,1,0:T(8,128)S(1)}, f32[2,256,128]{2,1,0:T(8,128)S(1)}, u32[]{:S(2)}, u32[]{:S(2)}) collective-permute-start(f32[2,256,128]{2,1,0:T(8,128)S(1)} %get-tuple-element.98), channel_id=1, source_target_pairs={{0,4},{4,0},{8,12},{12,8},{16,20},{20,16},{24,28},{28,24},{1,5},{5... | collective-permute-start | bytes 786440 | tf_op jit(solution)/shard_map/ppermute | solution.py:702

commit v9 on v8

--- a/solution.py
+++ b/solution.py
@@ -350,7 +350,7 @@
 
 
 def last_rows_kernel(
-    lane, at_ref, high, low, outer_high, outer_low, y1, y1_ends, y3, y2_low, y2_high, below, above, y4_low, y4_high, send, held
+    lane, foreign, at_ref, high, low, outer_high, outer_low, y1, y1_ends, y3, y2_low, y2_high, below, above, y4, held
 ):
     size, columns = below.shape[1:]
     count = high.shape[0]
@@ -358,17 +358,24 @@
     row = lambda weight, start: apply_row(*weight, held, start * size, columns)
     outer = lambda at: (outer_high[at], outer_low[at])
     main = lambda at: (high[at], low[at])
-    hold_all(held, (below[0], below[1], y2_low[0], y2_low[1], y2_high[0], y2_high[1], above[0], above[1]))
-    lower = 2.0 * row(outer(0), 0) - y1_ends[0, :, lanes]
-    low_own = 2.0 * row(outer(1), 1) - y1_ends[1, :, lanes]
-    high_own = 2.0 * row(main(count - 1), 4) - y1[count - 2, :, lanes]
-    upper = 2.0 * row(outer(2), 5) - y1_ends[2, :, lanes]
-    hold_all(held, (lower, low_own, y3[0, :, lanes], y3[1, :, lanes], y3[2, :, lanes], y3[3, :, lanes], high_own, upper))
-    y4_low[0] = 2.0 * row(outer(1), 0) - y2_low[0]
-    y4_low[1] = 2.0 * row(main(1), 1) - y2_low[1]
-    y4_high[0] = 2.0 * row(main(count - 2), 4) - y2_high[0]
-    y4_high[1] = 2.0 * row(main(count - 1), 5) - y2_high[1]
-    send[...] = jnp.where(at_ref[0] == 0, y4_high[...], y4_low[...])
+
+    @pl.when((at_ref[0] == 0) == foreign)
+    def _():
+        hold_all(held, (y2_high[0], y2_high[1], above[0], above[1]))
+        inside = 2.0 * row(main(count - 1), 0) - y1[count - 2, :, lanes]
+        outside = 2.0 * row(outer(2), 1) - y1_ends[2, :, lanes]
+        hold_all(held, (y3[2, :, lanes], y3[3, :, lanes], inside, outside))
+        y4[0] = 2.0 * row(main(count - 2), 0) - y2_high[0]
+        y4[1] = 2.0 * row(main(count - 1), 1) - y2_high[1]
+
+    @pl.when((at_ref[0] == 0) != foreign)
+    def _():
+        hold_all(held, (below[0], below[1], y2_low[0], y2_low[1]))
+        outside = 2.0 * row(outer(0), 0) - y1_ends[0, :, lanes]
+        inside = 2.0 * row(outer(1), 1) - y1_ends[1, :, lanes]
+        hold_all(held, (outside, inside, y3[0, :, lanes], y3[1, :, lanes]))
+        y4[0] = 2.0 * row(outer(1), 0) - y2_low[0]
+        y4[1] = 2.0 * row(main(1), 1) - y2_low[1]
 
 
 def fold_kernel(at_ref, keep_ref, other_ref, send_ref, stay_ref):
@@ -468,11 +475,11 @@
 
 
 def finish_kernel(chunks, at_ref, *refs):
-    sources, out_ref, sems = refs[: 3 * chunks], refs[-2], refs[-1]
+    sources, out_ref, sems = refs[: 2 * chunks], refs[-2], refs[-1]
     acts = []
     for chunk in range(chunks):
-        y4_low, y4_high, far = sources[3 * chunk : 3 * chunk + 3]
-        pairs = ((0, y4_low, 0, False), (0, far, 0, True), (1, y4_high, 2, False), (1, far, 2, True))
+        own, far = sources[2 * chunk : 2 * chunk + 2]
+        pairs = ((0, own, 0, False), (0, far, 0, True), (1, own, 2, False), (1, far, 2, True))
         acts.append(place_pairs(out_ref, sems, at_ref[0], chunks, chunk, far.shape[2], pairs))
     for act in acts:
         act(lambda copy: copy.start())
@@ -608,14 +615,14 @@
     )(at, high, low, y0, y1, *ends)
 
 
-def last_rows(at, lane, high, low, outer_high, outer_low, y1, y1_ends, y3, y2_low, y2_high, below, above):
+def last_rows(at, lane, foreign, high, low, outer_high, outer_low, y1, y1_ends, y3, y2_low, y2_high, below, above):
     size, columns = below.shape[1:]
     return pl.pallas_call(
-        functools.partial(last_rows_kernel, lane),
+        functools.partial(last_rows_kernel, lane, foreign),
         in_specs=[SCALARS] + [VMEM] * 11,
-        out_specs=[VMEM] * 3,
-        out_shape=[near_core(below.shape)] * 3,
-        scratch_shapes=[pltpu.VMEM(held_shape(8 * size, columns), jnp.bfloat16)],
+        out_specs=VMEM,
+        out_shape=near_core(below.shape),
+        scratch_shapes=[pltpu.VMEM(held_shape(4 * size, columns), jnp.bfloat16)],
         compiler_params=PARAMS,
     )(at, high, low, outer_high, outer_low, y1, y1_ends, y3, y2_low, y2_high, close_by(below), close_by(above))
 
@@ -688,10 +695,10 @@
     chunks = len(parts)
     return pl.pallas_call(
         functools.partial(finish_kernel, chunks),
-        in_specs=[SCALARS] + [ANY] * (3 * chunks + 1),
+        in_specs=[SCALARS] + [ANY] * (2 * chunks + 1),
         out_specs=ANY,
         out_shape=jax.ShapeDtypeStruct(result.shape, jnp.float32),
-        input_output_aliases={1 + 3 * chunks: 0},
+        input_output_aliases={1 + 2 * chunks: 0},
         scratch_shapes=[pltpu.SemaphoreType.DMA((chunks, 4))],
         compiler_params=PARAMS,
     )(at, *[value for part in parts for value in part], result)
@@ -757,8 +764,8 @@
     holds = [(e, p) for e in range(elems) for p in range(width) if e % 2 == p % 2]
     outer = lax.ppermute(last, ("elem", "pts"), [(flat(e, p), flat(e + (2 if p % 2 else -2), p)) for e, p in holds])
     passed = lax.ppermute(outer, ("elem", "pts"), [(flat(e, p), flat(e ^ 1, p)) for e, p in holds])
-    got[chunks:], both = lax.optimization_barrier((got[chunks:], both))
-
+
+    outer, got[-1] = lax.optimization_barrier((outer, got[-1]))
     below = shifted(arranged_pair(at, 2, 1, own, got[chunks:]), "elem", 2)
     y0 = arranged(at, own, got)
     both_near = flipped(both, "pts", 1)
@@ -777,13 +784,12 @@
     near = flipped(near, "elem", 1)
     parts = []
     for c in range(chunks):
-        y4_low, y4_high, far = last_rows(
-            at, c * part, high, low, high_outer, low_outer, y1, y1_ends, y3, ends[c], ends[chunks + c], belows[c], aboves[c]
-        )
-        parts.append((y4_low, y4_high, flipped(far, "elem", 1)))
+        given = (high, low, high_outer, low_outer, y1, y1_ends, y3, ends[c], ends[chunks + c], belows[c], aboves[c])
+        far = flipped(last_rows(at, c * part, True, *given), "elem", 1)
+        parts.append((last_rows(at, c * part, False, *given), far))
     if part % 128:
-        y4_low, y4_high, far = parts[0]
-        mine = jnp.where(side == 0, jnp.concatenate([y4_low, y4[:2]]), jnp.concatenate([y4[2:], y4_high]))
+        ((ends_own, far),) = parts
+        mine = jnp.where(side == 0, jnp.concatenate([ends_own, y4[:2]]), jnp.concatenate([y4[2:], ends_own]))
         theirs = jnp.where(side == 0, jnp.concatenate([far, near]), jnp.concatenate([near, far]))
         swap = lambda first, second: jnp.concatenate([first, second], axis=2)
         result = jnp.where(side == 0, swap(mine, theirs), swap(theirs, mine))

time: 124 us -> 123 us (level)
  waiting for transfers between devices: 49 us -> 44.9 us
  Pallas kernels: 40.4 us -> 42.1 us
  starting transfers between devices: 33.2 us -> 34.9 us
    ppermute x7, waiting for transfers between devices: 9.02 us -> 6.77 us  [shifted(): lax.ppermute(value, axis, [(i, (i + steps) % count) for i in range(count)])]
    ppermute x17, waiting for transfers between devices: 30.4 us -> 28.6 us  [flipped(): return lax.ppermute(value, axis, [(i, i ^ bit) for i in range(count)])]
    ppermute x17, starting transfers between devices: 16.2 us -> 17.9 us  [flipped(): return lax.ppermute(value, axis, [(i, i ^ bit) for i in range(count)])]
    pallas_call x2 -> x4, Pallas kernels: 4.95 us -> 6.66 us  [last_rows(): pl.pallas_call(functools.partial(last_rows_kernel, lane, foreign), in_spe...]
  transfers between devices with their start and end apart: 26 -> 26, of which waited for: 10 -> 12; matrix products, arithmetic and copies ran while one was open for 0% -> 0% of each run, Pallas kernels for 26% -> 27%
where the time goes in v9:
time: 123 us
  waiting for transfers between devices  44.9 us (37%)
  Pallas kernels  42.1 us (34%)
  starting transfers between devices  34.9 us (28%)
    ppermute x17, waiting for transfers between devices, flipped(): return lax.ppermute(value, axis, [(i, i ^ bit) for i in range(count)])  28.6 us
    ppermute x17, starting transfers between devices, flipped(): return lax.ppermute(value, axis, [(i, i ^ bit) for i in range(count)])  17.9 us
    ppermute x7, starting transfers between devices, shifted(): lax.ppermute(value, axis, [(i, (i + steps) % count) for i in range(count)])  13.3 us
    ppermute x1, waiting for transfers between devices, body(): lax.ppermute(last, ('elem', 'pts'), [(flat(e, p), flat(e + (2 if p % 2 el...  9.52 us
    pallas_call x1, Pallas kernels, blocks(): pl.pallas_call(functools.partial(blocks_kernel, faces_total), in_specs=[S...  7.62 us
    ppermute x7, waiting for transfers between devices, shifted(): lax.ppermute(value, axis, [(i, (i + steps) % count) for i in range(count)])  6.77 us
    pallas_call x4, Pallas kernels, last_rows(): pl.pallas_call(functools.partial(last_rows_kernel, lane, foreign), in_spe...  6.66 us
    pallas_call x1, Pallas kernels, middle_rows(): pl.pallas_call(functools.partial(middle_kernel, chunks), in_specs=[SCALAR...  5.2 us
  transfers between devices with their start and end apart: 26, of which 12 were waited for; matrix products, arithmetic and copies ran while one was open for 0% of the time, Pallas kernels for 27%

profile of v9, /device:TPU:0, one launch (start us, length us, event | category | flops | bytes accessed | tf_op | source)
XLA Modules:
  0.0 123.1 jit_solution(15765104561913481369)
XLA Ops:
  0.8 2.1 %shard_map.64 = (f32[256,128]{1,0:T(8,128)S(1)}, f32[2,256,128]{2,1,0:T(8,128)S(1)}, f32[2,256,128]{2,1,0:T(8,128)S(1)}, f32[2,256,128]{2,1,0:T(8,128)S(1)}, f32[2,256,128]{2,1,0:T(8,128)S(1)}) custom-call(s32[4]{0:T(128)S(1)} %pad_add_fusion.at_ref, s32[4,4,64]{2,1,0:T(4,128)S(1)} %copy-done, f32[4,512,256]{2,1,0:T(8,128)} %basis_ref.3, f32[4,256,512]{2,1,0:T(8,128)} %bitcast.6), custom_call_target="tpu_custom_call" | custom-call | tf_op jit(solution)/shard_map/pallas_call | solution.py:492
  2.8 3.0 %collective-permute-start = (f32[2,256,128]{2,1,0:T(8,128)S(1)}, f32[2,256,128]{2,1,0:T(8,128)S(1)}, u32[]{:S(2)}, u32[]{:S(2)}) collective-permute-start(f32[2,256,128]{2,1,0:T(8,128)S(1)} %get-tuple-element.48), channel_id=1, source_target_pairs={{0,4},{4,0},{8,12},{12,8},{16,20},{20,16},{24,28},{28,24},{1,5},{5... | collective-permute-start | bytes 786440 | tf_op jit(solution)/shard_map/ppermute | solution.py:709
  5.9 3.5 %collective-permute-start.1 = (f32[256,128]{1,0:T(8,128)S(1)}, f32[256,128]{1,0:T(8,128)S(1)}, u32[]{:S(2)}, u32[]{:S(2)}) collective-permute-start(f32[256,128]{1,0:T(8,128)S(1)} %get-tuple-element.50), channel_id=1, source_target_pairs={{0,28},{4,0},{8,4},{12,8},{16,12},{20,16},{24,20},{28,24},{1,29},{... | collective-permute-start | bytes 393224 | tf_op jit(solution)/shard_map/ppermute | solution.py:714
  9.4 7.6 %shard_map.65 = (f32[2,392,256]{2,1,0:T(8,128)S(1)}, f32[2,392,256]{2,1,0:T(8,128)S(1)}, f32[256,256]{1,0:T(8,128)S(1)}) custom-call(s32[4]{0:T(128)S(1)} %pad_add_fusion.at_ref, s32[4,4,64]{2,1,0:T(4,128)S(1)} %copy-done, f32[4,512]{1,0:T(4,128)S(1)} %copy-done.1, s32[4,64]{1,0:T(4,128)S(1)} %copy-done.2, f32[4,512,256]{2,1,0:T(8,128)} %basis_ref.3, ...), custom_call_target="tpu_custom_call" | custom-call | tf_op jit(solution)/shard_map/pallas_call | solution.py:506
  18.4 2.3 %collective-permute-done.3.other_ref = f32[2,392,256]{2,1,0:T(8,128)S(1)} collective-permute-done((f32[2,392,256]{2,1,0:T(8,128)S(1)}, f32[2,392,256]{2,1,0:T(8,128)S(1)}, u32[]{:S(2)}, u32[]{:S(2)}) %collective-permute-start.3) | collective-permute-done | bytes 802848 | tf_op jit(solution)/shard_map/ppermute | solution.py:709
  21.3 1.6 %collective-permute-start.4 = (f32[1,392,256]{2,1,0:T(8,128)S(1)}, f32[1,392,256]{2,1,0:T(8,128)S(1)}, u32[]{:S(2)}, u32[]{:S(2)}) collective-permute-start(f32[1,392,256]{2,1,0:T(8,128)S(1)} %get-tuple-element.58), channel_id=1, source_target_pairs={{0,2},{1,3},{2,0},{3,1},{4,6},{5,7},{6,4},{7,5},{8,10},{9,11},{10,... | collective-permute-start | bytes 1204232 | tf_op jit(solution)/shard_map/ppermute | solution.py:709
  22.9 8.1 %collective-permute-done.2.refs_1_ = f32[2,256,128]{2,1,0:T(8,128)S(1)} collective-permute-done((f32[2,256,128]{2,1,0:T(8,128)S(1)}, f32[2,256,128]{2,1,0:T(8,128)S(1)}, u32[]{:S(2)}, u32[]{:S(2)}) %collective-permute-start.2) | collective-permute-done | bytes 262176 | tf_op jit(solution)/shard_map/ppermute | solution.py:709
  30.9 1.6 %shard_map.67 = f32[2,256,256]{2,1,0:T(8,128)S(1)} custom-call(s32[4]{0:T(128)S(1)} %pad_add_fusion.at_ref, f32[4,256,512]{2,1,0:T(8,128)} %bitcast.7, f32[2,256,128]{2,1,0:T(8,128)S(1)} %collective-permute-done.refs_0_, f32[2,256,128]{2,1,0:T(8,128)S(1)} %collective-permute-done.2.refs_1_), custom_call_target="tpu_custom_call" | custom-call | tf_op jit(solution)/shard_map/pallas_call | solution.py:660
  32.7 1.8 %collective-permute-start.5 = (f32[2,256,256]{2,1,0:T(8,128)S(1)}, f32[2,256,256]{2,1,0:T(8,128)S(1)}, u32[]{:S(2)}, u32[]{:S(2)}) collective-permute-start(f32[2,256,256]{2,1,0:T(8,128)S(1)} %shard_map.67), channel_id=1, source_target_pairs={{0,24},{4,28},{8,0},{12,4},{16,8},{20,12},{24,16},{28,20},{1,25},{... | collective-permute-start | bytes 1572872 | tf_op jit(solution)/shard_map/ppermute | solution.py:714
  34.5 1.6 %collective-permute-start.6 = (f32[1,392,256]{2,1,0:T(8,128)S(1)}, f32[1,392,256]{2,1,0:T(8,128)S(1)}, u32[]{:S(2)}, u32[]{:S(2)}) collective-permute-start(f32[1,392,256]{2,1,0:T(8,128)S(1)} %shard_map.69.refs_0_.mine_ref), channel_id=1, source_target_pairs={{0,2},{1,3},{2,0},{3,1},{4,6},{5,7},{6,4},{7,5},{8,10},{9,11},{10,... | collective-permute-start | bytes 1204232 | tf_op jit(solution)/shard_map/ppermute | solution.py:709
  36.4 1.7 %collective-permute-start.8 = (f32[2,256,128]{2,1,0:T(8,128)S(1)}, f32[2,256,128]{2,1,0:T(8,128)S(1)}, u32[]{:S(2)}, u32[]{:S(2)}) collective-permute-start(f32[2,256,128]{2,1,0:T(8,128)S(1)} %get-tuple-element.62), channel_id=1, source_target_pairs={{0,4},{4,0},{8,12},{12,8},{16,20},{20,16},{24,28},{28,24},{1,5},{5... | collective-permute-start | bytes 786440 | tf_op jit(solution)/shard_map/ppermute | solution.py:709
  38.1 13.5 %collective-permute-done.8.refs_0_.refs_2_ = f32[2,256,128]{2,1,0:T(8,128)S(1)} collective-permute-done((f32[2,256,128]{2,1,0:T(8,128)S(1)}, f32[2,256,128]{2,1,0:T(8,128)S(1)}, u32[]{:S(2)}, u32[]{:S(2)}) %collective-permute-start.8) | collective-permute-done | bytes 262176 | tf_op jit(solution)/shard_map/ppermute | solution.py:709
  52.5 2.4 %collective-permute-start.14 = (f32[1,648,256]{2,1,0:T(8,128)S(1)}, f32[1,648,256]{2,1,0:T(8,128)S(1)}, u32[]{:S(2)}, u32[]{:S(2)}) collective-permute-start(f32[1,648,256]{2,1,0:T(8,128)S(1)} %shard_map.72), channel_id=1, source_target_pairs={{0,24},{2,26},{5,13},{7,15},{8,0},{10,2},{13,21},{15,23},{16,8},{1... | collective-permute-start | bytes 1990664 | tf_op jit(solution)/shard_map/ppermute | solution.py:765
  55.5 9.5 %collective-permute-done.14.first_ref = f32[1,648,256]{2,1,0:T(8,128)S(1)} collective-permute-done((f32[1,648,256]{2,1,0:T(8,128)S(1)}, f32[1,648,256]{2,1,0:T(8,128)S(1)}, u32[]{:S(2)}, u32[]{:S(2)}) %collective-permute-start.14) | collective-permute-done | bytes 663584 | tf_op jit(solution)/shard_map/ppermute | solution.py:765
  69.6 3.1 %shard_map.70 = (bf16[8,256,768]{2,1,0:T(8,128)(2,1)S(1)}, bf16[8,256,768]{2,1,0:T(8,128)(2,1)S(1)}) custom-call(s32[4]{0:T(128)S(1)} %pad_add_fusion.at_ref, f32[1,392,256]{2,1,0:T(8,128)S(1)} %shard_map.69.refs_0_.mine_ref, f32[1,392,256]{2,1,0:T(8,128)S(1)} %collective-permute-done.11.refs_1_, ...), custom_call_target="tpu_custom_call" | custom-call | tf_op jit(solution)/shard_map/pallas_call | solution.py:537
  72.7 1.9 %shard_map.74.y0 = f32[8,256,256]{2,1,0:T(8,128)S(1)} custom-call(s32[4]{0:T(128)S(1)} %pad_add_fusion.at_ref, f32[4,256,512]{2,1,0:T(8,128)} %bitcast.9, f32[2,256,128]{2,1,0:T(8,128)S(1)} %collective-permute-done.refs_0_, f32[2,256,128]{2,1,0:T(8,128)S(1)} %collective-permute-done.2.refs_1_, f32[2,256,128]{2,1,0:T(8,128)S(1)} %collective-permute-done.8.refs_0_.refs_2_, ...), custom_call_target="tpu_custom_call" | custom-call | tf_op jit(solution)/shard_map/pallas_call | solution.py:672
  76.2 2.3 %shard_map.75.y1 = f32[7,256,256]{2,1,0:T(8,128)S(1)} custom-call(bf16[8,256,768]{2,1,0:T(8,128)(2,1)S(1)} %get-tuple-element.67.high.high_in, bf16[8,256,768]{2,1,0:T(8,128)(2,1)S(1)} %get-tuple-element.68.low.low_in, f32[8,256,256]{2,1,0:T(8,128)S(1)} %shard_map.74.y0, f32[2,256,256]{2,1,0:T(8,128)S(1)} %collective-permute-done.5.above), custom_call_target="tpu_custom_call" | custom-call | tf_op jit(solution)/shard_map/pallas_call | solution.py:580
  79.7 2.1 %collective-permute-done.18.swapped_ref = f32[1,648,256]{2,1,0:T(8,128)S(1)} collective-permute-done((f32[1,648,256]{2,1,0:T(8,128)S(1)}, f32[1,648,256]{2,1,0:T(8,128)S(1)}, u32[]{:S(2)}, u32[]{:S(2)}) %collective-permute-start.18) | collective-permute-done | bytes 663584 | tf_op jit(solution)/shard_map/ppermute | solution.py:709
  82.8 2.6 %shard_map.78 = (f32[3,256,256]{2,1,0:T(8,128)S(1)}, f32[2,256,128]{2,1,0:T(8,128)S(1)}, f32[2,256,128]{2,1,0:T(8,128)S(1)}, f32[2,256,128]{2,1,0:T(8,128)S(1)}, f32[2,256,128]{2,1,0:T(8,128)S(1)}) custom-call(bf16[8,256,768]{2,1,0:T(8,128)(2,1)S(1)} %get-tuple-element.67.high.high_in, bf16[8,256,768]{2,1,0:T(8,128)(2,1)S(1)} %get-tuple-element.68.low.low_in, ...), custom_call_target="tpu_custom_call" | custom-call | tf_op jit(solution)/shard_map/pallas_call | solution.py:592
  85.5 3.8 %collective-permute-start.20 = (f32[2,256,128]{2,1,0:T(8,128)S(1)}, f32[2,256,128]{2,1,0:T(8,128)S(1)}, u32[]{:S(2)}, u32[]{:S(2)}) collective-permute-start(f32[2,256,128]{2,1,0:T(8,128)S(1)} %get-tuple-element.80.refs_0_.y2_low), channel_id=1, source_target_pairs={{0,24},{4,28},{8,0},{12,4},{16,8},{20,12},{24,16},{28,20},{1,25},{... | collective-permute-start | bytes 786440 | tf_op jit(solution)/shard_map/ppermute | solution.py:714
  89.3 5.2 %shard_map.79 = (f32[4,256,256]{2,1,0:T(8,128)S(1)}, f32[4,256,256]{2,1,0:T(8,128)S(1)}, f32[2,256,256]{2,1,0:T(8,128)S(1)}) custom-call(s32[4]{0:T(128)S(1)} %pad_add_fusion.at_ref, bf16[8,256,768]{2,1,0:T(8,128)(2,1)S(1)} %get-tuple-element.67.high.high_in, bf16[8,256,768]{2,1,0:T(8,128)(2,1)S(1)} %get-tuple-element.68.low.low_in, ...), custom_call_target="tpu_custom_call" | custom-call | tf_op jit(solution)/shard_map/pallas_call | solution.py:604
  94.5 2.9 %collective-permute-start.25 = (f32[2,256,256]{2,1,0:T(8,128)S(1)}, f32[2,256,256]{2,1,0:T(8,128)S(1)}, u32[]{:S(2)}, u32[]{:S(2)}) collective-permute-start(f32[2,256,256]{2,1,0:T(8,128)S(1)} %get-tuple-element.86), channel_id=1, source_target_pairs={{0,4},{4,0},{8,12},{12,8},{16,20},{20,16},{24,28},{28,24},{1,5},{5... | collective-permute-start | bytes 1572872 | tf_op jit(solution)/shard_map/ppermute | solution.py:709
  97.4 3.8 %collective-permute-start.23 = (f32[2,256,128]{2,1,0:T(8,128)S(1)}, f32[2,256,128]{2,1,0:T(8,128)S(1)}, u32[]{:S(2)}, u32[]{:S(2)}) collective-permute-start(f32[2,256,128]{2,1,0:T(8,128)S(1)} %get-tuple-element.81.refs_1_.y2_low), channel_id=1, source_target_pairs={{0,24},{4,28},{8,0},{12,4},{16,8},{20,12},{24,16},{28,20},{1,25},{... | collective-permute-start | bytes 786440 | tf_op jit(solution)/shard_map/ppermute | solution.py:714
  101.2 1.6 %shard_map.81 = f32[2,256,128]{2,1,0:T(8,128)S(1)} custom-call(s32[4]{0:T(128)S(1)} %pad_add_fusion.at_ref, bf16[8,256,768]{2,1,0:T(8,128)(2,1)S(1)} %get-tuple-element.67.high.high_in, bf16[8,256,768]{2,1,0:T(8,128)(2,1)S(1)} %get-tuple-element.68.low.low_in, bf16[3,256,768]{2,1,0:T(8,128)(2,1)S(1)} %get-tuple-element.75.outer_high, ...), custom_call_target="tpu_custom_call" | custom-call | tf_op jit(solution)/shard_map/pallas_call | solution.py:620
  102.8 2.3 %collective-permute-start.21 = (f32[2,256,128]{2,1,0:T(8,128)S(1)}, f32[2,256,128]{2,1,0:T(8,128)S(1)}, u32[]{:S(2)}, u32[]{:S(2)}) collective-permute-start(f32[2,256,128]{2,1,0:T(8,128)S(1)} %shard_map.81), channel_id=1, source_target_pairs={{0,4},{4,0},{8,12},{12,8},{16,20},{20,16},{24,28},{28,24},{1,5},{5... | collective-permute-start | bytes 786440 | tf_op jit(solution)/shard_map/ppermute | solution.py:709
  105.1 3.3 %collective-permute-done.22.below = f32[2,256,128]{2,1,0:T(8,128)S(1)} collective-permute-done((f32[2,256,128]{2,1,0:T(8,128)S(1)}, f32[2,256,128]{2,1,0:T(8,128)S(1)}, u32[]{:S(2)}, u32[]{:S(2)}) %collective-permute-start.22) | collective-permute-done | bytes 262176 | tf_op jit(solution)/shard_map/ppermute | solution.py:714
  108.4 2.4 %collective-permute-done.23.above = f32[2,256,128]{2,1,0:T(8,128)S(1)} collective-permute-done((f32[2,256,128]{2,1,0:T(8,128)S(1)}, f32[2,256,128]{2,1,0:T(8,128)S(1)}, u32[]{:S(2)}, u32[]{:S(2)}) %collective-permute-start.23) | collective-permute-done | bytes 262176 | tf_op jit(solution)/shard_map/ppermute | solution.py:714
  110.9 1.6 %shard_map.83 = f32[2,256,128]{2,1,0:T(8,128)S(1)} custom-call(s32[4]{0:T(128)S(1)} %pad_add_fusion.at_ref, bf16[8,256,768]{2,1,0:T(8,128)(2,1)S(1)} %get-tuple-element.67.high.high_in, bf16[8,256,768]{2,1,0:T(8,128)(2,1)S(1)} %get-tuple-element.68.low.low_in, bf16[3,256,768]{2,1,0:T(8,128)(2,1)S(1)} %get-tuple-element.75.outer_high, ...), custom_call_target="tpu_custom_call" | custom-call | tf_op jit(solution)/shard_map/pallas_call | solution.py:620
  112.5 3.1 %collective-permute-start.24 = (f32[2,256,128]{2,1,0:T(8,128)S(1)}, f32[2,256,128]{2,1,0:T(8,128)S(1)}, u32[]{:S(2)}, u32[]{:S(2)}) collective-permute-start(f32[2,256,128]{2,1,0:T(8,128)S(1)} %shard_map.83), channel_id=1, source_target_pairs={{0,4},{4,0},{8,12},{12,8},{16,20},{20,16},{24,28},{28,24},{1,5},{5... | collective-permute-start | bytes 786440 | tf_op jit(solution)/shard_map/ppermute | solution.py:709
  115.6 1.7 %shard_map.80.refs_0_ = f32[2,256,128]{2,1,0:T(8,128)S(1)} custom-call(s32[4]{0:T(128)S(1)} %pad_add_fusion.at_ref, bf16[8,256,768]{2,1,0:T(8,128)(2,1)S(1)} %get-tuple-element.67.high.high_in, bf16[8,256,768]{2,1,0:T(8,128)(2,1)S(1)} %get-tuple-element.68.low.low_in, bf16[3,256,768]{2,1,0:T(8,128)(2,1)S(1)} %get-tuple-element.75.outer_high, ...), custom_call_target="tpu_custom_call" | custom-call | tf_op jit(solution)/shard_map/pallas_call | solution.py:620
  117.3 1.7 %shard_map.82.refs_2_ = f32[2,256,128]{2,1,0:T(8,128)S(1)} custom-call(s32[4]{0:T(128)S(1)} %pad_add_fusion.at_ref, bf16[8,256,768]{2,1,0:T(8,128)(2,1)S(1)} %get-tuple-element.67.high.high_in, bf16[8,256,768]{2,1,0:T(8,128)(2,1)S(1)} %get-tuple-element.68.low.low_in, bf16[3,256,768]{2,1,0:T(8,128)(2,1)S(1)} %get-tuple-element.75.outer_high, ...), custom_call_target="tpu_custom_call" | custom-call | tf_op jit(solution)/shard_map/pallas_call | solution.py:620
  121.3 1.6 %shard_map.85 = f32[4,256,512]{2,1,0:T(8,128)} custom-call(s32[4]{0:T(128)S(1)} %pad_add_fusion.at_ref, f32[2,256,128]{2,1,0:T(8,128)S(1)} %shard_map.80.refs_0_, f32[2,256,128]{2,1,0:T(8,128)S(1)} %collective-permute-done.21.refs_1_, f32[2,256,128]{2,1,0:T(8,128)S(1)} %shard_map.82.refs_2_, ...), custom_call_target="tpu_custom_call", output_to_operand_aliasing={{}: (5, {})} | custom-call | tf_op jit(solution)/shard_map/pallas_call | solution.py:696
  (49 shorter events, 15.4 us)
Async XLA Ops:
  0.1 0.7 copy-start
  0.8 8.6 %copy-start.1 = (f32[4,512]{1,0:T(4,128)S(1)}, f32[4,512]{1,0:T(4,128)}, u32[]{:S(2)}) copy-start(f32[4,512]{1,0:T(4,128)} %quad_ref.1) | copy-start | bytes 24580
  0.8 8.6 %copy-start.2 = (s32[4,64]{1,0:T(4,128)S(1)}, s32[4,64]{1,0:T(4,128)}, u32[]{:S(2)}) copy-start(s32[4,64]{1,0:T(4,128)} %pair_ref.3) | copy-start | bytes 3076
  2.8 15.5 %collective-permute-start = (f32[2,256,128]{2,1,0:T(8,128)S(1)}, f32[2,256,128]{2,1,0:T(8,128)S(1)}, u32[]{:S(2)}, u32[]{:S(2)}) collective-permute-start(f32[2,256,128]{2,1,0:T(8,128)S(1)} %get-tuple-element.48), channel_id=1, source_target_pairs={{0,4},{4,0},{8,12},{12,8},{16,20},{20,16},{24,28},{28,24},{1,5},{5... | collective-permute-start | bytes 786440 | tf_op jit(solution)/shard_map/ppermute | solution.py:709
  5.9 11.2 %collective-permute-start.1 = (f32[256,128]{1,0:T(8,128)S(1)}, f32[256,128]{1,0:T(8,128)S(1)}, u32[]{:S(2)}, u32[]{:S(2)}) collective-permute-start(f32[256,128]{1,0:T(8,128)S(1)} %get-tuple-element.50), channel_id=1, source_target_pairs={{0,28},{4,0},{8,4},{12,8},{16,12},{20,16},{24,20},{28,24},{1,29},{... | collective-permute-start | bytes 393224 | tf_op jit(solution)/shard_map/ppermute | solution.py:714
  18.3 2.4 %collective-permute-start.3 = (f32[2,392,256]{2,1,0:T(8,128)S(1)}, f32[2,392,256]{2,1,0:T(8,128)S(1)}, u32[]{:S(2)}, u32[]{:S(2)}) collective-permute-start(f32[2,392,256]{2,1,0:T(8,128)S(1)} %get-tuple-element.57), channel_id=1, source_target_pairs={{0,1},{1,0},{2,3},{3,2},{4,5},{5,4},{6,7},{7,6},{8,9},{9,8},{10,11... | collective-permute-start | bytes 2408456 | tf_op jit(solution)/shard_map/ppermute | solution.py:709
  21.3 11.4 %collective-permute-start.4 = (f32[1,392,256]{2,1,0:T(8,128)S(1)}, f32[1,392,256]{2,1,0:T(8,128)S(1)}, u32[]{:S(2)}, u32[]{:S(2)}) collective-permute-start(f32[1,392,256]{2,1,0:T(8,128)S(1)} %get-tuple-element.58), channel_id=1, source_target_pairs={{0,2},{1,3},{2,0},{3,1},{4,6},{5,7},{6,4},{7,5},{8,10},{9,11},{10,... | collective-permute-start | bytes 1204232 | tf_op jit(solution)/shard_map/ppermute | solution.py:709
  22.9 8.1 %collective-permute-start.2 = (f32[2,256,128]{2,1,0:T(8,128)S(1)}, f32[2,256,128]{2,1,0:T(8,128)S(1)}, u32[]{:S(2)}, u32[]{:S(2)}) collective-permute-start(f32[2,256,128]{2,1,0:T(8,128)S(1)} %get-tuple-element.55), channel_id=1, source_target_pairs={{0,4},{4,0},{8,12},{12,8},{16,20},{20,16},{24,28},{28,24},{1,5},{5... | collective-permute-start | bytes 786440 | tf_op jit(solution)/shard_map/ppermute | solution.py:709
  32.7 18.9 %collective-permute-start.5 = (f32[2,256,256]{2,1,0:T(8,128)S(1)}, f32[2,256,256]{2,1,0:T(8,128)S(1)}, u32[]{:S(2)}, u32[]{:S(2)}) collective-permute-start(f32[2,256,256]{2,1,0:T(8,128)S(1)} %shard_map.67), channel_id=1, source_target_pairs={{0,24},{4,28},{8,0},{12,4},{16,8},{20,12},{24,16},{28,20},{1,25},{... | collective-permute-start | bytes 1572872 | tf_op jit(solution)/shard_map/ppermute | solution.py:714
  34.5 17.1 %collective-permute-start.6 = (f32[1,392,256]{2,1,0:T(8,128)S(1)}, f32[1,392,256]{2,1,0:T(8,128)S(1)}, u32[]{:S(2)}, u32[]{:S(2)}) collective-permute-start(f32[1,392,256]{2,1,0:T(8,128)S(1)} %shard_map.69.refs_0_.mine_ref), channel_id=1, source_target_pairs={{0,2},{1,3},{2,0},{3,1},{4,6},{5,7},{6,4},{7,5},{8,10},{9,11},{10,... | collective-permute-start | bytes 1204232 | tf_op jit(solution)/shard_map/ppermute | solution.py:709
  36.1 15.6 %collective-permute-start.7 = (f32[1,392,256]{2,1,0:T(8,128)S(1)}, f32[1,392,256]{2,1,0:T(8,128)S(1)}, u32[]{:S(2)}, u32[]{:S(2)}) collective-permute-start(f32[1,392,256]{2,1,0:T(8,128)S(1)} %shard_map.69.refs_0_.mine_ref), channel_id=1, source_target_pairs={{0,4},{4,0},{8,12},{12,8},{16,20},{20,16},{24,28},{28,24},{1,5},{5... | collective-permute-start | bytes 1204232 | tf_op jit(solution)/shard_map/ppermute | solution.py:709
  36.4 15.2 %collective-permute-start.8 = (f32[2,256,128]{2,1,0:T(8,128)S(1)}, f32[2,256,128]{2,1,0:T(8,128)S(1)}, u32[]{:S(2)}, u32[]{:S(2)}) collective-permute-start(f32[2,256,128]{2,1,0:T(8,128)S(1)} %get-tuple-element.62), channel_id=1, source_target_pairs={{0,4},{4,0},{8,12},{12,8},{16,20},{20,16},{24,28},{28,24},{1,5},{5... | collective-permute-start | bytes 786440 | tf_op jit(solution)/shard_map/ppermute | solution.py:709
  52.5 12.6 %collective-permute-start.14 = (f32[1,648,256]{2,1,0:T(8,128)S(1)}, f32[1,648,256]{2,1,0:T(8,128)S(1)}, u32[]{:S(2)}, u32[]{:S(2)}) collective-permute-start(f32[1,648,256]{2,1,0:T(8,128)S(1)} %shard_map.72), channel_id=1, source_target_pairs={{0,24},{2,26},{5,13},{7,15},{8,0},{10,2},{13,21},{15,23},{16,8},{1... | collective-permute-start | bytes 1990664 | tf_op jit(solution)/shard_map/ppermute | solution.py:765
  54.8 12.5 %collective-permute-start.11 = (f32[1,392,256]{2,1,0:T(8,128)S(1)}, f32[1,392,256]{2,1,0:T(8,128)S(1)}, u32[]{:S(2)}, u32[]{:S(2)}) collective-permute-start(f32[1,392,256]{2,1,0:T(8,128)S(1)} %shard_map.69.refs_0_.mine_ref), channel_id=1, source_target_pairs={{0,1},{1,0},{2,3},{3,2},{4,5},{5,4},{6,7},{7,6},{8,9},{9,8},{10,11... | collective-permute-start | bytes 1204232 | tf_op jit(solution)/shard_map/ppermute | solution.py:709
  54.9 12.9 %collective-permute-start.9 = (f32[1,392,256]{2,1,0:T(8,128)S(1)}, f32[1,392,256]{2,1,0:T(8,128)S(1)}, u32[]{:S(2)}, u32[]{:S(2)}) collective-permute-start(f32[1,392,256]{2,1,0:T(8,128)S(1)} %collective-permute-done.7.refs_3_), channel_id=1, source_target_pairs={{0,2},{1,3},{2,0},{3,1},{4,6},{5,7},{6,4},{7,5},{8,10},{9,11},{10,... | collective-permute-start | bytes 1204232 | tf_op jit(solution)/shard_map/ppermute | solution.py:709
  55.5 10.9 %collective-permute-start.15 = (f32[2,256,128]{2,1,0:T(8,128)S(1)}, f32[2,256,128]{2,1,0:T(8,128)S(1)}, u32[]{:S(2)}, u32[]{:S(2)}) collective-permute-start(f32[2,256,128]{2,1,0:T(8,128)S(1)} %get-tuple-element.69), channel_id=1, source_target_pairs={{0,4},{4,0},{8,12},{12,8},{16,20},{20,16},{24,28},{28,24},{1,5},{5... | collective-permute-start | bytes 786440 | tf_op jit(solution)/shard_map/ppermute | solution.py:709
  65.0 14.5 %collective-permute-start.17 = (f32[1,648,256]{2,1,0:T(8,128)S(1)}, f32[1,648,256]{2,1,0:T(8,128)S(1)}, u32[]{:S(2)}, u32[]{:S(2)}) collective-permute-start(f32[1,648,256]{2,1,0:T(8,128)S(1)} %collective-permute-done.14.first_ref), channel_id=1, source_target_pairs={{0,4},{2,6},{5,1},{7,3},{8,12},{10,14},{13,9},{15,11},{16,20},{18,... | collective-permute-start | bytes 1990664 | tf_op jit(solution)/shard_map/ppermute | solution.py:766
  67.0 12.5 %collective-permute-start.16 = (f32[2,256,256]{2,1,0:T(8,128)S(1)}, f32[2,256,256]{2,1,0:T(8,128)S(1)}, u32[]{:S(2)}, u32[]{:S(2)}) collective-permute-start(f32[2,256,256]{2,1,0:T(8,128)S(1)} %shard_map.73), channel_id=1, source_target_pairs={{0,8},{4,12},{8,16},{12,20},{16,24},{20,28},{24,0},{28,4},{1,9},{5... | collective-permute-start | bytes 1572872 | tf_op jit(solution)/shard_map/ppermute | solution.py:714
  67.3 1.7 %collective-permute-start.12 = (f32[1,392,256]{2,1,0:T(8,128)S(1)}, f32[1,392,256]{2,1,0:T(8,128)S(1)}, u32[]{:S(2)}, u32[]{:S(2)}) collective-permute-start(f32[1,392,256]{2,1,0:T(8,128)S(1)} %collective-permute-done.6.refs_2_.beside_ref), channel_id=1, source_target_pairs={{0,1},{1,0},{2,3},{3,2},{4,5},{5,4},{6,7},{7,6},{8,9},{9,8},{10,11... | collective-permute-start | bytes 1204232 | tf_op jit(solution)/shard_map/ppermute | solution.py:709
  67.3 2.3 %collective-permute-start.13 = (f32[1,392,256]{2,1,0:T(8,128)S(1)}, f32[1,392,256]{2,1,0:T(8,128)S(1)}, u32[]{:S(2)}, u32[]{:S(2)}) collective-permute-start(f32[1,392,256]{2,1,0:T(8,128)S(1)} %collective-permute-done.7.refs_3_), channel_id=1, source_target_pairs={{0,1},{1,0},{2,3},{3,2},{4,5},{5,4},{6,7},{7,6},{8,9},{9,8},{10,11... | collective-permute-start | bytes 1204232 | tf_op jit(solution)/shard_map/ppermute | solution.py:709
  67.8 6.8 %collective-permute-start.10 = (f32[1,392,256]{2,1,0:T(8,128)S(1)}, f32[1,392,256]{2,1,0:T(8,128)S(1)}, u32[]{:S(2)}, u32[]{:S(2)}) collective-permute-start(f32[1,392,256]{2,1,0:T(8,128)S(1)} %collective-permute-done.9.refs_0_), channel_id=1, source_target_pairs={{0,1},{1,0},{2,3},{3,2},{4,5},{5,4},{6,7},{7,6},{8,9},{9,8},{10,11... | collective-permute-start | bytes 1204232 | tf_op jit(solution)/shard_map/ppermute | solution.py:709
  79.6 2.2 %collective-permute-start.18 = (f32[1,648,256]{2,1,0:T(8,128)S(1)}, f32[1,648,256]{2,1,0:T(8,128)S(1)}, u32[]{:S(2)}, u32[]{:S(2)}) collective-permute-start(f32[1,648,256]{2,1,0:T(8,128)S(1)} %shard_map.76.kept_ref), channel_id=1, source_target_pairs={{0,1},{1,0},{2,3},{3,2},{4,5},{5,4},{6,7},{7,6},{8,9},{9,8},{10,11... | collective-permute-start | bytes 1990664 | tf_op jit(solution)/shard_map/ppermute | solution.py:709
  85.4 15.8 %collective-permute-start.19 = (f32[2,256,128]{2,1,0:T(8,128)S(1)}, f32[2,256,128]{2,1,0:T(8,128)S(1)}, u32[]{:S(2)}, u32[]{:S(2)}) collective-permute-start(f32[2,256,128]{2,1,0:T(8,128)S(1)} %get-tuple-element.82.refs_2_.y2_high), channel_id=1, source_target_pairs={{0,8},{4,12},{8,16},{12,20},{16,24},{20,28},{24,0},{28,4},{1,9},{5... | collective-permute-start | bytes 786440 | tf_op jit(solution)/shard_map/ppermute | solution.py:714
  85.5 15.8 %collective-permute-start.20 = (f32[2,256,128]{2,1,0:T(8,128)S(1)}, f32[2,256,128]{2,1,0:T(8,128)S(1)}, u32[]{:S(2)}, u32[]{:S(2)}) collective-permute-start(f32[2,256,128]{2,1,0:T(8,128)S(1)} %get-tuple-element.80.refs_0_.y2_low), channel_id=1, source_target_pairs={{0,24},{4,28},{8,0},{12,4},{16,8},{20,12},{24,16},{28,20},{1,25},{... | collective-permute-start | bytes 786440 | tf_op jit(solution)/shard_map/ppermute | solution.py:714
  94.5 24.6 %collective-permute-start.25 = (f32[2,256,256]{2,1,0:T(8,128)S(1)}, f32[2,256,256]{2,1,0:T(8,128)S(1)}, u32[]{:S(2)}, u32[]{:S(2)}) collective-permute-start(f32[2,256,256]{2,1,0:T(8,128)S(1)} %get-tuple-element.86), channel_id=1, source_target_pairs={{0,4},{4,0},{8,12},{12,8},{16,20},{20,16},{24,28},{28,24},{1,5},{5... | collective-permute-start | bytes 1572872 | tf_op jit(solution)/shard_map/ppermute | solution.py:709
  97.4 11.0 %collective-permute-start.22 = (f32[2,256,128]{2,1,0:T(8,128)S(1)}, f32[2,256,128]{2,1,0:T(8,128)S(1)}, u32[]{:S(2)}, u32[]{:S(2)}) collective-permute-start(f32[2,256,128]{2,1,0:T(8,128)S(1)} %get-tuple-element.83.refs_3_.y2_high), channel_id=1, source_target_pairs={{0,8},{4,12},{8,16},{12,20},{16,24},{20,28},{24,0},{28,4},{1,9},{5... | collective-permute-start | bytes 786440 | tf_op jit(solution)/shard_map/ppermute | solution.py:714
  97.4 13.5 %collective-permute-start.23 = (f32[2,256,128]{2,1,0:T(8,128)S(1)}, f32[2,256,128]{2,1,0:T(8,128)S(1)}, u32[]{:S(2)}, u32[]{:S(2)}) collective-permute-start(f32[2,256,128]{2,1,0:T(8,128)S(1)} %get-tuple-element.81.refs_1_.y2_low), channel_id=1, source_target_pairs={{0,24},{4,28},{8,0},{12,4},{16,8},{20,12},{24,16},{28,20},{1,25},{... | collective-permute-start | bytes 786440 | tf_op jit(solution)/shard_map/ppermute | solution.py:714
  102.8 17.8 %collective-permute-start.21 = (f32[2,256,128]{2,1,0:T(8,128)S(1)}, f32[2,256,128]{2,1,0:T(8,128)S(1)}, u32[]{:S(2)}, u32[]{:S(2)}) collective-permute-start(f32[2,256,128]{2,1,0:T(8,128)S(1)} %shard_map.81), channel_id=1, source_target_pairs={{0,4},{4,0},{8,12},{12,8},{16,20},{20,16},{24,28},{28,24},{1,5},{5... | collective-permute-start | bytes 786440 | tf_op jit(solution)/shard_map/ppermute | solution.py:709
  112.5 8.8 %collective-permute-start.24 = (f32[2,256,128]{2,1,0:T(8,128)S(1)}, f32[2,256,128]{2,1,0:T(8,128)S(1)}, u32[]{:S(2)}, u32[]{:S(2)}) collective-permute-start(f32[2,256,128]{2,1,0:T(8,128)S(1)} %shard_map.83), channel_id=1, source_target_pairs={{0,4},{4,0},{8,12},{12,8},{16,20},{20,16},{24,28},{28,24},{1,5},{5... | collective-permute-start | bytes 786440 | tf_op jit(solution)/shard_map/ppermute | solution.py:709

commit v10 on v9

--- a/solution.py
+++ b/solution.py
@@ -352,7 +352,7 @@
 def last_rows_kernel(
     lane, foreign, at_ref, high, low, outer_high, outer_low, y1, y1_ends, y3, y2_low, y2_high, below, above, y4, held
 ):
-    size, columns = below.shape[1:]
+    size, columns = y4.shape[1:]
     count = high.shape[0]
     lanes = slice(lane, lane + columns)
     row = lambda weight, start: apply_row(*weight, held, start * size, columns)
@@ -376,6 +376,15 @@
         hold_all(held, (outside, inside, y3[0, :, lanes], y3[1, :, lanes]))
         y4[0] = 2.0 * row(outer(1), 0) - y2_low[0]
         y4[1] = 2.0 * row(main(1), 1) - y2_low[1]
+
+
+def own_rows_kernel(chunks, at_ref, *refs):
+    shared, groups, (y4, held) = refs[:7], refs[7:-2], refs[-2:]
+    joined = [
+        [jnp.concatenate([ref[at] for ref in groups[group * chunks : (group + 1) * chunks]], axis=1) for at in range(2)]
+        for group in range(4)
+    ]
+    last_rows_kernel(0, False, at_ref, *shared, *joined, y4, held)
 
 
 def fold_kernel(at_ref, keep_ref, other_ref, send_ref, stay_ref):
@@ -462,8 +471,10 @@
     return moved
 
 
-def collect_kernel(at_ref, y4, near, out_ref, sems):
+def collect_kernel(at_ref, y4, own, near, out_ref, sems):
     pairs = (
+        (0, own, 0, False),
+        (1, own, 2, False),
         (0, y4.at[pl.ds(0, 2)], 2, False),
         (0, near, 2, True),
         (1, y4.at[pl.ds(2, 2)], 0, False),
@@ -475,11 +486,11 @@
 
 
 def finish_kernel(chunks, at_ref, *refs):
-    sources, out_ref, sems = refs[: 2 * chunks], refs[-2], refs[-1]
+    sources, out_ref, sems = refs[:chunks], refs[-2], refs[-1]
     acts = []
     for chunk in range(chunks):
-        own, far = sources[2 * chunk : 2 * chunk + 2]
-        pairs = ((0, own, 0, False), (0, far, 0, True), (1, own, 2, False), (1, far, 2, True))
+        far = sources[chunk]
+        pairs = ((0, far, 0, True), (1, far, 2, True))
         acts.append(place_pairs(out_ref, sems, at_ref[0], chunks, chunk, far.shape[2], pairs))
     for act in acts:
         act(lambda copy: copy.start())
@@ -627,6 +638,19 @@
     )(at, high, low, outer_high, outer_low, y1, y1_ends, y3, y2_low, y2_high, close_by(below), close_by(above))
 
 
+def own_rows(at, shared, groups):
+    chunks = len(groups[0])
+    _, size, width = groups[0][0].shape
+    return pl.pallas_call(
+        functools.partial(own_rows_kernel, chunks),
+        in_specs=[SCALARS] + [VMEM] * (7 + 4 * chunks),
+        out_specs=VMEM,
+        out_shape=near_core((2, size, chunks * width)),
+        scratch_shapes=[pltpu.VMEM(held_shape(4 * size, chunks * width), jnp.bfloat16)],
+        compiler_params=PARAMS,
+    )(at, *shared, *[value for group in groups for value in group])
+
+
 def folded(lane, keep, other):
     shape = (keep.shape[0] // 2, *keep.shape[1:])
     return pl.pallas_call(
@@ -679,29 +703,29 @@
     )(at, far_off(vector), *got)
 
 
-def collected(at, y4, near):
+def collected(at, y4, own, near):
     _, size, columns = near.shape
     return pl.pallas_call(
         collect_kernel,
-        in_specs=[SCALARS, ANY, ANY],
+        in_specs=[SCALARS, ANY, ANY, ANY],
         out_specs=ANY,
         out_shape=jax.ShapeDtypeStruct((4, size, 2 * columns), jnp.float32),
-        scratch_shapes=[pltpu.SemaphoreType.DMA((1, 4))],
-        compiler_params=PARAMS,
-    )(at, y4, near)
+        scratch_shapes=[pltpu.SemaphoreType.DMA((1, 6))],
+        compiler_params=PARAMS,
+    )(at, y4, own, near)
 
 
 def finished(at, parts, result):
     chunks = len(parts)
     return pl.pallas_call(
         functools.partial(finish_kernel, chunks),
-        in_specs=[SCALARS] + [ANY] * (2 * chunks + 1),
+        in_specs=[SCALARS] + [ANY] * (chunks + 1),
         out_specs=ANY,
         out_shape=jax.ShapeDtypeStruct(result.shape, jnp.float32),
-        input_output_aliases={1 + 2 * chunks: 0},
+        input_output_aliases={1 + chunks: 0},
         scratch_shapes=[pltpu.SemaphoreType.DMA((chunks, 4))],
         compiler_params=PARAMS,
-    )(at, *[value for part in parts for value in part], result)
+    )(at, *parts, result)
 
 
 def flipped(value, axis, bit):
@@ -786,15 +810,17 @@
     for c in range(chunks):
         given = (high, low, high_outer, low_outer, y1, y1_ends, y3, ends[c], ends[chunks + c], belows[c], aboves[c])
         far = flipped(last_rows(at, c * part, True, *given), "elem", 1)
-        parts.append((last_rows(at, c * part, False, *given), far))
+        parts.append(far)
+    shared = (high, low, high_outer, low_outer, y1, y1_ends, y3)
+    ends_own = own_rows(at, shared, (ends[:chunks], ends[chunks:], belows, aboves))
     if part % 128:
-        ((ends_own, far),) = parts
+        (far,) = parts
         mine = jnp.where(side == 0, jnp.concatenate([ends_own, y4[:2]]), jnp.concatenate([y4[2:], ends_own]))
         theirs = jnp.where(side == 0, jnp.concatenate([far, near]), jnp.concatenate([near, far]))
         swap = lambda first, second: jnp.concatenate([first, second], axis=2)
         result = jnp.where(side == 0, swap(mine, theirs), swap(theirs, mine))
     else:
-        result = finished(at, parts, collected(at, y4, near))
+        result = finished(at, parts, collected(at, y4, ends_own, near))
     return result.reshape(count * size, columns)
 
 

time: 123 us -> 123 us (level)
    pallas_call x4 -> x2, Pallas kernels: 6.66 us -> 3.19 us  [last_rows(): pl.pallas_call(functools.partial(last_rows_kernel, lane, foreign), in_spe...]
    pallas_call x1 -> x2, Pallas kernels: 1.55 us -> 4.03 us  [the longest x1 2.3 us: own_rows(): pl.pallas_call(functools.partial(own_rows_kernel, chunks), in_specs=[SCAL...]
  transfers between devices with their start and end apart: 26 -> 26, of which waited for: 12 -> 12; matrix products, arithmetic and copies ran while one was open for 0% -> 0% of each run, Pallas kernels for 27% -> 26%
where the time goes in v10:
time: 123 us
  waiting for transfers between devices  45.9 us (37%)
  Pallas kernels  40.9 us (33%)
  starting transfers between devices  34.9 us (28%)
    ppermute x17, waiting for transfers between devices, flipped(): return lax.ppermute(value, axis, [(i, i ^ bit) for i in range(count)])  29.6 us
    ppermute x17, starting transfers between devices, flipped(): return lax.ppermute(value, axis, [(i, i ^ bit) for i in range(count)])  17.9 us
    ppermute x7, starting transfers between devices, shifted(): lax.ppermute(value, axis, [(i, (i + steps) % count) for i in range(count)])  13.3 us
    ppermute x1, waiting for transfers between devices, body(): lax.ppermute(last, ('elem', 'pts'), [(flat(e, p), flat(e + (2 if p % 2 el...  9.52 us
    pallas_call x1, Pallas kernels, blocks(): pl.pallas_call(functools.partial(blocks_kernel, faces_total), in_specs=[S...  7.62 us
    ppermute x7, waiting for transfers between devices, shifted(): lax.ppermute(value, axis, [(i, (i + steps) % count) for i in range(count)])  6.77 us
    pallas_call x1, Pallas kernels, middle_rows(): pl.pallas_call(functools.partial(middle_kernel, chunks), in_specs=[SCALAR...  5.2 us
    pallas_call x2, Pallas kernels, last_rows(): pl.pallas_call(functools.partial(last_rows_kernel, lane, foreign), in_spe...  3.19 us
  transfers between devices with their start and end apart: 26, of which 12 were waited for; matrix products, arithmetic and copies ran while one was open for 0% of the time, Pallas kernels for 26%

profile of v10, /device:TPU:0, one launch (start us, length us, event | category | flops | bytes accessed | tf_op | source)
XLA Modules:
  0.0 122.9 jit_solution(15385647766048077887)
XLA Ops:
  0.8 2.1 %shard_map.64 = (f32[256,128]{1,0:T(8,128)S(1)}, f32[2,256,128]{2,1,0:T(8,128)S(1)}, f32[2,256,128]{2,1,0:T(8,128)S(1)}, f32[2,256,128]{2,1,0:T(8,128)S(1)}, f32[2,256,128]{2,1,0:T(8,128)S(1)}) custom-call(s32[4]{0:T(128)S(1)} %pad_add_fusion.at_ref, s32[4,4,64]{2,1,0:T(4,128)S(1)} %copy-done, f32[4,512,256]{2,1,0:T(8,128)} %basis_ref.3, f32[4,256,512]{2,1,0:T(8,128)} %bitcast.6), custom_call_target="tpu_custom_call" | custom-call | tf_op jit(solution)/shard_map/pallas_call | solution.py:503
  2.8 3.0 %collective-permute-start = (f32[2,256,128]{2,1,0:T(8,128)S(1)}, f32[2,256,128]{2,1,0:T(8,128)S(1)}, u32[]{:S(2)}, u32[]{:S(2)}) collective-permute-start(f32[2,256,128]{2,1,0:T(8,128)S(1)} %get-tuple-element.48), channel_id=1, source_target_pairs={{0,4},{4,0},{8,12},{12,8},{16,20},{20,16},{24,28},{28,24},{1,5},{5... | collective-permute-start | bytes 786440 | tf_op jit(solution)/shard_map/ppermute | solution.py:733
  5.9 3.5 %collective-permute-start.1 = (f32[256,128]{1,0:T(8,128)S(1)}, f32[256,128]{1,0:T(8,128)S(1)}, u32[]{:S(2)}, u32[]{:S(2)}) collective-permute-start(f32[256,128]{1,0:T(8,128)S(1)} %get-tuple-element.50), channel_id=1, source_target_pairs={{0,28},{4,0},{8,4},{12,8},{16,12},{20,16},{24,20},{28,24},{1,29},{... | collective-permute-start | bytes 393224 | tf_op jit(solution)/shard_map/ppermute | solution.py:738
  9.4 7.6 %shard_map.65 = (f32[2,392,256]{2,1,0:T(8,128)S(1)}, f32[2,392,256]{2,1,0:T(8,128)S(1)}, f32[256,256]{1,0:T(8,128)S(1)}) custom-call(s32[4]{0:T(128)S(1)} %pad_add_fusion.at_ref, s32[4,4,64]{2,1,0:T(4,128)S(1)} %copy-done, f32[4,512]{1,0:T(4,128)S(1)} %copy-done.1, s32[4,64]{1,0:T(4,128)S(1)} %copy-done.2, f32[4,512,256]{2,1,0:T(8,128)} %basis_ref.3, ...), custom_call_target="tpu_custom_call" | custom-call | tf_op jit(solution)/shard_map/pallas_call | solution.py:517
  18.4 2.3 %collective-permute-done.3.other_ref = f32[2,392,256]{2,1,0:T(8,128)S(1)} collective-permute-done((f32[2,392,256]{2,1,0:T(8,128)S(1)}, f32[2,392,256]{2,1,0:T(8,128)S(1)}, u32[]{:S(2)}, u32[]{:S(2)}) %collective-permute-start.3) | collective-permute-done | bytes 802848 | tf_op jit(solution)/shard_map/ppermute | solution.py:733
  21.3 1.6 %collective-permute-start.4 = (f32[1,392,256]{2,1,0:T(8,128)S(1)}, f32[1,392,256]{2,1,0:T(8,128)S(1)}, u32[]{:S(2)}, u32[]{:S(2)}) collective-permute-start(f32[1,392,256]{2,1,0:T(8,128)S(1)} %get-tuple-element.58), channel_id=1, source_target_pairs={{0,2},{1,3},{2,0},{3,1},{4,6},{5,7},{6,4},{7,5},{8,10},{9,11},{10,... | collective-permute-start | bytes 1204232 | tf_op jit(solution)/shard_map/ppermute | solution.py:733
  22.9 8.1 %collective-permute-done.2.refs_1_ = f32[2,256,128]{2,1,0:T(8,128)S(1)} collective-permute-done((f32[2,256,128]{2,1,0:T(8,128)S(1)}, f32[2,256,128]{2,1,0:T(8,128)S(1)}, u32[]{:S(2)}, u32[]{:S(2)}) %collective-permute-start.2) | collective-permute-done | bytes 262176 | tf_op jit(solution)/shard_map/ppermute | solution.py:733
  30.9 1.6 %shard_map.67 = f32[2,256,256]{2,1,0:T(8,128)S(1)} custom-call(s32[4]{0:T(128)S(1)} %pad_add_fusion.at_ref, f32[4,256,512]{2,1,0:T(8,128)} %bitcast.7, f32[2,256,128]{2,1,0:T(8,128)S(1)} %collective-permute-done.refs_0_, f32[2,256,128]{2,1,0:T(8,128)S(1)} %collective-permute-done.2.refs_1_), custom_call_target="tpu_custom_call" | custom-call | tf_op jit(solution)/shard_map/pallas_call | solution.py:684
  32.7 1.8 %collective-permute-start.5 = (f32[2,256,256]{2,1,0:T(8,128)S(1)}, f32[2,256,256]{2,1,0:T(8,128)S(1)}, u32[]{:S(2)}, u32[]{:S(2)}) collective-permute-start(f32[2,256,256]{2,1,0:T(8,128)S(1)} %shard_map.67), channel_id=1, source_target_pairs={{0,24},{4,28},{8,0},{12,4},{16,8},{20,12},{24,16},{28,20},{1,25},{... | collective-permute-start | bytes 1572872 | tf_op jit(solution)/shard_map/ppermute | solution.py:738
  34.5 1.6 %collective-permute-start.6 = (f32[1,392,256]{2,1,0:T(8,128)S(1)}, f32[1,392,256]{2,1,0:T(8,128)S(1)}, u32[]{:S(2)}, u32[]{:S(2)}) collective-permute-start(f32[1,392,256]{2,1,0:T(8,128)S(1)} %shard_map.69.refs_0_.mine_ref), channel_id=1, source_target_pairs={{0,2},{1,3},{2,0},{3,1},{4,6},{5,7},{6,4},{7,5},{8,10},{9,11},{10,... | collective-permute-start | bytes 1204232 | tf_op jit(solution)/shard_map/ppermute | solution.py:733
  36.4 1.7 %collective-permute-start.8 = (f32[2,256,128]{2,1,0:T(8,128)S(1)}, f32[2,256,128]{2,1,0:T(8,128)S(1)}, u32[]{:S(2)}, u32[]{:S(2)}) collective-permute-start(f32[2,256,128]{2,1,0:T(8,128)S(1)} %get-tuple-element.62), channel_id=1, source_target_pairs={{0,4},{4,0},{8,12},{12,8},{16,20},{20,16},{24,28},{28,24},{1,5},{5... | collective-permute-start | bytes 786440 | tf_op jit(solution)/shard_map/ppermute | solution.py:733
  38.1 13.5 %collective-permute-done.8.refs_0_.refs_2_ = f32[2,256,128]{2,1,0:T(8,128)S(1)} collective-permute-done((f32[2,256,128]{2,1,0:T(8,128)S(1)}, f32[2,256,128]{2,1,0:T(8,128)S(1)}, u32[]{:S(2)}, u32[]{:S(2)}) %collective-permute-start.8) | collective-permute-done | bytes 262176 | tf_op jit(solution)/shard_map/ppermute | solution.py:733
  52.5 2.4 %collective-permute-start.14 = (f32[1,648,256]{2,1,0:T(8,128)S(1)}, f32[1,648,256]{2,1,0:T(8,128)S(1)}, u32[]{:S(2)}, u32[]{:S(2)}) collective-permute-start(f32[1,648,256]{2,1,0:T(8,128)S(1)} %shard_map.72), channel_id=1, source_target_pairs={{0,24},{2,26},{5,13},{7,15},{8,0},{10,2},{13,21},{15,23},{16,8},{1... | collective-permute-start | bytes 1990664 | tf_op jit(solution)/shard_map/ppermute | solution.py:789
  55.5 9.5 %collective-permute-done.14.first_ref = f32[1,648,256]{2,1,0:T(8,128)S(1)} collective-permute-done((f32[1,648,256]{2,1,0:T(8,128)S(1)}, f32[1,648,256]{2,1,0:T(8,128)S(1)}, u32[]{:S(2)}, u32[]{:S(2)}) %collective-permute-start.14) | collective-permute-done | bytes 663584 | tf_op jit(solution)/shard_map/ppermute | solution.py:789
  69.6 3.1 %shard_map.70 = (bf16[8,256,768]{2,1,0:T(8,128)(2,1)S(1)}, bf16[8,256,768]{2,1,0:T(8,128)(2,1)S(1)}) custom-call(s32[4]{0:T(128)S(1)} %pad_add_fusion.at_ref, f32[1,392,256]{2,1,0:T(8,128)S(1)} %shard_map.69.refs_0_.mine_ref, f32[1,392,256]{2,1,0:T(8,128)S(1)} %collective-permute-done.11.refs_1_, ...), custom_call_target="tpu_custom_call" | custom-call | tf_op jit(solution)/shard_map/pallas_call | solution.py:548
  72.7 1.9 %shard_map.74.y0 = f32[8,256,256]{2,1,0:T(8,128)S(1)} custom-call(s32[4]{0:T(128)S(1)} %pad_add_fusion.at_ref, f32[4,256,512]{2,1,0:T(8,128)} %bitcast.9, f32[2,256,128]{2,1,0:T(8,128)S(1)} %collective-permute-done.refs_0_, f32[2,256,128]{2,1,0:T(8,128)S(1)} %collective-permute-done.2.refs_1_, f32[2,256,128]{2,1,0:T(8,128)S(1)} %collective-permute-done.8.refs_0_.refs_2_, ...), custom_call_target="tpu_custom_call" | custom-call | tf_op jit(solution)/shard_map/pallas_call | solution.py:696
  76.2 2.3 %shard_map.75.y1.refs_4_ = f32[7,256,256]{2,1,0:T(8,128)S(1)} custom-call(bf16[8,256,768]{2,1,0:T(8,128)(2,1)S(1)} %get-tuple-element.67.high.high_in.refs_0_, bf16[8,256,768]{2,1,0:T(8,128)(2,1)S(1)} %get-tuple-element.68.low.low_in.refs_1_, f32[8,256,256]{2,1,0:T(8,128)S(1)} %shard_map.74.y0, f32[2,256,256]{2,1,0:T(8,128)S(1)} %collective-permute-done.5.above), custom_call_target="tpu_custom_call" | custom-call | tf_op jit(solution)/shard_map/pallas_call | solution.py:591
  79.7 2.1 %collective-permute-done.18.swapped_ref = f32[1,648,256]{2,1,0:T(8,128)S(1)} collective-permute-done((f32[1,648,256]{2,1,0:T(8,128)S(1)}, f32[1,648,256]{2,1,0:T(8,128)S(1)}, u32[]{:S(2)}, u32[]{:S(2)}) %collective-permute-start.18) | collective-permute-done | bytes 663584 | tf_op jit(solution)/shard_map/ppermute | solution.py:733
  82.8 2.5 %shard_map.78 = (f32[3,256,256]{2,1,0:T(8,128)S(1)}, f32[2,256,128]{2,1,0:T(8,128)S(1)}, f32[2,256,128]{2,1,0:T(8,128)S(1)}, f32[2,256,128]{2,1,0:T(8,128)S(1)}, f32[2,256,128]{2,1,0:T(8,128)S(1)}) custom-call(bf16[8,256,768]{2,1,0:T(8,128)(2,1)S(1)} %get-tuple-element.67.high.high_in.refs_0_, bf16[8,256,768]{2,1,0:T(8,128)(2,1)S(1)} %get-tuple-element.68.low.low_in.refs_1_, ...), custom_call_target="tpu_custom_call" | custom-call | tf_op jit(solution)/shard_map/pallas_call | solution.py:603
  85.5 3.8 %collective-permute-start.20 = (f32[2,256,128]{2,1,0:T(8,128)S(1)}, f32[2,256,128]{2,1,0:T(8,128)S(1)}, u32[]{:S(2)}, u32[]{:S(2)}) collective-permute-start(f32[2,256,128]{2,1,0:T(8,128)S(1)} %get-tuple-element.80.refs_0_.y2_low.refs_7_), channel_id=1, source_target_pairs={{0,24},{4,28},{8,0},{12,4},{16,8},{20,12},{24,16},{28,20},{1,25},{... | collective-permute-start | bytes 786440 | tf_op jit(solution)/shard_map/ppermute | solution.py:738
  89.3 5.2 %shard_map.79 = (f32[4,256,256]{2,1,0:T(8,128)S(1)}, f32[4,256,256]{2,1,0:T(8,128)S(1)}, f32[2,256,256]{2,1,0:T(8,128)S(1)}) custom-call(s32[4]{0:T(128)S(1)} %pad_add_fusion.at_ref, bf16[8,256,768]{2,1,0:T(8,128)(2,1)S(1)} %get-tuple-element.67.high.high_in.refs_0_, bf16[8,256,768]{2,1,0:T(8,128)(2,1)S(1)} %get-tuple-element.68.low.low_in.refs_1_, ...), custom_call_target="tpu_custom_call" | custom-call | tf_op jit(solution)/shard_map/pallas_call | solution.py:615
  94.5 2.9 %collective-permute-start.25 = (f32[2,256,256]{2,1,0:T(8,128)S(1)}, f32[2,256,256]{2,1,0:T(8,128)S(1)}, u32[]{:S(2)}, u32[]{:S(2)}) collective-permute-start(f32[2,256,256]{2,1,0:T(8,128)S(1)} %get-tuple-element.86), channel_id=1, source_target_pairs={{0,4},{4,0},{8,12},{12,8},{16,20},{20,16},{24,28},{28,24},{1,5},{5... | collective-permute-start | bytes 1572872 | tf_op jit(solution)/shard_map/ppermute | solution.py:733
  97.4 3.8 %collective-permute-start.23 = (f32[2,256,128]{2,1,0:T(8,128)S(1)}, f32[2,256,128]{2,1,0:T(8,128)S(1)}, u32[]{:S(2)}, u32[]{:S(2)}) collective-permute-start(f32[2,256,128]{2,1,0:T(8,128)S(1)} %get-tuple-element.81.refs_1_.y2_low.refs_8_), channel_id=1, source_target_pairs={{0,24},{4,28},{8,0},{12,4},{16,8},{20,12},{24,16},{28,20},{1,25},{... | collective-permute-start | bytes 786440 | tf_op jit(solution)/shard_map/ppermute | solution.py:738
  101.2 1.6 %shard_map.80 = f32[2,256,128]{2,1,0:T(8,128)S(1)} custom-call(s32[4]{0:T(128)S(1)} %pad_add_fusion.at_ref, bf16[8,256,768]{2,1,0:T(8,128)(2,1)S(1)} %get-tuple-element.67.high.high_in.refs_0_, bf16[8,256,768]{2,1,0:T(8,128)(2,1)S(1)} %get-tuple-element.68.low.low_in.refs_1_, bf16[3,256,768]{2,1,0:T(8,128)(2,1)S(1)} %get-tuple-element.75.outer_high.refs_2_, ...), custom_call_target="tpu_custom_call" | custom-call | tf_op jit(solution)/shard_map/pallas_call | solution.py:631
  102.8 2.3 %collective-permute-start.21 = (f32[2,256,128]{2,1,0:T(8,128)S(1)}, f32[2,256,128]{2,1,0:T(8,128)S(1)}, u32[]{:S(2)}, u32[]{:S(2)}) collective-permute-start(f32[2,256,128]{2,1,0:T(8,128)S(1)} %shard_map.80), channel_id=1, source_target_pairs={{0,4},{4,0},{8,12},{12,8},{16,20},{20,16},{24,28},{28,24},{1,5},{5... | collective-permute-start | bytes 786440 | tf_op jit(solution)/shard_map/ppermute | solution.py:733
  105.1 3.3 %collective-permute-done.22.below.refs_12_ = f32[2,256,128]{2,1,0:T(8,128)S(1)} collective-permute-done((f32[2,256,128]{2,1,0:T(8,128)S(1)}, f32[2,256,128]{2,1,0:T(8,128)S(1)}, u32[]{:S(2)}, u32[]{:S(2)}) %collective-permute-start.22) | collective-permute-done | bytes 262176 | tf_op jit(solution)/shard_map/ppermute | solution.py:738
  108.4 2.4 %collective-permute-done.23.above.refs_14_ = f32[2,256,128]{2,1,0:T(8,128)S(1)} collective-permute-done((f32[2,256,128]{2,1,0:T(8,128)S(1)}, f32[2,256,128]{2,1,0:T(8,128)S(1)}, u32[]{:S(2)}, u32[]{:S(2)}) %collective-permute-start.23) | collective-permute-done | bytes 262176 | tf_op jit(solution)/shard_map/ppermute | solution.py:738
  110.9 1.6 %shard_map.81 = f32[2,256,128]{2,1,0:T(8,128)S(1)} custom-call(s32[4]{0:T(128)S(1)} %pad_add_fusion.at_ref, bf16[8,256,768]{2,1,0:T(8,128)(2,1)S(1)} %get-tuple-element.67.high.high_in.refs_0_, bf16[8,256,768]{2,1,0:T(8,128)(2,1)S(1)} %get-tuple-element.68.low.low_in.refs_1_, bf16[3,256,768]{2,1,0:T(8,128)(2,1)S(1)} %get-tuple-element.75.outer_high.refs_2_, ...), custom_call_target="tpu_custom_call" | custom-call | tf_op jit(solution)/shard_map/pallas_call | solution.py:631
  112.5 3.1 %collective-permute-start.24 = (f32[2,256,128]{2,1,0:T(8,128)S(1)}, f32[2,256,128]{2,1,0:T(8,128)S(1)}, u32[]{:S(2)}, u32[]{:S(2)}) collective-permute-start(f32[2,256,128]{2,1,0:T(8,128)S(1)} %shard_map.81), channel_id=1, source_target_pairs={{0,4},{4,0},{8,12},{12,8},{16,20},{20,16},{24,28},{28,24},{1,5},{5... | collective-permute-start | bytes 786440 | tf_op jit(solution)/shard_map/ppermute | solution.py:733
  115.6 2.3 %shard_map.82.own = f32[2,256,256]{2,1,0:T(8,128)S(1)} custom-call(s32[4]{0:T(128)S(1)} %pad_add_fusion.at_ref, bf16[8,256,768]{2,1,0:T(8,128)(2,1)S(1)} %get-tuple-element.67.high.high_in.refs_0_, bf16[8,256,768]{2,1,0:T(8,128)(2,1)S(1)} %get-tuple-element.68.low.low_in.refs_1_, bf16[3,256,768]{2,1,0:T(8,128)(2,1)S(1)} %get-tuple-element.75.outer_high.refs_2_, ...), custom_call_target="tpu_custom_call" | custom-call | tf_op jit(solution)/shard_map/pallas_call | solution.py:644
  117.9 1.7 %shard_map.83.refs_2_ = f32[4,256,512]{2,1,0:T(8,128)} custom-call(s32[4]{0:T(128)S(1)} %pad_add_fusion.at_ref, f32[4,256,256]{2,1,0:T(8,128)S(1)} %get-tuple-element.85.y4, f32[2,256,256]{2,1,0:T(8,128)S(1)} %shard_map.82.own, f32[2,256,256]{2,1,0:T(8,128)S(1)} %collective-permute-done.25.near), custom_call_target="tpu_custom_call" | custom-call | tf_op jit(solution)/shard_map/pallas_call | solution.py:708
  119.6 1.7 %collective-permute-done.24.refs_1_ = f32[2,256,128]{2,1,0:T(8,128)S(1)} collective-permute-done((f32[2,256,128]{2,1,0:T(8,128)S(1)}, f32[2,256,128]{2,1,0:T(8,128)S(1)}, u32[]{:S(2)}, u32[]{:S(2)}) %collective-permute-start.24) | collective-permute-done | bytes 262176 | tf_op jit(solution)/shard_map/ppermute | solution.py:733
  (48 shorter events, 14.5 us)
Async XLA Ops:
  0.1 0.7 copy-start
  0.8 8.6 %copy-start.1 = (f32[4,512]{1,0:T(4,128)S(1)}, f32[4,512]{1,0:T(4,128)}, u32[]{:S(2)}) copy-start(f32[4,512]{1,0:T(4,128)} %quad_ref.1) | copy-start | bytes 24580
  0.8 8.6 %copy-start.2 = (s32[4,64]{1,0:T(4,128)S(1)}, s32[4,64]{1,0:T(4,128)}, u32[]{:S(2)}) copy-start(s32[4,64]{1,0:T(4,128)} %pair_ref.3) | copy-start | bytes 3076
  2.8 15.5 %collective-permute-start = (f32[2,256,128]{2,1,0:T(8,128)S(1)}, f32[2,256,128]{2,1,0:T(8,128)S(1)}, u32[]{:S(2)}, u32[]{:S(2)}) collective-permute-start(f32[2,256,128]{2,1,0:T(8,128)S(1)} %get-tuple-element.48), channel_id=1, source_target_pairs={{0,4},{4,0},{8,12},{12,8},{16,20},{20,16},{24,28},{28,24},{1,5},{5... | collective-permute-start | bytes 786440 | tf_op jit(solution)/shard_map/ppermute | solution.py:733
  5.9 11.2 %collective-permute-start.1 = (f32[256,128]{1,0:T(8,128)S(1)}, f32[256,128]{1,0:T(8,128)S(1)}, u32[]{:S(2)}, u32[]{:S(2)}) collective-permute-start(f32[256,128]{1,0:T(8,128)S(1)} %get-tuple-element.50), channel_id=1, source_target_pairs={{0,28},{4,0},{8,4},{12,8},{16,12},{20,16},{24,20},{28,24},{1,29},{... | collective-permute-start | bytes 393224 | tf_op jit(solution)/shard_map/ppermute | solution.py:738
  18.3 2.4 %collective-permute-start.3 = (f32[2,392,256]{2,1,0:T(8,128)S(1)}, f32[2,392,256]{2,1,0:T(8,128)S(1)}, u32[]{:S(2)}, u32[]{:S(2)}) collective-permute-start(f32[2,392,256]{2,1,0:T(8,128)S(1)} %get-tuple-element.57), channel_id=1, source_target_pairs={{0,1},{1,0},{2,3},{3,2},{4,5},{5,4},{6,7},{7,6},{8,9},{9,8},{10,11... | collective-permute-start | bytes 2408456 | tf_op jit(solution)/shard_map/ppermute | solution.py:733
  21.3 11.4 %collective-permute-start.4 = (f32[1,392,256]{2,1,0:T(8,128)S(1)}, f32[1,392,256]{2,1,0:T(8,128)S(1)}, u32[]{:S(2)}, u32[]{:S(2)}) collective-permute-start(f32[1,392,256]{2,1,0:T(8,128)S(1)} %get-tuple-element.58), channel_id=1, source_target_pairs={{0,2},{1,3},{2,0},{3,1},{4,6},{5,7},{6,4},{7,5},{8,10},{9,11},{10,... | collective-permute-start | bytes 1204232 | tf_op jit(solution)/shard_map/ppermute | solution.py:733
  22.9 8.1 %collective-permute-start.2 = (f32[2,256,128]{2,1,0:T(8,128)S(1)}, f32[2,256,128]{2,1,0:T(8,128)S(1)}, u32[]{:S(2)}, u32[]{:S(2)}) collective-permute-start(f32[2,256,128]{2,1,0:T(8,128)S(1)} %get-tuple-element.55), channel_id=1, source_target_pairs={{0,4},{4,0},{8,12},{12,8},{16,20},{20,16},{24,28},{28,24},{1,5},{5... | collective-permute-start | bytes 786440 | tf_op jit(solution)/shard_map/ppermute | solution.py:733
  32.7 18.9 %collective-permute-start.5 = (f32[2,256,256]{2,1,0:T(8,128)S(1)}, f32[2,256,256]{2,1,0:T(8,128)S(1)}, u32[]{:S(2)}, u32[]{:S(2)}) collective-permute-start(f32[2,256,256]{2,1,0:T(8,128)S(1)} %shard_map.67), channel_id=1, source_target_pairs={{0,24},{4,28},{8,0},{12,4},{16,8},{20,12},{24,16},{28,20},{1,25},{... | collective-permute-start | bytes 1572872 | tf_op jit(solution)/shard_map/ppermute | solution.py:738
  34.5 17.1 %collective-permute-start.6 = (f32[1,392,256]{2,1,0:T(8,128)S(1)}, f32[1,392,256]{2,1,0:T(8,128)S(1)}, u32[]{:S(2)}, u32[]{:S(2)}) collective-permute-start(f32[1,392,256]{2,1,0:T(8,128)S(1)} %shard_map.69.refs_0_.mine_ref), channel_id=1, source_target_pairs={{0,2},{1,3},{2,0},{3,1},{4,6},{5,7},{6,4},{7,5},{8,10},{9,11},{10,... | collective-permute-start | bytes 1204232 | tf_op jit(solution)/shard_map/ppermute | solution.py:733
  36.1 15.6 %collective-permute-start.7 = (f32[1,392,256]{2,1,0:T(8,128)S(1)}, f32[1,392,256]{2,1,0:T(8,128)S(1)}, u32[]{:S(2)}, u32[]{:S(2)}) collective-permute-start(f32[1,392,256]{2,1,0:T(8,128)S(1)} %shard_map.69.refs_0_.mine_ref), channel_id=1, source_target_pairs={{0,4},{4,0},{8,12},{12,8},{16,20},{20,16},{24,28},{28,24},{1,5},{5... | collective-permute-start | bytes 1204232 | tf_op jit(solution)/shard_map/ppermute | solution.py:733
  36.4 15.2 %collective-permute-start.8 = (f32[2,256,128]{2,1,0:T(8,128)S(1)}, f32[2,256,128]{2,1,0:T(8,128)S(1)}, u32[]{:S(2)}, u32[]{:S(2)}) collective-permute-start(f32[2,256,128]{2,1,0:T(8,128)S(1)} %get-tuple-element.62), channel_id=1, source_target_pairs={{0,4},{4,0},{8,12},{12,8},{16,20},{20,16},{24,28},{28,24},{1,5},{5... | collective-permute-start | bytes 786440 | tf_op jit(solution)/shard_map/ppermute | solution.py:733
  52.5 12.6 %collective-permute-start.14 = (f32[1,648,256]{2,1,0:T(8,128)S(1)}, f32[1,648,256]{2,1,0:T(8,128)S(1)}, u32[]{:S(2)}, u32[]{:S(2)}) collective-permute-start(f32[1,648,256]{2,1,0:T(8,128)S(1)} %shard_map.72), channel_id=1, source_target_pairs={{0,24},{2,26},{5,13},{7,15},{8,0},{10,2},{13,21},{15,23},{16,8},{1... | collective-permute-start | bytes 1990664 | tf_op jit(solution)/shard_map/ppermute | solution.py:789
  54.8 12.5 %collective-permute-start.11 = (f32[1,392,256]{2,1,0:T(8,128)S(1)}, f32[1,392,256]{2,1,0:T(8,128)S(1)}, u32[]{:S(2)}, u32[]{:S(2)}) collective-permute-start(f32[1,392,256]{2,1,0:T(8,128)S(1)} %shard_map.69.refs_0_.mine_ref), channel_id=1, source_target_pairs={{0,1},{1,0},{2,3},{3,2},{4,5},{5,4},{6,7},{7,6},{8,9},{9,8},{10,11... | collective-permute-start | bytes 1204232 | tf_op jit(solution)/shard_map/ppermute | solution.py:733
  54.9 12.9 %collective-permute-start.9 = (f32[1,392,256]{2,1,0:T(8,128)S(1)}, f32[1,392,256]{2,1,0:T(8,128)S(1)}, u32[]{:S(2)}, u32[]{:S(2)}) collective-permute-start(f32[1,392,256]{2,1,0:T(8,128)S(1)} %collective-permute-done.7.refs_3_), channel_id=1, source_target_pairs={{0,2},{1,3},{2,0},{3,1},{4,6},{5,7},{6,4},{7,5},{8,10},{9,11},{10,... | collective-permute-start | bytes 1204232 | tf_op jit(solution)/shard_map/ppermute | solution.py:733
  55.5 10.9 %collective-permute-start.15 = (f32[2,256,128]{2,1,0:T(8,128)S(1)}, f32[2,256,128]{2,1,0:T(8,128)S(1)}, u32[]{:S(2)}, u32[]{:S(2)}) collective-permute-start(f32[2,256,128]{2,1,0:T(8,128)S(1)} %get-tuple-element.69), channel_id=1, source_target_pairs={{0,4},{4,0},{8,12},{12,8},{16,20},{20,16},{24,28},{28,24},{1,5},{5... | collective-permute-start | bytes 786440 | tf_op jit(solution)/shard_map/ppermute | solution.py:733
  65.0 14.5 %collective-permute-start.17 = (f32[1,648,256]{2,1,0:T(8,128)S(1)}, f32[1,648,256]{2,1,0:T(8,128)S(1)}, u32[]{:S(2)}, u32[]{:S(2)}) collective-permute-start(f32[1,648,256]{2,1,0:T(8,128)S(1)} %collective-permute-done.14.first_ref), channel_id=1, source_target_pairs={{0,4},{2,6},{5,1},{7,3},{8,12},{10,14},{13,9},{15,11},{16,20},{18,... | collective-permute-start | bytes 1990664 | tf_op jit(solution)/shard_map/ppermute | solution.py:790
  67.0 12.5 %collective-permute-start.16 = (f32[2,256,256]{2,1,0:T(8,128)S(1)}, f32[2,256,256]{2,1,0:T(8,128)S(1)}, u32[]{:S(2)}, u32[]{:S(2)}) collective-permute-start(f32[2,256,256]{2,1,0:T(8,128)S(1)} %shard_map.73), channel_id=1, source_target_pairs={{0,8},{4,12},{8,16},{12,20},{16,24},{20,28},{24,0},{28,4},{1,9},{5... | collective-permute-start | bytes 1572872 | tf_op jit(solution)/shard_map/ppermute | solution.py:738
  67.3 1.7 %collective-permute-start.12 = (f32[1,392,256]{2,1,0:T(8,128)S(1)}, f32[1,392,256]{2,1,0:T(8,128)S(1)}, u32[]{:S(2)}, u32[]{:S(2)}) collective-permute-start(f32[1,392,256]{2,1,0:T(8,128)S(1)} %collective-permute-done.6.refs_2_.beside_ref), channel_id=1, source_target_pairs={{0,1},{1,0},{2,3},{3,2},{4,5},{5,4},{6,7},{7,6},{8,9},{9,8},{10,11... | collective-permute-start | bytes 1204232 | tf_op jit(solution)/shard_map/ppermute | solution.py:733
  67.3 2.3 %collective-permute-start.13 = (f32[1,392,256]{2,1,0:T(8,128)S(1)}, f32[1,392,256]{2,1,0:T(8,128)S(1)}, u32[]{:S(2)}, u32[]{:S(2)}) collective-permute-start(f32[1,392,256]{2,1,0:T(8,128)S(1)} %collective-permute-done.7.refs_3_), channel_id=1, source_target_pairs={{0,1},{1,0},{2,3},{3,2},{4,5},{5,4},{6,7},{7,6},{8,9},{9,8},{10,11... | collective-permute-start | bytes 1204232 | tf_op jit(solution)/shard_map/ppermute | solution.py:733
  67.8 6.8 %collective-permute-start.10 = (f32[1,392,256]{2,1,0:T(8,128)S(1)}, f32[1,392,256]{2,1,0:T(8,128)S(1)}, u32[]{:S(2)}, u32[]{:S(2)}) collective-permute-start(f32[1,392,256]{2,1,0:T(8,128)S(1)} %collective-permute-done.9.refs_0_), channel_id=1, source_target_pairs={{0,1},{1,0},{2,3},{3,2},{4,5},{5,4},{6,7},{7,6},{8,9},{9,8},{10,11... | collective-permute-start | bytes 1204232 | tf_op jit(solution)/shard_map/ppermute | solution.py:733
  79.6 2.2 %collective-permute-start.18 = (f32[1,648,256]{2,1,0:T(8,128)S(1)}, f32[1,648,256]{2,1,0:T(8,128)S(1)}, u32[]{:S(2)}, u32[]{:S(2)}) collective-permute-start(f32[1,648,256]{2,1,0:T(8,128)S(1)} %shard_map.76.kept_ref), channel_id=1, source_target_pairs={{0,1},{1,0},{2,3},{3,2},{4,5},{5,4},{6,7},{7,6},{8,9},{9,8},{10,11... | collective-permute-start | bytes 1990664 | tf_op jit(solution)/shard_map/ppermute | solution.py:733
  85.4 15.8 %collective-permute-start.19 = (f32[2,256,128]{2,1,0:T(8,128)S(1)}, f32[2,256,128]{2,1,0:T(8,128)S(1)}, u32[]{:S(2)}, u32[]{:S(2)}) collective-permute-start(f32[2,256,128]{2,1,0:T(8,128)S(1)} %get-tuple-element.82.refs_2_.y2_high.refs_9_), channel_id=1, source_target_pairs={{0,8},{4,12},{8,16},{12,20},{16,24},{20,28},{24,0},{28,4},{1,9},{5... | collective-permute-start | bytes 786440 | tf_op jit(solution)/shard_map/ppermute | solution.py:738
  85.5 15.8 %collective-permute-start.20 = (f32[2,256,128]{2,1,0:T(8,128)S(1)}, f32[2,256,128]{2,1,0:T(8,128)S(1)}, u32[]{:S(2)}, u32[]{:S(2)}) collective-permute-start(f32[2,256,128]{2,1,0:T(8,128)S(1)} %get-tuple-element.80.refs_0_.y2_low.refs_7_), channel_id=1, source_target_pairs={{0,24},{4,28},{8,0},{12,4},{16,8},{20,12},{24,16},{28,20},{1,25},{... | collective-permute-start | bytes 786440 | tf_op jit(solution)/shard_map/ppermute | solution.py:738
  94.5 23.4 %collective-permute-start.25 = (f32[2,256,256]{2,1,0:T(8,128)S(1)}, f32[2,256,256]{2,1,0:T(8,128)S(1)}, u32[]{:S(2)}, u32[]{:S(2)}) collective-permute-start(f32[2,256,256]{2,1,0:T(8,128)S(1)} %get-tuple-element.86), channel_id=1, source_target_pairs={{0,4},{4,0},{8,12},{12,8},{16,20},{20,16},{24,28},{28,24},{1,5},{5... | collective-permute-start | bytes 1572872 | tf_op jit(solution)/shard_map/ppermute | solution.py:733
  97.4 11.0 %collective-permute-start.22 = (f32[2,256,128]{2,1,0:T(8,128)S(1)}, f32[2,256,128]{2,1,0:T(8,128)S(1)}, u32[]{:S(2)}, u32[]{:S(2)}) collective-permute-start(f32[2,256,128]{2,1,0:T(8,128)S(1)} %get-tuple-element.83.refs_3_.y2_high.refs_10_), channel_id=1, source_target_pairs={{0,8},{4,12},{8,16},{12,20},{16,24},{20,28},{24,0},{28,4},{1,9},{5... | collective-permute-start | bytes 786440 | tf_op jit(solution)/shard_map/ppermute | solution.py:738
  97.4 13.5 %collective-permute-start.23 = (f32[2,256,128]{2,1,0:T(8,128)S(1)}, f32[2,256,128]{2,1,0:T(8,128)S(1)}, u32[]{:S(2)}, u32[]{:S(2)}) collective-permute-start(f32[2,256,128]{2,1,0:T(8,128)S(1)} %get-tuple-element.81.refs_1_.y2_low.refs_8_), channel_id=1, source_target_pairs={{0,24},{4,28},{8,0},{12,4},{16,8},{20,12},{24,16},{28,20},{1,25},{... | collective-permute-start | bytes 786440 | tf_op jit(solution)/shard_map/ppermute | solution.py:738
  102.8 16.8 %collective-permute-start.21 = (f32[2,256,128]{2,1,0:T(8,128)S(1)}, f32[2,256,128]{2,1,0:T(8,128)S(1)}, u32[]{:S(2)}, u32[]{:S(2)}) collective-permute-start(f32[2,256,128]{2,1,0:T(8,128)S(1)} %shard_map.80), channel_id=1, source_target_pairs={{0,4},{4,0},{8,12},{12,8},{16,20},{20,16},{24,28},{28,24},{1,5},{5... | collective-permute-start | bytes 786440 | tf_op jit(solution)/shard_map/ppermute | solution.py:733
  112.5 8.8 %collective-permute-start.24 = (f32[2,256,128]{2,1,0:T(8,128)S(1)}, f32[2,256,128]{2,1,0:T(8,128)S(1)}, u32[]{:S(2)}, u32[]{:S(2)}) collective-permute-start(f32[2,256,128]{2,1,0:T(8,128)S(1)} %shard_map.81), channel_id=1, source_target_pairs={{0,4},{4,0},{8,12},{12,8},{16,20},{20,16},{24,28},{28,24},{1,5},{5... | collective-permute-start | bytes 786440 | tf_op jit(solution)/shard_map/ppermute | solution.py:733
